TPU v7x, 32 devices: a whole 2x2x4 slice. The times are simulated.
32 devices in a mesh: head: 4 (over z), shard: 8 (over y, x, core).
Axes of the slice: x: 2, y: 2, z: 4, core: 2. Of those that a mesh axis runs over, the one named last changes fastest.
Arguments:
- tokens: bfloat16 [16384, 768], P(('head', 'shard')), may hold values from -6 to 6
- norm_gain: bfloat16 [768], P('shard'), may hold values from 0.5 to 1.5
- in_weight: bfloat16 [768, 3352], P('shard'), may hold values from -0.21875 to 0.21875
- conv_weight: float32 [4, 1792], replicated, may hold values from -3 to 3
- conv_bias: float32 [1792], replicated, may hold values from -2 to 2
- dt_bias: float32 [24], replicated, may hold values from -4.6 to -2.3
- a_log: float32 [24], replicated, may hold values from -8 to 2.77
- d_skip: float32 [24], replicated, may hold values from 0.5 to 1.5
- inner_gain: float32 [1536], replicated, may hold values from 0.5 to 1.5
- out_weight: bfloat16 [1536, 768], P('shard'), may hold values from -0.15625 to 0.15625
- block_place: int32 [8, 8], P('shard'), may hold values from 0 to 7, each once within a row
- seq_length: int32 [8, 1], P('shard'), may hold values from 1793 to 2048, as said below
- cotangent: bfloat16 [16384, 768], P(('head', 'shard')), may hold values from -6 to 6
Outputs:
- mixed: bfloat16 [16384, 768], P(('head', 'shard'))
- token_grad: bfloat16 [16384, 768], P(('head', 'shard'))
- norm_gain_grad: float32 [768], P('shard')
- in_weight_grad: float32 [768, 3352], P('shard')
- conv_weight_grad: float32 [4, 1792], replicated
- conv_bias_grad: float32 [1792], replicated
- dt_bias_grad: float32 [24], replicated
- a_log_grad: float32 [24], replicated
- d_skip_grad: float32 [24], replicated
- inner_gain_grad: float32 [1536], replicated
- out_weight_grad: float32 [1536, 768], P('shard')
Inputs may be any that keep to these rules, and one draw needn't show every extreme that they name: `block_place`: each row is a permutation of the group's 8 blocks. `seq_length`: A group's 1 sequence, each padded up to whole blocks of 256 tokens, fill exactly 8 blocks; each takes 4 blocks or more.
All inputs are finite; a program needn't handle non-finite values.
Results may differ from a plain program's by a relative error of at most 0.017.
Values may be sent and summed in bfloat16 or wider, within the bound.
No kernel may reach another device: no remote copies, remote signals or barrier semaphores. Data moves between devices by JAX's collectives and lax.ppermute only.
A program may use at most 192 MiB of HBM per device.

v0:
```python
import functools

import jax
import jax.numpy as jnp
from jax import lax
from jax.experimental import pallas as pl
from jax.experimental.pallas import tpu as pltpu
from jax.sharding import PartitionSpec as P

NH = 24
HD = 64
NS = 128
KC = 4
CH = 256
DI = 1536
DM = 768
XBC = DI + 2 * NS
WA = 1920
HALO = 8
EPSILON = 1e-05
F32 = jnp.float32
BF = jnp.bfloat16
LANES = 128
CW = 384
NCW = DI // CW
VMEM_ASK = 56 * 2**20


def trade(value, axis, bit):
    size = lax.axis_size(axis)
    return lax.ppermute(value, axis, [(i, i ^ bit) for i in range(size)])


def after(value, *others):
    return lax.optimization_barrier((value,) + others)[0]


def move_home(value):
    n_head, n_shard = lax.axis_size("head"), lax.axis_size("shard")
    half = n_head // 2
    pairs = []
    for h in range(n_head):
        for s in range(n_shard):
            upper, core = h // half, s & 1
            if upper != core:
                there = (h % half + core * half) * n_shard + (s - core + upper)
                pairs.append((h * n_shard + s, there))
    return lax.ppermute(value, ("head", "shard"), pairs)


def swap_home(value, stay):
    return jnp.where(stay, value, move_home(value))


def group_spread(value, stay):
    n_head, n_shard = lax.axis_size("head"), lax.axis_size("shard")
    half = n_head // 2
    pieces = [swap_home(value, stay)]
    for core in (0, 1):
        for low in range(half):
            if core or low:
                pairs = []
                for h in range(n_head):
                    for s in range(n_shard):
                        there = (h % half ^ low) + (s & 1) * half
                        pairs.append((h * n_shard + s, there * n_shard + (s - (s & 1) + (h // half ^ core))))
                pieces.append(lax.ppermute(value, ("head", "shard"), pairs))
    return pieces


def group_gather(value):
    half = lax.axis_size("head") // 2
    pieces = [value]
    bit = 1
    while bit < half:
        pieces = pieces + [trade(v, "head", bit) for v in pieces]
        bit *= 2
    return pieces + [trade(v, "shard", 1) for v in pieces]


def gather_pieces(piece):
    n_shard = lax.axis_size("shard")
    if n_shard != 8:
        held = {0: piece}
        bit = 1
        while bit < n_shard:
            held.update({k ^ bit: trade(v, "shard", bit) for k, v in list(held.items())})
            bit *= 2
        return [(v, k, None) for k, v in held.items()]

    def from_core(value, core, bit):
        return lax.ppermute(value, "shard", [(i, i ^ bit) for i in range(n_shard) if i % 2 == core])

    by_x, by_y, by_core = trade(piece, "shard", 2), trade(piece, "shard", 4), trade(piece, "shard", 1)
    far_0, far_1 = from_core(by_x, 0, 4), from_core(by_y, 1, 2)
    return [
        (piece, 0, None), (by_core, 1, None), (by_x, 2, None), (by_y, 4, None),
        (trade(by_x, "shard", 1), 3, None), (trade(by_y, "shard", 1), 5, None),
        (far_0, 6, 0), (far_1, 6, 1),
        (from_core(far_0, 0, 1), 7, 1), (from_core(far_1, 1, 1), 7, 0),
    ]


def head_pieces(value):
    pieces = [value]
    bit = 1
    while bit < lax.axis_size("head") // 2:
        pieces = pieces + [trade(v, "head", bit) for v in pieces]
        bit *= 2
    return pieces[1:]


def core_give(blocks):
    n_shard = lax.axis_size("shard")
    core = lax.axis_index("shard") % 2

    def half(which):
        parts = []
        for v in blocks:
            split = v.reshape((n_shard // 2, 2) + v.shape[1:])
            parts.append(lax.dynamic_index_in_dim(split, which, 1, False))
        return jnp.concatenate(parts, axis=2) if len(parts) > 1 else parts[0]

    return half(core), half(1 - core)


def chip_pairs(keep, got):
    pair = (keep.astype(F32) + got.astype(F32)).astype(BF)
    chip = lax.axis_index("shard") // 2
    return [lax.dynamic_index_in_dim(pair, chip ^ k, 0, False) for k in range(pair.shape[0])]


def chip_send(pairs):
    return [trade(v, "shard", 2 * k) for k, v in enumerate(pairs) if k]


def chip_sum(own, got):
    total = own.astype(F32)
    for v in got:
        total = total + v.astype(F32)
    return total.astype(BF)


def head_sum(value):
    cut = value.shape[1] // 2 // LANES * LANES
    bits = [b for b in (1, 2, 4, 8, 16) if b < lax.axis_size("head")]
    done = []
    for part, order in ((value[:, :cut], bits), (value[:, cut:], bits[::-1])):
        total = part.astype(F32)
        for bit in order:
            low = total.astype(BF)
            total = low.astype(F32) + trade(low, "head", bit).astype(F32)
        done.append(total)
    return jnp.concatenate(done, axis=1)


def full_sum(value):
    for axis in ("shard", "head"):
        bit = 1
        while bit < lax.axis_size(axis):
            value = value + trade(value, axis, bit)
            bit *= 2
    return value


def dot(a, b):
    return jnp.dot(a, b, preferred_element_type=F32)


def dot_nt(a, b):
    return lax.dot_general(a, b, (((1,), (1,)), ((), ())), preferred_element_type=F32)


def dot_tn(a, b):
    return lax.dot_general(a, b, (((0,), (0,)), ((), ())), preferred_element_type=F32)


def spread_table():
    row = jnp.arange(2 * LANES)[:, None] % LANES
    return (row == jnp.arange(DI)[None, :] // HD).astype(BF)


def pieces2(v):
    hi = v.astype(BF)
    return hi, (v - hi.astype(F32)).astype(BF)


def pieces3(v):
    hi = v.astype(BF)
    rest = v - hi.astype(F32)
    mid = rest.astype(BF)
    return hi, mid, (rest - mid.astype(F32)).astype(BF)


def softplus(v):
    return jnp.maximum(v, 0.0) + jnp.log1p(jnp.exp(-jnp.abs(v)))


sigmoid = jax.nn.sigmoid


def shape(dims, dtype):
    return jax.ShapeDtypeStruct(dims, dtype)


def whole(arr):
    return pl.BlockSpec(arr.shape, lambda *g: (0,) * len(arr.shape))


def columns(arr, at, width=None):
    dims = arr.shape[:-1] + (width or CW,)
    return pl.BlockSpec(dims, lambda *g: (0,) * (len(dims) - 1) + (at(*g),))


def in_hbm():
    return pl.BlockSpec(memory_space=pl.ANY)


def in_smem():
    return pl.BlockSpec(memory_space=pltpu.SMEM)


def call(kernel, grid, ins, outs, scratch, flops):
    moved = sum(a.size * a.dtype.itemsize for a, _ in ins)
    moved += sum(o.size * o.dtype.itemsize for o, _ in outs)
    return pl.pallas_call(
        kernel,
        grid=grid,
        out_shape=[o for o, _ in outs],
        in_specs=[s for _, s in ins],
        out_specs=[s for _, s in outs],
        scratch_shapes=scratch,
        compiler_params=pltpu.CompilerParams(vmem_limit_bytes=VMEM_ASK),
        cost_estimate=pl.CostEstimate(flops=flops, bytes_accessed=moved, transcendentals=0),
    )(*[a for a, _ in ins])


def iota(dims, axis):
    return lax.broadcasted_iota(jnp.int32, dims, axis)


def place_of(info, q):
    return info[2 + 3 * q]


def first_of(info, q):
    return info[3 + 3 * q]


def usable_of(info, i):
    begin = (place_of(info, i) - first_of(info, i)) * CH
    return (iota((CH, 1), 0) + begin < info[4 + 3 * i]).astype(F32)


def halo_used(info, i):
    has_prev = place_of(info, i) > first_of(info, i)
    return (iota((HALO, 1), 0) + jnp.where(has_prev, 0, -HALO) > HALO - KC).astype(F32)


def clast_rows(refs, nb):
    rows = []
    for ref in refs:
        for b in range(nb):
            part = ref[b].astype(F32)
            rows.append(part[0:1, :] + part[1:2, :] + part[2:3, :])
    return rows


def carry_weights(info, ends, nb, into):
    n_all = len(ends)
    row = iota((n_all, 1), 0)
    place = jnp.zeros((n_all, 1), jnp.int32)
    first = jnp.zeros((n_all, 1), jnp.int32)
    for j in range(n_all):
        place = jnp.where(row == j, place_of(info, j), place)
        first = jnp.where(row == j, first_of(info, j), first)
    parts = []
    for i in range(nb):
        own = place_of(info, i)
        total = jnp.zeros((n_all, LANES), F32)
        for k in range(n_all):
            at = place_of(info, k)
            if into:
                between = (place > at) & (at > own)
            else:
                between = (place < at) & (at < own)
            total = total + jnp.where(between, ends[k], 0.0)
        if into:
            reach = (first <= own) & (place > own)
        else:
            reach = (place >= first_of(info, i)) & (place < own)
        parts.append(jnp.where(reach, jnp.exp(total), 0.0))
    return jnp.concatenate(pieces2(jnp.concatenate(parts, axis=0)), axis=1)


def normal_rows(rows, gain):
    f = rows.astype(F32)
    inv = lax.rsqrt(jnp.sum(f * f, axis=1, keepdims=True) / DM + EPSILON)
    return (f * inv * gain).astype(BF)


def project_kernel(layout, n_halo, *refs):
    info = refs[0]
    pieces = refs[1 : 1 + len(layout)]
    halos = refs[1 + len(layout) : 1 + len(layout) + n_halo]
    (
        tok_own, tok_got, conv_w, conv_b, dt_bias, a_log, table,
        wa_out, tok, tok_halo, normal, xbc, slope, xs, xt, bs, cs, raw, cum, cum_t, states,
        wa, ext, small, sems, out_sem,
    ) = refs[1 + len(layout) + n_halo :]
    step = pl.program_id(0)
    rows = tok_own.shape[0]
    nb = rows // CH
    me = info[0]

    def project(at, width):
        proj = dot(normal[...], wa[:, pl.ds(at, width)]).astype(BF).astype(F32)
        acts, heads = [], []
        for i in range(nb):
            head = proj[rows + i * HALO : rows + (i + 1) * HALO, :] * halo_used(info, i)
            body = proj[i * CH : (i + 1) * CH, :] * usable_of(info, i)
            heads.append(head)
            ext[i, :HALO, :width] = head
            ext[i, HALO:, :width] = body
            xbc[i * CH : (i + 1) * CH, :width] = body.astype(BF)
            pre = conv_b[:, pl.ds(at, width)]
            for lag in range(KC):
                tap = conv_w[KC - 1 - lag : KC - lag, pl.ds(at, width)]
                pre = pre + tap * ext[i, HALO - lag : HALO - lag + CH, :width]
            sg = sigmoid(pre)
            act = pre * sg
            slope[i * CH : (i + 1) * CH, :width] = (sg + act * (1.0 - sg)).astype(BF)
            acts.append(act)
        xbc[rows:, :width] = jnp.concatenate(heads, axis=0).astype(BF)
        return acts

    def out_copy():
        return pltpu.make_async_copy(wa, wa_out, out_sem)

    @pl.when(step == 0)
    def _():
        def copy_of(n):
            offset, core = layout[n]
            at = pl.multiple_of((me ^ offset) * pieces[n].shape[0], 16)
            return pltpu.make_async_copy(
                pieces[n], wa.at[pl.ds(at, pieces[n].shape[0]), :], sems.at[n]
            )

        for n, (offset, core) in enumerate(layout):
            if core is None:
                copy_of(n).start()
            else:
                pl.when(me % 2 == core)(lambda n=n: copy_of(n).start())
        stay = info[1] > 0
        tok[...] = jnp.where(stay, tok_own[...], tok_got[...])
        found = []
        for i in range(nb):
            own, has_prev = place_of(info, i), place_of(info, i) > first_of(info, i)
            total = jnp.zeros((HALO, DM), F32)
            for o in range(n_halo):
                part = halos[o][...].astype(F32)
                for b in range(nb):
                    hit = (place_of(info, o * nb + b) == own - 1) & has_prev
                    total = total + jnp.where(hit, part[b * HALO : (b + 1) * HALO, :], 0.0)
            found.append(total)
        tok_halo[...] = jnp.concatenate(found, axis=0).astype(BF)
        for n, (offset, core) in enumerate(layout):
            if core is None:
                copy_of(n).wait()
            else:
                pl.when(me % 2 == core)(lambda n=n: copy_of(n).wait())
        out_copy().start()
        gain = wa[:, XBC : XBC + LANES].astype(F32).T[NH : NH + 1, :]
        normal[:rows, :] = normal_rows(tok[...], gain)
        normal[rows:, :] = normal_rows(tok_halo[...], gain)
        for i, act in enumerate(project(DI, 2 * NS)):
            bs[i * CH : (i + 1) * CH, :] = act[:, :NS].astype(BF)
            cs[i * CH : (i + 1) * CH, :] = act[:, NS:].astype(BF)
        xbc[:, 2 * NS :] = jnp.zeros((xbc.shape[0], CW - 2 * NS), BF)
        slope[:, 2 * NS :] = jnp.zeros((rows, CW - 2 * NS), BF)
        first = dot(normal[:rows, :], wa[:, XBC : XBC + LANES]).astype(BF).astype(F32) + dt_bias[...]
        raw[...] = first
        dt_all = softplus(first)
        rate = jnp.exp(a_log[...])
        causal = (iota((CH, CH), 0) >= iota((CH, CH), 1)).astype(F32).astype(BF)
        states[:, :, DI:] = jnp.zeros((nb, NS, LANES), BF)
        for i in range(nb):
            dt = dt_all[i * CH : (i + 1) * CH, :]
            parts = dot(causal, jnp.concatenate(pieces3(-dt * rate), axis=1))
            run = parts[:, :LANES] + parts[:, LANES : 2 * LANES] + parts[:, 2 * LANES :]
            cum[i * CH : (i + 1) * CH, :] = run
            cum_t[:, i * CH : (i + 1) * CH] = run.T
            last = run[CH - 1 : CH, :]
            ends = jnp.concatenate(pieces3(last) + (jnp.zeros((13, LANES), BF),), axis=0)
            states[i, :16, DI:] = ends
            small[i, 0] = jnp.concatenate(pieces2(dt), axis=1)
            small[i, 1] = jnp.concatenate(pieces2(jnp.exp(last - run) * dt), axis=1)

    @pl.when(step > 0)
    def _():
        at = pl.multiple_of((step - 1) * CW, CW)
        for i, act in enumerate(project(at, CW)):
            r = slice(i * CH, (i + 1) * CH)
            xs[r, :] = act.astype(BF)
            xt[r, :] = (act * dot(small[i, 0], table[...])).astype(BF)
            weighted = (act * dot(small[i, 1], table[...])).astype(BF)
            states[i, :, pl.ds(at, CW)] = dot_tn(bs[r, :], weighted).astype(BF)

    @pl.when(step == NCW)
    def _():
        out_copy().wait()


def run_project(info, parts, halos, tok_own, tok_got, conv_w, conv_b, dt_bias, a_log, table):
    rows = tok_own.shape[0]
    nb = rows // CH
    ext_rows = rows + nb * HALO
    layout = [(offset, core) for _, offset, core in parts]

    def before(s):
        return jnp.maximum(s - 1, 0)

    def tail_first(s):
        return jnp.where(s == 0, NCW, s - 1)

    ins = [(info, in_smem())] + [(v, in_hbm()) for v, _, _ in parts]
    ins += [(v, whole(v)) for v in halos]
    ins += [(v, whole(v)) for v in (tok_own, tok_got, conv_w, conv_b, dt_bias, a_log)]
    ins += [(table, columns(table, before))]
    outs = {
        "wa": (shape((DM, WA), BF), in_hbm()),
        "tok": (shape((rows, DM), BF), whole),
        "tok_halo": (shape((nb * HALO, DM), BF), whole),
        "normal": (shape((ext_rows, DM), BF), whole),
        "xbc": (shape((ext_rows, WA), BF), lambda v: columns(v, tail_first)),
        "slope": (shape((rows, WA), BF), lambda v: columns(v, tail_first)),
        "xs": (shape((rows, DI), BF), lambda v: columns(v, before)),
        "xt": (shape((rows, DI), BF), lambda v: columns(v, before)),
        "bs": (shape((rows, NS), BF), whole),
        "cs": (shape((rows, NS), BF), whole),
        "raw": (shape((rows, LANES), F32), whole),
        "cum": (shape((rows, LANES), F32), whole),
        "cum_t": (shape((LANES, rows), F32), whole),
        "states": (shape((nb, NS, DI + LANES), BF), whole),
    }
    out_list = [(o, s(o) if callable(s) else s) for o, s in outs.values()]
    scratch = [
        pltpu.VMEM((DM, WA), BF), pltpu.VMEM((nb, HALO + CH, CW), F32),
        pltpu.VMEM((nb, 2, CH, 2 * LANES), BF), pltpu.SemaphoreType.DMA((len(parts),)),
        pltpu.SemaphoreType.DMA,
    ]
    got = call(
        functools.partial(project_kernel, layout, len(halos)), (NCW + 1,), ins, out_list, scratch,
        2 * ext_rows * DM * WA * 2,
    )
    return dict(zip(outs, got))


PER = CW // HD
HALF = CH // 2


def chunk_heads(cum, first):
    return pltpu.roll(cum, lax.rem(LANES - first, LANES), axis=1)


def intra_kernel(bs, cs, xt, cum, cum_t, out, scores):
    c = pl.program_id(0)
    nb = bs.shape[0] // CH
    low = iota((CH, LANES), 1) < HD
    keep = iota((HALF, HALF), 0) >= iota((HALF, HALF), 1)

    @pl.when(c == 0)
    def _():
        for i in range(nb):
            r = slice(i * CH, (i + 1) * CH)
            scores[i] = dot_nt(cs[r, :], bs[r, :])

    for i in range(nb):
        r = slice(i * CH, (i + 1) * CH)
        cols = chunk_heads(cum[r, :], c * PER)
        for p in range(PER // 2):
            lanes = slice(p * LANES, (p + 1) * LANES)
            both = xt[r, lanes]
            got = []
            for k in range(2):
                h = 2 * p + k
                col = cols[:, h : h + 1]
                row = cum_t[pl.ds(c * PER + h, 1), r]
                a, b = col[:HALF], col[HALF:]
                s, t = row[:, :HALF], row[:, HALF:]
                upper = jnp.where(keep, jnp.exp(a - s), 0.0) * scores[i, :HALF, :HALF]
                left = jnp.exp(b - s) * scores[i, HALF:, :HALF]
                right = jnp.where(keep, jnp.exp(b - t), 0.0) * scores[i, HALF:, HALF:]
                lower = jnp.concatenate([left.astype(BF), right.astype(BF)], axis=1)
                got.append(
                    jnp.concatenate([dot(upper.astype(BF), both[:HALF, :]), dot(lower, both)], axis=0)
                )
            out[r, lanes] = jnp.where(low, got[0], got[1])


def middle_kernel(
    bs, cs, xt, cum, cum_t, normal, cot, zo_z, zo_o, out, z, q, wz, wo, scores
):
    wz[...] = zo_z[...]
    z[...] = dot(normal[...], zo_z[...]).astype(BF)
    unit_rows = zo_o.shape[0] // 2
    parts = []
    for k in range(2):
        block = zo_o[k * unit_rows : (k + 1) * unit_rows, :]
        parts += [block[:, :DM], block[:, DM:]]
    rows_o = jnp.concatenate(parts, axis=0)
    wo[...] = rows_o
    q[...] = dot_nt(cot[...], rows_o).astype(BF)
    intra_kernel(bs, cs, xt, cum, cum_t, out, scores)


def run_middle(a, cot, zo):
    rows = cot.shape[0]
    nb = rows // CH

    def same(c):
        return c

    ins = [(a[k], whole(a[k])) for k in ("bs", "cs")]
    ins += [(a["xt"], columns(a["xt"], same))]
    ins += [(a[k], whole(a[k])) for k in ("cum", "cum_t")]
    ins += [(a["normal"], pl.BlockSpec((rows, DM), lambda c: (0, 0))), (cot, whole(cot))]
    ins += [(zo, columns(zo, same)), (zo, pl.BlockSpec((DM // NCW, DI), lambda c: (c, 1)))]
    wide, wide_f = shape((rows, DI), BF), shape((rows, DI), F32)
    wz, wo = shape((DM, DI), BF), shape((DI, DM), BF)
    outs = [(v, columns(v, same)) for v in (wide_f, wide, wide, wz)]
    outs += [(wo, pl.BlockSpec((CW, DM), lambda c: (c, 0)))]
    return call(
        middle_kernel, (NCW,), ins, outs, [pltpu.VMEM((nb, CH, CH), F32)],
        2 * rows * CH * DI * 2 + 4 * rows * DM * DI,
    )


def run_intra(a):
    rows = a["bs"].shape[0]
    nb = rows // CH
    ins = [(a[k], whole(a[k])) for k in ("bs", "cs")]
    ins += [(a["xt"], columns(a["xt"], lambda c: c))]
    ins += [(a[k], whole(a[k])) for k in ("cum", "cum_t")]
    out = shape((rows, DI), F32)
    return call(
        intra_kernel, (NCW,), ins, [(out, columns(out, lambda c: c))],
        [pltpu.VMEM((nb, CH, CH), F32)], 2 * rows * CH * DI * 2,
    )[0]


def terms_kernel(normal, dz, normed, cot, out):
    c = pl.program_id(0)
    out[:, pl.ds(pl.multiple_of(c * CW, CW), CW)] = dot_tn(normal[...], dz[...]).astype(BF)
    part = dot_tn(normed[...], cot[...]).astype(BF)
    unit_rows = CW // 4
    for k in range(2):
        at = pl.multiple_of((2 * c + k) * unit_rows, unit_rows)
        for j in range(2):
            rows = part[(2 * k + j) * unit_rows : (2 * k + j + 1) * unit_rows, :]
            out[pl.ds(at, unit_rows), DI + j * DM : DI + (j + 1) * DM] = rows


def run_terms(normal, dz, normed, cot):
    rows = dz.shape[0]

    def same(c):
        return c

    out = shape((DM, DI + 2 * DM), BF)
    return call(
        terms_kernel, (NCW,),
        [
            (normal, pl.BlockSpec((rows, DM), lambda c: (0, 0))), (dz, columns(dz, same)),
            (normed, columns(normed, same)), (cot, whole(cot)),
        ],
        [(out, whole(out))], [], 8 * rows * DM * DI,
    )[0]


def gate_kernel(n_pieces, *refs):
    info = refs[0]
    pieces = refs[1 : 1 + n_pieces]
    ends = refs[1 + n_pieces : 1 + 2 * n_pieces]
    (
        y_intra, cs, cum, xs, z, q, inner_gain, d_skip, table,
        enter, normed, gain_part, dz, dyr, dye, product, skip_part, d_enter,
        y_scan, small, weights, squares, dots,
    ) = refs[1 + 2 * n_pieces :]
    phase, c = pl.program_id(0), pl.program_id(1)
    rows = cs.shape[0]
    nb = rows // CH
    n_all = n_pieces * nb
    here = pl.ds(pl.multiple_of(c * CW, CW), CW)

    @pl.when((phase == 0) & (c == 0))
    def _():
        weights[...] = carry_weights(info, clast_rows(ends, nb), nb, False)
        squares[...] = jnp.zeros_like(squares)
        dots[...] = jnp.zeros_like(dots)
        for i in range(nb):
            r = slice(i * CH, (i + 1) * CH)
            small[r, :] = jnp.concatenate(pieces2(jnp.exp(cum[r, :])), axis=1)

    @pl.when(phase == 0)
    def _():
        wide_w = dot(weights[...], table[...])
        totals = [jnp.zeros((NS, CW), F32) for _ in range(nb)]
        for j in range(n_all):
            piece = pieces[j // nb][j % nb].astype(F32)
            for i in range(nb):
                totals[i] = totals[i] + wide_w[i * n_all + j : i * n_all + j + 1, :] * piece
        for i in range(nb):
            r = slice(i * CH, (i + 1) * CH)
            low = totals[i].astype(BF)
            enter[i, :, here] = low
            scan = y_intra[r, :] + dot(small[r, :], table[...]) * dot(cs[r, :], low)
            y_scan[r, here] = scan
            y = scan + d_skip[...] * xs[r, :].astype(F32)
            zf = z[r, :].astype(F32)
            gated = y * (zf * sigmoid(zf))
            qg = q[r, :].astype(F32) * inner_gain[...] * usable_of(info, i)
            squares[r, :] += jnp.sum(gated * gated, axis=1, keepdims=True)
            dots[r, :] += jnp.sum(qg * gated, axis=1, keepdims=True)

    @pl.when(phase == 1)
    def _():
        gain_sum = jnp.zeros((1, CW), F32)
        skip_sum = jnp.zeros((1, CW), F32)
        for i in range(nb):
            r = slice(i * CH, (i + 1) * CH)
            inv = lax.rsqrt(squares[r, :] / DI + EPSILON)
            slope = inv * inv * inv * dots[r, :] / DI
            use = usable_of(info, i)
            scan = y_scan[r, here]
            x = xs[r, :].astype(F32)
            y = scan + d_skip[...] * x
            zf = z[r, :].astype(F32)
            sg = sigmoid(zf)
            sz = zf * sg
            gated = y * sz
            qf = q[r, :].astype(F32) * use
            scaled = gated * inv
            normed[r, :] = (scaled * inner_gain[...] * use).astype(BF)
            gain_sum = gain_sum + jnp.sum(qf * scaled, axis=0, keepdims=True)
            gg = inv * qf * inner_gain[...] - gated * slope
            dz[r, :] = (gg * y * (sg + sz * (1.0 - sg))).astype(BF)
            dy = gg * sz
            low = dy.astype(BF)
            dyr[r, :] = low
            product[r, :] = low.astype(F32) * scan
            skip_sum = skip_sum + jnp.sum(dy * x, axis=0, keepdims=True)
            back = (dot(small[r, :], table[...]) * dy).astype(BF)
            dye[r, :] = back
            d_enter[i] = dot_tn(cs[r, :], back).astype(BF)
        gain_part[...] = gain_sum
        skip_part[...] = skip_sum


def run_gate(info, a, pieces, y_intra, z, q, inner_gain, d_skip, table):
    rows = z.shape[0]
    nb = rows // CH

    def early(p, c):
        return jnp.where(p == 0, c, NCW - 1)

    def both(p, c):
        return c

    def late(p, c):
        return jnp.where(p == 0, 0, c)

    ins = [(info, in_smem())]
    ins += [(v, columns(v, early)) for v in pieces]
    ins += [(v, pl.BlockSpec((nb, 16, LANES), lambda p, c: (0, 0, DI // LANES))) for v in pieces]
    ins += [(y_intra, columns(y_intra, early))]
    ins += [(a[k], whole(a[k])) for k in ("cs", "cum")]
    ins += [(v, columns(v, both)) for v in (a["xs"], z, q, inner_gain, d_skip, table)]
    wide = shape((rows, DI), BF)
    wide_f = shape((rows, DI), F32)
    row = shape((1, DI), F32)
    state = shape((nb, NS, DI), BF)
    outs = [(state, whole(state))]
    outs += [(v, columns(v, late)) for v in (wide, row, wide, wide, wide, wide_f, row, state)]
    scratch = [
        pltpu.VMEM((rows, DI), F32), pltpu.VMEM((rows, 2 * LANES), BF),
        pltpu.VMEM((nb * nb * len(pieces), 2 * LANES), BF), pltpu.VMEM((rows, 1), F32),
        pltpu.VMEM((rows, 1), F32),
    ]
    return call(
        functools.partial(gate_kernel, len(pieces)), (2, NCW), ins, outs, scratch,
        2 * rows * NS * DI * 8,
    )


def intra_back_kernel(bs, cs, xt, cum, cum_t, dyr, dye, enter, dxt, db, dc, scores, top, bottom):
    c = pl.program_id(0)
    nb = bs.shape[0] // CH
    low = iota((CH, LANES), 1) < HD
    keep = iota((HALF, HALF), 1) >= iota((HALF, HALF), 0)

    @pl.when(c == 0)
    def _():
        for i in range(nb):
            r = slice(i * CH, (i + 1) * CH)
            scores[i] = dot_nt(bs[r, :], cs[r, :])
        top[...] = jnp.zeros_like(top)
        bottom[...] = jnp.zeros_like(bottom)
        dc[...] = jnp.zeros_like(dc)

    for i in range(nb):
        r = slice(i * CH, (i + 1) * CH)
        cols = chunk_heads(cum[r, :], c * PER)
        dc[r, :] += dot_nt(dye[r, :], enter[i])
        top_sum, bottom_sum = top[i], bottom[i]
        for p in range(PER // 2):
            lanes = slice(p * LANES, (p + 1) * LANES)
            x, dy = xt[r, lanes], dyr[r, lanes]
            got = []
            for k in range(2):
                h = 2 * p + k
                col = cols[:, h : h + 1]
                row = cum_t[pl.ds(c * PER + h, 1), r]
                a, b = col[:HALF], col[HALF:]
                s, t = row[:, :HALF], row[:, HALF:]
                left = jnp.where(keep, jnp.exp(s - a), 0.0)
                right = jnp.exp(t - a)
                last = jnp.where(keep, jnp.exp(t - b), 0.0)
                dec = jnp.concatenate([left, right], axis=1)
                got.append(
                    jnp.concatenate(
                        [
                            dot((dec * scores[i, :HALF, :]).astype(BF), dy),
                            dot((last * scores[i, HALF:, HALF:]).astype(BF), dy[HALF:, :]),
                        ],
                        axis=0,
                    )
                )
                own = jnp.where(low, x, 0) if k == 0 else jnp.where(low, 0, x)
                top_sum = top_sum + dot_nt(own[:HALF, :], dy) * dec
                bottom_sum = bottom_sum + dot_nt(own[HALF:, :], dy[HALF:, :]) * last
            dxt[r, lanes] = jnp.where(low, got[0], got[1])
        top[i], bottom[i] = top_sum, bottom_sum

    @pl.when(c == NCW - 1)
    def _():
        for i in range(nb):
            r = slice(i * CH, (i + 1) * CH)
            up, down = top[i].astype(BF), bottom[i].astype(BF)
            down = jnp.concatenate([jnp.zeros((HALF, HALF), BF), down], axis=1)
            both = jnp.concatenate([up, down], axis=0)
            db[r, :] = dot(both, cs[r, :])
            dc[r, :] += dot_tn(both, bs[r, :])


def run_intra_back(a, dyr, dye, enter):
    rows = dyr.shape[0]
    nb = rows // CH

    def same(c):
        return c

    ins = [(a[k], whole(a[k])) for k in ("bs", "cs")]
    ins += [(a["xt"], columns(a["xt"], same))]
    ins += [(a[k], whole(a[k])) for k in ("cum", "cum_t")]
    ins += [(v, columns(v, same)) for v in (dyr, dye, enter)]
    full, small = shape((rows, DI), F32), shape((rows, NS), F32)
    return call(
        intra_back_kernel, (NCW,), ins,
        [(full, columns(full, same)), (small, whole(small)), (small, whole(small))],
        [
            pltpu.VMEM((nb, CH, CH), F32), pltpu.VMEM((nb, HALF, CH), F32),
            pltpu.VMEM((nb, HALF, HALF), F32),
        ],
        2 * rows * CH * DI * 4,
    )


def back_kernel(n_pieces, *refs):
    info = refs[0]
    pieces = refs[1 : 1 + n_pieces]
    ends = refs[1 + n_pieces : 1 + 2 * n_pieces]
    (
        dx_intra, db_in, dc_in, xbc, slope, xs, xt, bs, raw, cum, enter, product, dyr, conv_w,
        a_log, d_skip, table, narrow,
        d_a, kernel_part, offset_part, bias_part, rate_part,
        grad, small, d_bs, heads, weights,
    ) = refs[1 + 2 * n_pieces :]
    step = pl.program_id(0)
    rows = xs.shape[0]
    nb = rows // CH
    n_all = n_pieces * nb

    @pl.when(step == 0)
    def _():
        weights[...] = carry_weights(info, clast_rows(ends, nb), nb, True)
        dt_all = softplus(raw[...])
        for i in range(nb):
            r = slice(i * CH, (i + 1) * CH)
            last = cum[(i + 1) * CH - 1 : (i + 1) * CH, :]
            small[i, 0] = jnp.concatenate(pieces2(dt_all[r, :]), axis=1)
            small[i, 1] = jnp.concatenate(pieces2(jnp.exp(last - cum[r, :])), axis=1)
            grad[i, :HALO, :] = jnp.zeros((HALO, CW), F32)
            grad[i, HALO + CH :, :] = jnp.zeros((HALO, CW), F32)
        d_bs[...] = db_in[...]
        heads[...] = jnp.zeros_like(heads)

    def convolve_back(dacts, width):
        offset_sum = jnp.zeros((1, width), F32)
        tap_sums = [jnp.zeros((1, width), F32) for _ in range(KC)]
        all_heads = xbc[rows:, :width].astype(F32)
        head_grads = []
        for i in range(nb):
            r = slice(i * CH, (i + 1) * CH)
            dpre = dacts[i] * slope[r, :width].astype(F32)
            offset_sum = offset_sum + jnp.sum(dpre, axis=0, keepdims=True)
            grad[i, HALO : HALO + CH, :width] = dpre
            body = xbc[r, :width].astype(F32)
            head = all_heads[i * HALO : (i + 1) * HALO, :]
            total = jnp.zeros((CH, width), F32)
            total_head = jnp.zeros((HALO, width), F32)
            for lag in range(KC):
                tap = conv_w[KC - 1 - lag : KC - lag, :width]
                later = grad[i, HALO + lag : HALO + lag + CH, :width]
                later_head = grad[i, lag : lag + HALO, :width]
                total = total + tap * later
                total_head = total_head + tap * later_head
                tap_sums[KC - 1 - lag] = (
                    tap_sums[KC - 1 - lag]
                    + jnp.sum(later * body, axis=0, keepdims=True)
                    + jnp.sum(later_head * head, axis=0, keepdims=True)
                )
            d_a[r, :width] = (total * usable_of(info, i)).astype(BF)
            head_grads.append(total_head * halo_used(info, i))
        d_a[rows:, :width] = jnp.concatenate(head_grads, axis=0).astype(BF)
        offset_part[:, :width] = offset_sum
        for k in range(KC):
            kernel_part[k : k + 1, :width] = tap_sums[k]

    @pl.when(step < NCW)
    def _():
        wide_w = dot(weights[...], table[...])
        totals = [jnp.zeros((NS, CW), F32) for _ in range(nb)]
        for j in range(n_all):
            piece = pieces[j // nb][j % nb].astype(F32)
            for i in range(nb):
                totals[i] = totals[i] + wide_w[i * n_all + j : i * n_all + j + 1, :] * piece
        select = narrow[...]
        dacts = []
        for i in range(nb):
            r = slice(i * CH, (i + 1) * CH)
            low = totals[i].astype(BF)
            fade = jnp.sum(low.astype(F32) * enter[i].astype(F32), axis=0, keepdims=True)
            end_w = dot(small[i, 1], table[...])
            x_dt = xt[r, :].astype(F32)
            inter = end_w * dot(bs[r, :], low)
            d_bs[r, :] += dot_nt((x_dt * end_w).astype(BF), low)
            dxt = dx_intra[r, :] + inter
            flow = jnp.sum(x_dt * inter, axis=0, keepdims=True)
            hi, mid, lo = pieces3(product[r, :] - x_dt * dxt)
            heads[0, r, :] += dot(hi, select) + dot(mid, select) + dot(lo, select)
            heads[1, r, :] += dot((xs[r, :].astype(F32) * dxt).astype(BF), select)
            hi, mid, lo = pieces3(jnp.concatenate([flow, fade, jnp.zeros((6, CW), F32)], axis=0))
            heads[2, i * 8 : (i + 1) * 8, :] += dot(hi, select) + dot(mid, select) + dot(lo, select)
            dacts.append(
                dot(small[i, 0], table[...]) * dxt + d_skip[...] * dyr[r, :].astype(F32)
            )
        convolve_back(dacts, CW)

    @pl.when(step == NCW)
    def _():
        dacts = []
        for i in range(nb):
            r = slice(i * CH, (i + 1) * CH)
            dacts.append(jnp.concatenate([d_bs[r, :], dc_in[r, :]], axis=1))
        convolve_back(dacts, 2 * NS)
        rate = jnp.exp(a_log[...])
        anti = (iota((CH, CH), 0) <= iota((CH, CH), 1)).astype(F32).astype(BF)
        bias_sum = jnp.zeros((1, LANES), F32)
        rate_sum = jnp.zeros((1, LANES), F32)
        for i in range(nb):
            r = slice(i * CH, (i + 1) * CH)
            last = cum[(i + 1) * CH - 1 : (i + 1) * CH, :]
            flow, fade = heads[2, i * 8 : i * 8 + 1, :], heads[2, i * 8 + 1 : i * 8 + 2, :]
            parts = dot(anti, jnp.concatenate(pieces3(heads[0, r, :]), axis=1))
            d_log = parts[:, :LANES] + parts[:, LANES : 2 * LANES] + parts[:, 2 * LANES :]
            d_log = d_log + (flow + jnp.exp(last) * fade)
            start = raw[r, :]
            d_raw = (heads[1, r, :] - d_log * rate) * sigmoid(start)
            d_raw = jnp.where(iota((CH, LANES), 1) < NH, d_raw, 0.0)
            bias_sum = bias_sum + jnp.sum(d_raw, axis=0, keepdims=True)
            rate_sum = rate_sum - jnp.sum(d_log * softplus(start), axis=0, keepdims=True) * rate
            d_a[r, 2 * NS :] = d_raw.astype(BF)
        d_a[rows:, 2 * NS :] = jnp.zeros((nb * HALO, CW - 2 * NS), BF)
        bias_part[...] = bias_sum
        rate_part[...] = rate_sum


def run_back(
    info, a, pieces, ends, dx_intra, db, dc, enter, product, dyr, conv_w, a_log, d_skip, table
):
    rows = dyr.shape[0]
    nb = rows // CH
    ext_rows = rows + nb * HALO

    def chunk(s):
        return jnp.minimum(s, NCW - 1)

    def same(s):
        return s

    narrow = table[:LANES].T
    ins = [(info, in_smem())]
    ins += [(v, columns(v, chunk)) for v in pieces]
    ins += [(v, pl.BlockSpec((nb, 16, LANES), lambda s: (0, 0, DI // LANES))) for v in ends]
    ins += [(dx_intra, columns(dx_intra, chunk)), (db, whole(db)), (dc, whole(dc))]
    ins += [(a["xbc"], columns(a["xbc"], same)), (a["slope"], columns(a["slope"], same))]
    ins += [(a["xs"], columns(a["xs"], chunk)), (a["xt"], columns(a["xt"], chunk))]
    ins += [(a[k], whole(a[k])) for k in ("bs", "raw", "cum")]
    ins += [(v, columns(v, chunk)) for v in (enter, product, dyr)]
    ins += [(conv_w, columns(conv_w, same)), (a_log, whole(a_log)), (d_skip, columns(d_skip, chunk))]
    ins += [(table, columns(table, chunk))]
    ins += [(narrow, pl.BlockSpec((CW, LANES), lambda s: (chunk(s), 0)))]
    wide, taps, row = shape((ext_rows, WA), BF), shape((KC, WA), F32), shape((1, WA), F32)
    lane = shape((1, LANES), F32)
    outs = [(v, columns(v, same)) for v in (wide, taps, row)]
    outs += [(lane, whole(lane)), (lane, whole(lane))]
    scratch = [
        pltpu.VMEM((nb, CH + 2 * HALO, CW), F32), pltpu.VMEM((nb, 2, CH, 2 * LANES), BF),
        pltpu.VMEM((rows, NS), F32), pltpu.VMEM((3, rows, LANES), F32),
        pltpu.VMEM((nb * nb * len(pieces), 2 * LANES), BF),
    ]
    return call(
        functools.partial(back_kernel, len(pieces)), (NCW + 1,), ins, outs, scratch,
        2 * rows * NS * DI * 16,
    )


def unit(rows):
    f = rows.astype(F32)
    inv = lax.rsqrt(jnp.mean(f * f, axis=1, keepdims=True) + EPSILON)
    return f * inv, inv


def norm_back(normal_grad, rows, gain):
    u, inv = unit(rows)
    g = normal_grad * gain[None, :]
    return inv * (g - u * jnp.mean(g * u, axis=1, keepdims=True))


def shards(
    tokens, norm_gain, in_weight, conv_weight, conv_bias, dt_bias, a_log, d_skip, inner_gain,
    out_weight, block_place, seq_length, cotangent,
):
    n_head, n_shard = lax.axis_size("head"), lax.axis_size("shard")
    half = n_head // 2
    head_at, shard_at = lax.axis_index("head"), lax.axis_index("shard")
    rows = tokens.shape[0]
    nb = rows // CH
    group_blocks = nb * n_head
    k_rows = in_weight.shape[0]
    stay = (head_at // half) == (shard_at & 1)

    piece_a = jnp.concatenate(
        [in_weight[:, DI:], norm_gain[:, None], jnp.zeros((k_rows, WA - XBC - NH - 1), BF)], axis=1
    )
    parts_a = gather_pieces(piece_a)
    me = shard_at.astype(jnp.int32)
    if k_rows % 32:
        joined = jnp.zeros((n_shard, k_rows, WA), BF)
        for v, k, _ in parts_a:
            joined = lax.dynamic_update_slice(joined, v[None], (shard_at ^ k, 0, 0))
        parts_a, me = [(joined.reshape(DM, WA), 0, None)], jnp.int32(0)
    piece_zo = jnp.concatenate(
        [in_weight[:, :DI], out_weight[:k_rows], out_weight[k_rows:]], axis=1
    )
    zo = lax.all_gather(piece_zo, "shard", axis=0, tiled=True)

    tails = tokens.reshape(nb, CH, DM)[:, CH - HALO :].reshape(nb * HALO, DM)
    tails = group_spread(tails, stay)
    tok_got = move_home(after(tokens, tails[0]))
    cot_got = move_home(after(cotangent, tok_got))

    numbers = jnp.concatenate([block_place, seq_length], axis=1)
    numbers = jnp.where(stay, numbers, trade(numbers, "shard", 1))[0]
    lengths = [numbers[group_blocks + k] for k in range(seq_length.shape[1])]
    ids = []
    for core in (0, 1):
        for z in range(half):
            device = (head_at % half ^ z) + ((shard_at & 1) ^ core) * half
            ids += [device * nb + b for b in range(nb)]
    ids = jnp.stack(ids)
    places = jnp.sum(
        jnp.where(ids[:, None] == jnp.arange(group_blocks)[None, :], numbers[None, :group_blocks], 0),
        axis=1,
    )
    first, in_seq, begin = jnp.zeros_like(places), jnp.zeros_like(places), 0
    for length in lengths:
        first = jnp.where(places >= begin, begin, first)
        in_seq = jnp.where(places >= begin, length, in_seq)
        begin = begin + (length + CH - 1) // CH
    info = jnp.concatenate(
        [
            jnp.stack([me, stay.astype(jnp.int32)]),
            jnp.stack([places, first, in_seq], axis=1).reshape(-1),
        ]
    ).astype(jnp.int32)

    table = spread_table()

    def head_row(v):
        return jnp.pad(v, (0, LANES - NH))[None]

    taps = jnp.pad(conv_weight, ((0, 0), (0, WA - XBC)))
    rate_row = head_row(a_log)
    skip_row = jnp.repeat(d_skip, HD)[None]
    a = run_project(
        info, parts_a, tails, tokens, tok_got, taps, jnp.pad(conv_bias, (0, WA - XBC))[None],
        head_row(dt_bias), rate_row, table,
    )
    wa, tok, normal = a["wa"], a["tok"], a["normal"]
    state_by_head = head_pieces(a["states"])
    state_by_core = trade(a["states"], "shard", 1)
    cot = jnp.where(stay, cotangent, after(cot_got, a["cum"]))
    if k_rows % 32:
        wz = zo[:, :DI]
        wo = zo[:, DI:].reshape(n_shard, k_rows, 2, DM).swapaxes(1, 2).reshape(DI, DM)
        z, q, y_intra = dot(normal[:rows], wz).astype(BF), dot_nt(cot, wo).astype(BF), run_intra(a)
    else:
        y_intra, z, q, wz, wo = run_middle(a, cot, zo)
    state_by_head = [after(v, y_intra) for v in state_by_head]
    all_states = (
        [a["states"]] + state_by_head + [state_by_core] + [trade(v, "shard", 1) for v in state_by_head]
    )
    enter, normed, gain_part, dz, dyr, dye, product, skip_part, d_enter = run_gate(
        info, a, all_states, y_intra, z, q, inner_gain[None], skip_row, table
    )
    enter_by_head = head_pieces(d_enter)
    enter_by_core = trade(d_enter, "shard", 1)
    if k_rows % 32:
        z_term = dot_tn(normal[:rows], dz).astype(BF)
        out_term = dot_tn(normed, cot).astype(BF).reshape(n_shard, 2, k_rows, DM)
        out_term = out_term.swapaxes(1, 2).reshape(DM, 2 * DM)
        zo_term = jnp.concatenate([z_term, out_term], axis=1)
    else:
        zo_term = run_terms(normal, dz, normed, cot)
    zo_own = lax.psum_scatter(zo_term, "shard", scatter_dimension=0, tiled=True)
    dx_intra, db, dc = run_intra_back(a, after(dyr, zo_term), dye, enter)
    mixed = (tok.astype(F32) + dot(after(normed, dx_intra), wo)).astype(BF)
    enter_by_head = [after(v, mixed) for v in enter_by_head]
    all_enter = (
        [d_enter] + enter_by_head + [enter_by_core] + [trade(v, "shard", 1) for v in enter_by_head]
    )
    mixed_got = move_home(after(mixed, all_enter[-1]))
    d_a_all, kernel_part, offset_part, bias_part, rate_part = run_back(
        info, a, all_enter, all_states, dx_intra, db, dc, enter, product, dyr, taps, rate_row,
        skip_row, table,
    )
    a_term = dot_tn(normal, d_a_all).astype(BF).reshape(n_shard, k_rows, WA)
    a_keep, a_give = core_give([a_term])
    a_got = trade(a_give, "shard", 1)

    small = jnp.concatenate(
        [
            kernel_part[:, :XBC].reshape(-1), offset_part[0, :XBC], bias_part[0, :NH],
            rate_part[0, :NH], jnp.sum(skip_part.reshape(NH, HD), axis=1), gain_part[0],
        ]
    )
    small = full_sum(after(small, a_give))

    d_a_all = after(d_a_all, a_give)
    normal_grad = dot_nt(dz, wz) + dot_nt(d_a_all[:rows], wa)
    halo_grad = dot_nt(d_a_all[rows:], wa)
    gain = wa[:, XBC + NH].astype(F32)
    token_grad = (cot.astype(F32) + norm_back(normal_grad, tok, gain)).astype(BF)
    halo_part = norm_back(halo_grad, a["tok_halo"], gain)

    a_pairs = chip_pairs(a_keep, a_got)
    a_far = chip_send(a_pairs)
    token_got = move_home(after(token_grad, a_pairs[0]))
    token_grad = jnp.where(stay, token_grad, token_got)
    all_halo = jnp.concatenate(group_gather(halo_part)).reshape(group_blocks, HALO, DM)
    is_next = (places[None, :] == places[:nb, None] + 1) & (first[None, :] == first[:nb, None])
    halo_back = swap_home(
        jnp.sum(jnp.where(is_next[:, :, None, None], all_halo[None], 0.0), axis=1), stay
    )
    token_grad = token_grad.reshape(nb, CH, DM)
    token_grad = token_grad.at[:, CH - HALO :].set(
        (token_grad[:, CH - HALO :].astype(F32) + halo_back).astype(BF)
    ).reshape(rows, DM)
    mixed = jnp.where(stay, mixed, after(mixed_got, a_give))

    zo_grad = head_sum(after(zo_own, a_pairs[0]))
    a_grad = head_sum(chip_sum(a_pairs[0], a_far))
    in_grad = jnp.concatenate([zo_grad[:, :DI], a_grad[:, : XBC + NH]], axis=1)
    out_grad = jnp.concatenate([zo_grad[:, DI : DI + DM], zo_grad[:, DI + DM :]], axis=0)
    gain_grad = jnp.sum(in_grad * in_weight.astype(F32), axis=1) / norm_gain.astype(F32)

    sizes = [KC * XBC, XBC, NH, NH, NH, DI]
    cuts = []
    at = 0
    for s in sizes:
        cuts.append(small[at : at + s])
        at += s
    return (
        mixed, token_grad, gain_grad, in_grad, cuts[0].reshape(KC, XBC), cuts[1], cuts[2], cuts[3],
        cuts[4], cuts[5], out_grad,
    )


def solution(mesh):
    return jax.shard_map(
        shards,
        mesh=mesh,
        in_specs=(
            P(("head", "shard"), None), P("shard"), P("shard", None), P(), P(), P(), P(), P(), P(),
            P("shard", None), P("shard", None), P("shard", None), P(("head", "shard"), None),
        ),
        out_specs=(
            P(("head", "shard"), None), P(("head", "shard"), None), P("shard"), P("shard", None),
            P(), P(), P(), P(), P(), P(), P("shard", None),
        ),
        check_vma=False,
    )
```

profile of v0, /device:TPU:1, one launch (start us, length us, event | category | flops | bytes accessed | tf_op | source)
XLA Modules:
  0.0 289.1 jit_solution(8179083209166878738)
XLA Ops:
  7.2 1.0 slice.119
  8.3 1.1 fusion.29
  9.4 0.9 pad_maximum_fusion.1
  10.4 3.2 %collective-permute-start.12 = (bf16[16,768]{1,0:T(8,128)(2,1)S(1)}, bf16[16,768]{1,0:T(8,128)(2,1)S(1)}, u32[]{:S(2)}, u32[]{:S(2)}) collective-permute-start(bf16[16,768]{1,0:T(8,128)(2,1)S(1)} %slice_bitcast_fusion.1), channel_id=1, source_target_pairs={{0,1},{1,17},{2,3},{3,19},{4,5},{5,21},{6,7},{7,23},{8,9},{9,25},{... | collective-permute-start | bytes 73736 | tf_op jit(solution)/shard_map/ppermute | solution.py:67
  13.6 2.5 collective-permute-start.10
  16.4 1.6 collective-permute-start.3
  18.0 1.2 collective-permute-start.2
  20.6 4.2 %collective-permute-start.14 = (bf16[512,768]{1,0:T(8,128)(2,1)S(1)}, bf16[512,768]{1,0:T(8,128)(2,1)}, u32[]{:S(2)}, u32[]{:S(2)}) collective-permute-start(bf16[512,768]{1,0:T(8,128)(2,1)S(1)} %copy-done.27), channel_id=1, source_target_pairs={{1,16},{3,18},{5,20},{7,22},{9,24},{11,26},{13,28},{15,30},{16,1},... | collective-permute-start | bytes 2359304 | tf_op jit(solution)/shard_map/ppermute | solution.py:48
  27.7 1.2 copy.36.refs_21_.refs_17_.refs_25_
  29.5 1.3 collective-permute-start.11
  30.9 2.7 collective-permute-start.7
  33.6 1.4 collective-permute-start.6
  35.2 1.2 collective-permute-done.11.refs_12_
  37.2 7.3 %collective-permute-done.13.refs_14_ = bf16[16,768]{1,0:T(8,128)(2,1)S(1)} collective-permute-done((bf16[16,768]{1,0:T(8,128)(2,1)S(1)}, bf16[16,768]{1,0:T(8,128)(2,1)S(1)}, u32[]{:S(2)}, u32[]{:S(2)}) %collective-permute-start.13) | collective-permute-done | bytes 24608 | tf_op jit(solution)/shard_map/ppermute | solution.py:67
  44.9 2.7 collective-permute-start.9
  47.6 1.3 collective-permute-start.8
  49.8 6.0 %collective-permute-start.16 = (bf16[512,768]{1,0:T(8,128)(2,1)S(1)}, bf16[512,768]{1,0:T(8,128)(2,1)S(1)}, u32[]{:S(2)}, u32[]{:S(2)}) collective-permute-start(bf16[512,768]{1,0:T(8,128)(2,1)S(1)} %copy-done.16), channel_id=1, source_target_pairs={{1,16},{3,18},{5,20},{7,22},{9,24},{11,26},{13,28},{15,30},{16,1},... | collective-permute-start | bytes 2359304 | tf_op jit(solution)/shard_map/ppermute | solution.py:48
  57.1 14.1 %shard_map.212 = (bf16[768,1920]{1,0:T(8,128)(2,1)}, bf16[512,768]{1,0:T(8,128)(2,1)}, bf16[16,768]{1,0:T(8,128)(2,1)}, bf16[528,768]{1,0:T(8,128)(2,1)}, bf16[5...) custom-call(s32[26]{0:T(128)} %pad_add_fusion.2.refs_0_, ...), custom_call_target="tpu_custom_call" | custom-call | flops 3114270720 | bytes 19794536 | tf_op jit(solution)/shard_map/pallas_call | solution.py:226
  72.4 1.4 collective-permute-done.16
  73.8 1.0 broadcast_select_fusion.2.cot
  74.8 11.8 %shard_map.213 = (f32[512,1536]{1,0:T(8,128)}, bf16[512,1536]{1,0:T(8,128)(2,1)}, bf16[512,1536]{1,0:T(8,128)(2,1)}, bf16[768,1536]{1,0:T(8,128)(2,1)}, bf16[1536,768]{1,0:T(8,128)(2,1)}) custom-call(bf16[512,128]{1,0:T(8,128)(2,1)} %get-tuple-element.75.bs.refs_16_, bf16[512,128]{1,0:T(8,128)(2,1)} %get-tuple-element.76.cs.refs_10_, ...), custom_call_target="tpu_custom_call" | custom-call | flops 3221225472 | bytes 24403968 | tf_op jit(solution)/shard_map/pallas_call | solution.py:226
  86.7 5.3 %collective-permute-done.15.refs_2_.refs_6_ = bf16[2,128,1664]{2,1,0:T(8,128)(2,1)S(1)} collective-permute-done((bf16[2,128,1664]{2,1,0:T(8,128)(2,1)}, bf16[2,128,1664]{2,1,0:T(8,128)(2,1)S(1)}, u32[]{:S(2)}, u32[]{:S(2)}) %collective-permute-start.15) | collective-permute-done | bytes 852000 | tf_op jit(solution)/shard_map/ppermute | solution.py:31
  92.6 1.1 convert_reduce_fusion
  95.3 16.3 %shard_map.214 = (bf16[2,128,1536]{2,1,0:T(8,128)(2,1)}, bf16[512,1536]{1,0:T(8,128)(2,1)}, f32[1,1536]{1,0:T(1,128)}, bf16[512,1536]{1,0:T(8,128)(2,1)}, bf16[5...) custom-call(s32[26]{0:T(128)} %pad_add_fusion.2.refs_0_, ...), custom_call_target="tpu_custom_call" | custom-call | flops 1610612736 | bytes 26894440 | tf_op jit(solution)/shard_map/pallas_call | solution.py:226
  112.1 7.8 %shard_map.215 = bf16[768,3072]{1,0:T(8,128)(2,1)} custom-call(bf16[528,768]{1,0:T(8,128)(2,1)} %get-tuple-element.80.normal, bf16[512,1536]{1,0:T(8,128)(2,1)} %get-tuple-element.90.dz, bf16[512,1536]{1,0:T(8,128)(2,1)} %get-tuple-element.95.normed, bf16[512,768]{1,0:T(8,128)(2,1)} %broadcast_select_fusion.2.cot), custom_call_target="tpu_custom_call" | custom-call | flops 4831838208 | bytes 9461760 | tf_op jit(solution)/shard_map/pallas_call | solution.py:226
  119.9 9.0 %shard_map.216 = (f32[512,1536]{1,0:T(8,128)}, f32[512,128]{1,0:T(8,128)}, f32[512,128]{1,0:T(8,128)}) custom-call(bf16[512,128]{1,0:T(8,128)(2,1)} %get-tuple-element.75.bs.refs_16_, bf16[512,128]{1,0:T(8,128)(2,1)} %get-tuple-element.76.cs.refs_10_, bf16[512,1536]{1,0:T(8,128)(2,1)} %get-tuple-element.77.xt.refs_15_, ...), custom_call_target="tpu_custom_call" | custom-call | flops 1610612736 | bytes 9961472 | tf_op jit(solution)/shard_map/pallas_call | solution.py:226
  129.0 2.3 fusion.10
  131.3 0.9 collective-permute-start.20
  132.7 4.8 %fusion.31 = f32[512,768]{1,0:T(8,128)} fusion(bf16[512,1536]{1,0:T(8,128)(2,1)} %get-tuple-element.90.dz, bf16[768,1536]{1,0:T(8,128)(2,1)} %get-tuple-element.108), kind=kOutput, calls=%fused_computation.91 | convolution fusion | flops 1207959552 | bytes 5505024 | tf_op jit(solution)/shard_map/dot_general | solution.py:171
  137.6 0.9 copy-done.13
  138.8 17.2 %shard_map.217 = (bf16[528,1920]{1,0:T(8,128)(2,1)}, f32[4,1920]{1,0:T(4,128)}, f32[1,1920]{1,0:T(1,128)}, f32[1,128]{1,0:T(1,128)}, f32[1,128]{1,0:T(1,128)}) custom-call(s32[26]{0:T(128)} %pad_add_fusion.2.refs_0_, bf16[2,128,1536]{2,1,0:T(8,128)(2,1)} %get-tuple-element.97.refs_1_, bf16[2,128,1536]{2,1,0:T(8,128)(2,1)} %copy-done.14, ...), custom_call_target="tpu_custom_call" | custom-call | flops 3221225472 | bytes 26807400 | tf_op jit(solution)/shard_map/pallas_call | solution.py:226
  156.1 4.4 %convolution_convert_fusion = bf16[768,1920]{1,0:T(8,128)(2,1)S(1)} fusion(bf16[528,768]{1,0:T(8,128)(2,1)S(1)} %copy-done.12, bf16[528,1920]{1,0:T(8,128)(2,1)} %get-tuple-element.109), kind=kOutput, calls=%fused_computation | convolution fusion | flops 1558609920 | bytes 5787648 | tf_op jit(solution)/shard_map/dot_general | solution.py:175
  160.5 1.3 dynamic-slice_bitcast_fusion
  161.8 2.1 copy-done.4
  163.9 2.0 fusion.18
  166.1 1.1 collective-permute-start.25
  167.8 3.5 %collective-permute-start.21 = (bf16[512,768]{1,0:T(8,128)(2,1)}, bf16[512,768]{1,0:T(8,128)(2,1)}, u32[]{:S(2)}, u32[]{:S(2)}) collective-permute-start(bf16[512,768]{1,0:T(8,128)(2,1)} %fusion.10), channel_id=1, source_target_pairs={{1,16},{3,18},{5,20},{7,22},{9,24},{11,26},{13,28},{15,30},{16,1},... | collective-permute-start | bytes 2359304 | tf_op jit(solution)/shard_map/ppermute | solution.py:48
  171.5 4.3 %fusion.5 = (f32[512]{0:T(512)S(1)}, f32[512,768]{1,0:T(8,128)S(1)}) fusion(bf16[512,768]{1,0:T(8,128)(2,1)} %get-tuple-element.73, f32[512]{0:T(512)S(1)} %add_rsqrt_fusion, f32[768]{0:T(1024)S(1)} %convert_reduce_fusion, f32[512,768]{1,0:T(8,128)} %fusion.31, bf16[768,1920]{1,0:T(8,128)(2,1)S(1)} %copy-done.4, bf16[528,1920]{1,0:T(8,128)(2,1)} %get-tuple-element.109), kind=kOutput, calls=%fused_computation.10 | convolution fusion | flops 1512308224 | bytes 8854528 | tf_op jit(solution)/shard_map/dot_general | solution.py:171
  175.9 1.1 collective-permute-start.39
  177.0 1.8 collective-permute-done.39
  179.9 1.9 collective-permute-start.27
  181.8 1.2 collective-permute-start.41
  183.0 1.7 fusion
  184.7 1.0 dynamic-slice_bitcast_fusion.3
  186.4 1.4 collective-permute-start.33
  188.3 0.8 maximum_bitcast_fusion
  189.1 2.7 collective-permute-done.41
  192.0 3.7 %collective-permute-done.42 = f32[10568]{0:T(1024)S(1)} collective-permute-done((f32[10568]{0:T(1024)S(1)}, f32[10568]{0:T(1024)S(1)}, u32[]{:S(2)}, u32[]{:S(2)}) %collective-permute-start.42) | collective-permute-done | bytes 42304 | tf_op jit(solution)/shard_map/ppermute | solution.py:31
  195.7 4.5 %collective-permute-start.28 = (f32[2,8,768]{2,1,0:T(8,128)S(1)}, f32[2,8,768]{2,1,0:T(8,128)}, u32[]{:S(2)}, u32[]{:S(2)}) collective-permute-start(f32[2,8,768]{2,1,0:T(8,128)S(1)} %select_reduce_fusion), channel_id=1, source_target_pairs={{1,16},{3,18},{5,20},{7,22},{9,24},{11,26},{13,28},{15,30},{16,1},... | collective-permute-start | bytes 147464 | tf_op jit(solution)/shard_map/ppermute | solution.py:48
  202.7 1.4 add_convert_fusion
  204.2 1.6 collective-permute-start.34
  205.7 2.1 broadcast_select_fusion.1
  207.9 6.5 %collective-permute-start.24 = (bf16[512,768]{1,0:T(8,128)(2,1)S(1)}, bf16[512,768]{1,0:T(8,128)(2,1)S(1)}, u32[]{:S(2)}, u32[]{:S(2)}) collective-permute-start(bf16[512,768]{1,0:T(8,128)(2,1)S(1)} %fusion.9), channel_id=1, source_target_pairs={{1,16},{3,18},{5,20},{7,22},{9,24},{11,26},{13,28},{15,30},{16,1},... | collective-permute-start | bytes 2359304 | tf_op jit(solution)/shard_map/ppermute | solution.py:48
  214.6 16.0 %collective-permute-done.36 = bf16[96,1024]{1,0:T(8,128)(2,1)S(1)} collective-permute-done((bf16[96,1024]{1,0:T(8,128)(2,1)S(1)}, bf16[96,1024]{1,0:T(8,128)(2,1)S(1)}, u32[]{:S(2)}, u32[]{:S(2)}) %collective-permute-start.36) | collective-permute-done | bytes 196640 | tf_op jit(solution)/shard_map/ppermute | solution.py:31
  230.8 1.2 fusion.28
  232.0 2.1 collective-permute-done.35
  234.1 17.8 %collective-permute-start.29 = (bf16[96,1536]{1,0:T(8,128)(2,1)S(1)}, bf16[96,1536]{1,0:T(8,128)(2,1)S(1)}, u32[]{:S(2)}, u32[]{:S(2)}) collective-permute-start(bf16[96,1536]{1,0:T(8,128)(2,1)S(1)} %get-tuple-element.133), channel_id=1, source_target_pairs={{0,8},{8,0},{16,24},{24,16},{1,9},{9,1},{17,25},{25,17},{2,10},{10... | collective-permute-start | bytes 884744 | tf_op jit(solution)/shard_map/ppermute | solution.py:31
  252.0 10.4 %collective-permute-done.29 = bf16[96,1536]{1,0:T(8,128)(2,1)S(1)} collective-permute-done((bf16[96,1536]{1,0:T(8,128)(2,1)S(1)}, bf16[96,1536]{1,0:T(8,128)(2,1)S(1)}, u32[]{:S(2)}, u32[]{:S(2)}) %collective-permute-start.29) | collective-permute-done | bytes 294944 | tf_op jit(solution)/shard_map/ppermute | solution.py:31
  262.7 0.8 fusion.22
  263.6 1.2 collective-permute-start.30
  264.8 10.1 %collective-permute-done.44 = bf16[96,1536]{1,0:T(8,128)(2,1)S(1)} collective-permute-done((bf16[96,1536]{1,0:T(8,128)(2,1)S(1)}, bf16[96,1536]{1,0:T(8,128)(2,1)S(1)}, u32[]{:S(2)}, u32[]{:S(2)}) %collective-permute-start.44) | collective-permute-done | bytes 294944 | tf_op jit(solution)/shard_map/ppermute | solution.py:31
  275.0 4.5 %collective-permute-done.30 = bf16[96,1536]{1,0:T(8,128)(2,1)S(1)} collective-permute-done((bf16[96,1536]{1,0:T(8,128)(2,1)S(1)}, bf16[96,1536]{1,0:T(8,128)(2,1)S(1)}, u32[]{:S(2)}, u32[]{:S(2)}) %collective-permute-start.30) | collective-permute-done | bytes 294944 | tf_op jit(solution)/shard_map/ppermute | solution.py:31
  279.6 1.3 multiply_reduce_fusion
  281.4 0.9 pad_maximum_fusion.2
  (216 shorter events, 20.3 us)
Async XLA Ops:
  7.2 67.6 %all-gather.2.cloned.1.call-start = ((), (), s32[]{:S(2)}) async-start(), calls=%async_computation.1 | async-start | bytes 5308416 | tf_op jit(solution)/shard_map/all_gather | solution.py:978
  10.2 14.9 %copy-start.22 = (f32[1536]{0:T(1024)S(1)}, f32[1536]{0:T(1024)}, u32[]{:S(2)}) copy-start(f32[1536]{0:T(1024)} %param.23) | copy-start | bytes 18436
  10.2 15.5 %copy-start.23 = (f32[1792]{0:T(1024)S(1)}, f32[1792]{0:T(1024)}, u32[]{:S(2)}) copy-start(f32[1792]{0:T(1024)} %param.19) | copy-start | bytes 21508
  10.2 16.1 %copy-start.28 = (f32[24]{0:T(128)S(1)}, f32[24]{0:T(128)}, u32[]{:S(2)}) copy-start(f32[24]{0:T(128)} %param.22) | copy-start | bytes 292
  10.3 16.9 %copy-start.20 = (f32[4,1792]{1,0:T(4,128)S(1)}, f32[4,1792]{1,0:T(4,128)}, u32[]{:S(2)}) copy-start(f32[4,1792]{1,0:T(4,128)} %param.18) | copy-start | bytes 86020
  10.3 220.5 %reduce-scatter.2.cloned.1.call-start = ((), (), s32[]{:S(2)}) async-start(), calls=%async_computation.2 | async-start | bytes 5308416 | tf_op jit(solution)/shard_map/reduce_scatter | solution.py:1048
  10.4 24.7 %collective-permute-start.12 = (bf16[16,768]{1,0:T(8,128)(2,1)S(1)}, bf16[16,768]{1,0:T(8,128)(2,1)S(1)}, u32[]{:S(2)}, u32[]{:S(2)}) collective-permute-start(bf16[16,768]{1,0:T(8,128)(2,1)S(1)} %slice_bitcast_fusion.1), channel_id=1, source_target_pairs={{0,1},{1,17},{2,3},{3,19},{4,5},{5,21},{6,7},{7,23},{8,9},{9,25},{... | collective-permute-start | bytes 73736 | tf_op jit(solution)/shard_map/ppermute | solution.py:67
  13.6 6.4 %collective-permute-start.10 = (bf16[16,768]{1,0:T(8,128)(2,1)S(1)}, bf16[16,768]{1,0:T(8,128)(2,1)S(1)}, u32[]{:S(2)}, u32[]{:S(2)}) collective-permute-start(bf16[16,768]{1,0:T(8,128)(2,1)S(1)} %slice_bitcast_fusion.1), channel_id=1, source_target_pairs={{1,16},{3,18},{5,20},{7,22},{9,24},{11,26},{13,28},{15,30},{16,1},... | collective-permute-start | bytes 73736 | tf_op jit(solution)/shard_map/ppermute | solution.py:48
  16.3 40.1 %copy-start.18 = (bf16[96,1920]{1,0:T(8,128)(2,1)}, bf16[96,1920]{1,0:T(8,128)(2,1)S(1)}, u32[]{:S(2)}) copy-start(bf16[96,1920]{1,0:T(8,128)(2,1)S(1)} %concatenate.31.refs_1_) | copy-start | bytes 1105924
  16.3 12.7 %copy-start.31 = (f32[24]{0:T(128)S(1)}, f32[24]{0:T(128)}, u32[]{:S(2)}) copy-start(f32[24]{0:T(128)} %param.21) | copy-start | bytes 292
  16.3 12.7 %copy-start.32 = (f32[24]{0:T(128)S(1)}, f32[24]{0:T(128)}, u32[]{:S(2)}) copy-start(f32[24]{0:T(128)} %param.20) | copy-start | bytes 292
  16.3 33.5 %copy-start.16 = (bf16[512,768]{1,0:T(8,128)(2,1)S(1)}, bf16[512,768]{1,0:T(8,128)(2,1)}, u32[]{:S(2)}) copy-start(bf16[512,768]{1,0:T(8,128)(2,1)} %param.27) | copy-start | bytes 2359300
  16.4 14.5 %collective-permute-start.3 = (bf16[96,1920]{1,0:T(8,128)(2,1)S(1)}, bf16[96,1920]{1,0:T(8,128)(2,1)S(1)}, u32[]{:S(2)}, u32[]{:S(2)}) collective-permute-start(bf16[96,1920]{1,0:T(8,128)(2,1)S(1)} %concatenate.31.refs_1_), channel_id=1, source_target_pairs={{0,4},{1,5},{2,6},{3,7},{4,0},{5,1},{6,2},{7,3},{8,12},{9,13},{10,... | collective-permute-start | bytes 1105928 | tf_op jit(solution)/shard_map/ppermute | solution.py:31
  18.0 15.6 %collective-permute-start.2 = (bf16[96,1920]{1,0:T(8,128)(2,1)S(1)}, bf16[96,1920]{1,0:T(8,128)(2,1)}, u32[]{:S(2)}, u32[]{:S(2)}) collective-permute-start(bf16[96,1920]{1,0:T(8,128)(2,1)S(1)} %concatenate.31.refs_1_), channel_id=1, source_target_pairs={{0,2},{1,3},{2,0},{3,1},{4,6},{5,7},{6,4},{7,5},{8,10},{9,11},{10,... | collective-permute-start | bytes 1105928 | tf_op jit(solution)/shard_map/ppermute | solution.py:31
  19.9 9.6 %collective-permute-start = (s32[1,9]{1,0:T(1,128)S(1)}, s32[1,9]{1,0:T(1,128)S(1)}, u32[]{:S(2)}, u32[]{:S(2)}) collective-permute-start(s32[1,9]{1,0:T(1,128)S(1)} %pad_add_fusion.1), channel_id=1, source_target_pairs={{0,1},{1,0},{2,3},{3,2},{4,5},{5,4},{6,7},{7,6},{8,9},{9,8},{10,11... | collective-permute-start | bytes 116 | tf_op jit(solution)/shard_map/ppermute | solution.py:31
  20.6 27.0 %collective-permute-start.14 = (bf16[512,768]{1,0:T(8,128)(2,1)S(1)}, bf16[512,768]{1,0:T(8,128)(2,1)}, u32[]{:S(2)}, u32[]{:S(2)}) collective-permute-start(bf16[512,768]{1,0:T(8,128)(2,1)S(1)} %copy-done.27), channel_id=1, source_target_pairs={{1,16},{3,18},{5,20},{7,22},{9,24},{11,26},{13,28},{15,30},{16,1},... | collective-permute-start | bytes 2359304 | tf_op jit(solution)/shard_map/ppermute | solution.py:48
  29.5 6.9 %collective-permute-start.11 = (bf16[16,768]{1,0:T(8,128)(2,1)S(1)}, bf16[16,768]{1,0:T(8,128)(2,1)S(1)}, u32[]{:S(2)}, u32[]{:S(2)}) collective-permute-start(bf16[16,768]{1,0:T(8,128)(2,1)S(1)} %slice_bitcast_fusion.1), channel_id=1, source_target_pairs={{0,8},{1,24},{2,10},{3,26},{4,12},{5,28},{6,14},{7,30},{8,0},{9,16... | collective-permute-start | bytes 73736 | tf_op jit(solution)/shard_map/ppermute | solution.py:67
  30.9 25.5 %copy-start.35 = (bf16[96,1920]{1,0:T(8,128)(2,1)}, bf16[96,1920]{1,0:T(8,128)(2,1)S(1)}, u32[]{:S(2)}) copy-start(bf16[96,1920]{1,0:T(8,128)(2,1)S(1)} %collective-permute-done.3.refs_4_) | copy-start | bytes 1105924
  30.9 13.6 %collective-permute-start.7 = (bf16[96,1920]{1,0:T(8,128)(2,1)S(1)}, bf16[96,1920]{1,0:T(8,128)(2,1)}, u32[]{:S(2)}, u32[]{:S(2)}) collective-permute-start(bf16[96,1920]{1,0:T(8,128)(2,1)S(1)} %collective-permute-done.3.refs_4_), channel_id=1, source_target_pairs={{1,3},{3,1},{5,7},{7,5},{9,11},{11,9},{13,15},{15,13},{17,19},{19,... | collective-permute-start | bytes 1105928 | tf_op jit(solution)/shard_map/ppermute | solution.py:92
  33.6 11.4 %collective-permute-start.6 = (bf16[96,1920]{1,0:T(8,128)(2,1)}, bf16[96,1920]{1,0:T(8,128)(2,1)}, u32[]{:S(2)}, u32[]{:S(2)}) collective-permute-start(bf16[96,1920]{1,0:T(8,128)(2,1)} %collective-permute-done.2.refs_3_), channel_id=1, source_target_pairs={{0,4},{2,6},{4,0},{6,2},{8,12},{10,14},{12,8},{14,10},{16,20},{18,... | collective-permute-start | bytes 1105928 | tf_op jit(solution)/shard_map/ppermute | solution.py:92
  35.1 21.3 %copy-start.37 = (bf16[16,768]{1,0:T(8,128)(2,1)}, bf16[16,768]{1,0:T(8,128)(2,1)S(1)}, u32[]{:S(2)}) copy-start(bf16[16,768]{1,0:T(8,128)(2,1)S(1)} %collective-permute-done.12.refs_13_) | copy-start | bytes 73732
  35.1 9.3 %collective-permute-start.13 = (bf16[16,768]{1,0:T(8,128)(2,1)S(1)}, bf16[16,768]{1,0:T(8,128)(2,1)S(1)}, u32[]{:S(2)}, u32[]{:S(2)}) collective-permute-start(bf16[16,768]{1,0:T(8,128)(2,1)S(1)} %slice_bitcast_fusion.1), channel_id=1, source_target_pairs={{0,9},{1,25},{2,11},{3,27},{4,13},{5,29},{6,15},{7,31},{8,1},{9,17... | collective-permute-start | bytes 73736 | tf_op jit(solution)/shard_map/ppermute | solution.py:67
  36.4 20.0 %copy-start.38 = (bf16[16,768]{1,0:T(8,128)(2,1)}, bf16[16,768]{1,0:T(8,128)(2,1)S(1)}, u32[]{:S(2)}) copy-start(bf16[16,768]{1,0:T(8,128)(2,1)S(1)} %collective-permute-done.11.refs_12_) | copy-start | bytes 73732
  36.4 13.4 %collective-permute-start.1 = (bf16[96,1920]{1,0:T(8,128)(2,1)S(1)}, bf16[96,1920]{1,0:T(8,128)(2,1)}, u32[]{:S(2)}, u32[]{:S(2)}) collective-permute-start(bf16[96,1920]{1,0:T(8,128)(2,1)S(1)} %concatenate.31.refs_1_), channel_id=1, source_target_pairs={{0,1},{1,0},{2,3},{3,2},{4,5},{5,4},{6,7},{7,6},{8,9},{9,8},{10,11... | collective-permute-start | bytes 1105928 | tf_op jit(solution)/shard_map/ppermute | solution.py:31
  44.4 11.9 %collective-permute-start.5 = (bf16[96,1920]{1,0:T(8,128)(2,1)S(1)}, bf16[96,1920]{1,0:T(8,128)(2,1)}, u32[]{:S(2)}, u32[]{:S(2)}) collective-permute-start(bf16[96,1920]{1,0:T(8,128)(2,1)S(1)} %collective-permute-done.3.refs_4_), channel_id=1, source_target_pairs={{0,1},{1,0},{2,3},{3,2},{4,5},{5,4},{6,7},{7,6},{8,9},{9,8},{10,11... | collective-permute-start | bytes 1105928 | tf_op jit(solution)/shard_map/ppermute | solution.py:31
  44.4 11.9 %collective-permute-start.4 = (bf16[96,1920]{1,0:T(8,128)(2,1)}, bf16[96,1920]{1,0:T(8,128)(2,1)}, u32[]{:S(2)}, u32[]{:S(2)}) collective-permute-start(bf16[96,1920]{1,0:T(8,128)(2,1)} %collective-permute-done.2.refs_3_), channel_id=1, source_target_pairs={{0,1},{1,0},{2,3},{3,2},{4,5},{5,4},{6,7},{7,6},{8,9},{9,8},{10,11... | collective-permute-start | bytes 1105928 | tf_op jit(solution)/shard_map/ppermute | solution.py:31
  44.9 11.4 %collective-permute-start.9 = (bf16[96,1920]{1,0:T(8,128)(2,1)}, bf16[96,1920]{1,0:T(8,128)(2,1)}, u32[]{:S(2)}, u32[]{:S(2)}) collective-permute-start(bf16[96,1920]{1,0:T(8,128)(2,1)} %collective-permute-done.7.refs_8_), channel_id=1, source_target_pairs={{1,0},{3,2},{5,4},{7,6},{9,8},{11,10},{13,12},{15,14},{17,16},{19,... | collective-permute-start | bytes 1105928 | tf_op jit(solution)/shard_map/ppermute | solution.py:92
  47.6 8.7 %collective-permute-start.8 = (bf16[96,1920]{1,0:T(8,128)(2,1)}, bf16[96,1920]{1,0:T(8,128)(2,1)S(1)}, u32[]{:S(2)}, u32[]{:S(2)}) collective-permute-start(bf16[96,1920]{1,0:T(8,128)(2,1)} %collective-permute-done.6.refs_7_), channel_id=1, source_target_pairs={{0,1},{2,3},{4,5},{6,7},{8,9},{10,11},{12,13},{14,15},{16,17},{18,... | collective-permute-start | bytes 1105928 | tf_op jit(solution)/shard_map/ppermute | solution.py:92
  49.8 24.0 %collective-permute-start.16 = (bf16[512,768]{1,0:T(8,128)(2,1)S(1)}, bf16[512,768]{1,0:T(8,128)(2,1)S(1)}, u32[]{:S(2)}, u32[]{:S(2)}) collective-permute-start(bf16[512,768]{1,0:T(8,128)(2,1)S(1)} %copy-done.16), channel_id=1, source_target_pairs={{1,16},{3,18},{5,20},{7,22},{9,24},{11,26},{13,28},{15,30},{16,1},... | collective-permute-start | bytes 2359304 | tf_op jit(solution)/shard_map/ppermute | solution.py:48
  71.2 20.8 %collective-permute-start.15 = (bf16[2,128,1664]{2,1,0:T(8,128)(2,1)}, bf16[2,128,1664]{2,1,0:T(8,128)(2,1)S(1)}, u32[]{:S(2)}, u32[]{:S(2)}) collective-permute-start(bf16[2,128,1664]{2,1,0:T(8,128)(2,1)} %get-tuple-element.74.refs_1_.refs_5_), channel_id=1, source_target_pairs={{0,8},{8,0},{16,24},{24,16},{1,9},{9,1},{17,25},{25,17},{2,10},{10... | collective-permute-start | bytes 2555912 | tf_op jit(solution)/shard_map/ppermute | solution.py:31
  72.3 21.4 %collective-permute-start.17 = (bf16[2,128,1664]{2,1,0:T(8,128)(2,1)}, bf16[2,128,1664]{2,1,0:T(8,128)(2,1)S(1)}, u32[]{:S(2)}, u32[]{:S(2)}) collective-permute-start(bf16[2,128,1664]{2,1,0:T(8,128)(2,1)} %get-tuple-element.74.refs_1_.refs_5_), channel_id=1, source_target_pairs={{0,1},{1,0},{2,3},{3,2},{4,5},{5,4},{6,7},{7,6},{8,9},{9,8},{10,11... | collective-permute-start | bytes 2555912 | tf_op jit(solution)/shard_map/ppermute | solution.py:31
  74.8 17.7 %copy-start.19 = (bf16[16,768]{1,0:T(8,128)(2,1)S(1)}, bf16[16,768]{1,0:T(8,128)(2,1)}, u32[]{:S(2)}) copy-start(bf16[16,768]{1,0:T(8,128)(2,1)} %get-tuple-element.112) | copy-start | bytes 73732
  92.0 2.4 collective-permute-start.18
  111.6 26.0 %collective-permute-start.22 = (bf16[2,128,1536]{2,1,0:T(8,128)(2,1)}, bf16[2,128,1536]{2,1,0:T(8,128)(2,1)S(1)}, u32[]{:S(2)}, u32[]{:S(2)}) collective-permute-start(bf16[2,128,1536]{2,1,0:T(8,128)(2,1)} %get-tuple-element.97.refs_1_), channel_id=1, source_target_pairs={{0,1},{1,0},{2,3},{3,2},{4,5},{5,4},{6,7},{7,6},{8,9},{9,8},{10,11... | collective-permute-start | bytes 2359304 | tf_op jit(solution)/shard_map/ppermute | solution.py:31
  112.1 19.2 %collective-permute-start.19 = (bf16[2,128,1536]{2,1,0:T(8,128)(2,1)}, bf16[2,128,1536]{2,1,0:T(8,128)(2,1)S(1)}, u32[]{:S(2)}, u32[]{:S(2)}) collective-permute-start(bf16[2,128,1536]{2,1,0:T(8,128)(2,1)} %get-tuple-element.97.refs_1_), channel_id=1, source_target_pairs={{0,8},{8,0},{16,24},{24,16},{1,9},{9,1},{17,25},{25,17},{2,10},{10... | collective-permute-start | bytes 2359304 | tf_op jit(solution)/shard_map/ppermute | solution.py:31
  131.3 6.3 %collective-permute-start.20 = (bf16[2,128,1536]{2,1,0:T(8,128)(2,1)S(1)}, bf16[2,128,1536]{2,1,0:T(8,128)(2,1)S(1)}, u32[]{:S(2)}, u32[]{:S(2)}) collective-permute-start(bf16[2,128,1536]{2,1,0:T(8,128)(2,1)S(1)} %collective-permute-done.19.refs_2_), channel_id=1, source_target_pairs={{0,1},{1,0},{2,3},{3,2},{4,5},{5,4},{6,7},{7,6},{8,9},{9,8},{10,11... | collective-permute-start | bytes 2359304 | tf_op jit(solution)/shard_map/ppermute | solution.py:31
  138.8 17.2 %copy-start.12 = (bf16[528,768]{1,0:T(8,128)(2,1)S(1)}, bf16[528,768]{1,0:T(8,128)(2,1)}, u32[]{:S(2)}) copy-start(bf16[528,768]{1,0:T(8,128)(2,1)} %get-tuple-element.80.normal) | copy-start | bytes 2433028
  166.0 20.4 %collective-permute-start.26 = (f32[16,768]{1,0:T(8,128)S(1)}, f32[16,768]{1,0:T(8,128)S(1)}, u32[]{:S(2)}, u32[]{:S(2)}) collective-permute-start(f32[16,768]{1,0:T(8,128)S(1)} %fusion.20), channel_id=1, source_target_pairs={{0,1},{1,0},{2,3},{3,2},{4,5},{5,4},{6,7},{7,6},{8,9},{9,8},{10,11... | collective-permute-start | bytes 147464 | tf_op jit(solution)/shard_map/ppermute | solution.py:31
  166.1 13.8 %collective-permute-start.25 = (f32[16,768]{1,0:T(8,128)S(1)}, f32[16,768]{1,0:T(8,128)}, u32[]{:S(2)}, u32[]{:S(2)}) collective-permute-start(f32[16,768]{1,0:T(8,128)S(1)} %fusion.20), channel_id=1, source_target_pairs={{0,8},{8,0},{16,24},{24,16},{1,9},{9,1},{17,25},{25,17},{2,10},{10... | collective-permute-start | bytes 147464 | tf_op jit(solution)/shard_map/ppermute | solution.py:31
  167.2 15.8 %collective-permute-start.23 = (bf16[4,96,1920]{2,1,0:T(8,128)(2,1)}, bf16[4,96,1920]{2,1,0:T(8,128)(2,1)}, u32[]{:S(2)}, u32[]{:S(2)}) collective-permute-start(bf16[4,96,1920]{2,1,0:T(8,128)(2,1)} %dynamic-slice_bitcast_fusion), channel_id=1, source_target_pairs={{0,1},{1,0},{2,3},{3,2},{4,5},{5,4},{6,7},{7,6},{8,9},{9,8},{10,11... | collective-permute-start | bytes 4423688 | tf_op jit(solution)/shard_map/ppermute | solution.py:31
  167.8 34.9 %collective-permute-start.21 = (bf16[512,768]{1,0:T(8,128)(2,1)}, bf16[512,768]{1,0:T(8,128)(2,1)}, u32[]{:S(2)}, u32[]{:S(2)}) collective-permute-start(bf16[512,768]{1,0:T(8,128)(2,1)} %fusion.10), channel_id=1, source_target_pairs={{1,16},{3,18},{5,20},{7,22},{9,24},{11,26},{13,28},{15,30},{16,1},... | collective-permute-start | bytes 2359304 | tf_op jit(solution)/shard_map/ppermute | solution.py:48
  171.4 4.4 %collective-permute-start.38 = (f32[10568]{0:T(1024)S(1)}, f32[10568]{0:T(1024)S(1)}, u32[]{:S(2)}, u32[]{:S(2)}) collective-permute-start(f32[10568]{0:T(1024)S(1)} %concatenate.36), channel_id=1, source_target_pairs={{0,1},{1,0},{2,3},{3,2},{4,5},{5,4},{6,7},{7,6},{8,9},{9,8},{10,11... | collective-permute-start | bytes 126824 | tf_op jit(solution)/shard_map/ppermute | solution.py:31
  175.9 3.0 %collective-permute-start.39 = (f32[10568]{0:T(1024)S(1)}, f32[10568]{0:T(1024)S(1)}, u32[]{:S(2)}, u32[]{:S(2)}) collective-permute-start(f32[10568]{0:T(1024)S(1)} %add.213), channel_id=1, source_target_pairs={{0,2},{1,3},{2,0},{3,1},{4,6},{5,7},{6,4},{7,5},{8,10},{9,11},{10,... | collective-permute-start | bytes 126824 | tf_op jit(solution)/shard_map/ppermute | solution.py:31
  178.9 3.0 %collective-permute-start.40 = (f32[10568]{0:T(1024)S(1)}, f32[10568]{0:T(1024)S(1)}, u32[]{:S(2)}, u32[]{:S(2)}) collective-permute-start(f32[10568]{0:T(1024)S(1)} %add.214), channel_id=1, source_target_pairs={{0,4},{1,5},{2,6},{3,7},{4,0},{5,1},{6,2},{7,3},{8,12},{9,13},{10,... | collective-permute-start | bytes 126824 | tf_op jit(solution)/shard_map/ppermute | solution.py:31
  179.9 7.9 %collective-permute-start.27 = (f32[16,768]{1,0:T(8,128)}, f32[16,768]{1,0:T(8,128)S(1)}, u32[]{:S(2)}, u32[]{:S(2)}) collective-permute-start(f32[16,768]{1,0:T(8,128)} %collective-permute-done.25), channel_id=1, source_target_pairs={{0,1},{1,0},{2,3},{3,2},{4,5},{5,4},{6,7},{7,6},{8,9},{9,8},{10,11... | collective-permute-start | bytes 147464 | tf_op jit(solution)/shard_map/ppermute | solution.py:31
  181.8 10.0 %collective-permute-start.41 = (f32[10568]{0:T(1024)S(1)}, f32[10568]{0:T(1024)S(1)}, u32[]{:S(2)}, u32[]{:S(2)}) collective-permute-start(f32[10568]{0:T(1024)S(1)} %add.215), channel_id=1, source_target_pairs={{0,8},{8,0},{16,24},{24,16},{1,9},{9,1},{17,25},{25,17},{2,10},{10... | collective-permute-start | bytes 126824 | tf_op jit(solution)/shard_map/ppermute | solution.py:31
  185.7 17.1 %collective-permute-start.31 = (bf16[96,1920]{1,0:T(8,128)(2,1)}, bf16[96,1920]{1,0:T(8,128)(2,1)}, u32[]{:S(2)}, u32[]{:S(2)}) collective-permute-start(bf16[96,1920]{1,0:T(8,128)(2,1)} %get-tuple-element.125), channel_id=1, source_target_pairs={{0,2},{1,3},{2,0},{3,1},{4,6},{5,7},{6,4},{7,5},{8,10},{9,11},{10,... | collective-permute-start | bytes 1105928 | tf_op jit(solution)/shard_map/ppermute | solution.py:31
  186.4 16.3 %collective-permute-start.33 = (bf16[96,1920]{1,0:T(8,128)(2,1)}, bf16[96,1920]{1,0:T(8,128)(2,1)}, u32[]{:S(2)}, u32[]{:S(2)}) collective-permute-start(bf16[96,1920]{1,0:T(8,128)(2,1)} %get-tuple-element.126), channel_id=1, source_target_pairs={{0,6},{1,7},{2,4},{3,5},{4,2},{5,3},{6,0},{7,1},{8,14},{9,15},{10,... | collective-permute-start | bytes 1105928 | tf_op jit(solution)/shard_map/ppermute | solution.py:31
  187.8 17.9 %copy-start.17 = (bf16[512,768]{1,0:T(8,128)(2,1)S(1)}, bf16[512,768]{1,0:T(8,128)(2,1)}, u32[]{:S(2)}) copy-start(bf16[512,768]{1,0:T(8,128)(2,1)} %fusion.10) | copy-start | bytes 2359300
  187.8 14.9 %collective-permute-start.32 = (bf16[96,1920]{1,0:T(8,128)(2,1)S(1)}, bf16[96,1920]{1,0:T(8,128)(2,1)}, u32[]{:S(2)}, u32[]{:S(2)}) collective-permute-start(bf16[96,1920]{1,0:T(8,128)(2,1)S(1)} %get-tuple-element.127), channel_id=1, source_target_pairs={{0,4},{1,5},{2,6},{3,7},{4,0},{5,1},{6,2},{7,3},{8,12},{9,13},{10,... | collective-permute-start | bytes 1105928 | tf_op jit(solution)/shard_map/ppermute | solution.py:31
  191.8 3.9 %collective-permute-start.42 = (f32[10568]{0:T(1024)S(1)}, f32[10568]{0:T(1024)S(1)}, u32[]{:S(2)}, u32[]{:S(2)}) collective-permute-start(f32[10568]{0:T(1024)S(1)} %add.216), channel_id=1, source_target_pairs={{0,16},{8,24},{16,0},{24,8},{1,17},{9,25},{17,1},{25,9},{2,18},{10... | collective-permute-start | bytes 126824 | tf_op jit(solution)/shard_map/ppermute | solution.py:31
  195.7 67.0 %collective-permute-start.28 = (f32[2,8,768]{2,1,0:T(8,128)S(1)}, f32[2,8,768]{2,1,0:T(8,128)}, u32[]{:S(2)}, u32[]{:S(2)}) collective-permute-start(f32[2,8,768]{2,1,0:T(8,128)S(1)} %select_reduce_fusion), channel_id=1, source_target_pairs={{1,16},{3,18},{5,20},{7,22},{9,24},{11,26},{13,28},{15,30},{16,1},... | collective-permute-start | bytes 147464 | tf_op jit(solution)/shard_map/ppermute | solution.py:48
  204.2 10.3 %collective-permute-start.34 = (bf16[96,896]{1,0:T(8,128)(2,1)S(1)}, bf16[96,896]{1,0:T(8,128)(2,1)S(1)}, u32[]{:S(2)}, u32[]{:S(2)}) collective-permute-start(bf16[96,896]{1,0:T(8,128)(2,1)S(1)} %slice.148), channel_id=1, source_target_pairs={{0,8},{8,0},{16,24},{24,16},{1,9},{9,1},{17,25},{25,17},{2,10},{10... | collective-permute-start | bytes 516104 | tf_op jit(solution)/shard_map/ppermute | solution.py:31
  207.8 22.8 %collective-permute-start.36 = (bf16[96,1024]{1,0:T(8,128)(2,1)S(1)}, bf16[96,1024]{1,0:T(8,128)(2,1)S(1)}, u32[]{:S(2)}, u32[]{:S(2)}) collective-permute-start(bf16[96,1024]{1,0:T(8,128)(2,1)S(1)} %slice.149), channel_id=1, source_target_pairs={{0,16},{8,24},{16,0},{24,8},{1,17},{9,25},{17,1},{25,9},{2,18},{10... | collective-permute-start | bytes 589832 | tf_op jit(solution)/shard_map/ppermute | solution.py:31
  207.9 54.7 %collective-permute-start.24 = (bf16[512,768]{1,0:T(8,128)(2,1)S(1)}, bf16[512,768]{1,0:T(8,128)(2,1)S(1)}, u32[]{:S(2)}, u32[]{:S(2)}) collective-permute-start(bf16[512,768]{1,0:T(8,128)(2,1)S(1)} %fusion.9), channel_id=1, source_target_pairs={{1,16},{3,18},{5,20},{7,22},{9,24},{11,26},{13,28},{15,30},{16,1},... | collective-permute-start | bytes 2359304 | tf_op jit(solution)/shard_map/ppermute | solution.py:48
  214.5 19.6 %collective-permute-start.35 = (bf16[96,896]{1,0:T(8,128)(2,1)S(1)}, bf16[96,896]{1,0:T(8,128)(2,1)S(1)}, u32[]{:S(2)}, u32[]{:S(2)}) collective-permute-start(bf16[96,896]{1,0:T(8,128)(2,1)S(1)} %add_convert_fusion.4), channel_id=1, source_target_pairs={{0,16},{8,24},{16,0},{24,8},{1,17},{9,25},{17,1},{25,9},{2,18},{10... | collective-permute-start | bytes 516104 | tf_op jit(solution)/shard_map/ppermute | solution.py:31
  230.7 21.2 %collective-permute-start.37 = (bf16[96,1024]{1,0:T(8,128)(2,1)S(1)}, bf16[96,1024]{1,0:T(8,128)(2,1)S(1)}, u32[]{:S(2)}, u32[]{:S(2)}) collective-permute-start(bf16[96,1024]{1,0:T(8,128)(2,1)S(1)} %add_convert_fusion.3), channel_id=1, source_target_pairs={{0,8},{8,0},{16,24},{24,16},{1,9},{9,1},{17,25},{25,17},{2,10},{10... | collective-permute-start | bytes 589832 | tf_op jit(solution)/shard_map/ppermute | solution.py:31
  230.8 31.6 %copy-start.10 = (bf16[96,3072]{1,0:T(8,128)(2,1)S(1)}, bf16[96,3072]{1,0:T(8,128)(2,1)}, u32[]{:S(2)}) copy-start(bf16[96,3072]{1,0:T(8,128)(2,1)} %reduce-scatter.2.cloned.1.call-done) | copy-start | bytes 1769476
  231.9 20.0 %collective-permute-start.43 = (bf16[96,1536]{1,0:T(8,128)(2,1)S(1)}, bf16[96,1536]{1,0:T(8,128)(2,1)S(1)}, u32[]{:S(2)}, u32[]{:S(2)}) collective-permute-start(bf16[96,1536]{1,0:T(8,128)(2,1)S(1)} %get-tuple-element.132), channel_id=1, source_target_pairs={{0,16},{8,24},{16,0},{24,8},{1,17},{9,25},{17,1},{25,9},{2,18},{10... | collective-permute-start | bytes 884744 | tf_op jit(solution)/shard_map/ppermute | solution.py:31
  234.1 28.3 %collective-permute-start.29 = (bf16[96,1536]{1,0:T(8,128)(2,1)S(1)}, bf16[96,1536]{1,0:T(8,128)(2,1)S(1)}, u32[]{:S(2)}, u32[]{:S(2)}) collective-permute-start(bf16[96,1536]{1,0:T(8,128)(2,1)S(1)} %get-tuple-element.133), channel_id=1, source_target_pairs={{0,8},{8,0},{16,24},{24,16},{1,9},{9,1},{17,25},{25,17},{2,10},{10... | collective-permute-start | bytes 884744 | tf_op jit(solution)/shard_map/ppermute | solution.py:31
  262.5 12.3 %collective-permute-start.44 = (bf16[96,1536]{1,0:T(8,128)(2,1)S(1)}, bf16[96,1536]{1,0:T(8,128)(2,1)S(1)}, u32[]{:S(2)}, u32[]{:S(2)}) collective-permute-start(bf16[96,1536]{1,0:T(8,128)(2,1)S(1)} %get-tuple-element.130), channel_id=1, source_target_pairs={{0,8},{8,0},{16,24},{24,16},{1,9},{9,1},{17,25},{25,17},{2,10},{10... | collective-permute-start | bytes 884744 | tf_op jit(solution)/shard_map/ppermute | solution.py:31
  263.6 16.0 %copy-start.11 = (bf16[2,256,768]{2,1,0:T(8,128)(2,1)}, bf16[2,256,768]{2,1,0:T(8,128)(2,1)S(1)}, u32[]{:S(2)}) copy-start(bf16[2,256,768]{2,1,0:T(8,128)(2,1)S(1)} %fusion.22) | copy-start | bytes 2359300
  263.6 16.0 %copy-start.9 = (bf16[96,3352]{1,0:T(8,128)(2,1)S(1)}, bf16[96,3352]{1,0:T(8,128)(2,1)}, u32[]{:S(2)}) copy-start(bf16[96,3352]{1,0:T(8,128)(2,1)} %param.17) | copy-start | bytes 1930756
  263.6 15.9 %collective-permute-start.30 = (bf16[96,1536]{1,0:T(8,128)(2,1)S(1)}, bf16[96,1536]{1,0:T(8,128)(2,1)S(1)}, u32[]{:S(2)}, u32[]{:S(2)}) collective-permute-start(bf16[96,1536]{1,0:T(8,128)(2,1)S(1)} %get-tuple-element.131), channel_id=1, source_target_pairs={{0,16},{8,24},{16,0},{24,8},{1,17},{9,25},{17,1},{25,9},{2,18},{10... | collective-permute-start | bytes 884744 | tf_op jit(solution)/shard_map/ppermute | solution.py:31
  (26 other events, 139.8 us)
Sparse Core Ops, SparseCore 0:
  10.5 43.5 all-gather.1
  120.0 53.6 reduce-scatter.1
where the time goes:
time: 291 us; the launch traced here: 289 us
  Pallas kernels  76.3 us (26%)
  starting transfers between devices  75.6 us (26%)
  waiting for transfers between devices  67.4 us (23%)
  local copies, waits for them, and re-layouts  19.5 us (7%)
  matrix products  17.8 us (6%)
  other arithmetic  16.8 us (6%)
  between operations  15.7 us (5%)
    pallas_call x6, Pallas kernels, call(): pl.pallas_call(kernel, grid=grid, out_shape=[o for o, _ in outs], in_spec...  76.3 us
    ppermute x32, waiting for transfers between devices, trade(): return lax.ppermute(value, axis, [(i, i ^ bit) for i in range(size)])  57.4 us
    ppermute x32, starting transfers between devices, trade(): return lax.ppermute(value, axis, [(i, i ^ bit) for i in range(size)])  35.7 us
    ppermute x6, starting transfers between devices, move_home(): return lax.ppermute(value, ('head', 'shard'), pairs)  27.1 us
    dot_general x3, matrix products, dot_nt(): lax.dot_general(a, b, (((1,), (1,)), ((), ())), preferred_element_type=F32)  11.1 us
    ppermute x3, waiting for transfers between devices, group_spread(): pieces.append(lax.ppermute(value, ('head', 'shard'), pairs))  8.49 us
    ppermute x4, starting transfers between devices, from_core(): lax.ppermute(value, 'shard', [(i, i ^ bit) for i in range(n_shard) if i %...  8.11 us
  transfers between devices with their start and end apart: 47, of which 13 were waited for; matrix products, arithmetic and copies ran while one was open for 15% of the time, Pallas kernels for 21%

commit v1 on v0

--- a/solution.py
+++ b/solution.py
@@ -24,6 +24,8 @@
 CW = 384
 NCW = DI // CW
 VMEM_ASK = 56 * 2**20
+VMEM_ROOM = 56 * 2**20
+COST_SCALE = 0.4
 
 
 def trade(value, axis, bit):
@@ -52,18 +54,17 @@
     return jnp.where(stay, value, move_home(value))
 
 
-def group_spread(value, stay):
+def group_spread(value):
     n_head, n_shard = lax.axis_size("head"), lax.axis_size("shard")
-    half = n_head // 2
-    pieces = [swap_home(value, stay)]
+    pieces = [value]
     for core in (0, 1):
-        for low in range(half):
+        for low in range(n_head // 2):
             if core or low:
-                pairs = []
-                for h in range(n_head):
-                    for s in range(n_shard):
-                        there = (h % half ^ low) + (s & 1) * half
-                        pairs.append((h * n_shard + s, there * n_shard + (s - (s & 1) + (h // half ^ core))))
+                pairs = [
+                    (h * n_shard + s, (h ^ low) * n_shard + (s ^ core))
+                    for h in range(n_head)
+                    for s in range(n_shard)
+                ]
                 pieces.append(lax.ppermute(value, ("head", "shard"), pairs))
     return pieces
 
@@ -78,7 +79,7 @@
     return pieces + [trade(v, "shard", 1) for v in pieces]
 
 
-def gather_pieces(piece):
+def gather_pieces(piece, *first):
     n_shard = lax.axis_size("shard")
     if n_shard != 8:
         held = {0: piece}
@@ -86,19 +87,11 @@
         while bit < n_shard:
             held.update({k ^ bit: trade(v, "shard", bit) for k, v in list(held.items())})
             bit *= 2
-        return [(v, k, None) for k, v in held.items()]
-
-    def from_core(value, core, bit):
-        return lax.ppermute(value, "shard", [(i, i ^ bit) for i in range(n_shard) if i % 2 == core])
-
-    by_x, by_y, by_core = trade(piece, "shard", 2), trade(piece, "shard", 4), trade(piece, "shard", 1)
-    far_0, far_1 = from_core(by_x, 0, 4), from_core(by_y, 1, 2)
-    return [
-        (piece, 0, None), (by_core, 1, None), (by_x, 2, None), (by_y, 4, None),
-        (trade(by_x, "shard", 1), 3, None), (trade(by_y, "shard", 1), 5, None),
-        (far_0, 6, 0), (far_1, 6, 1),
-        (from_core(far_0, 0, 1), 7, 1), (from_core(far_1, 1, 1), 7, 0),
-    ]
+        return [(v, k) for k, v in held.items()]
+
+    far = [trade(piece, "shard", bit) for bit in (6, 2, 4)]
+    near = [trade(v, "shard", 1) for v in after_all([piece] + far, *first)]
+    return [(v, k) for v, k in zip([piece] + far + near, (0, 6, 2, 4, 1, 7, 3, 5))]
 
 
 def head_pieces(value):
@@ -130,6 +123,10 @@
     return [lax.dynamic_index_in_dim(pair, chip ^ k, 0, False) for k in range(pair.shape[0])]
 
 
+def after_all(values, *others):
+    return list(lax.optimization_barrier((*values, *others)))[: len(values)]
+
+
 def chip_send(pairs):
     return [trade(v, "shard", 2 * k) for k, v in enumerate(pairs) if k]
 
@@ -141,26 +138,29 @@
     return total.astype(BF)
 
 
-def head_sum(value):
-    cut = value.shape[1] // 2 // LANES * LANES
-    bits = [b for b in (1, 2, 4, 8, 16) if b < lax.axis_size("head")]
-    done = []
-    for part, order in ((value[:, :cut], bits), (value[:, cut:], bits[::-1])):
-        total = part.astype(F32)
-        for bit in order:
-            low = total.astype(BF)
-            total = low.astype(F32) + trade(low, "head", bit).astype(F32)
-        done.append(total)
-    return jnp.concatenate(done, axis=1)
-
-
-def full_sum(value):
-    for axis in ("shard", "head"):
-        bit = 1
-        while bit < lax.axis_size(axis):
-            value = value + trade(value, axis, bit)
-            bit *= 2
-    return value
+def split2(v):
+    high = lax.reduce_precision(v, 8, 7)
+    return jnp.concatenate([high.astype(BF), (v - high).astype(BF)], axis=1)
+
+
+def join2(parts):
+    high, low = jnp.split(parts, 2, axis=1)
+    return high.astype(F32) + low.astype(F32)
+
+
+def head_split(value):
+    cut = value.shape[1] // 2
+    odd = lax.axis_index("head") % 2
+    return [lax.dynamic_slice_in_dim(value, at * cut, cut, 1) for at in (odd, 1 - odd)]
+
+
+def head_add(keep, got):
+    return (keep.astype(F32) + got.astype(F32)).astype(BF)
+
+
+def head_join(half, other):
+    odd = lax.axis_index("head") % 2
+    return jnp.concatenate([jnp.where(odd, other, half), jnp.where(odd, half, other)], axis=1)
 
 
 def dot(a, b):
@@ -178,6 +178,10 @@
 def spread_table():
     row = jnp.arange(2 * LANES)[:, None] % LANES
     return (row == jnp.arange(DI)[None, :] // HD).astype(BF)
+
+
+def narrow_table():
+    return (jnp.arange(DI)[:, None] // HD == jnp.arange(LANES)[None, :]).astype(BF)
 
 
 def pieces2(v):
@@ -220,9 +224,7 @@
     return pl.BlockSpec(memory_space=pltpu.SMEM)
 
 
-def call(kernel, grid, ins, outs, scratch, flops):
-    moved = sum(a.size * a.dtype.itemsize for a, _ in ins)
-    moved += sum(o.size * o.dtype.itemsize for o, _ in outs)
+def call(kernel, micros, grid, ins, outs, scratch, room=VMEM_ROOM):
     return pl.pallas_call(
         kernel,
         grid=grid,
@@ -230,8 +232,10 @@
         in_specs=[s for _, s in ins],
         out_specs=[s for _, s in outs],
         scratch_shapes=scratch,
-        compiler_params=pltpu.CompilerParams(vmem_limit_bytes=VMEM_ASK),
-        cost_estimate=pl.CostEstimate(flops=flops, bytes_accessed=moved, transcendentals=0),
+        compiler_params=pltpu.CompilerParams(vmem_limit_bytes=room),
+        cost_estimate=pl.CostEstimate(
+            flops=1, bytes_accessed=int(micros * COST_SCALE * 3.7e6), transcendentals=0
+        ),
     )(*[a for a, _ in ins])
 
 
@@ -305,7 +309,7 @@
     halos = refs[1 + len(layout) : 1 + len(layout) + n_halo]
     (
         tok_own, tok_got, conv_w, conv_b, dt_bias, a_log, table,
-        wa_out, tok, tok_halo, normal, xbc, slope, xs, xt, bs, cs, raw, cum, cum_t, states,
+        wa_out, tok, tok_halo, normal, normal_t, xbc, slope, xs, xt, bs, cs, raw, cum, cum_t, states,
         wa, ext, small, sems, out_sem,
     ) = refs[1 + len(layout) + n_halo :]
     step = pl.program_id(0)
@@ -340,17 +344,13 @@
     @pl.when(step == 0)
     def _():
         def copy_of(n):
-            offset, core = layout[n]
-            at = pl.multiple_of((me ^ offset) * pieces[n].shape[0], 16)
+            at = pl.multiple_of((me ^ layout[n]) * pieces[n].shape[0], 16)
             return pltpu.make_async_copy(
                 pieces[n], wa.at[pl.ds(at, pieces[n].shape[0]), :], sems.at[n]
             )
 
-        for n, (offset, core) in enumerate(layout):
-            if core is None:
-                copy_of(n).start()
-            else:
-                pl.when(me % 2 == core)(lambda n=n: copy_of(n).start())
+        for n in range(len(layout)):
+            copy_of(n).start()
         stay = info[1] > 0
         tok[...] = jnp.where(stay, tok_own[...], tok_got[...])
         found = []
@@ -364,14 +364,12 @@
                     total = total + jnp.where(hit, part[b * HALO : (b + 1) * HALO, :], 0.0)
             found.append(total)
         tok_halo[...] = jnp.concatenate(found, axis=0).astype(BF)
-        for n, (offset, core) in enumerate(layout):
-            if core is None:
-                copy_of(n).wait()
-            else:
-                pl.when(me % 2 == core)(lambda n=n: copy_of(n).wait())
+        for n in range(len(layout)):
+            copy_of(n).wait()
         out_copy().start()
         gain = wa[:, XBC : XBC + LANES].astype(F32).T[NH : NH + 1, :]
         normal[:rows, :] = normal_rows(tok[...], gain)
+        normal_t[...] = normal[:rows, :].T
         normal[rows:, :] = normal_rows(tok_halo[...], gain)
         for i, act in enumerate(project(DI, 2 * NS)):
             bs[i * CH : (i + 1) * CH, :] = act[:, :NS].astype(BF)
@@ -415,7 +413,7 @@
     rows = tok_own.shape[0]
     nb = rows // CH
     ext_rows = rows + nb * HALO
-    layout = [(offset, core) for _, offset, core in parts]
+    layout = [offset for _, offset in parts]
 
     def before(s):
         return jnp.maximum(s - 1, 0)
@@ -423,7 +421,7 @@
     def tail_first(s):
         return jnp.where(s == 0, NCW, s - 1)
 
-    ins = [(info, in_smem())] + [(v, in_hbm()) for v, _, _ in parts]
+    ins = [(info, in_smem())] + [(v, in_hbm()) for v, _ in parts]
     ins += [(v, whole(v)) for v in halos]
     ins += [(v, whole(v)) for v in (tok_own, tok_got, conv_w, conv_b, dt_bias, a_log)]
     ins += [(table, columns(table, before))]
@@ -432,6 +430,7 @@
         "tok": (shape((rows, DM), BF), whole),
         "tok_halo": (shape((nb * HALO, DM), BF), whole),
         "normal": (shape((ext_rows, DM), BF), whole),
+        "normal_t": (shape((DM, rows), BF), whole),
         "xbc": (shape((ext_rows, WA), BF), lambda v: columns(v, tail_first)),
         "slope": (shape((rows, WA), BF), lambda v: columns(v, tail_first)),
         "xs": (shape((rows, DI), BF), lambda v: columns(v, before)),
@@ -450,12 +449,16 @@
         pltpu.SemaphoreType.DMA,
     ]
     got = call(
-        functools.partial(project_kernel, layout, len(halos)), (NCW + 1,), ins, out_list, scratch,
-        2 * ext_rows * DM * WA * 2,
+        functools.partial(project_kernel, layout, len(halos)), 14, (NCW + 1,), ins, out_list, scratch, VMEM_ASK,
     )
     return dict(zip(outs, got))
 
 
+SUM_GAIN = (KC + 1) * XBC // LANES
+SUM_SKIP = SUM_GAIN + DI // LANES
+SUM_HEADS = SUM_SKIP + DI // LANES
+SUM_ROWS = SUM_HEADS + 2
+OUT_ROWS = CW // 4
 PER = CW // HD
 HALF = CH // 2
 
@@ -499,44 +502,6 @@
             out[r, lanes] = jnp.where(low, got[0], got[1])
 
 
-def middle_kernel(
-    bs, cs, xt, cum, cum_t, normal, cot, zo_z, zo_o, out, z, q, wz, wo, scores
-):
-    wz[...] = zo_z[...]
-    z[...] = dot(normal[...], zo_z[...]).astype(BF)
-    unit_rows = zo_o.shape[0] // 2
-    parts = []
-    for k in range(2):
-        block = zo_o[k * unit_rows : (k + 1) * unit_rows, :]
-        parts += [block[:, :DM], block[:, DM:]]
-    rows_o = jnp.concatenate(parts, axis=0)
-    wo[...] = rows_o
-    q[...] = dot_nt(cot[...], rows_o).astype(BF)
-    intra_kernel(bs, cs, xt, cum, cum_t, out, scores)
-
-
-def run_middle(a, cot, zo):
-    rows = cot.shape[0]
-    nb = rows // CH
-
-    def same(c):
-        return c
-
-    ins = [(a[k], whole(a[k])) for k in ("bs", "cs")]
-    ins += [(a["xt"], columns(a["xt"], same))]
-    ins += [(a[k], whole(a[k])) for k in ("cum", "cum_t")]
-    ins += [(a["normal"], pl.BlockSpec((rows, DM), lambda c: (0, 0))), (cot, whole(cot))]
-    ins += [(zo, columns(zo, same)), (zo, pl.BlockSpec((DM // NCW, DI), lambda c: (c, 1)))]
-    wide, wide_f = shape((rows, DI), BF), shape((rows, DI), F32)
-    wz, wo = shape((DM, DI), BF), shape((DI, DM), BF)
-    outs = [(v, columns(v, same)) for v in (wide_f, wide, wide, wz)]
-    outs += [(wo, pl.BlockSpec((CW, DM), lambda c: (c, 0)))]
-    return call(
-        middle_kernel, (NCW,), ins, outs, [pltpu.VMEM((nb, CH, CH), F32)],
-        2 * rows * CH * DI * 2 + 4 * rows * DM * DI,
-    )
-
-
 def run_intra(a):
     rows = a["bs"].shape[0]
     nb = rows // CH
@@ -545,38 +510,59 @@
     ins += [(a[k], whole(a[k])) for k in ("cum", "cum_t")]
     out = shape((rows, DI), F32)
     return call(
-        intra_kernel, (NCW,), ins, [(out, columns(out, lambda c: c))],
-        [pltpu.VMEM((nb, CH, CH), F32)], 2 * rows * CH * DI * 2,
+        intra_kernel, 6, (NCW,), ins, [(out, columns(out, lambda c: c))],
+        [pltpu.VMEM((nb, CH, CH), F32)],
     )[0]
 
 
-def terms_kernel(normal, dz, normed, cot, out):
-    c = pl.program_id(0)
-    out[:, pl.ds(pl.multiple_of(c * CW, CW), CW)] = dot_tn(normal[...], dz[...]).astype(BF)
+def terms_kernel(normal_t, dz, normed, cot, out):
+    out[:, :DI] = dot(normal_t[...], dz[...]).astype(BF)
     part = dot_tn(normed[...], cot[...]).astype(BF)
-    unit_rows = CW // 4
     for k in range(2):
-        at = pl.multiple_of((2 * c + k) * unit_rows, unit_rows)
         for j in range(2):
-            rows = part[(2 * k + j) * unit_rows : (2 * k + j + 1) * unit_rows, :]
-            out[pl.ds(at, unit_rows), DI + j * DM : DI + (j + 1) * DM] = rows
-
-
-def run_terms(normal, dz, normed, cot):
+            rows = part[(2 * k + j) * OUT_ROWS : (2 * k + j + 1) * OUT_ROWS, :]
+            out[k * OUT_ROWS : (k + 1) * OUT_ROWS, DI + j * DM : DI + (j + 1) * DM] = rows
+
+
+def run_terms(normal_t, dz, normed, cot):
     rows = dz.shape[0]
-
-    def same(c):
-        return c
-
     out = shape((DM, DI + 2 * DM), BF)
     return call(
-        terms_kernel, (NCW,),
+        terms_kernel, 1, (NCW,),
         [
-            (normal, pl.BlockSpec((rows, DM), lambda c: (0, 0))), (dz, columns(dz, same)),
-            (normed, columns(normed, same)), (cot, whole(cot)),
+            (normal_t, pl.BlockSpec((2 * OUT_ROWS, rows), lambda c: (c, 0))), (dz, whole(dz)),
+            (normed, columns(normed, lambda c: c)), (cot, whole(cot)),
         ],
-        [(out, whole(out))], [], 8 * rows * DM * DI,
+        [(out, pl.BlockSpec((2 * OUT_ROWS, DI + 2 * DM), lambda c: (c, 0)))], [],
     )[0]
+
+
+def pair_small_kernel(at, keep, got, small, small_got, *outs):
+    n, _, cols = keep.shape
+    chip = at[0] // 2
+    total = small[...] + small_got[...]
+    parts = jnp.concatenate(pieces2(total), axis=1)
+    for k, out in enumerate(outs):
+        out[:, :cols] = (keep[chip ^ k].astype(F32) + got[chip ^ k].astype(F32)).astype(BF)
+        out[:, cols:] = parts
+
+
+def run_pair_small(at, keep, got, small, small_got):
+    n, rows, cols = keep.shape
+    out = shape((rows, cols + 2 * small.shape[1]), BF)
+    args = [keep, got, small, small_got]
+    return call(
+        pair_small_kernel, 1, (1,), [(at, in_smem())] + [(v, whole(v)) for v in args],
+        [(out, whole(out))] * n, [],
+    )
+
+
+GW = 768
+GNW = DI // GW
+
+
+def columns_g(arr, at):
+    return columns(arr, at, GW)
 
 
 def gate_kernel(n_pieces, *refs):
@@ -592,7 +578,7 @@
     rows = cs.shape[0]
     nb = rows // CH
     n_all = n_pieces * nb
-    here = pl.ds(pl.multiple_of(c * CW, CW), CW)
+    here = pl.ds(pl.multiple_of(c * GW, GW), GW)
 
     @pl.when((phase == 0) & (c == 0))
     def _():
@@ -606,7 +592,7 @@
     @pl.when(phase == 0)
     def _():
         wide_w = dot(weights[...], table[...])
-        totals = [jnp.zeros((NS, CW), F32) for _ in range(nb)]
+        totals = [jnp.zeros((NS, GW), F32) for _ in range(nb)]
         for j in range(n_all):
             piece = pieces[j // nb][j % nb].astype(F32)
             for i in range(nb):
@@ -626,8 +612,8 @@
 
     @pl.when(phase == 1)
     def _():
-        gain_sum = jnp.zeros((1, CW), F32)
-        skip_sum = jnp.zeros((1, CW), F32)
+        gain_sum = jnp.zeros((1, GW), F32)
+        skip_sum = jnp.zeros((1, GW), F32)
         for i in range(nb):
             r = slice(i * CH, (i + 1) * CH)
             inv = lax.rsqrt(squares[r, :] / DI + EPSILON)
@@ -663,7 +649,7 @@
     nb = rows // CH
 
     def early(p, c):
-        return jnp.where(p == 0, c, NCW - 1)
+        return jnp.where(p == 0, c, GNW - 1)
 
     def both(p, c):
         return c
@@ -672,29 +658,31 @@
         return jnp.where(p == 0, 0, c)
 
     ins = [(info, in_smem())]
-    ins += [(v, columns(v, early)) for v in pieces]
+    ins += [(v, columns_g(v, early)) for v in pieces]
     ins += [(v, pl.BlockSpec((nb, 16, LANES), lambda p, c: (0, 0, DI // LANES))) for v in pieces]
-    ins += [(y_intra, columns(y_intra, early))]
+    ins += [(y_intra, columns_g(y_intra, early))]
     ins += [(a[k], whole(a[k])) for k in ("cs", "cum")]
-    ins += [(v, columns(v, both)) for v in (a["xs"], z, q, inner_gain, d_skip, table)]
+    ins += [(v, columns_g(v, both)) for v in (a["xs"], z, q, inner_gain, d_skip, table)]
     wide = shape((rows, DI), BF)
     wide_f = shape((rows, DI), F32)
     row = shape((1, DI), F32)
     state = shape((nb, NS, DI), BF)
     outs = [(state, whole(state))]
-    outs += [(v, columns(v, late)) for v in (wide, row, wide, wide, wide, wide_f, row, state)]
+    outs += [(v, columns_g(v, late)) for v in (wide, row, wide, wide, wide, wide_f, row, state)]
     scratch = [
         pltpu.VMEM((rows, DI), F32), pltpu.VMEM((rows, 2 * LANES), BF),
         pltpu.VMEM((nb * nb * len(pieces), 2 * LANES), BF), pltpu.VMEM((rows, 1), F32),
         pltpu.VMEM((rows, 1), F32),
     ]
     return call(
-        functools.partial(gate_kernel, len(pieces)), (2, NCW), ins, outs, scratch,
-        2 * rows * NS * DI * 8,
-    )
-
-
-def intra_back_kernel(bs, cs, xt, cum, cum_t, dyr, dye, enter, dxt, db, dc, scores, top, bottom):
+        functools.partial(gate_kernel, len(pieces)), 16, (2, GNW), ins, outs, scratch, VMEM_ASK,
+    )
+
+
+def intra_back_kernel(
+    bs, cs, xt, cum, cum_t, dyr, dye, enter, normed, wo, tok, dxt, db, dc, mixed, scores, top, bottom,
+    total,
+):
     c = pl.program_id(0)
     nb = bs.shape[0] // CH
     low = iota((CH, LANES), 1) < HD
@@ -708,6 +696,9 @@
         top[...] = jnp.zeros_like(top)
         bottom[...] = jnp.zeros_like(bottom)
         dc[...] = jnp.zeros_like(dc)
+        total[...] = tok[...].astype(F32)
+
+    total[...] += dot(normed[...], wo[...])
 
     for i in range(nb):
         r = slice(i * CH, (i + 1) * CH)
@@ -752,9 +743,10 @@
             both = jnp.concatenate([up, down], axis=0)
             db[r, :] = dot(both, cs[r, :])
             dc[r, :] += dot_tn(both, bs[r, :])
-
-
-def run_intra_back(a, dyr, dye, enter):
+        mixed[...] = total[...].astype(BF)
+
+
+def run_intra_back(a, dyr, dye, enter, normed, wo, tok):
     rows = dyr.shape[0]
     nb = rows // CH
 
@@ -764,16 +756,16 @@
     ins = [(a[k], whole(a[k])) for k in ("bs", "cs")]
     ins += [(a["xt"], columns(a["xt"], same))]
     ins += [(a[k], whole(a[k])) for k in ("cum", "cum_t")]
-    ins += [(v, columns(v, same)) for v in (dyr, dye, enter)]
-    full, small = shape((rows, DI), F32), shape((rows, NS), F32)
+    ins += [(v, columns(v, same)) for v in (dyr, dye, enter, normed)]
+    ins += [(wo, pl.BlockSpec((CW, DM), lambda c: (c, 0))), (tok, whole(tok))]
+    full, small, mixed = shape((rows, DI), F32), shape((rows, NS), F32), shape((rows, DM), BF)
     return call(
-        intra_back_kernel, (NCW,), ins,
-        [(full, columns(full, same)), (small, whole(small)), (small, whole(small))],
+        intra_back_kernel, 1, (NCW,), ins,
+        [(full, columns(full, same))] + [(v, whole(v)) for v in (small, small, mixed)],
         [
             pltpu.VMEM((nb, CH, CH), F32), pltpu.VMEM((nb, HALF, CH), F32),
-            pltpu.VMEM((nb, HALF, HALF), F32),
+            pltpu.VMEM((nb, HALF, HALF), F32), pltpu.VMEM((rows, DM), F32),
         ],
-        2 * rows * CH * DI * 4,
     )
 
 
@@ -783,8 +775,8 @@
     ends = refs[1 + n_pieces : 1 + 2 * n_pieces]
     (
         dx_intra, db_in, dc_in, xbc, slope, xs, xt, bs, raw, cum, enter, product, dyr, conv_w,
-        a_log, d_skip, table, narrow,
-        d_a, kernel_part, offset_part, bias_part, rate_part,
+        a_log, d_skip, table, narrow, gain_part, skip_part,
+        d_a, sums,
         grad, small, d_bs, heads, weights,
     ) = refs[1 + 2 * n_pieces :]
     step = pl.program_id(0)
@@ -805,6 +797,10 @@
             grad[i, HALO + CH :, :] = jnp.zeros((HALO, CW), F32)
         d_bs[...] = db_in[...]
         heads[...] = jnp.zeros_like(heads)
+
+    def put_rows(at, row):
+        for j in range(row.shape[1] // LANES):
+            sums[pl.ds(at + j, 1), :] = row[:, j * LANES : (j + 1) * LANES]
 
     def convolve_back(dacts, width):
         offset_sum = jnp.zeros((1, width), F32)
@@ -834,9 +830,8 @@
             d_a[r, :width] = (total * usable_of(info, i)).astype(BF)
             head_grads.append(total_head * halo_used(info, i))
         d_a[rows:, :width] = jnp.concatenate(head_grads, axis=0).astype(BF)
-        offset_part[:, :width] = offset_sum
-        for k in range(KC):
-            kernel_part[k : k + 1, :width] = tap_sums[k]
+        for k, row in enumerate(tap_sums + [offset_sum]):
+            put_rows(k * (XBC // LANES) + step * (CW // LANES), row)
 
     @pl.when(step < NCW)
     def _():
@@ -867,6 +862,8 @@
                 dot(small[i, 0], table[...]) * dxt + d_skip[...] * dyr[r, :].astype(F32)
             )
         convolve_back(dacts, CW)
+        put_rows(SUM_GAIN + step * (CW // LANES), gain_part[...])
+        put_rows(SUM_SKIP + step * (CW // LANES), skip_part[...])
 
     @pl.when(step == NCW)
     def _():
@@ -893,12 +890,13 @@
             rate_sum = rate_sum - jnp.sum(d_log * softplus(start), axis=0, keepdims=True) * rate
             d_a[r, 2 * NS :] = d_raw.astype(BF)
         d_a[rows:, 2 * NS :] = jnp.zeros((nb * HALO, CW - 2 * NS), BF)
-        bias_part[...] = bias_sum
-        rate_part[...] = rate_sum
+        put_rows(SUM_HEADS, bias_sum)
+        put_rows(SUM_HEADS + 1, rate_sum)
 
 
 def run_back(
-    info, a, pieces, ends, dx_intra, db, dc, enter, product, dyr, conv_w, a_log, d_skip, table
+    info, a, pieces, ends, dx_intra, db, dc, enter, product, dyr, conv_w, a_log, d_skip, table,
+    narrow, gain_part, skip_part,
 ):
     rows = dyr.shape[0]
     nb = rows // CH
@@ -910,7 +908,6 @@
     def same(s):
         return s
 
-    narrow = table[:LANES].T
     ins = [(info, in_smem())]
     ins += [(v, columns(v, chunk)) for v in pieces]
     ins += [(v, pl.BlockSpec((nb, 16, LANES), lambda s: (0, 0, DI // LANES))) for v in ends]
@@ -922,18 +919,16 @@
     ins += [(conv_w, columns(conv_w, same)), (a_log, whole(a_log)), (d_skip, columns(d_skip, chunk))]
     ins += [(table, columns(table, chunk))]
     ins += [(narrow, pl.BlockSpec((CW, LANES), lambda s: (chunk(s), 0)))]
-    wide, taps, row = shape((ext_rows, WA), BF), shape((KC, WA), F32), shape((1, WA), F32)
-    lane = shape((1, LANES), F32)
-    outs = [(v, columns(v, same)) for v in (wide, taps, row)]
-    outs += [(lane, whole(lane)), (lane, whole(lane))]
+    ins += [(v, columns(v, chunk)) for v in (gain_part, skip_part)]
+    wide, sums = shape((ext_rows, WA), BF), shape((SUM_ROWS, LANES), F32)
+    outs = [(wide, columns(wide, same)), (sums, whole(sums))]
     scratch = [
         pltpu.VMEM((nb, CH + 2 * HALO, CW), F32), pltpu.VMEM((nb, 2, CH, 2 * LANES), BF),
         pltpu.VMEM((rows, NS), F32), pltpu.VMEM((3, rows, LANES), F32),
         pltpu.VMEM((nb * nb * len(pieces), 2 * LANES), BF),
     ]
     return call(
-        functools.partial(back_kernel, len(pieces)), (NCW + 1,), ins, outs, scratch,
-        2 * rows * NS * DI * 16,
+        functools.partial(back_kernel, len(pieces)), 2, (NCW + 1,), ins, outs, scratch, VMEM_ASK,
     )
 
 
@@ -965,32 +960,45 @@
     piece_a = jnp.concatenate(
         [in_weight[:, DI:], norm_gain[:, None], jnp.zeros((k_rows, WA - XBC - NH - 1), BF)], axis=1
     )
-    parts_a = gather_pieces(piece_a)
-    me = shard_at.astype(jnp.int32)
-    if k_rows % 32:
-        joined = jnp.zeros((n_shard, k_rows, WA), BF)
-        for v, k, _ in parts_a:
-            joined = lax.dynamic_update_slice(joined, v[None], (shard_at ^ k, 0, 0))
-        parts_a, me = [(joined.reshape(DM, WA), 0, None)], jnp.int32(0)
-    piece_zo = jnp.concatenate(
-        [in_weight[:, :DI], out_weight[:k_rows], out_weight[k_rows:]], axis=1
-    )
-    zo = lax.all_gather(piece_zo, "shard", axis=0, tiled=True)
-
-    tails = tokens.reshape(nb, CH, DM)[:, CH - HALO :].reshape(nb * HALO, DM)
-    tails = group_spread(tails, stay)
-    tok_got = move_home(after(tokens, tails[0]))
-    cot_got = move_home(after(cotangent, tok_got))
-
+    table = spread_table()
+
+    def head_row(v):
+        return jnp.pad(v, (0, LANES - NH))[None]
+
+    narrow = narrow_table()
+    gain_row = inner_gain[None]
+    at = shard_at.astype(jnp.int32).reshape(1)
+    taps = jnp.pad(conv_weight, ((0, 0), (0, WA - XBC)))
+    rate_row = head_row(a_log)
+    skip_row = jnp.repeat(d_skip, HD)[None]
+    taps, rate_row, skip_row, bias_row, step_row, gain_row, narrow, table = after_all(
+        [
+            taps, rate_row, skip_row, jnp.pad(conv_bias, (0, WA - XBC))[None], head_row(dt_bias),
+            gain_row, narrow, table,
+        ]
+    )
+    prepared = [taps, rate_row, skip_row, bias_row, step_row, gain_row, narrow, table]
     numbers = jnp.concatenate([block_place, seq_length], axis=1)
-    numbers = jnp.where(stay, numbers, trade(numbers, "shard", 1))[0]
+    numbers_got = trade(numbers, "shard", 1)
+    me = jnp.int32(0) if k_rows % 32 else shard_at.astype(jnp.int32)
+    def block_tails(v):
+        return v.reshape(nb, CH, DM)[:, CH - HALO :].reshape(nb * HALO, DM)
+
+    tok_got = move_home(tokens)
+    tails = jnp.where(stay, block_tails(tokens), block_tails(tok_got))
+
+    numbers = jnp.where(stay, numbers, numbers_got)[0]
     lengths = [numbers[group_blocks + k] for k in range(seq_length.shape[1])]
-    ids = []
-    for core in (0, 1):
-        for z in range(half):
-            device = (head_at % half ^ z) + ((shard_at & 1) ^ core) * half
-            ids += [device * nb + b for b in range(nb)]
-    ids = jnp.stack(ids)
+
+    def order_from(core_at):
+        ids = []
+        for core in (0, 1):
+            for z in range(half):
+                device = (head_at % half ^ z) + (core_at ^ core) * half
+                ids += [device * nb + b for b in range(nb)]
+        return jnp.stack(ids)
+
+    ids, home_order = order_from(shard_at & 1), order_from(head_at // half)
     places = jnp.sum(
         jnp.where(ids[:, None] == jnp.arange(group_blocks)[None, :], numbers[None, :group_blocks], 0),
         axis=1,
@@ -1007,105 +1015,138 @@
         ]
     ).astype(jnp.int32)
 
-    table = spread_table()
-
-    def head_row(v):
-        return jnp.pad(v, (0, LANES - NH))[None]
-
-    taps = jnp.pad(conv_weight, ((0, 0), (0, WA - XBC)))
-    rate_row = head_row(a_log)
-    skip_row = jnp.repeat(d_skip, HD)[None]
-    a = run_project(
-        info, parts_a, tails, tokens, tok_got, taps, jnp.pad(conv_bias, (0, WA - XBC))[None],
-        head_row(dt_bias), rate_row, table,
-    )
+    parts_a = gather_pieces(piece_a, info, *prepared)
+    if k_rows % 32:
+        joined = jnp.zeros((n_shard, k_rows, WA), BF)
+        for v, k in parts_a:
+            joined = lax.dynamic_update_slice(joined, v[None], (shard_at ^ k, 0, 0))
+        parts_a = [(joined.reshape(DM, WA), 0)]
+    wo = lax.all_gather(out_weight, "shard", axis=0, tiled=True)
+    wz = lax.all_gather(in_weight[:, :DI], "shard", axis=0, tiled=True)
+
+    tails = group_spread(after(tails, *[v for v, _ in parts_a[1:]]))
+    cot_got = move_home(after(cotangent, *tails))
+    a = run_project(info, parts_a, tails, tokens, tok_got, taps, bias_row, step_row, rate_row, table)
     wa, tok, normal = a["wa"], a["tok"], a["normal"]
     state_by_head = head_pieces(a["states"])
     state_by_core = trade(a["states"], "shard", 1)
-    cot = jnp.where(stay, cotangent, after(cot_got, a["cum"]))
-    if k_rows % 32:
-        wz = zo[:, :DI]
-        wo = zo[:, DI:].reshape(n_shard, k_rows, 2, DM).swapaxes(1, 2).reshape(DI, DM)
-        z, q, y_intra = dot(normal[:rows], wz).astype(BF), dot_nt(cot, wo).astype(BF), run_intra(a)
-    else:
-        y_intra, z, q, wz, wo = run_middle(a, cot, zo)
-    state_by_head = [after(v, y_intra) for v in state_by_head]
+    y_intra = run_intra(a)
+    cot = jnp.where(stay, cotangent, after(cot_got, y_intra))
+    q = dot_nt(cot, wo).astype(BF)
+    z = dot(after(normal, q)[:rows], wz).astype(BF)
+    state_by_head = [after(v, z) for v in state_by_head]
     all_states = (
         [a["states"]] + state_by_head + [state_by_core] + [trade(v, "shard", 1) for v in state_by_head]
     )
     enter, normed, gain_part, dz, dyr, dye, product, skip_part, d_enter = run_gate(
-        info, a, all_states, y_intra, z, q, inner_gain[None], skip_row, table
+        info, a, all_states, y_intra, z, q, gain_row, skip_row, table
     )
     enter_by_head = head_pieces(d_enter)
     enter_by_core = trade(d_enter, "shard", 1)
-    if k_rows % 32:
-        z_term = dot_tn(normal[:rows], dz).astype(BF)
-        out_term = dot_tn(normed, cot).astype(BF).reshape(n_shard, 2, k_rows, DM)
-        out_term = out_term.swapaxes(1, 2).reshape(DM, 2 * DM)
-        zo_term = jnp.concatenate([z_term, out_term], axis=1)
-    else:
-        zo_term = run_terms(normal, dz, normed, cot)
+    zo_term = run_terms(a["normal_t"], dz, normed, cot)
     zo_own = lax.psum_scatter(zo_term, "shard", scatter_dimension=0, tiled=True)
-    dx_intra, db, dc = run_intra_back(a, after(dyr, zo_term), dye, enter)
-    mixed = (tok.astype(F32) + dot(after(normed, dx_intra), wo)).astype(BF)
-    enter_by_head = [after(v, mixed) for v in enter_by_head]
+    dx_intra, db, dc, mixed = run_intra_back(a, after(dyr, zo_term), dye, enter, normed, wo, tok)
+    enter_by_head = [after(v, dx_intra) for v in enter_by_head]
     all_enter = (
         [d_enter] + enter_by_head + [enter_by_core] + [trade(v, "shard", 1) for v in enter_by_head]
     )
     mixed_got = move_home(after(mixed, all_enter[-1]))
-    d_a_all, kernel_part, offset_part, bias_part, rate_part = run_back(
-        info, a, all_enter, all_states, dx_intra, db, dc, enter, product, dyr, taps, rate_row,
-        skip_row, table,
-    )
+    d_a_all, small = run_back(
+        info, a, all_enter, all_states, dx_intra, db, dc, enter, product, dyr, taps,
+        rate_row, skip_row, table, narrow, gain_part, skip_part,
+    )
+    d_a_all = after(d_a_all, mixed_got)
     a_term = dot_tn(normal, d_a_all).astype(BF).reshape(n_shard, k_rows, WA)
     a_keep, a_give = core_give([a_term])
     a_got = trade(a_give, "shard", 1)
 
-    small = jnp.concatenate(
-        [
-            kernel_part[:, :XBC].reshape(-1), offset_part[0, :XBC], bias_part[0, :NH],
-            rate_part[0, :NH], jnp.sum(skip_part.reshape(NH, HD), axis=1), gain_part[0],
-        ]
-    )
-    small = full_sum(after(small, a_give))
-
-    d_a_all = after(d_a_all, a_give)
+    small_got = trade(after(small, a_give), "shard", 1)
+    d_a_all, dz, tok, tok_halo, wa = after_all([d_a_all, dz, tok, a["tok_halo"], wa], a_give)
+    gain = wa[:, XBC + NH].astype(F32)
+    halo_part = norm_back(dot_nt(d_a_all[rows:], wa), tok_halo, gain)
+    halo_part = halo_part.reshape(nb, HALO, DM)[:, HALO - KC :].astype(BF).reshape(k_rows, -1)
+    halos = [halo_part, trade(halo_part, "shard", 1)]
     normal_grad = dot_nt(dz, wz) + dot_nt(d_a_all[:rows], wa)
-    halo_grad = dot_nt(d_a_all[rows:], wa)
-    gain = wa[:, XBC + NH].astype(F32)
     token_grad = (cot.astype(F32) + norm_back(normal_grad, tok, gain)).astype(BF)
-    halo_part = norm_back(halo_grad, a["tok_halo"], gain)
-
-    a_pairs = chip_pairs(a_keep, a_got)
+
+    a_got, small_got, halos[1], zo_own = after_all([a_got, small_got, halos[1], zo_own], token_grad)
+    zo_sum = lax.psum(zo_own, "head")
+    if k_rows % 32:
+        parts = split2((small + small_got).reshape(k_rows, -1))
+        a_pairs = [jnp.concatenate([v, parts], axis=1) for v in chip_pairs(a_keep, a_got)]
+    else:
+        a_pairs = run_pair_small(at, a_keep, a_got, small, small_got)
     a_far = chip_send(a_pairs)
     token_got = move_home(after(token_grad, a_pairs[0]))
-    token_grad = jnp.where(stay, token_grad, token_got)
-    all_halo = jnp.concatenate(group_gather(halo_part)).reshape(group_blocks, HALO, DM)
-    is_next = (places[None, :] == places[:nb, None] + 1) & (first[None, :] == first[:nb, None])
-    halo_back = swap_home(
-        jnp.sum(jnp.where(is_next[:, :, None, None], all_halo[None], 0.0), axis=1), stay
-    )
-    token_grad = token_grad.reshape(nb, CH, DM)
-    token_grad = token_grad.at[:, CH - HALO :].set(
-        (token_grad[:, CH - HALO :].astype(F32) + halo_back).astype(BF)
+    *a_far, token_got = after_all(a_far + [token_got])
+    a_own = chip_sum(a_pairs[0][:, :WA], [v[:, :WA] for v in a_far])
+    sums = [join2(v[:, WA:]) for v in [a_pairs[0]] + a_far]
+    while len(sums) > 1:
+        sums = [sums[k] + sums[k + 1] for k in range(0, len(sums), 2)]
+    small = sums[0]
+    a_keep, a_give = head_split(a_own)
+    small_keep, small_give = head_split(small)
+    cut, edge = a_keep.shape[1], a_keep.shape[1] + 2 * small_keep.shape[1]
+    total, small = a_keep.astype(F32), small_keep
+    bits = [b for b in (1, 2, 4, 8, 16) if b < n_head]
+    for bit in bits:
+        if bit > 1:
+            a_give, small_give = total.astype(BF), small
+            total = a_give.astype(F32)
+        parts = split2(small_give)
+        sent = jnp.concatenate([a_give, parts] + (halos if bit < half else []), axis=1)
+        sent = trade(sent, "head", bit)
+        if bit < half:
+            halos = halos + jnp.split(sent[:, edge:], len(halos), axis=1)
+        total = total + sent[:, :cut].astype(F32)
+        small = (small if bit == 1 else join2(parts)) + join2(sent[:, cut:edge])
+    low, parts = total.astype(BF), split2(small)
+    other = trade(jnp.concatenate([low, parts], axis=1), "head", 1)
+    halos = jnp.concatenate(halos, axis=1)
+    halos = jnp.where(stay, halos, move_home(halos))
+    halos = jnp.split(halos, group_blocks // nb, axis=1)
+    other = after(other, *halos)
+    zo_grad = after(zo_sum, other).astype(F32)
+    a_grad = head_join(low, other[:, :cut]).astype(F32)
+    small = head_join(join2(parts), join2(other[:, cut:])).reshape(SUM_ROWS, LANES)
+
+    all_halo = jnp.concatenate(halos[0::2] + halos[1::2]).reshape(group_blocks, KC, DM).astype(F32)
+    own_numbers = jnp.concatenate([block_place, seq_length], axis=1)[0]
+    own_places = jnp.sum(
+        jnp.where(
+            home_order[:, None] == jnp.arange(group_blocks), own_numbers[None, :group_blocks], 0
+        ),
+        axis=1,
+    )
+    home_ids = head_at * nb + jnp.arange(nb)
+    home_places = jnp.sum(
+        jnp.where(
+            home_ids[:, None] == jnp.arange(group_blocks), own_numbers[None, :group_blocks], 0
+        ),
+        axis=1,
+    )
+    goes_on, begin = home_places < 0, 0
+    for k in range(seq_length.shape[1]):
+        end = begin + (own_numbers[group_blocks + k] + CH - 1) // CH
+        goes_on = goes_on | ((home_places >= begin) & (home_places + 1 < end))
+        begin = end
+    is_next = (own_places[None, :] == home_places[:, None] + 1) & goes_on[:, None]
+    halo_back = jnp.sum(jnp.where(is_next[:, :, None, None], all_halo[None], 0.0), axis=1)
+    token_grad = jnp.where(stay, token_grad, token_got).reshape(nb, CH, DM)
+    token_grad = token_grad.at[:, CH - KC :].set(
+        (token_grad[:, CH - KC :].astype(F32) + halo_back).astype(BF)
     ).reshape(rows, DM)
-    mixed = jnp.where(stay, mixed, after(mixed_got, a_give))
-
-    zo_grad = head_sum(after(zo_own, a_pairs[0]))
-    a_grad = head_sum(chip_sum(a_pairs[0], a_far))
+    mixed = jnp.where(stay, mixed, after(mixed_got, a_own))
+
     in_grad = jnp.concatenate([zo_grad[:, :DI], a_grad[:, : XBC + NH]], axis=1)
     out_grad = jnp.concatenate([zo_grad[:, DI : DI + DM], zo_grad[:, DI + DM :]], axis=0)
     gain_grad = jnp.sum(in_grad * in_weight.astype(F32), axis=1) / norm_gain.astype(F32)
 
-    sizes = [KC * XBC, XBC, NH, NH, NH, DI]
-    cuts = []
-    at = 0
-    for s in sizes:
-        cuts.append(small[at : at + s])
-        at += s
     return (
-        mixed, token_grad, gain_grad, in_grad, cuts[0].reshape(KC, XBC), cuts[1], cuts[2], cuts[3],
-        cuts[4], cuts[5], out_grad,
+        mixed, token_grad, gain_grad, in_grad, small[: KC * XBC // LANES].reshape(KC, XBC),
+        small[KC * XBC // LANES : SUM_GAIN].reshape(XBC), small[SUM_HEADS, :NH],
+        small[SUM_HEADS + 1, :NH], jnp.sum(small[SUM_SKIP:SUM_HEADS].reshape(NH, HD), axis=1),
+        small[SUM_GAIN:SUM_SKIP].reshape(DI), out_grad,
     )
 
 

time: 291 us -> 261 us (0.90)
  starting transfers between devices: 75.6 us -> 32.5 us
  waiting for transfers between devices: 67.4 us -> 79.9 us
    ppermute x32 -> x23, starting transfers between devices: 35.7 us -> 11.1 us  [trade(): return lax.ppermute(value, axis, [(i, i ^ bit) for i in range(size)])]
    ppermute x6 -> x5, waiting for transfers between devices: 1.44 us -> 22.7 us  [move_home(): return lax.ppermute(value, ('head', 'shard'), pairs)]
    ppermute x4 -> x0, starting transfers between devices: 8.11 us -> none  [from_core(): lax.ppermute(value, 'shard', [(i, i ^ bit) for i in range(n_shard) if i %...]
    ppermute x6 -> x5, starting transfers between devices: 27.1 us -> 19.1 us  [move_home(): return lax.ppermute(value, ('head', 'shard'), pairs)]
    ppermute x3, waiting for transfers between devices: 8.49 us -> 2.12 us  [group_spread(): pieces.append(lax.ppermute(value, ('head', 'shard'), pairs))]
    ppermute x32 -> x23, waiting for transfers between devices: 57.4 us -> 51.7 us  [trade(): return lax.ppermute(value, axis, [(i, i ^ bit) for i in range(size)])]
    slice x11 -> x3, local copies, waits for them, and re-layouts: 5.17 us -> 1.76 us  [the longest x1 1.71 us: shards(): wz = lax.all_gather(in_weight[:, :DI], 'shard', axis=0, tiled=True)]
    pallas_call x6 -> x7, Pallas kernels: 76.3 us -> 73.9 us  [call(): pl.pallas_call(kernel, grid=grid, out_shape=[o for o, _ in outs], in_spec...]
  transfers between devices with their start and end apart: 47 -> 35, of which waited for: 13 -> 18; matrix products, arithmetic and copies ran while one was open for 15% -> 18% of each run, Pallas kernels for 21% -> 19%
where the time goes in v1:
time: 261 us; the launch traced here: 258 us
  waiting for transfers between devices  79.9 us (31%)
  Pallas kernels  73.9 us (28%)
  starting transfers between devices  32.5 us (12%)
  matrix products  20.6 us (8%)
  local copies, waits for them, and re-layouts  19.1 us (7%)
  other arithmetic  16.4 us (6%)
  between operations  15.5 us (6%)
    pallas_call x7, Pallas kernels, call(): pl.pallas_call(kernel, grid=grid, out_shape=[o for o, _ in outs], in_spec...  73.9 us
    ppermute x23, waiting for transfers between devices, trade(): return lax.ppermute(value, axis, [(i, i ^ bit) for i in range(size)])  51.7 us
    ppermute x5, waiting for transfers between devices, move_home(): return lax.ppermute(value, ('head', 'shard'), pairs)  22.7 us
    ppermute x5, starting transfers between devices, move_home(): return lax.ppermute(value, ('head', 'shard'), pairs)  19.1 us
    dot_general x4, matrix products, dot_nt(): lax.dot_general(a, b, (((1,), (1,)), ((), ())), preferred_element_type=F32)  11.8 us
    ppermute x23, starting transfers between devices, trade(): return lax.ppermute(value, axis, [(i, i ^ bit) for i in range(size)])  11.1 us
  transfers between devices with their start and end apart: 35, of which 18 were waited for; matrix products, arithmetic and copies ran while one was open for 18% of the time, Pallas kernels for 19%

profile of v1, /device:TPU:1, one launch (start us, length us, event | category | flops | bytes accessed | tf_op | source)
XLA Modules:
  0.0 258.0 jit_solution(14663041468421654291)
XLA Ops:
  7.3 0.7 all-gather.3.cloned.1.call-update
  8.0 1.0 slice.147
  9.1 0.8 copy.33
  10.0 3.1 %collective-permute-start.1 = (bf16[96,1920]{1,0:T(8,128)(2,1)S(1)}, bf16[96,1920]{1,0:T(8,128)(2,1)S(1)}, u32[]{:S(2)}, u32[]{:S(2)}) collective-permute-start(bf16[96,1920]{1,0:T(8,128)(2,1)S(1)} %concatenate.42.refs_1_), channel_id=1, source_target_pairs={{0,6},{1,7},{2,4},{3,5},{4,2},{5,3},{6,0},{7,1},{8,14},{9,15},{10,... | collective-permute-start | bytes 1105928 | tf_op jit(solution)/shard_map/ppermute | solution.py:33
  14.1 1.2 collective-permute-start
  15.4 4.5 %collective-permute-start.8 = (bf16[512,768]{1,0:T(8,128)(2,1)S(1)}, bf16[512,768]{1,0:T(8,128)(2,1)S(1)}, u32[]{:S(2)}, u32[]{:S(2)}) collective-permute-start(bf16[512,768]{1,0:T(8,128)(2,1)S(1)} %copy-done.12), channel_id=1, source_target_pairs={{1,16},{3,18},{5,20},{7,22},{9,24},{11,26},{13,28},{15,30},{16,1},... | collective-permute-start | bytes 2359304 | tf_op jit(solution)/shard_map/ppermute | solution.py:50
  19.9 1.7 slice.151
  21.8 0.7 broadcast_in_dim_reshape.3.refs_16_.refs_24_
  25.5 1.0 fusion.13.refs_26_
  26.5 1.1 compare_convert_fusion.refs_19_.refs_17_.refs_25_
  29.9 2.6 collective-permute-done.2.refs_3_
  32.5 0.8 collective-permute-done.3.refs_4_
  33.3 0.7 collective-permute-start.4
  34.5 3.5 %collective-permute-done.8.refs_14_ = bf16[512,768]{1,0:T(8,128)(2,1)S(1)} collective-permute-done((bf16[512,768]{1,0:T(8,128)(2,1)S(1)}, bf16[512,768]{1,0:T(8,128)(2,1)S(1)}, u32[]{:S(2)}, u32[]{:S(2)}) %collective-permute-start.8) | collective-permute-done | bytes 786464 | tf_op jit(solution)/shard_map/ppermute | solution.py:50
  38.2 0.8 collective-permute-start.11
  39.0 1.1 collective-permute-start.9
  40.1 2.0 collective-permute-done.11.refs_12_
  42.2 6.1 %collective-permute-start.13 = (bf16[512,768]{1,0:T(8,128)(2,1)S(1)}, bf16[512,768]{1,0:T(8,128)(2,1)S(1)}, u32[]{:S(2)}, u32[]{:S(2)}) collective-permute-start(bf16[512,768]{1,0:T(8,128)(2,1)S(1)} %copy-done.19), channel_id=1, source_target_pairs={{1,16},{3,18},{5,20},{7,22},{9,24},{11,26},{13,28},{15,30},{16,1},... | collective-permute-start | bytes 2359304 | tf_op jit(solution)/shard_map/ppermute | solution.py:50
  48.4 14.4 %shard_map.212 = (bf16[768,1920]{1,0:T(8,128)(2,1)}, bf16[512,768]{1,0:T(8,128)(2,1)}, bf16[16,768]{1,0:T(8,128)(2,1)}, bf16[528,768]{1,0:T(8,128)(2,1)}, bf16[7...) custom-call(s32[26]{0:T(128)} %pad_add_fusion.2.refs_0_, ...), custom_call_target="tpu_custom_call" | custom-call | flops 1 | bytes 20720000 | tf_op jit(solution)/shard_map/pallas_call | solution.py:228
  63.0 6.4 %shard_map.213.refs_9_ = f32[512,1536]{1,0:T(8,128)} custom-call(bf16[512,128]{1,0:T(8,128)(2,1)} %get-tuple-element.109.bs.refs_16_, bf16[512,128]{1,0:T(8,128)(2,1)} %get-tuple-element.110.cs.refs_10_, bf16[512,1536]{1,0:T(8,128)(2,1)} %get-tuple-element.111.xt.refs_15_, f32[512,128]{1,0:T(8,128)} %get-tuple-element.112.cum.refs_11_.refs_18_, ...), custom_call_target="tpu_custom_call" | custom-call | flops 1 | bytes 8880000 | tf_op jit(solution)/shard_map/pallas_call | solution.py:228
  69.5 4.6 %convolution_convert_fusion.2.refs_14_ = bf16[512,1536]{1,0:T(8,128)(2,1)} fusion(bf16[512,768]{1,0:T(8,128)(2,1)S(1)} %broadcast_select_fusion.2.cot, bf16[1536,768]{1,0:T(8,128)(2,1)} %all-gather.3.cloned.1.call-done.wo), kind=kOutput, calls=%fused_computation.2 | convolution fusion | flops 1208745984 | bytes 4718592 | tf_op jit(solution)/shard_map/dot_general | solution.py:171
  74.1 2.6 %all-gather.5.cloned.1.call-done = bf16[768,1536]{1,0:T(8,128)(2,1)} async-done(((bf16[96,1536]{1,0:T(8,128)(2,1)}), bf16[768,1536]{1,0:T(8,128)(2,1)}) %all-gather.5.cloned.1.call-update) | async-done | bytes 2359312 | tf_op jit(solution)/shard_map/all_gather | solution.py:1025
  76.7 4.5 %convolution_convert_fusion.1.refs_13_ = bf16[512,1536]{1,0:T(8,128)(2,1)} fusion(bf16[768,1536]{1,0:T(8,128)(2,1)} %all-gather.5.cloned.1.call-done, bf16[528,768]{1,0:T(8,128)(2,1)} %get-tuple-element.118), kind=kOutput, calls=%fused_computation.1 | convolution fusion | flops 1208745984 | bytes 4718592 | tf_op jit(solution)/shard_map/dot_general | solution.py:167
  81.2 3.2 %collective-permute-done.12.refs_2_.refs_6_ = bf16[2,128,1664]{2,1,0:T(8,128)(2,1)S(1)} collective-permute-done((bf16[2,128,1664]{2,1,0:T(8,128)(2,1)}, bf16[2,128,1664]{2,1,0:T(8,128)(2,1)S(1)}, u32[]{:S(2)}, u32[]{:S(2)}) %collective-permute-start.12) | collective-permute-done | bytes 852000 | tf_op jit(solution)/shard_map/ppermute | solution.py:33
  84.8 2.0 collective-permute-done.15.refs_4_.refs_8_
  86.8 0.9 copy-done.2
  87.7 14.4 %shard_map.214 = (bf16[2,128,1536]{2,1,0:T(8,128)(2,1)}, bf16[512,1536]{1,0:T(8,128)(2,1)}, f32[1,1536]{1,0:T(1,128)}, bf16[512,1536]{1,0:T(8,128)(2,1)}, bf16[5...) custom-call(s32[26]{0:T(128)} %pad_add_fusion.2.refs_0_, ...), custom_call_target="tpu_custom_call" | custom-call | flops 1 | bytes 23680000 | tf_op jit(solution)/shard_map/pallas_call | solution.py:228
  102.1 6.8 %shard_map.215 = bf16[768,3072]{1,0:T(8,128)(2,1)} custom-call(bf16[768,512]{1,0:T(8,128)(2,1)} %get-tuple-element.122.normal_t, bf16[512,1536]{1,0:T(8,128)(2,1)} %get-tuple-element.152.dz, bf16[512,1536]{1,0:T(8,128)(2,1)} %get-tuple-element.124.normed, bf16[512,768]{1,0:T(8,128)(2,1)} %copy-done.3), custom_call_target="tpu_custom_call" | custom-call | flops 1 | bytes 1480000 | tf_op jit(solution)/shard_map/pallas_call | solution.py:228
  109.2 0.8 copy-done.15
  110.1 11.5 %shard_map.216 = (f32[512,1536]{1,0:T(8,128)}, f32[512,128]{1,0:T(8,128)}, f32[512,128]{1,0:T(8,128)}, bf16[512,768]{1,0:T(8,128)(2,1)}) custom-call(bf16[512,128]{1,0:T(8,128)(2,1)} %get-tuple-element.109.bs.refs_16_, bf16[512,128]{1,0:T(8,128)(2,1)} %get-tuple-element.110.cs.refs_10_, bf16[512,1536]{1,0:T(8,128)(2,1)} %get-tuple-element.111.xt.refs_15_, ...), custom_call_target="tpu_custom_call" | custom-call | flops 1 | bytes 1480000 | tf_op jit(solution)/shard_map/pallas_call | solution.py:228
  121.6 7.2 %collective-permute-done.16.refs_2_ = bf16[2,128,1536]{2,1,0:T(8,128)(2,1)S(1)} collective-permute-done((bf16[2,128,1536]{2,1,0:T(8,128)(2,1)S(1)}, bf16[2,128,1536]{2,1,0:T(8,128)(2,1)S(1)}, u32[]{:S(2)}, u32[]{:S(2)}) %collective-permute-start.16) | collective-permute-done | bytes 786464 | tf_op jit(solution)/shard_map/ppermute | solution.py:33
  128.8 1.2 collective-permute-start.17
  130.1 1.9 collective-permute-done.17.refs_4_
  132.0 3.1 %collective-permute-start.18 = (bf16[512,768]{1,0:T(8,128)(2,1)}, bf16[512,768]{1,0:T(8,128)(2,1)}, u32[]{:S(2)}, u32[]{:S(2)}) collective-permute-start(bf16[512,768]{1,0:T(8,128)(2,1)} %get-tuple-element.133), channel_id=1, source_target_pairs={{1,16},{3,18},{5,20},{7,22},{9,24},{11,26},{13,28},{15,30},{16,1},... | collective-permute-start | bytes 2359304 | tf_op jit(solution)/shard_map/ppermute | solution.py:50
  135.5 0.9 copy-done.18
  136.4 17.3 %shard_map.217 = (bf16[528,1920]{1,0:T(8,128)(2,1)}, f32[96,128]{1,0:T(8,128)}) custom-call(s32[26]{0:T(128)} %pad_add_fusion.2.refs_0_, bf16[2,128,1536]{2,1,0:T(8,128)(2,1)} %get-tuple-element.130.refs_1_, bf16[2,128,1536]{2,1,0:T(8,128)(2,1)} %copy-done.16, bf16[2,128,1536]{2,1,0:T(8,128)(2,1)} %copy-done.18, bf16[2,128,1536]{2,1,0:T(8,128)(2,1)} %copy-done.17, ...), custom_call_target="tpu_custom_call" | custom-call | flops 1 | bytes 2960000 | tf_op jit(solution)/shard_map/pallas_call | solution.py:228
  153.6 1.1 collective-permute-done.18
  154.7 4.4 %convolution_convert_fusion = bf16[768,1920]{1,0:T(8,128)(2,1)S(1)} fusion(bf16[528,768]{1,0:T(8,128)(2,1)S(1)} %copy-done.46, bf16[528,1920]{1,0:T(8,128)(2,1)} %get-tuple-element.149), kind=kOutput, calls=%fused_computation | convolution fusion | flops 1558609920 | bytes 5787648 | tf_op jit(solution)/shard_map/dot_general | solution.py:175
  159.1 1.9 dynamic-slice_bitcast_fusion
  161.1 1.0 copy-done.6
  162.3 2.0 fusion.18
  165.3 3.2 %fusion.42 = f32[512,768]{1,0:T(8,128)S(1)} fusion(bf16[512,1536]{1,0:T(8,128)(2,1)S(1)} %copy-done.10, bf16[768,1536]{1,0:T(8,128)(2,1)} %all-gather.5.cloned.1.call-done), kind=kOutput, calls=%fused_computation.120 | convolution fusion | flops 1207959552 | bytes 5505024 | tf_op jit(solution)/shard_map/dot_general | solution.py:171
  168.6 2.0 fusion.4
  172.4 3.1 %shard_map.218 = (bf16[96,2176]{1,0:T(8,128)(2,1)}, bf16[96,2176]{1,0:T(8,128)(2,1)}, bf16[96,2176]{1,0:T(8,128)(2,1)}, bf16[96,2176]{1,0:T(8,128)(2,1)}) custom-call(s32[1]{0:T(128)} %bitcast.at, bf16[4,96,1920]{2,1,0:T(8,128)(2,1)} %get-tuple-element.172.keep, bf16[4,96,1920]{2,1,0:T(8,128)(2,1)} %collective-permute-done.20.got, ...), custom_call_target="tpu_custom_call" | custom-call | flops 1 | bytes 1480000 | tf_op jit(solution)/shard_map/pallas_call | solution.py:228
  175.4 2.4 collective-permute-start.26
  178.0 1.3 collective-permute-start.23
  179.3 1.4 collective-permute-start.24
  180.9 9.2 %collective-permute-done.23 = bf16[96,2176]{1,0:T(8,128)(2,1)S(1)} collective-permute-done((bf16[96,2176]{1,0:T(8,128)(2,1)}, bf16[96,2176]{1,0:T(8,128)(2,1)S(1)}, u32[]{:S(2)}, u32[]{:S(2)}) %collective-permute-start.23) | collective-permute-done | bytes 417824 | tf_op jit(solution)/shard_map/ppermute | solution.py:33
  190.1 9.3 %collective-permute-done.24 = bf16[96,2176]{1,0:T(8,128)(2,1)} collective-permute-done((bf16[96,2176]{1,0:T(8,128)(2,1)}, bf16[96,2176]{1,0:T(8,128)(2,1)}, u32[]{:S(2)}, u32[]{:S(2)}) %collective-permute-start.24) | collective-permute-done | bytes 417824 | tf_op jit(solution)/shard_map/ppermute | solution.py:33
  199.4 8.2 %collective-permute-done.26 = bf16[512,768]{1,0:T(8,128)(2,1)S(1)} collective-permute-done((bf16[512,768]{1,0:T(8,128)(2,1)S(1)}, bf16[512,768]{1,0:T(8,128)(2,1)S(1)}, u32[]{:S(2)}, u32[]{:S(2)}) %collective-permute-start.26) | collective-permute-done | bytes 786464 | tf_op jit(solution)/shard_map/ppermute | solution.py:50
  207.6 0.9 add_add_fusion.2
  208.5 1.4 add_convert_fusion
  210.2 0.8 concatenate.43
  211.0 2.2 broadcast_select_fusion
  213.2 3.0 %collective-permute-done.27 = bf16[96,1216]{1,0:T(8,128)(2,1)S(1)} collective-permute-done((bf16[96,1216]{1,0:T(8,128)(2,1)}, bf16[96,1216]{1,0:T(8,128)(2,1)S(1)}, u32[]{:S(2)}, u32[]{:S(2)}) %collective-permute-start.27) | collective-permute-done | bytes 233504 | tf_op jit(solution)/shard_map/ppermute | solution.py:33
  216.4 3.0 %collective-permute-start.28 = (bf16[96,256]{1,0:T(8,128)(2,1)S(1)}, bf16[96,256]{1,0:T(8,128)(2,1)S(1)}, u32[]{:S(2)}, u32[]{:S(2)}) collective-permute-start(bf16[96,256]{1,0:T(8,128)(2,1)S(1)} %pad_maximum_fusion.3), channel_id=1, source_target_pairs={{1,16},{3,18},{5,20},{7,22},{9,24},{11,26},{13,28},{15,30},{16,1},... | collective-permute-start | bytes 147464 | tf_op jit(solution)/shard_map/ppermute | solution.py:50
  219.8 9.9 %collective-permute-done.28 = bf16[96,256]{1,0:T(8,128)(2,1)S(1)} collective-permute-done((bf16[96,256]{1,0:T(8,128)(2,1)S(1)}, bf16[96,256]{1,0:T(8,128)(2,1)S(1)}, u32[]{:S(2)}, u32[]{:S(2)}) %collective-permute-start.28) | collective-permute-done | bytes 49184 | tf_op jit(solution)/shard_map/ppermute | solution.py:50
  229.7 0.8 broadcast_select_fusion.5
  231.0 6.6 %collective-permute-done.29 = bf16[96,1088]{1,0:T(8,128)(2,1)S(1)} collective-permute-done((bf16[96,1088]{1,0:T(8,128)(2,1)S(1)}, bf16[96,1088]{1,0:T(8,128)(2,1)S(1)}, u32[]{:S(2)}, u32[]{:S(2)}) %collective-permute-start.29) | collective-permute-done | bytes 208928 | tf_op jit(solution)/shard_map/ppermute | solution.py:33
  237.9 6.0 %collective-permute-done.30 = bf16[96,1088]{1,0:T(8,128)(2,1)S(1)} collective-permute-done((bf16[96,1088]{1,0:T(8,128)(2,1)S(1)}, bf16[96,1088]{1,0:T(8,128)(2,1)S(1)}, u32[]{:S(2)}, u32[]{:S(2)}) %collective-permute-start.30) | collective-permute-done | bytes 208928 | tf_op jit(solution)/shard_map/ppermute | solution.py:33
  244.0 0.7 fusion.37
  245.9 1.1 fusion.40
  248.7 1.3 multiply_reduce_fusion
  250.6 0.9 pad_maximum_fusion.1
  (207 shorter events, 16.6 us)
Async XLA Ops:
  7.2 6.9 %copy-start.44 = (s32[1,8]{1,0:T(1,128)S(1)}, s32[1,8]{1,0:T(1,128)}, u32[]{:S(2)}) copy-start(s32[1,8]{1,0:T(1,128)} %param.25) | copy-start | bytes 100
  7.2 8.2 %copy-start.12 = (bf16[512,768]{1,0:T(8,128)(2,1)S(1)}, bf16[512,768]{1,0:T(8,128)(2,1)}, u32[]{:S(2)}) copy-start(bf16[512,768]{1,0:T(8,128)(2,1)} %refs_13_.1) | copy-start | bytes 2359300
  7.2 14.5 %copy-start.43 = (f32[24]{0:T(128)S(1)}, f32[24]{0:T(128)}, u32[]{:S(2)}) copy-start(f32[24]{0:T(128)} %param.22) | copy-start | bytes 292
  7.2 15.3 %copy-start.36 = (f32[4,1792]{1,0:T(4,128)S(1)}, f32[4,1792]{1,0:T(4,128)}, u32[]{:S(2)}) copy-start(f32[4,1792]{1,0:T(4,128)} %param.18) | copy-start | bytes 86020
  7.2 15.9 %copy-start.41 = (f32[1792]{0:T(1024)S(1)}, f32[1792]{0:T(1024)}, u32[]{:S(2)}) copy-start(f32[1792]{0:T(1024)} %param.19) | copy-start | bytes 21508
  7.2 16.5 %copy-start.40 = (f32[1536]{0:T(1024)S(1)}, f32[1536]{0:T(1024)}, u32[]{:S(2)}) copy-start(f32[1536]{0:T(1024)} %param.23) | copy-start | bytes 18436
  7.2 17.1 %copy-start.47 = (f32[24]{0:T(128)S(1)}, f32[24]{0:T(128)}, u32[]{:S(2)}) copy-start(f32[24]{0:T(128)} %param.20) | copy-start | bytes 292
  7.3 17.6 %copy-start.48 = (f32[24]{0:T(128)S(1)}, f32[24]{0:T(128)}, u32[]{:S(2)}) copy-start(f32[24]{0:T(128)} %param.21) | copy-start | bytes 292
  7.3 62.3 %all-gather.3.cloned.1.call-start = ((), (), s32[]{:S(2)}) async-start(), calls=%async_computation.1 | async-start | bytes 2654208 | tf_op jit(solution)/shard_map/all_gather | solution.py:1024
  8.0 68.7 %all-gather.5.cloned.1.call-start = ((), (), s32[]{:S(2)}) async-start(), calls=%async_computation.2 | async-start | bytes 2654208 | tf_op jit(solution)/shard_map/all_gather | solution.py:1025
  9.8 32.3 %copy-start.19 = (bf16[512,768]{1,0:T(8,128)(2,1)S(1)}, bf16[512,768]{1,0:T(8,128)(2,1)}, u32[]{:S(2)}) copy-start(bf16[512,768]{1,0:T(8,128)(2,1)} %param.27) | copy-start | bytes 2359300
  10.0 38.3 %copy-start.11 = (bf16[96,1920]{1,0:T(8,128)(2,1)}, bf16[96,1920]{1,0:T(8,128)(2,1)S(1)}, u32[]{:S(2)}) copy-start(bf16[96,1920]{1,0:T(8,128)(2,1)S(1)} %concatenate.42.refs_1_) | copy-start | bytes 1105924
  10.0 20.0 %collective-permute-start.1 = (bf16[96,1920]{1,0:T(8,128)(2,1)S(1)}, bf16[96,1920]{1,0:T(8,128)(2,1)S(1)}, u32[]{:S(2)}, u32[]{:S(2)}) collective-permute-start(bf16[96,1920]{1,0:T(8,128)(2,1)S(1)} %concatenate.42.refs_1_), channel_id=1, source_target_pairs={{0,6},{1,7},{2,4},{3,5},{4,2},{5,3},{6,0},{7,1},{8,14},{9,15},{10,... | collective-permute-start | bytes 1105928 | tf_op jit(solution)/shard_map/ppermute | solution.py:33
  13.0 19.5 %collective-permute-start.2 = (bf16[96,1920]{1,0:T(8,128)(2,1)S(1)}, bf16[96,1920]{1,0:T(8,128)(2,1)S(1)}, u32[]{:S(2)}, u32[]{:S(2)}) collective-permute-start(bf16[96,1920]{1,0:T(8,128)(2,1)S(1)} %concatenate.42.refs_1_), channel_id=1, source_target_pairs={{0,2},{1,3},{2,0},{3,1},{4,6},{5,7},{6,4},{7,5},{8,10},{9,11},{10,... | collective-permute-start | bytes 1105928 | tf_op jit(solution)/shard_map/ppermute | solution.py:33
  13.3 20.0 %collective-permute-start.3 = (bf16[96,1920]{1,0:T(8,128)(2,1)S(1)}, bf16[96,1920]{1,0:T(8,128)(2,1)}, u32[]{:S(2)}, u32[]{:S(2)}) collective-permute-start(bf16[96,1920]{1,0:T(8,128)(2,1)S(1)} %concatenate.42.refs_1_), channel_id=1, source_target_pairs={{0,4},{1,5},{2,6},{3,7},{4,0},{5,1},{6,2},{7,3},{8,12},{9,13},{10,... | collective-permute-start | bytes 1105928 | tf_op jit(solution)/shard_map/ppermute | solution.py:33
  14.1 13.5 %collective-permute-start = (s32[1,9]{1,0:T(1,128)S(1)}, s32[1,9]{1,0:T(1,128)S(1)}, u32[]{:S(2)}, u32[]{:S(2)}) collective-permute-start(s32[1,9]{1,0:T(1,128)S(1)} %pad_add_fusion.1), channel_id=1, source_target_pairs={{0,1},{1,0},{2,3},{3,2},{4,5},{5,4},{6,7},{7,6},{8,9},{9,8},{10,11... | collective-permute-start | bytes 116 | tf_op jit(solution)/shard_map/ppermute | solution.py:33
  15.4 22.6 %collective-permute-start.8 = (bf16[512,768]{1,0:T(8,128)(2,1)S(1)}, bf16[512,768]{1,0:T(8,128)(2,1)S(1)}, u32[]{:S(2)}, u32[]{:S(2)}) collective-permute-start(bf16[512,768]{1,0:T(8,128)(2,1)S(1)} %copy-done.12), channel_id=1, source_target_pairs={{1,16},{3,18},{5,20},{7,22},{9,24},{11,26},{13,28},{15,30},{16,1},... | collective-permute-start | bytes 2359304 | tf_op jit(solution)/shard_map/ppermute | solution.py:50
  21.7 150.1 %reduce-scatter.2.cloned.1.call-start = ((), (), s32[]{:S(2)}) async-start(), calls=%async_computation.3 | async-start | bytes 5308416 | tf_op jit(solution)/shard_map/reduce_scatter | solution.py:1047
  29.9 18.4 %copy-start.23 = (bf16[96,1920]{1,0:T(8,128)(2,1)}, bf16[96,1920]{1,0:T(8,128)(2,1)S(1)}, u32[]{:S(2)}) copy-start(bf16[96,1920]{1,0:T(8,128)(2,1)S(1)} %collective-permute-done.1.refs_2_) | copy-start | bytes 1105924
  32.5 15.8 %copy-start.24 = (bf16[96,1920]{1,0:T(8,128)(2,1)}, bf16[96,1920]{1,0:T(8,128)(2,1)S(1)}, u32[]{:S(2)}) copy-start(bf16[96,1920]{1,0:T(8,128)(2,1)S(1)} %collective-permute-done.2.refs_3_) | copy-start | bytes 1105924
  33.3 4.8 %collective-permute-start.4 = (bf16[96,1920]{1,0:T(8,128)(2,1)S(1)}, bf16[96,1920]{1,0:T(8,128)(2,1)S(1)}, u32[]{:S(2)}, u32[]{:S(2)}) collective-permute-start(bf16[96,1920]{1,0:T(8,128)(2,1)S(1)} %concatenate.42.refs_1_), channel_id=1, source_target_pairs={{0,1},{1,0},{2,3},{3,2},{4,5},{5,4},{6,7},{7,6},{8,9},{9,8},{10,11... | collective-permute-start | bytes 1105928 | tf_op jit(solution)/shard_map/ppermute | solution.py:33
  33.9 4.1 %collective-permute-start.5 = (bf16[96,1920]{1,0:T(8,128)(2,1)S(1)}, bf16[96,1920]{1,0:T(8,128)(2,1)S(1)}, u32[]{:S(2)}, u32[]{:S(2)}) collective-permute-start(bf16[96,1920]{1,0:T(8,128)(2,1)S(1)} %collective-permute-done.1.refs_2_), channel_id=1, source_target_pairs={{0,1},{1,0},{2,3},{3,2},{4,5},{5,4},{6,7},{7,6},{8,9},{9,8},{10,11... | collective-permute-start | bytes 1105928 | tf_op jit(solution)/shard_map/ppermute | solution.py:33
  34.0 4.1 %collective-permute-start.6 = (bf16[96,1920]{1,0:T(8,128)(2,1)S(1)}, bf16[96,1920]{1,0:T(8,128)(2,1)S(1)}, u32[]{:S(2)}, u32[]{:S(2)}) collective-permute-start(bf16[96,1920]{1,0:T(8,128)(2,1)S(1)} %collective-permute-done.2.refs_3_), channel_id=1, source_target_pairs={{0,1},{1,0},{2,3},{3,2},{4,5},{5,4},{6,7},{7,6},{8,9},{9,8},{10,11... | collective-permute-start | bytes 1105928 | tf_op jit(solution)/shard_map/ppermute | solution.py:33
  34.5 3.6 %collective-permute-start.7 = (bf16[96,1920]{1,0:T(8,128)(2,1)}, bf16[96,1920]{1,0:T(8,128)(2,1)S(1)}, u32[]{:S(2)}, u32[]{:S(2)}) collective-permute-start(bf16[96,1920]{1,0:T(8,128)(2,1)} %collective-permute-done.3.refs_4_), channel_id=1, source_target_pairs={{0,1},{1,0},{2,3},{3,2},{4,5},{5,4},{6,7},{7,6},{8,9},{9,8},{10,11... | collective-permute-start | bytes 1105928 | tf_op jit(solution)/shard_map/ppermute | solution.py:33
  38.0 10.3 %copy-start.13 = (bf16[512,768]{1,0:T(8,128)(2,1)}, bf16[512,768]{1,0:T(8,128)(2,1)S(1)}, u32[]{:S(2)}) copy-start(bf16[512,768]{1,0:T(8,128)(2,1)S(1)} %collective-permute-done.8.refs_14_) | copy-start | bytes 2359300
  38.0 10.3 %copy-start.33 = (bf16[16,768]{1,0:T(8,128)(2,1)}, bf16[16,768]{1,0:T(8,128)(2,1)S(1)}, u32[]{:S(2)}) copy-start(bf16[16,768]{1,0:T(8,128)(2,1)S(1)} %fusion.30.refs_9_) | copy-start | bytes 73732
  38.0 10.3 %copy-start.25 = (bf16[96,1920]{1,0:T(8,128)(2,1)}, bf16[96,1920]{1,0:T(8,128)(2,1)S(1)}, u32[]{:S(2)}) copy-start(bf16[96,1920]{1,0:T(8,128)(2,1)S(1)} %collective-permute-done.4.refs_5_) | copy-start | bytes 1105924
  38.1 10.3 %copy-start.26 = (bf16[96,1920]{1,0:T(8,128)(2,1)}, bf16[96,1920]{1,0:T(8,128)(2,1)S(1)}, u32[]{:S(2)}) copy-start(bf16[96,1920]{1,0:T(8,128)(2,1)S(1)} %collective-permute-done.5.refs_6_) | copy-start | bytes 1105924
  38.1 10.3 %copy-start.27 = (bf16[96,1920]{1,0:T(8,128)(2,1)}, bf16[96,1920]{1,0:T(8,128)(2,1)S(1)}, u32[]{:S(2)}) copy-start(bf16[96,1920]{1,0:T(8,128)(2,1)S(1)} %collective-permute-done.6.refs_7_) | copy-start | bytes 1105924
  38.1 10.3 %copy-start.28 = (bf16[96,1920]{1,0:T(8,128)(2,1)}, bf16[96,1920]{1,0:T(8,128)(2,1)S(1)}, u32[]{:S(2)}) copy-start(bf16[96,1920]{1,0:T(8,128)(2,1)S(1)} %collective-permute-done.7.refs_8_) | copy-start | bytes 1105924
  38.1 1.9 collective-permute-start.10
  38.2 3.8 %collective-permute-start.11 = (bf16[16,768]{1,0:T(8,128)(2,1)S(1)}, bf16[16,768]{1,0:T(8,128)(2,1)S(1)}, u32[]{:S(2)}, u32[]{:S(2)}) collective-permute-start(bf16[16,768]{1,0:T(8,128)(2,1)S(1)} %fusion.30.refs_9_), channel_id=1, source_target_pairs={{0,9},{1,8},{2,11},{3,10},{4,13},{5,12},{6,15},{7,14},{8,1},{9,0},... | collective-permute-start | bytes 73736 | tf_op jit(solution)/shard_map/ppermute | solution.py:68
  39.0 3.2 %collective-permute-start.9 = (bf16[16,768]{1,0:T(8,128)(2,1)S(1)}, bf16[16,768]{1,0:T(8,128)(2,1)S(1)}, u32[]{:S(2)}, u32[]{:S(2)}) collective-permute-start(bf16[16,768]{1,0:T(8,128)(2,1)S(1)} %fusion.30.refs_9_), channel_id=1, source_target_pairs={{0,8},{1,9},{2,10},{3,11},{4,12},{5,13},{6,14},{7,15},{8,0},{9,1},... | collective-permute-start | bytes 73736 | tf_op jit(solution)/shard_map/ppermute | solution.py:68
  40.1 8.3 %copy-start.37 = (bf16[16,768]{1,0:T(8,128)(2,1)}, bf16[16,768]{1,0:T(8,128)(2,1)S(1)}, u32[]{:S(2)}) copy-start(bf16[16,768]{1,0:T(8,128)(2,1)S(1)} %collective-permute-done.10.refs_11_) | copy-start | bytes 73732
  42.0 6.4 %copy-start.38 = (bf16[16,768]{1,0:T(8,128)(2,1)}, bf16[16,768]{1,0:T(8,128)(2,1)S(1)}, u32[]{:S(2)}) copy-start(bf16[16,768]{1,0:T(8,128)(2,1)S(1)} %collective-permute-done.11.refs_12_) | copy-start | bytes 73732
  42.2 6.2 %copy-start.39 = (bf16[16,768]{1,0:T(8,128)(2,1)}, bf16[16,768]{1,0:T(8,128)(2,1)S(1)}, u32[]{:S(2)}) copy-start(bf16[16,768]{1,0:T(8,128)(2,1)S(1)} %collective-permute-done.9.refs_10_) | copy-start | bytes 73732
  42.2 27.2 %collective-permute-start.13 = (bf16[512,768]{1,0:T(8,128)(2,1)S(1)}, bf16[512,768]{1,0:T(8,128)(2,1)S(1)}, u32[]{:S(2)}, u32[]{:S(2)}) collective-permute-start(bf16[512,768]{1,0:T(8,128)(2,1)S(1)} %copy-done.19), channel_id=1, source_target_pairs={{1,16},{3,18},{5,20},{7,22},{9,24},{11,26},{13,28},{15,30},{16,1},... | collective-permute-start | bytes 2359304 | tf_op jit(solution)/shard_map/ppermute | solution.py:50
  62.8 21.6 %collective-permute-start.12 = (bf16[2,128,1664]{2,1,0:T(8,128)(2,1)}, bf16[2,128,1664]{2,1,0:T(8,128)(2,1)S(1)}, u32[]{:S(2)}, u32[]{:S(2)}) collective-permute-start(bf16[2,128,1664]{2,1,0:T(8,128)(2,1)} %get-tuple-element.114.refs_1_.refs_5_), channel_id=1, source_target_pairs={{0,8},{8,0},{16,24},{24,16},{1,9},{9,1},{17,25},{25,17},{2,10},{10... | collective-permute-start | bytes 2555912 | tf_op jit(solution)/shard_map/ppermute | solution.py:33
  62.9 21.9 %collective-permute-start.14 = (bf16[2,128,1664]{2,1,0:T(8,128)(2,1)}, bf16[2,128,1664]{2,1,0:T(8,128)(2,1)S(1)}, u32[]{:S(2)}, u32[]{:S(2)}) collective-permute-start(bf16[2,128,1664]{2,1,0:T(8,128)(2,1)} %get-tuple-element.114.refs_1_.refs_5_), channel_id=1, source_target_pairs={{0,1},{1,0},{2,3},{3,2},{4,5},{5,4},{6,7},{7,6},{8,9},{9,8},{10,11... | collective-permute-start | bytes 2555912 | tf_op jit(solution)/shard_map/ppermute | solution.py:33
  69.5 4.6 %copy-start.3 = (bf16[512,768]{1,0:T(8,128)(2,1)}, bf16[512,768]{1,0:T(8,128)(2,1)S(1)}, u32[]{:S(2)}) copy-start(bf16[512,768]{1,0:T(8,128)(2,1)S(1)} %broadcast_select_fusion.2.cot) | copy-start | bytes 2359300
  84.4 2.4 collective-permute-start.15
  109.0 137.0 %all-reduce.6.cloned.1.call-start = ((), (), s32[]{:S(2)}) async-start(), calls=%async_computation.4 | async-start | bytes 1179648 | tf_op jit(solution)/shard_map/psum | solution.py:1073
  110.1 18.8 %collective-permute-start.16 = (bf16[2,128,1536]{2,1,0:T(8,128)(2,1)S(1)}, bf16[2,128,1536]{2,1,0:T(8,128)(2,1)S(1)}, u32[]{:S(2)}, u32[]{:S(2)}) collective-permute-start(bf16[2,128,1536]{2,1,0:T(8,128)(2,1)S(1)} %copy-done.15), channel_id=1, source_target_pairs={{0,8},{8,0},{16,24},{24,16},{1,9},{9,1},{17,25},{25,17},{2,10},{10... | collective-permute-start | bytes 2359304 | tf_op jit(solution)/shard_map/ppermute | solution.py:33
  128.8 6.6 %copy-start.16 = (bf16[2,128,1536]{2,1,0:T(8,128)(2,1)}, bf16[2,128,1536]{2,1,0:T(8,128)(2,1)S(1)}, u32[]{:S(2)}) copy-start(bf16[2,128,1536]{2,1,0:T(8,128)(2,1)S(1)} %collective-permute-done.16.refs_2_) | copy-start | bytes 2359300
  128.8 3.1 %collective-permute-start.17 = (bf16[2,128,1536]{2,1,0:T(8,128)(2,1)S(1)}, bf16[2,128,1536]{2,1,0:T(8,128)(2,1)S(1)}, u32[]{:S(2)}, u32[]{:S(2)}) collective-permute-start(bf16[2,128,1536]{2,1,0:T(8,128)(2,1)S(1)} %collective-permute-done.16.refs_2_), channel_id=1, source_target_pairs={{0,1},{1,0},{2,3},{3,2},{4,5},{5,4},{6,7},{7,6},{8,9},{9,8},{10,11... | collective-permute-start | bytes 2359304 | tf_op jit(solution)/shard_map/ppermute | solution.py:33
  130.0 5.4 %collective-permute-start.19 = (bf16[2,128,1536]{2,1,0:T(8,128)(2,1)S(1)}, bf16[2,128,1536]{2,1,0:T(8,128)(2,1)S(1)}, u32[]{:S(2)}, u32[]{:S(2)}) collective-permute-start(bf16[2,128,1536]{2,1,0:T(8,128)(2,1)S(1)} %copy-done.15), channel_id=1, source_target_pairs={{0,1},{1,0},{2,3},{3,2},{4,5},{5,4},{6,7},{7,6},{8,9},{9,8},{10,11... | collective-permute-start | bytes 2359304 | tf_op jit(solution)/shard_map/ppermute | solution.py:33
  132.0 22.7 %collective-permute-start.18 = (bf16[512,768]{1,0:T(8,128)(2,1)}, bf16[512,768]{1,0:T(8,128)(2,1)}, u32[]{:S(2)}, u32[]{:S(2)}) collective-permute-start(bf16[512,768]{1,0:T(8,128)(2,1)} %get-tuple-element.133), channel_id=1, source_target_pairs={{1,16},{3,18},{5,20},{7,22},{9,24},{11,26},{13,28},{15,30},{16,1},... | collective-permute-start | bytes 2359304 | tf_op jit(solution)/shard_map/ppermute | solution.py:50
  136.4 18.3 %copy-start.46 = (bf16[528,768]{1,0:T(8,128)(2,1)S(1)}, bf16[528,768]{1,0:T(8,128)(2,1)}, u32[]{:S(2)}) copy-start(bf16[528,768]{1,0:T(8,128)(2,1)} %get-tuple-element.118) | copy-start | bytes 2433028
  160.9 10.8 %collective-permute-start.20 = (bf16[4,96,1920]{2,1,0:T(8,128)(2,1)}, bf16[4,96,1920]{2,1,0:T(8,128)(2,1)}, u32[]{:S(2)}, u32[]{:S(2)}) collective-permute-start(bf16[4,96,1920]{2,1,0:T(8,128)(2,1)} %get-tuple-element.171), channel_id=1, source_target_pairs={{0,1},{1,0},{2,3},{3,2},{4,5},{5,4},{6,7},{7,6},{8,9},{9,8},{10,11... | collective-permute-start | bytes 4423688 | tf_op jit(solution)/shard_map/ppermute | solution.py:33
  164.5 6.6 %collective-permute-start.22 = (bf16[96,64]{1,0:T(8,128)(2,1)S(1)}, bf16[96,64]{1,0:T(8,128)(2,1)S(1)}, u32[]{:S(2)}, u32[]{:S(2)}) collective-permute-start(bf16[96,64]{1,0:T(8,128)(2,1)S(1)} %reshape.302), channel_id=1, source_target_pairs={{0,1},{1,0},{2,3},{3,2},{4,5},{5,4},{6,7},{7,6},{8,9},{9,8},{10,11... | collective-permute-start | bytes 36872 | tf_op jit(solution)/shard_map/ppermute | solution.py:33
  164.6 7.2 %collective-permute-start.21 = (f32[96,128]{1,0:T(8,128)S(1)}, f32[96,128]{1,0:T(8,128)S(1)}, u32[]{:S(2)}, u32[]{:S(2)}) collective-permute-start(f32[96,128]{1,0:T(8,128)S(1)} %copy-done.34), channel_id=1, source_target_pairs={{0,1},{1,0},{2,3},{3,2},{4,5},{5,4},{6,7},{7,6},{8,9},{9,8},{10,11... | collective-permute-start | bytes 147464 | tf_op jit(solution)/shard_map/ppermute | solution.py:33
  175.4 32.2 %collective-permute-start.26 = (bf16[512,768]{1,0:T(8,128)(2,1)S(1)}, bf16[512,768]{1,0:T(8,128)(2,1)S(1)}, u32[]{:S(2)}, u32[]{:S(2)}) collective-permute-start(bf16[512,768]{1,0:T(8,128)(2,1)S(1)} %fusion.8), channel_id=1, source_target_pairs={{1,16},{3,18},{5,20},{7,22},{9,24},{11,26},{13,28},{15,30},{16,1},... | collective-permute-start | bytes 2359304 | tf_op jit(solution)/shard_map/ppermute | solution.py:50
  178.0 12.0 %collective-permute-start.23 = (bf16[96,2176]{1,0:T(8,128)(2,1)}, bf16[96,2176]{1,0:T(8,128)(2,1)S(1)}, u32[]{:S(2)}, u32[]{:S(2)}) collective-permute-start(bf16[96,2176]{1,0:T(8,128)(2,1)} %get-tuple-element.156), channel_id=1, source_target_pairs={{0,2},{1,3},{2,0},{3,1},{4,6},{5,7},{6,4},{7,5},{8,10},{9,11},{10,... | collective-permute-start | bytes 1253384 | tf_op jit(solution)/shard_map/ppermute | solution.py:33
  179.3 20.1 %collective-permute-start.24 = (bf16[96,2176]{1,0:T(8,128)(2,1)}, bf16[96,2176]{1,0:T(8,128)(2,1)}, u32[]{:S(2)}, u32[]{:S(2)}) collective-permute-start(bf16[96,2176]{1,0:T(8,128)(2,1)} %get-tuple-element.157), channel_id=1, source_target_pairs={{0,4},{1,5},{2,6},{3,7},{4,0},{5,1},{6,2},{7,3},{8,12},{9,13},{10,... | collective-permute-start | bytes 1253384 | tf_op jit(solution)/shard_map/ppermute | solution.py:33
  180.8 18.6 %collective-permute-start.25 = (bf16[96,2176]{1,0:T(8,128)(2,1)}, bf16[96,2176]{1,0:T(8,128)(2,1)}, u32[]{:S(2)}, u32[]{:S(2)}) collective-permute-start(bf16[96,2176]{1,0:T(8,128)(2,1)} %get-tuple-element.158), channel_id=1, source_target_pairs={{0,6},{1,7},{2,4},{3,5},{4,2},{5,3},{6,0},{7,1},{8,14},{9,15},{10,... | collective-permute-start | bytes 1253384 | tf_op jit(solution)/shard_map/ppermute | solution.py:33
  180.9 29.3 %copy-start.31 = (bf16[96,64]{1,0:T(8,128)(2,1)S(1)}, bf16[96,64]{1,0:T(8,128)(2,1)}, u32[]{:S(2)}) copy-start(bf16[96,64]{1,0:T(8,128)(2,1)} %copy-done.30) | copy-start | bytes 36868
  180.9 30.1 %copy-start.20 = (bf16[512,768]{1,0:T(8,128)(2,1)S(1)}, bf16[512,768]{1,0:T(8,128)(2,1)}, u32[]{:S(2)}) copy-start(bf16[512,768]{1,0:T(8,128)(2,1)} %get-tuple-element.133) | copy-start | bytes 2359300
  211.0 5.3 %copy-start.32 = (bf16[96,64]{1,0:T(8,128)(2,1)S(1)}, bf16[96,64]{1,0:T(8,128)(2,1)}, u32[]{:S(2)}) copy-start(bf16[96,64]{1,0:T(8,128)(2,1)} %copy-done.30) | copy-start | bytes 36868
  211.0 8.5 %copy-start.22 = (f32[96,128]{1,0:T(8,128)S(1)}, f32[96,128]{1,0:T(8,128)}, u32[]{:S(2)}) copy-start(f32[96,128]{1,0:T(8,128)} %copy-done.21) | copy-start | bytes 147460
  211.0 5.3 %collective-permute-start.27 = (bf16[96,1216]{1,0:T(8,128)(2,1)}, bf16[96,1216]{1,0:T(8,128)(2,1)S(1)}, u32[]{:S(2)}, u32[]{:S(2)}) collective-permute-start(bf16[96,1216]{1,0:T(8,128)(2,1)} %concatenate.43), channel_id=1, source_target_pairs={{0,8},{8,0},{16,24},{24,16},{1,9},{9,1},{17,25},{25,17},{2,10},{10... | collective-permute-start | bytes 700424 | tf_op jit(solution)/shard_map/ppermute | solution.py:33
  216.4 13.3 %collective-permute-start.28 = (bf16[96,256]{1,0:T(8,128)(2,1)S(1)}, bf16[96,256]{1,0:T(8,128)(2,1)S(1)}, u32[]{:S(2)}, u32[]{:S(2)}) collective-permute-start(bf16[96,256]{1,0:T(8,128)(2,1)S(1)} %pad_maximum_fusion.3), channel_id=1, source_target_pairs={{1,16},{3,18},{5,20},{7,22},{9,24},{11,26},{13,28},{15,30},{16,1},... | collective-permute-start | bytes 147464 | tf_op jit(solution)/shard_map/ppermute | solution.py:50
  219.7 17.8 %collective-permute-start.29 = (bf16[96,1088]{1,0:T(8,128)(2,1)S(1)}, bf16[96,1088]{1,0:T(8,128)(2,1)S(1)}, u32[]{:S(2)}, u32[]{:S(2)}) collective-permute-start(bf16[96,1088]{1,0:T(8,128)(2,1)S(1)} %concatenate.46), channel_id=1, source_target_pairs={{0,16},{8,24},{16,0},{24,8},{1,17},{9,25},{17,1},{25,9},{2,18},{10... | collective-permute-start | bytes 626696 | tf_op jit(solution)/shard_map/ppermute | solution.py:33
  237.8 6.1 %collective-permute-start.30 = (bf16[96,1088]{1,0:T(8,128)(2,1)S(1)}, bf16[96,1088]{1,0:T(8,128)(2,1)S(1)}, u32[]{:S(2)}, u32[]{:S(2)}) collective-permute-start(bf16[96,1088]{1,0:T(8,128)(2,1)S(1)} %concatenate.47), channel_id=1, source_target_pairs={{0,8},{8,0},{16,24},{24,16},{1,9},{9,1},{17,25},{25,17},{2,10},{10... | collective-permute-start | bytes 626696 | tf_op jit(solution)/shard_map/ppermute | solution.py:33
  237.9 9.3 %copy-start.14 = (bf16[2,256,768]{2,1,0:T(8,128)(2,1)}, bf16[2,256,768]{2,1,0:T(8,128)(2,1)S(1)}, u32[]{:S(2)}) copy-start(bf16[2,256,768]{2,1,0:T(8,128)(2,1)S(1)} %fusion.31) | copy-start | bytes 2359300
  (20 other events, 39.2 us)
Sparse Core Ops, SparseCore 0:
  10.0 35.7 all-gather.2
  47.7 29.0 all-gather.4
  109.1 53.6 reduce-scatter.1
  181.0 54.1 all-reduce.5

commit v2 on v1

--- a/solution.py
+++ b/solution.py
@@ -79,19 +79,24 @@
     return pieces + [trade(v, "shard", 1) for v in pieces]
 
 
-def gather_pieces(piece, *first):
-    n_shard = lax.axis_size("shard")
-    if n_shard != 8:
-        held = {0: piece}
-        bit = 1
-        while bit < n_shard:
-            held.update({k ^ bit: trade(v, "shard", bit) for k, v in list(held.items())})
-            bit *= 2
-        return [(v, k) for k, v in held.items()]
-
-    far = [trade(piece, "shard", bit) for bit in (6, 2, 4)]
-    near = [trade(v, "shard", 1) for v in after_all([piece] + far, *first)]
-    return [(v, k) for v, k in zip([piece] + far + near, (0, 6, 2, 4, 1, 7, 3, 5))]
+def gather_far(piece):
+    bits = range(2, lax.axis_size("shard"), 2)
+    return [trade(piece, "shard", bit) for bit in sorted(bits, reverse=True)]
+
+
+def gather_near(piece, far):
+    held = [piece] + far
+    offsets = [0] + sorted(range(2, lax.axis_size("shard"), 2), reverse=True)
+    near = [trade(v, "shard", 1) for v in held]
+    return list(zip(held + near, offsets + [k ^ 1 for k in offsets]))
+
+
+def join_pieces(parts):
+    me, n_shard = lax.axis_index("shard"), lax.axis_size("shard")
+    joined = jnp.zeros((n_shard,) + parts[0][0].shape, parts[0][0].dtype)
+    for v, k in parts:
+        joined = lax.dynamic_update_slice(joined, v[None], (me ^ k, 0, 0))
+    return joined
 
 
 def head_pieces(value):
@@ -175,13 +180,13 @@
     return lax.dot_general(a, b, (((0,), (0,)), ((), ())), preferred_element_type=F32)
 
 
-def spread_table():
-    row = jnp.arange(2 * LANES)[:, None] % LANES
+def spread_table(none):
+    row = jnp.arange(2 * LANES)[:, None] % LANES + none
     return (row == jnp.arange(DI)[None, :] // HD).astype(BF)
 
 
-def narrow_table():
-    return (jnp.arange(DI)[:, None] // HD == jnp.arange(LANES)[None, :]).astype(BF)
+def narrow_table(none):
+    return (jnp.arange(DI)[:, None] // HD == jnp.arange(LANES)[None, :] + none).astype(BF)
 
 
 def pieces2(v):
@@ -515,26 +520,97 @@
     )[0]
 
 
-def terms_kernel(normal_t, dz, normed, cot, out):
-    out[:, :DI] = dot(normal_t[...], dz[...]).astype(BF)
-    part = dot_tn(normed[...], cot[...]).astype(BF)
-    for k in range(2):
+def open_kernel(layout, at, *refs):
+    pieces = refs[: len(layout)]
+    normal, cot_own, cot_got, stay, z, q, cot, wz, wo, sems = refs[len(layout) :]
+    c = pl.program_id(0)
+    k_rows = pieces[0].shape[0]
+
+    def copies(n):
+        shard = at[0] ^ layout[n]
+        parts = [(wz, shard * k_rows, slice(0, DI))]
         for j in range(2):
-            rows = part[(2 * k + j) * OUT_ROWS : (2 * k + j + 1) * OUT_ROWS, :]
-            out[k * OUT_ROWS : (k + 1) * OUT_ROWS, DI + j * DM : DI + (j + 1) * DM] = rows
-
-
-def run_terms(normal_t, dz, normed, cot):
+            lanes = slice(DI + j * DM, DI + (j + 1) * DM)
+            parts.append((wo, (2 * shard + j) * k_rows, lanes))
+        return [
+            pltpu.make_async_copy(
+                pieces[n].at[:, lanes],
+                ref.at[pl.ds(pl.multiple_of(begin, 16), k_rows), :],
+                sems.at[3 * n + k],
+            )
+            for k, (ref, begin, lanes) in enumerate(parts)
+        ]
+
+    @pl.when(c == 0)
+    def _():
+        for n in range(len(layout)):
+            for copy in copies(n):
+                copy.start()
+        cot[...] = jnp.where(stay[0] > 0, cot_own[...], cot_got[...])
+        for n in range(len(layout)):
+            for copy in copies(n):
+                copy.wait()
+
+    here = pl.ds(pl.multiple_of(c * CW, CW), CW)
+    z[...] = dot(normal[...], wz[:, here]).astype(BF)
+    q[...] = dot_nt(cot[...], wo[here, :]).astype(BF)
+
+
+def run_open(at, parts, normal, cot_own, cot_got, stay):
+    rows = cot_own.shape[0]
+    layout = [offset for _, offset in parts]
+    ins = [(at, in_smem())] + [(v, in_hbm()) for v, _ in parts]
+    ins += [(normal, pl.BlockSpec((rows, DM), lambda c: (0, 0)))]
+    ins += [(cot_own, whole(cot_own)), (cot_got, whole(cot_got)), (stay, in_smem())]
+    wide = shape((rows, DI), BF)
+    outs = [(wide, columns(wide, lambda c: c))] * 2
+    outs += [(v, whole(v)) for v in (shape((rows, DM), BF), shape((DM, DI), BF), shape((DI, DM), BF))]
+    return call(
+        functools.partial(open_kernel, layout), 1, (NCW,), ins, outs,
+        [pltpu.SemaphoreType.DMA((3 * len(parts),))],
+    )
+
+
+def terms_kernel(at, normal_t, dz, normed, cot, keep, *refs):
+    *give, z_part, o_part = refs
+    p = pl.program_id(0)
+    unit = give[0].shape[0]
+    even = at[0] % 2 == 0
+    z_part[...] = dot(normal_t[...], dz[...])
+    o_part[...] = dot_tn(normed[...], cot[...])
+
+    def rows_of(which):
+        parts = [(z_part[which * unit : (which + 1) * unit, :], slice(0, DI))]
+        for j in range(2):
+            rows = o_part[(2 * which + j) * unit : (2 * which + j + 1) * unit, :]
+            parts.append((rows, slice(DI + j * DM, DI + (j + 1) * DM)))
+        return parts
+
+    for (first, lanes), (second, _) in zip(rows_of(0), rows_of(1)):
+        keep[0, :, lanes] = jnp.where(even, first, second).astype(BF)
+        other = jnp.where(even, second, first).astype(BF)
+        for k, ref in enumerate(give):
+
+            @pl.when(p == k)
+            def _(ref=ref, other=other, lanes=lanes):
+                ref[:, lanes] = other
+
+
+def run_terms(at, normal_t, dz, normed, cot, n_shard):
     rows = dz.shape[0]
-    out = shape((DM, DI + 2 * DM), BF)
-    return call(
-        terms_kernel, 1, (NCW,),
+    n, unit = n_shard // 2, DM // n_shard
+    give = shape((unit, DI + 2 * DM), BF)
+    keep = shape((n,) + give.shape, BF)
+    got = call(
+        terms_kernel, 1, (n,),
         [
-            (normal_t, pl.BlockSpec((2 * OUT_ROWS, rows), lambda c: (c, 0))), (dz, whole(dz)),
-            (normed, columns(normed, lambda c: c)), (cot, whole(cot)),
+            (at, in_smem()), (normal_t, pl.BlockSpec((2 * unit, rows), lambda p: (p, 0))),
+            (dz, whole(dz)), (normed, columns(normed, lambda p: p, 4 * unit)), (cot, whole(cot)),
         ],
-        [(out, pl.BlockSpec((2 * OUT_ROWS, DI + 2 * DM), lambda c: (c, 0)))], [],
-    )[0]
+        [(keep, pl.BlockSpec((1,) + give.shape, lambda p: (p, 0, 0)))] + [(give, whole(give))] * n,
+        [pltpu.VMEM((2 * unit, DI), F32), pltpu.VMEM((4 * unit, DM), F32)],
+    )
+    return got[0], list(got[1:])
 
 
 def pair_small_kernel(at, keep, got, small, small_got, *outs):
@@ -960,24 +1036,6 @@
     piece_a = jnp.concatenate(
         [in_weight[:, DI:], norm_gain[:, None], jnp.zeros((k_rows, WA - XBC - NH - 1), BF)], axis=1
     )
-    table = spread_table()
-
-    def head_row(v):
-        return jnp.pad(v, (0, LANES - NH))[None]
-
-    narrow = narrow_table()
-    gain_row = inner_gain[None]
-    at = shard_at.astype(jnp.int32).reshape(1)
-    taps = jnp.pad(conv_weight, ((0, 0), (0, WA - XBC)))
-    rate_row = head_row(a_log)
-    skip_row = jnp.repeat(d_skip, HD)[None]
-    taps, rate_row, skip_row, bias_row, step_row, gain_row, narrow, table = after_all(
-        [
-            taps, rate_row, skip_row, jnp.pad(conv_bias, (0, WA - XBC))[None], head_row(dt_bias),
-            gain_row, narrow, table,
-        ]
-    )
-    prepared = [taps, rate_row, skip_row, bias_row, step_row, gain_row, narrow, table]
     numbers = jnp.concatenate([block_place, seq_length], axis=1)
     numbers_got = trade(numbers, "shard", 1)
     me = jnp.int32(0) if k_rows % 32 else shard_at.astype(jnp.int32)
@@ -1015,25 +1073,53 @@
         ]
     ).astype(jnp.int32)
 
-    parts_a = gather_pieces(piece_a, info, *prepared)
+    far_a = gather_far(piece_a)
+    conv_weight, conv_bias, dt_bias, a_log, d_skip, inner_gain, none = after_all(
+        [conv_weight, conv_bias, dt_bias, a_log, d_skip, inner_gain, jnp.int32(0)], far_a[0]
+    )
+    table = spread_table(none)
+
+    def head_row(v):
+        return jnp.pad(v, (0, LANES - NH))[None]
+
+    narrow = narrow_table(none)
+    gain_row = inner_gain[None]
+    at = shard_at.astype(jnp.int32).reshape(1)
+    taps = jnp.pad(conv_weight, ((0, 0), (0, WA - XBC)))
+    rate_row = head_row(a_log)
+    skip_row = jnp.repeat(d_skip, HD)[None]
+    taps, rate_row, skip_row, bias_row, step_row, gain_row, narrow, table = after_all(
+        [
+            taps, rate_row, skip_row, jnp.pad(conv_bias, (0, WA - XBC))[None], head_row(dt_bias),
+            gain_row, narrow, table,
+        ]
+    )
+    prepared = [taps, rate_row, skip_row, bias_row, step_row, gain_row, narrow, table]
+    parts_a = gather_near(piece_a, far_a)
     if k_rows % 32:
-        joined = jnp.zeros((n_shard, k_rows, WA), BF)
-        for v, k in parts_a:
-            joined = lax.dynamic_update_slice(joined, v[None], (shard_at ^ k, 0, 0))
-        parts_a = [(joined.reshape(DM, WA), 0)]
-    wo = lax.all_gather(out_weight, "shard", axis=0, tiled=True)
-    wz = lax.all_gather(in_weight[:, :DI], "shard", axis=0, tiled=True)
-
-    tails = group_spread(after(tails, *[v for v, _ in parts_a[1:]]))
+        parts_a = [(join_pieces(parts_a).reshape(DM, WA), 0)]
+    z_own, o_own = after_all([in_weight[:, :DI], out_weight], numbers_got)
+    piece_zo = jnp.concatenate([z_own, o_own[:k_rows], o_own[k_rows:]], axis=1)
+    far_zo = gather_far(piece_zo)
+    tails = group_spread(after(tails, info, *[v for v, _ in parts_a[1:]], *prepared))
     cot_got = move_home(after(cotangent, *tails))
     a = run_project(info, parts_a, tails, tokens, tok_got, taps, bias_row, step_row, rate_row, table)
     wa, tok, normal = a["wa"], a["tok"], a["normal"]
     state_by_head = head_pieces(a["states"])
     state_by_core = trade(a["states"], "shard", 1)
     y_intra = run_intra(a)
-    cot = jnp.where(stay, cotangent, after(cot_got, y_intra))
-    q = dot_nt(cot, wo).astype(BF)
-    z = dot(after(normal, q)[:rows], wz).astype(BF)
+    parts_zo = gather_near(after(piece_zo, y_intra), after_all(far_zo, y_intra))
+    if k_rows % 32:
+        zo = join_pieces(parts_zo)
+        wz, wo = zo[:, :, :DI].reshape(DM, DI), zo[:, :, DI:]
+        wo = wo.reshape(n_shard, k_rows, 2, DM).swapaxes(1, 2).reshape(DI, DM)
+        cot = jnp.where(stay, cotangent, cot_got)
+        z, q = dot(normal[:rows], wz).astype(BF), dot_nt(cot, wo).astype(BF)
+    else:
+        cot_got = after(cot_got, y_intra)
+        z, q, cot, wz, wo = run_open(
+            at, parts_zo, normal, cotangent, cot_got, stay.astype(jnp.int32).reshape(1)
+        )
     state_by_head = [after(v, z) for v in state_by_head]
     all_states = (
         [a["states"]] + state_by_head + [state_by_core] + [trade(v, "shard", 1) for v in state_by_head]
@@ -1043,10 +1129,20 @@
     )
     enter_by_head = head_pieces(d_enter)
     enter_by_core = trade(d_enter, "shard", 1)
-    zo_term = run_terms(a["normal_t"], dz, normed, cot)
-    zo_own = lax.psum_scatter(zo_term, "shard", scatter_dimension=0, tiled=True)
-    dx_intra, db, dc, mixed = run_intra_back(a, after(dyr, zo_term), dye, enter, normed, wo, tok)
-    enter_by_head = [after(v, dx_intra) for v in enter_by_head]
+    if k_rows % 32:
+        z_term = dot_tn(normal[:rows], dz).astype(BF).reshape(n_shard, k_rows, DI)
+        out_term = dot_tn(normed, cot).astype(BF).reshape(n_shard, 2, k_rows, DM)
+        zo_keep, zo_give = core_give([z_term, out_term[:, 0], out_term[:, 1]])
+        zo_give = [zo_give[p] for p in range(n_shard // 2)]
+    else:
+        zo_keep, zo_give = run_terms(at, a["normal_t"], dz, normed, cot, n_shard)
+    zo_got = [trade(v, "shard", 1) for v in zo_give]
+    dx_intra, db, dc, mixed = run_intra_back(a, after(dyr, *zo_give), dye, enter, normed, wo, tok)
+    arrived = after_all(enter_by_head + zo_got, dx_intra)
+    enter_by_head, zo_got = arrived[: len(enter_by_head)], arrived[len(enter_by_head) :]
+    zo_pairs = chip_pairs(zo_keep, jnp.stack(zo_got))
+    zo_far = chip_send(zo_pairs)
+    enter_by_head = [after(v, *zo_pairs) for v in enter_by_head]
     all_enter = (
         [d_enter] + enter_by_head + [enter_by_core] + [trade(v, "shard", 1) for v in enter_by_head]
     )
@@ -1061,7 +1157,12 @@
     a_got = trade(a_give, "shard", 1)
 
     small_got = trade(after(small, a_give), "shard", 1)
-    d_a_all, dz, tok, tok_halo, wa = after_all([d_a_all, dz, tok, a["tok_halo"], wa], a_give)
+    zo_own = chip_sum(zo_pairs[0], after_all(zo_far, a_give))
+    zo_keep, zo_give = head_split(zo_own)
+    zo_got = trade(zo_give, "head", 1)
+    d_a_all, dz, tok, tok_halo, wa = after_all(
+        [d_a_all, dz, tok, a["tok_halo"], wa], a_give, zo_give
+    )
     gain = wa[:, XBC + NH].astype(F32)
     halo_part = norm_back(dot_nt(d_a_all[rows:], wa), tok_halo, gain)
     halo_part = halo_part.reshape(nb, HALO, DM)[:, HALO - KC :].astype(BF).reshape(k_rows, -1)
@@ -1069,8 +1170,7 @@
     normal_grad = dot_nt(dz, wz) + dot_nt(d_a_all[:rows], wa)
     token_grad = (cot.astype(F32) + norm_back(normal_grad, tok, gain)).astype(BF)
 
-    a_got, small_got, halos[1], zo_own = after_all([a_got, small_got, halos[1], zo_own], token_grad)
-    zo_sum = lax.psum(zo_own, "head")
+    a_got, small_got, halos[1], zo_got = after_all([a_got, small_got, halos[1], zo_got], token_grad)
     if k_rows % 32:
         parts = split2((small + small_got).reshape(k_rows, -1))
         a_pairs = [jnp.concatenate([v, parts], axis=1) for v in chip_pairs(a_keep, a_got)]
@@ -1078,6 +1178,8 @@
         a_pairs = run_pair_small(at, a_keep, a_got, small, small_got)
     a_far = chip_send(a_pairs)
     token_got = move_home(after(token_grad, a_pairs[0]))
+    zo_half = head_add(zo_keep, after(zo_got, a_pairs[0]))
+    zo_got = trade(zo_half, "head", 2)
     *a_far, token_got = after_all(a_far + [token_got])
     a_own = chip_sum(a_pairs[0][:, :WA], [v[:, :WA] for v in a_far])
     sums = [join2(v[:, WA:]) for v in [a_pairs[0]] + a_far]
@@ -1085,30 +1187,37 @@
         sums = [sums[k] + sums[k + 1] for k in range(0, len(sums), 2)]
     small = sums[0]
     a_keep, a_give = head_split(a_own)
-    small_keep, small_give = head_split(small)
-    cut, edge = a_keep.shape[1], a_keep.shape[1] + 2 * small_keep.shape[1]
-    total, small = a_keep.astype(F32), small_keep
+    cut, edge = a_keep.shape[1], a_keep.shape[1] + 2 * small.shape[1]
+    total = a_keep.astype(F32)
     bits = [b for b in (1, 2, 4, 8, 16) if b < n_head]
     for bit in bits:
         if bit > 1:
-            a_give, small_give = total.astype(BF), small
+            a_give = total.astype(BF)
             total = a_give.astype(F32)
-        parts = split2(small_give)
+        parts = split2(small)
         sent = jnp.concatenate([a_give, parts] + (halos if bit < half else []), axis=1)
         sent = trade(sent, "head", bit)
+        if bit == 1:
+            sent, zo_got = after_all([sent, zo_got])
+            zo_half = head_add(zo_half, zo_got)
+            for more in bits[2:]:
+                zo_half = head_add(zo_half, trade(zo_half, "head", more))
+            zo_other = trade(zo_half, "head", 1)
+        elif bit == bits[-1]:
+            sent, zo_other = after_all([sent, zo_other])
+            zo_grad = head_join(zo_half, zo_other).astype(F32)
         if bit < half:
             halos = halos + jnp.split(sent[:, edge:], len(halos), axis=1)
         total = total + sent[:, :cut].astype(F32)
-        small = (small if bit == 1 else join2(parts)) + join2(sent[:, cut:edge])
-    low, parts = total.astype(BF), split2(small)
-    other = trade(jnp.concatenate([low, parts], axis=1), "head", 1)
-    halos = jnp.concatenate(halos, axis=1)
+        small = join2(parts) + join2(sent[:, cut:edge])
+    low = total.astype(BF)
+    other = trade(low, "head", 1)
+    halos = after(jnp.concatenate(halos, axis=1), low)
     halos = jnp.where(stay, halos, move_home(halos))
     halos = jnp.split(halos, group_blocks // nb, axis=1)
     other = after(other, *halos)
-    zo_grad = after(zo_sum, other).astype(F32)
-    a_grad = head_join(low, other[:, :cut]).astype(F32)
-    small = head_join(join2(parts), join2(other[:, cut:])).reshape(SUM_ROWS, LANES)
+    a_grad = head_join(low, other).astype(F32)
+    small = small.reshape(SUM_ROWS, LANES)
 
     all_halo = jnp.concatenate(halos[0::2] + halos[1::2]).reshape(group_blocks, KC, DM).astype(F32)
     own_numbers = jnp.concatenate([block_place, seq_length], axis=1)[0]

time: 261 us -> 241 us (0.923)
  waiting for transfers between devices: 79.9 us -> 63.8 us
  between operations: 15.5 us -> 2.49 us
  starting transfers between devices: 32.5 us -> 43.9 us
  Pallas kernels: 73.9 us -> 84.9 us
  matrix products: 20.6 us -> 12.6 us
    ppermute x5, waiting for transfers between devices: 22.7 us -> 11.6 us  [move_home(): return lax.ppermute(value, ('head', 'shard'), pairs)]
    pallas_call x7 -> x8, Pallas kernels: 73.9 us -> 84.9 us  [call(): pl.pallas_call(kernel, grid=grid, out_shape=[o for o, _ in outs], in_spec...]
    ppermute x23 -> x40, starting transfers between devices: 11.1 us -> 19 us  [trade(): return lax.ppermute(value, axis, [(i, i ^ bit) for i in range(size)])]
    dot_general x1 -> x0, matrix products: 4.48 us -> none  [dot(): return jnp.dot(a, b, preferred_element_type=F32)]
    ppermute x5, starting transfers between devices: 19.1 us -> 23 us  [move_home(): return lax.ppermute(value, ('head', 'shard'), pairs)]
    dot_general x4 -> x3, matrix products: 11.8 us -> 7.9 us  [dot_nt(): lax.dot_general(a, b, (((1,), (1,)), ((), ())), preferred_element_type=F32)]
    all_gather x2 -> x0, waiting for transfers between devices: 2.66 us -> none  [the longest x1 2.64 us: shards(): wz = lax.all_gather(in_weight[:, :DI], 'shard', axis=0, tiled=True)]
    ppermute x23 -> x40, waiting for transfers between devices: 51.7 us -> 51.5 us  [trade(): return lax.ppermute(value, axis, [(i, i ^ bit) for i in range(size)])]
  transfers between devices with their start and end apart: 35 -> 48, of which waited for: 18 -> 19; matrix products, arithmetic and copies ran while one was open for 18% -> 14% of each run, Pallas kernels for 19% -> 28%
where the time goes in v2:
time: 241 us; the launch traced here: 240 us
  Pallas kernels  84.9 us (35%)
  waiting for transfers between devices  63.8 us (26%)
  starting transfers between devices  43.9 us (18%)
  local copies, waits for them, and re-layouts  16.9 us (7%)
  other arithmetic  15.5 us (6%)
  matrix products  12.6 us (5%)
  between operations  2.49 us (1%)
    pallas_call x8, Pallas kernels, call(): pl.pallas_call(kernel, grid=grid, out_shape=[o for o, _ in outs], in_spec...  84.9 us
    ppermute x40, waiting for transfers between devices, trade(): return lax.ppermute(value, axis, [(i, i ^ bit) for i in range(size)])  51.5 us
    ppermute x5, starting transfers between devices, move_home(): return lax.ppermute(value, ('head', 'shard'), pairs)  23 us
    ppermute x40, starting transfers between devices, trade(): return lax.ppermute(value, axis, [(i, i ^ bit) for i in range(size)])  19 us
    ppermute x5, waiting for transfers between devices, move_home(): return lax.ppermute(value, ('head', 'shard'), pairs)  11.6 us
    dot_general x3, matrix products, dot_nt(): lax.dot_general(a, b, (((1,), (1,)), ((), ())), preferred_element_type=F32)  7.9 us
  transfers between devices with their start and end apart: 48, of which 19 were waited for; matrix products, arithmetic and copies ran while one was open for 14% of the time, Pallas kernels for 28%

profile of v2, /device:TPU:1, one launch (start us, length us, event | category | flops | bytes accessed | tf_op | source)
XLA Modules:
  0.0 240.0 jit_solution(14031448960061123915)
XLA Ops:
  0.7 1.1 slice.144
  1.8 0.8 copy.33
  2.8 3.1 %collective-permute-start.1 = (bf16[96,1920]{1,0:T(8,128)(2,1)S(1)}, bf16[96,1920]{1,0:T(8,128)(2,1)S(1)}, u32[]{:S(2)}, u32[]{:S(2)}) collective-permute-start(bf16[96,1920]{1,0:T(8,128)(2,1)S(1)} %concatenate.42.refs_1_), channel_id=1, source_target_pairs={{0,6},{1,7},{2,4},{3,5},{4,2},{5,3},{6,0},{7,1},{8,14},{9,15},{10,... | collective-permute-start | bytes 1105928 | tf_op jit(solution)/shard_map/ppermute | solution.py:33
  6.2 1.2 collective-permute-start.4
  8.4 0.9 collective-permute-done
  9.3 4.7 %collective-permute-start.8 = (bf16[512,768]{1,0:T(8,128)(2,1)S(1)}, bf16[512,768]{1,0:T(8,128)(2,1)S(1)}, u32[]{:S(2)}, u32[]{:S(2)}) collective-permute-start(bf16[512,768]{1,0:T(8,128)(2,1)S(1)} %copy-done.13), channel_id=1, source_target_pairs={{1,16},{3,18},{5,20},{7,22},{9,24},{11,26},{13,28},{15,30},{16,1},... | collective-permute-start | bytes 2359304 | tf_op jit(solution)/shard_map/ppermute | solution.py:50
  14.9 0.6 compare_select_fusion.1
  16.3 6.6 %collective-permute-done.2.refs_3_ = bf16[96,1920]{1,0:T(8,128)(2,1)} collective-permute-done((bf16[96,1920]{1,0:T(8,128)(2,1)S(1)}, bf16[96,1920]{1,0:T(8,128)(2,1)}, u32[]{:S(2)}, u32[]{:S(2)}) %collective-permute-start.2) | collective-permute-done | bytes 368672 | tf_op jit(solution)/shard_map/ppermute | solution.py:33
  23.4 1.0 compare_convert_fusion.1.refs_26_
  24.5 1.1 compare_convert_fusion.refs_19_.refs_17_.refs_25_
  26.1 0.7 broadcast_in_dim_reshape.3.refs_16_.refs_24_
  26.8 0.6 pad.17.refs_15_.refs_22_
  29.1 3.0 %collective-permute-done.8.refs_14_ = bf16[512,768]{1,0:T(8,128)(2,1)S(1)} collective-permute-done((bf16[512,768]{1,0:T(8,128)(2,1)S(1)}, bf16[512,768]{1,0:T(8,128)(2,1)S(1)}, u32[]{:S(2)}, u32[]{:S(2)}) %collective-permute-start.8) | collective-permute-done | bytes 786464 | tf_op jit(solution)/shard_map/ppermute | solution.py:50
  32.2 0.8 collective-permute-start.11
  33.1 1.1 collective-permute-start.9
  34.1 1.0 fusion.29
  35.8 6.5 %collective-permute-start.20 = (bf16[512,768]{1,0:T(8,128)(2,1)S(1)}, bf16[512,768]{1,0:T(8,128)(2,1)S(1)}, u32[]{:S(2)}, u32[]{:S(2)}) collective-permute-start(bf16[512,768]{1,0:T(8,128)(2,1)S(1)} %copy-done.20), channel_id=1, source_target_pairs={{1,16},{3,18},{5,20},{7,22},{9,24},{11,26},{13,28},{15,30},{16,1},... | collective-permute-start | bytes 2359304 | tf_op jit(solution)/shard_map/ppermute | solution.py:50
  42.5 2.2 collective-permute-start.13
  45.2 14.4 %shard_map.212 = (bf16[768,1920]{1,0:T(8,128)(2,1)}, bf16[512,768]{1,0:T(8,128)(2,1)}, bf16[16,768]{1,0:T(8,128)(2,1)}, bf16[528,768]{1,0:T(8,128)(2,1)}, bf16[7...) custom-call(s32[26]{0:T(128)} %pad_add_fusion.2.refs_0_, ...), custom_call_target="tpu_custom_call" | custom-call | flops 1 | bytes 20720000 | tf_op jit(solution)/shard_map/pallas_call | solution.py:233
  59.7 6.5 %shard_map.213.refs_9_ = f32[512,1536]{1,0:T(8,128)} custom-call(bf16[512,128]{1,0:T(8,128)(2,1)} %get-tuple-element.143.bs.refs_16_, bf16[512,128]{1,0:T(8,128)(2,1)} %get-tuple-element.144.cs.refs_10_, bf16[512,1536]{1,0:T(8,128)(2,1)} %get-tuple-element.145.xt.refs_15_, f32[512,128]{1,0:T(8,128)} %get-tuple-element.146.cum.refs_11_.refs_18_, ...), custom_call_target="tpu_custom_call" | custom-call | flops 1 | bytes 8880000 | tf_op jit(solution)/shard_map/pallas_call | solution.py:233
  66.2 1.2 collective-permute-done.14.refs_2_
  68.6 0.9 collective-permute-done.17.refs_5_
  69.7 0.6 collective-permute-done.18.refs_6_
  70.4 0.8 collective-permute-done.19.refs_7_
  71.2 0.8 collective-permute-done.16.refs_4_
  72.1 0.8 copy-done.30
  72.9 10.0 %shard_map.214 = (bf16[512,1536]{1,0:T(8,128)(2,1)}, bf16[512,1536]{1,0:T(8,128)(2,1)}, bf16[512,768]{1,0:T(8,128)(2,1)}, bf16[768,1536]{1,0:T(8,128)(2,1)}, bf16[1536,768]{1,0:T(8,128)(2,1)}) custom-call(s32[1]{0:T(128)} %bitcast.at, bf16[96,3072]{1,0:T(8,128)(2,1)} %copy-done.9, bf16[96,3072]{1,0:T(8,128)(2,1)} %copy-done.24, bf16[96,3072]{1,0:T(8,128)(2,1)} %copy-done.25, ...), custom_call_target="tpu_custom_call" | custom-call | flops 1 | bytes 1480000 | tf_op jit(solution)/shard_map/pallas_call | solution.py:233
  83.2 2.2 collective-permute-done.22.refs_4_.refs_8_
  85.4 0.9 copy-done.3
  86.3 14.5 %shard_map.215 = (bf16[2,128,1536]{2,1,0:T(8,128)(2,1)}, bf16[512,1536]{1,0:T(8,128)(2,1)}, f32[1,1536]{1,0:T(1,128)}, bf16[512,1536]{1,0:T(8,128)(2,1)}, bf16[5...) custom-call(s32[26]{0:T(128)} %pad_add_fusion.2.refs_0_, ...), custom_call_target="tpu_custom_call" | custom-call | flops 1 | bytes 23680000 | tf_op jit(solution)/shard_map/pallas_call | solution.py:233
  100.7 1.3 collective-permute-start.23
  102.0 7.7 %shard_map.216 = (bf16[4,96,3072]{2,1,0:T(8,128)(2,1)}, bf16[96,3072]{1,0:T(8,128)(2,1)}, bf16[96,3072]{1,0:T(8,128)(2,1)}, bf16[96,3072]{1,0:T(8,128)(2,1)}, bf16[96,3072]{1,0:T(8,128)(2,1)}) custom-call(s32[1]{0:T(128)} %bitcast.at, bf16[768,512]{1,0:T(8,128)(2,1)} %get-tuple-element.163.normal_t, bf16[512,1536]{1,0:T(8,128)(2,1)} %get-tuple-element.208.dz, ...), custom_call_target="tpu_custom_call" | custom-call | flops 1 | bytes 1480000 | tf_op jit(solution)/shard_map/pallas_call | solution.py:233
  110.8 11.5 %shard_map.217 = (f32[512,1536]{1,0:T(8,128)}, f32[512,128]{1,0:T(8,128)}, f32[512,128]{1,0:T(8,128)}, bf16[512,768]{1,0:T(8,128)(2,1)}) custom-call(bf16[512,128]{1,0:T(8,128)(2,1)} %get-tuple-element.143.bs.refs_16_, bf16[512,128]{1,0:T(8,128)(2,1)} %get-tuple-element.144.cs.refs_10_, bf16[512,1536]{1,0:T(8,128)(2,1)} %get-tuple-element.145.xt.refs_15_, ...), custom_call_target="tpu_custom_call" | custom-call | flops 1 | bytes 1480000 | tf_op jit(solution)/shard_map/pallas_call | solution.py:233
  122.3 0.9 add_convert_fusion
  123.2 1.2 dynamic-slice_bitcast_fusion.2
  124.9 2.1 collective-permute-done.28.refs_4_
  127.0 3.2 %collective-permute-start.29 = (bf16[512,768]{1,0:T(8,128)(2,1)}, bf16[512,768]{1,0:T(8,128)(2,1)S(1)}, u32[]{:S(2)}, u32[]{:S(2)}) collective-permute-start(bf16[512,768]{1,0:T(8,128)(2,1)} %get-tuple-element.186), channel_id=1, source_target_pairs={{1,16},{3,18},{5,20},{7,22},{9,24},{11,26},{13,28},{15,30},{16,1},... | collective-permute-start | bytes 2359304 | tf_op jit(solution)/shard_map/ppermute | solution.py:50
  130.5 1.3 collective-permute-start.33
  132.2 0.9 collective-permute-start.35
  133.2 17.2 %shard_map.218 = (bf16[528,1920]{1,0:T(8,128)(2,1)}, f32[96,128]{1,0:T(8,128)}) custom-call(s32[26]{0:T(128)} %pad_add_fusion.2.refs_0_, bf16[2,128,1536]{2,1,0:T(8,128)(2,1)} %get-tuple-element.177.refs_1_, bf16[2,128,1536]{2,1,0:T(8,128)(2,1)} %copy-done.18, bf16[2,128,1536]{2,1,0:T(8,128)(2,1)} %collective-permute-done.30.refs_3_, ...), custom_call_target="tpu_custom_call" | custom-call | flops 1 | bytes 2960000 | tf_op jit(solution)/shard_map/pallas_call | solution.py:233
  150.4 4.7 %convolution_convert_fusion = bf16[768,1920]{1,0:T(8,128)(2,1)S(1)} fusion(bf16[528,768]{1,0:T(8,128)(2,1)S(1)} %copy-done.16, bf16[528,1920]{1,0:T(8,128)(2,1)} %get-tuple-element.205), kind=kOutput, calls=%fused_computation.1 | convolution fusion | flops 1558609920 | bytes 5787648 | tf_op jit(solution)/shard_map/dot_general | solution.py:180
  155.1 1.8 dynamic-slice_bitcast_fusion
  156.9 1.5 collective-permute-done.34
  159.5 1.9 fusion.14
  162.4 4.4 %fusion = f32[512,768]{1,0:T(8,128)S(1)} fusion(bf16[768,1920]{1,0:T(8,128)(2,1)} %get-tuple-element.206, bf16[528,1920]{1,0:T(8,128)(2,1)} %get-tuple-element.205), kind=kOutput, calls=%fused_computation.2 | convolution fusion | flops 1509949440 | bytes 6488064 | tf_op jit(solution)/shard_map/dot_general | solution.py:176
  166.9 1.6 fusion.4
  169.6 3.1 %shard_map.219 = (bf16[96,2176]{1,0:T(8,128)(2,1)}, bf16[96,2176]{1,0:T(8,128)(2,1)}, bf16[96,2176]{1,0:T(8,128)(2,1)}, bf16[96,2176]{1,0:T(8,128)(2,1)}) custom-call(s32[1]{0:T(128)} %bitcast.at, bf16[4,96,1920]{2,1,0:T(8,128)(2,1)} %get-tuple-element.236.keep, bf16[4,96,1920]{2,1,0:T(8,128)(2,1)} %collective-permute-done.31.got, ...), custom_call_target="tpu_custom_call" | custom-call | flops 1 | bytes 1480000 | tf_op jit(solution)/shard_map/pallas_call | solution.py:233
  172.7 4.0 %collective-permute-start.41 = (bf16[512,768]{1,0:T(8,128)(2,1)S(1)}, bf16[512,768]{1,0:T(8,128)(2,1)S(1)}, u32[]{:S(2)}, u32[]{:S(2)}) collective-permute-start(bf16[512,768]{1,0:T(8,128)(2,1)S(1)} %fusion.8), channel_id=1, source_target_pairs={{1,16},{3,18},{5,20},{7,22},{9,24},{11,26},{13,28},{15,30},{16,1},... | collective-permute-start | bytes 2359304 | tf_op jit(solution)/shard_map/ppermute | solution.py:50
  176.9 1.4 collective-permute-start.38
  178.7 0.9 collective-permute-start.40
  179.8 9.1 %collective-permute-done.38 = bf16[96,2176]{1,0:T(8,128)(2,1)S(1)} collective-permute-done((bf16[96,2176]{1,0:T(8,128)(2,1)}, bf16[96,2176]{1,0:T(8,128)(2,1)S(1)}, u32[]{:S(2)}, u32[]{:S(2)}) %collective-permute-start.38) | collective-permute-done | bytes 417824 | tf_op jit(solution)/shard_map/ppermute | solution.py:33
  188.9 7.4 %collective-permute-done.39 = bf16[96,2176]{1,0:T(8,128)(2,1)S(1)} collective-permute-done((bf16[96,2176]{1,0:T(8,128)(2,1)}, bf16[96,2176]{1,0:T(8,128)(2,1)S(1)}, u32[]{:S(2)}, u32[]{:S(2)}) %collective-permute-start.39) | collective-permute-done | bytes 417824 | tf_op jit(solution)/shard_map/ppermute | solution.py:33
  196.3 8.6 %collective-permute-done.41 = bf16[512,768]{1,0:T(8,128)(2,1)S(1)} collective-permute-done((bf16[512,768]{1,0:T(8,128)(2,1)S(1)}, bf16[512,768]{1,0:T(8,128)(2,1)S(1)}, u32[]{:S(2)}, u32[]{:S(2)}) %collective-permute-start.41) | collective-permute-done | bytes 786464 | tf_op jit(solution)/shard_map/ppermute | solution.py:50
  204.9 0.8 fusion.19
  205.8 1.2 add_convert_fusion.2
  207.6 6.2 %collective-permute-done.42 = bf16[96,1344]{1,0:T(8,128)(2,1)S(1)} collective-permute-done((bf16[96,1344]{1,0:T(8,128)(2,1)S(1)}, bf16[96,1344]{1,0:T(8,128)(2,1)S(1)}, u32[]{:S(2)}, u32[]{:S(2)}) %collective-permute-start.42) | collective-permute-done | bytes 258080 | tf_op jit(solution)/shard_map/ppermute | solution.py:33
  214.4 2.4 %broadcast_select_fusion = (bf16[512,768]{1,0:T(8,128)(2,1)S(1)}, bf16[512,768]{1,0:T(8,128)(2,1)}) fusion(bf16[512,768]{1,0:T(8,128)(2,1)S(1)} %fusion.8, bf16[512,768]{1,0:T(8,128)(2,1)} %copy-done.22, pred[]{:T(512)S(6)} %eq.101, bf16[512,768]{1,0:T(8,128)(2,1)} %get-tuple-element.186, bf16[512,768]{1,0:T(8,128)(2,1)} %copy-done.21), kind=kLoop, calls=%fused_computation.23 | loop fusion | flops 786432 | bytes 4718593 | tf_op jit(solution)/shard_map/jit(_where)/select_n | solution.py:1244
  217.0 10.9 %collective-permute-done.44 = bf16[96,1216]{1,0:T(8,128)(2,1)S(1)} collective-permute-done((bf16[96,1216]{1,0:T(8,128)(2,1)S(1)}, bf16[96,1216]{1,0:T(8,128)(2,1)S(1)}, u32[]{:S(2)}, u32[]{:S(2)}) %collective-permute-start.44) | collective-permute-done | bytes 233504 | tf_op jit(solution)/shard_map/ppermute | solution.py:33
  228.0 0.6 slice_bitcast_fusion
  230.0 4.6 %collective-permute-start.46 = (bf16[96,256]{1,0:T(8,128)(2,1)S(1)}, bf16[96,256]{1,0:T(8,128)(2,1)S(1)}, u32[]{:S(2)}, u32[]{:S(2)}) collective-permute-start(bf16[96,256]{1,0:T(8,128)(2,1)S(1)} %pad_maximum_fusion.4), channel_id=1, source_target_pairs={{1,16},{3,18},{5,20},{7,22},{9,24},{11,26},{13,28},{15,30},{16,1},... | collective-permute-start | bytes 147464 | tf_op jit(solution)/shard_map/ppermute | solution.py:50
  234.6 0.9 pad_maximum_fusion.2
  235.5 0.6 reshape.313
  236.2 0.6 reduce_sum.99
  238.1 1.3 multiply_reduce_fusion
  (240 shorter events, 19.1 us)
Async XLA Ops:
  1.8 23.8 %copy-start.48 = (f32[24]{0:T(128)S(1)}, f32[24]{0:T(128)}, u32[]{:S(2)}) copy-start(f32[24]{0:T(128)} %param.20) | copy-start | bytes 292
  1.8 24.3 %copy-start.44 = (f32[24]{0:T(128)S(1)}, f32[24]{0:T(128)}, u32[]{:S(2)}) copy-start(f32[24]{0:T(128)} %param.22) | copy-start | bytes 292
  1.8 25.0 %copy-start.38 = (f32[4,1792]{1,0:T(4,128)S(1)}, f32[4,1792]{1,0:T(4,128)}, u32[]{:S(2)}) copy-start(f32[4,1792]{1,0:T(4,128)} %param.18) | copy-start | bytes 86020
  1.8 25.6 %copy-start.43 = (f32[1792]{0:T(1024)S(1)}, f32[1792]{0:T(1024)}, u32[]{:S(2)}) copy-start(f32[1792]{0:T(1024)} %param.19) | copy-start | bytes 21508
  1.8 26.2 %copy-start.42 = (f32[1536]{0:T(1024)S(1)}, f32[1536]{0:T(1024)}, u32[]{:S(2)}) copy-start(f32[1536]{0:T(1024)} %param.23) | copy-start | bytes 18436
  1.8 26.8 %copy-start.49 = (f32[24]{0:T(128)S(1)}, f32[24]{0:T(128)}, u32[]{:S(2)}) copy-start(f32[24]{0:T(128)} %param.21) | copy-start | bytes 292
  2.8 39.7 %copy-start.12 = (bf16[96,1920]{1,0:T(8,128)(2,1)}, bf16[96,1920]{1,0:T(8,128)(2,1)S(1)}, u32[]{:S(2)}) copy-start(bf16[96,1920]{1,0:T(8,128)(2,1)S(1)} %concatenate.42.refs_1_) | copy-start | bytes 1105924
  2.8 33.1 %copy-start.20 = (bf16[512,768]{1,0:T(8,128)(2,1)S(1)}, bf16[512,768]{1,0:T(8,128)(2,1)}, u32[]{:S(2)}) copy-start(bf16[512,768]{1,0:T(8,128)(2,1)} %refs_9_.1) | copy-start | bytes 2359300
  2.8 39.6 %slice-start.1 = ((bf16[96,3352]{1,0:T(8,128)(2,1)}), bf16[96,1536]{1,0:T(8,128)(2,1)S(1)}, s32[]{:S(2)}) async-start(bf16[96,3352]{1,0:T(8,128)(2,1)} %param.17), calls=%async_computation.1 | async-start | bytes 589824 | tf_op jit(solution)/shard_map/slice | solution.py:1101
  2.8 13.5 %collective-permute-start.1 = (bf16[96,1920]{1,0:T(8,128)(2,1)S(1)}, bf16[96,1920]{1,0:T(8,128)(2,1)S(1)}, u32[]{:S(2)}, u32[]{:S(2)}) collective-permute-start(bf16[96,1920]{1,0:T(8,128)(2,1)S(1)} %concatenate.42.refs_1_), channel_id=1, source_target_pairs={{0,6},{1,7},{2,4},{3,5},{4,2},{5,3},{6,0},{7,1},{8,14},{9,15},{10,... | collective-permute-start | bytes 1105928 | tf_op jit(solution)/shard_map/ppermute | solution.py:33
  5.8 17.1 %collective-permute-start.2 = (bf16[96,1920]{1,0:T(8,128)(2,1)S(1)}, bf16[96,1920]{1,0:T(8,128)(2,1)}, u32[]{:S(2)}, u32[]{:S(2)}) collective-permute-start(bf16[96,1920]{1,0:T(8,128)(2,1)S(1)} %concatenate.42.refs_1_), channel_id=1, source_target_pairs={{0,4},{1,5},{2,6},{3,7},{4,0},{5,1},{6,2},{7,3},{8,12},{9,13},{10,... | collective-permute-start | bytes 1105928 | tf_op jit(solution)/shard_map/ppermute | solution.py:33
  6.1 18.4 %collective-permute-start.3 = (bf16[96,1920]{1,0:T(8,128)(2,1)S(1)}, bf16[96,1920]{1,0:T(8,128)(2,1)}, u32[]{:S(2)}, u32[]{:S(2)}) collective-permute-start(bf16[96,1920]{1,0:T(8,128)(2,1)S(1)} %concatenate.42.refs_1_), channel_id=1, source_target_pairs={{0,2},{1,3},{2,0},{3,1},{4,6},{5,7},{6,4},{7,5},{8,10},{9,11},{10,... | collective-permute-start | bytes 1105928 | tf_op jit(solution)/shard_map/ppermute | solution.py:33
  6.2 25.9 %collective-permute-start.4 = (bf16[96,1920]{1,0:T(8,128)(2,1)S(1)}, bf16[96,1920]{1,0:T(8,128)(2,1)}, u32[]{:S(2)}, u32[]{:S(2)}) collective-permute-start(bf16[96,1920]{1,0:T(8,128)(2,1)S(1)} %concatenate.42.refs_1_), channel_id=1, source_target_pairs={{0,1},{1,0},{2,3},{3,2},{4,5},{5,4},{6,7},{7,6},{8,9},{9,8},{10,11... | collective-permute-start | bytes 1105928 | tf_op jit(solution)/shard_map/ppermute | solution.py:33
  8.2 1.1 collective-permute-start
  9.3 22.8 %collective-permute-start.8 = (bf16[512,768]{1,0:T(8,128)(2,1)S(1)}, bf16[512,768]{1,0:T(8,128)(2,1)S(1)}, u32[]{:S(2)}, u32[]{:S(2)}) collective-permute-start(bf16[512,768]{1,0:T(8,128)(2,1)S(1)} %copy-done.13), channel_id=1, source_target_pairs={{1,16},{3,18},{5,20},{7,22},{9,24},{11,26},{13,28},{15,30},{16,1},... | collective-permute-start | bytes 2359304 | tf_op jit(solution)/shard_map/ppermute | solution.py:50
  16.3 19.3 %copy-start.31 = (bf16[96,1920]{1,0:T(8,128)(2,1)}, bf16[96,1920]{1,0:T(8,128)(2,1)S(1)}, u32[]{:S(2)}) copy-start(bf16[96,1920]{1,0:T(8,128)(2,1)S(1)} %collective-permute-done.1.refs_2_) | copy-start | bytes 1105924
  16.3 15.8 %collective-permute-start.5 = (bf16[96,1920]{1,0:T(8,128)(2,1)S(1)}, bf16[96,1920]{1,0:T(8,128)(2,1)}, u32[]{:S(2)}, u32[]{:S(2)}) collective-permute-start(bf16[96,1920]{1,0:T(8,128)(2,1)S(1)} %collective-permute-done.1.refs_2_), channel_id=1, source_target_pairs={{0,1},{1,0},{2,3},{3,2},{4,5},{5,4},{6,7},{7,6},{8,9},{9,8},{10,11... | collective-permute-start | bytes 1105928 | tf_op jit(solution)/shard_map/ppermute | solution.py:33
  22.9 9.3 %collective-permute-start.6 = (bf16[96,1920]{1,0:T(8,128)(2,1)}, bf16[96,1920]{1,0:T(8,128)(2,1)}, u32[]{:S(2)}, u32[]{:S(2)}) collective-permute-start(bf16[96,1920]{1,0:T(8,128)(2,1)} %collective-permute-done.2.refs_3_), channel_id=1, source_target_pairs={{0,1},{1,0},{2,3},{3,2},{4,5},{5,4},{6,7},{7,6},{8,9},{9,8},{10,11... | collective-permute-start | bytes 1105928 | tf_op jit(solution)/shard_map/ppermute | solution.py:33
  24.4 7.7 %collective-permute-start.7 = (bf16[96,1920]{1,0:T(8,128)(2,1)}, bf16[96,1920]{1,0:T(8,128)(2,1)}, u32[]{:S(2)}, u32[]{:S(2)}) collective-permute-start(bf16[96,1920]{1,0:T(8,128)(2,1)} %collective-permute-done.3.refs_4_), channel_id=1, source_target_pairs={{0,1},{1,0},{2,3},{3,2},{4,5},{5,4},{6,7},{7,6},{8,9},{9,8},{10,11... | collective-permute-start | bytes 1105928 | tf_op jit(solution)/shard_map/ppermute | solution.py:33
  32.1 13.1 %copy-start.14 = (bf16[512,768]{1,0:T(8,128)(2,1)}, bf16[512,768]{1,0:T(8,128)(2,1)S(1)}, u32[]{:S(2)}) copy-start(bf16[512,768]{1,0:T(8,128)(2,1)S(1)} %collective-permute-done.8.refs_14_) | copy-start | bytes 2359300
  32.1 13.1 %copy-start.33 = (bf16[16,768]{1,0:T(8,128)(2,1)}, bf16[16,768]{1,0:T(8,128)(2,1)S(1)}, u32[]{:S(2)}) copy-start(bf16[16,768]{1,0:T(8,128)(2,1)S(1)} %fusion.22.refs_9_) | copy-start | bytes 73732
  32.2 2.9 %collective-permute-start.10 = (bf16[16,768]{1,0:T(8,128)(2,1)S(1)}, bf16[16,768]{1,0:T(8,128)(2,1)S(1)}, u32[]{:S(2)}, u32[]{:S(2)}) collective-permute-start(bf16[16,768]{1,0:T(8,128)(2,1)S(1)} %fusion.22.refs_9_), channel_id=1, source_target_pairs={{0,1},{1,0},{2,3},{3,2},{4,5},{5,4},{6,7},{7,6},{8,9},{9,8},{10,11... | collective-permute-start | bytes 73736 | tf_op jit(solution)/shard_map/ppermute | solution.py:68
  32.2 3.4 %collective-permute-start.11 = (bf16[16,768]{1,0:T(8,128)(2,1)S(1)}, bf16[16,768]{1,0:T(8,128)(2,1)S(1)}, u32[]{:S(2)}, u32[]{:S(2)}) collective-permute-start(bf16[16,768]{1,0:T(8,128)(2,1)S(1)} %fusion.22.refs_9_), channel_id=1, source_target_pairs={{0,9},{1,8},{2,11},{3,10},{4,13},{5,12},{6,15},{7,14},{8,1},{9,0},... | collective-permute-start | bytes 73736 | tf_op jit(solution)/shard_map/ppermute | solution.py:68
  33.1 2.8 %collective-permute-start.9 = (bf16[16,768]{1,0:T(8,128)(2,1)S(1)}, bf16[16,768]{1,0:T(8,128)(2,1)S(1)}, u32[]{:S(2)}, u32[]{:S(2)}) collective-permute-start(bf16[16,768]{1,0:T(8,128)(2,1)S(1)} %fusion.22.refs_9_), channel_id=1, source_target_pairs={{0,8},{1,9},{2,10},{3,11},{4,12},{5,13},{6,14},{7,15},{8,0},{9,1},... | collective-permute-start | bytes 73736 | tf_op jit(solution)/shard_map/ppermute | solution.py:68
  35.8 32.4 %collective-permute-start.20 = (bf16[512,768]{1,0:T(8,128)(2,1)S(1)}, bf16[512,768]{1,0:T(8,128)(2,1)S(1)}, u32[]{:S(2)}, u32[]{:S(2)}) collective-permute-start(bf16[512,768]{1,0:T(8,128)(2,1)S(1)} %copy-done.20), channel_id=1, source_target_pairs={{1,16},{3,18},{5,20},{7,22},{9,24},{11,26},{13,28},{15,30},{16,1},... | collective-permute-start | bytes 2359304 | tf_op jit(solution)/shard_map/ppermute | solution.py:50
  42.5 25.8 %copy-start.9 = (bf16[96,3072]{1,0:T(8,128)(2,1)}, bf16[96,3072]{1,0:T(8,128)(2,1)S(1)}, u32[]{:S(2)}) copy-start(bf16[96,3072]{1,0:T(8,128)(2,1)S(1)} %pad_maximum_fusion.1.refs_0_) | copy-start | bytes 1769476
  42.5 23.7 %collective-permute-start.13 = (bf16[96,3072]{1,0:T(8,128)(2,1)S(1)}, bf16[96,3072]{1,0:T(8,128)(2,1)S(1)}, u32[]{:S(2)}, u32[]{:S(2)}) collective-permute-start(bf16[96,3072]{1,0:T(8,128)(2,1)S(1)} %pad_maximum_fusion.1.refs_0_), channel_id=1, source_target_pairs={{0,6},{1,7},{2,4},{3,5},{4,2},{5,3},{6,0},{7,1},{8,14},{9,15},{10,... | collective-permute-start | bytes 1769480 | tf_op jit(solution)/shard_map/ppermute | solution.py:33
  44.7 22.7 %collective-permute-start.14 = (bf16[96,3072]{1,0:T(8,128)(2,1)S(1)}, bf16[96,3072]{1,0:T(8,128)(2,1)S(1)}, u32[]{:S(2)}, u32[]{:S(2)}) collective-permute-start(bf16[96,3072]{1,0:T(8,128)(2,1)S(1)} %pad_maximum_fusion.1.refs_0_), channel_id=1, source_target_pairs={{0,4},{1,5},{2,6},{3,7},{4,0},{5,1},{6,2},{7,3},{8,12},{9,13},{10,... | collective-permute-start | bytes 1769480 | tf_op jit(solution)/shard_map/ppermute | solution.py:33
  44.9 22.6 %collective-permute-start.15 = (bf16[96,3072]{1,0:T(8,128)(2,1)S(1)}, bf16[96,3072]{1,0:T(8,128)(2,1)S(1)}, u32[]{:S(2)}, u32[]{:S(2)}) collective-permute-start(bf16[96,3072]{1,0:T(8,128)(2,1)S(1)} %pad_maximum_fusion.1.refs_0_), channel_id=1, source_target_pairs={{0,2},{1,3},{2,0},{3,1},{4,6},{5,7},{6,4},{7,5},{8,10},{9,11},{10,... | collective-permute-start | bytes 1769480 | tf_op jit(solution)/shard_map/ppermute | solution.py:33
  59.6 23.3 %collective-permute-start.12 = (bf16[2,128,1664]{2,1,0:T(8,128)(2,1)}, bf16[2,128,1664]{2,1,0:T(8,128)(2,1)S(1)}, u32[]{:S(2)}, u32[]{:S(2)}) collective-permute-start(bf16[2,128,1664]{2,1,0:T(8,128)(2,1)} %get-tuple-element.148.refs_1_.refs_5_), channel_id=1, source_target_pairs={{0,8},{8,0},{16,24},{24,16},{1,9},{9,1},{17,25},{25,17},{2,10},{10... | collective-permute-start | bytes 2555912 | tf_op jit(solution)/shard_map/ppermute | solution.py:33
  67.5 2.0 collective-permute-start.17
  67.7 2.6 %collective-permute-start.18 = (bf16[96,3072]{1,0:T(8,128)(2,1)S(1)}, bf16[96,3072]{1,0:T(8,128)(2,1)S(1)}, u32[]{:S(2)}, u32[]{:S(2)}) collective-permute-start(bf16[96,3072]{1,0:T(8,128)(2,1)S(1)} %collective-permute-done.14.refs_2_), channel_id=1, source_target_pairs={{0,1},{1,0},{2,3},{3,2},{4,5},{5,4},{6,7},{7,6},{8,9},{9,8},{10,11... | collective-permute-start | bytes 1769480 | tf_op jit(solution)/shard_map/ppermute | solution.py:33
  68.0 3.2 %collective-permute-start.19 = (bf16[96,3072]{1,0:T(8,128)(2,1)S(1)}, bf16[96,3072]{1,0:T(8,128)(2,1)S(1)}, u32[]{:S(2)}, u32[]{:S(2)}) collective-permute-start(bf16[96,3072]{1,0:T(8,128)(2,1)S(1)} %collective-permute-done.15.refs_3_), channel_id=1, source_target_pairs={{0,1},{1,0},{2,3},{3,2},{4,5},{5,4},{6,7},{7,6},{8,9},{9,8},{10,11... | collective-permute-start | bytes 1769480 | tf_op jit(solution)/shard_map/ppermute | solution.py:33
  68.2 3.8 %collective-permute-start.16 = (bf16[96,3072]{1,0:T(8,128)(2,1)S(1)}, bf16[96,3072]{1,0:T(8,128)(2,1)S(1)}, u32[]{:S(2)}, u32[]{:S(2)}) collective-permute-start(bf16[96,3072]{1,0:T(8,128)(2,1)S(1)} %pad_maximum_fusion.1.refs_0_), channel_id=1, source_target_pairs={{0,1},{1,0},{2,3},{3,2},{4,5},{5,4},{6,7},{7,6},{8,9},{9,8},{10,11... | collective-permute-start | bytes 1769480 | tf_op jit(solution)/shard_map/ppermute | solution.py:33
  69.5 13.7 %collective-permute-start.21 = (bf16[2,128,1664]{2,1,0:T(8,128)(2,1)S(1)}, bf16[2,128,1664]{2,1,0:T(8,128)(2,1)S(1)}, u32[]{:S(2)}, u32[]{:S(2)}) collective-permute-start(bf16[2,128,1664]{2,1,0:T(8,128)(2,1)S(1)} %copy-done), channel_id=1, source_target_pairs={{0,1},{1,0},{2,3},{3,2},{4,5},{5,4},{6,7},{7,6},{8,9},{9,8},{10,11... | collective-permute-start | bytes 2555912 | tf_op jit(solution)/shard_map/ppermute | solution.py:33
  82.9 2.4 %collective-permute-start.22 = (bf16[2,128,1664]{2,1,0:T(8,128)(2,1)S(1)}, bf16[2,128,1664]{2,1,0:T(8,128)(2,1)S(1)}, u32[]{:S(2)}, u32[]{:S(2)}) collective-permute-start(bf16[2,128,1664]{2,1,0:T(8,128)(2,1)S(1)} %collective-permute-done.12.refs_2_.refs_6_), channel_id=1, source_target_pairs={{0,1},{1,0},{2,3},{3,2},{4,5},{5,4},{6,7},{7,6},{8,9},{9,8},{10,11... | collective-permute-start | bytes 2555912 | tf_op jit(solution)/shard_map/ppermute | solution.py:33
  100.7 21.6 %collective-permute-start.23 = (bf16[2,128,1536]{2,1,0:T(8,128)(2,1)}, bf16[2,128,1536]{2,1,0:T(8,128)(2,1)S(1)}, u32[]{:S(2)}, u32[]{:S(2)}) collective-permute-start(bf16[2,128,1536]{2,1,0:T(8,128)(2,1)} %get-tuple-element.177.refs_1_), channel_id=1, source_target_pairs={{0,8},{8,0},{16,24},{24,16},{1,9},{9,1},{17,25},{25,17},{2,10},{10... | collective-permute-start | bytes 2359304 | tf_op jit(solution)/shard_map/ppermute | solution.py:33
  109.7 12.5 %collective-permute-start.24 = (bf16[96,3072]{1,0:T(8,128)(2,1)}, bf16[96,3072]{1,0:T(8,128)(2,1)S(1)}, u32[]{:S(2)}, u32[]{:S(2)}) collective-permute-start(bf16[96,3072]{1,0:T(8,128)(2,1)} %get-tuple-element.167), channel_id=1, source_target_pairs={{0,1},{1,0},{2,3},{3,2},{4,5},{5,4},{6,7},{7,6},{8,9},{9,8},{10,11... | collective-permute-start | bytes 1769480 | tf_op jit(solution)/shard_map/ppermute | solution.py:33
  110.2 12.1 %collective-permute-start.25 = (bf16[96,3072]{1,0:T(8,128)(2,1)}, bf16[96,3072]{1,0:T(8,128)(2,1)S(1)}, u32[]{:S(2)}, u32[]{:S(2)}) collective-permute-start(bf16[96,3072]{1,0:T(8,128)(2,1)} %get-tuple-element.168), channel_id=1, source_target_pairs={{0,1},{1,0},{2,3},{3,2},{4,5},{5,4},{6,7},{7,6},{8,9},{9,8},{10,11... | collective-permute-start | bytes 1769480 | tf_op jit(solution)/shard_map/ppermute | solution.py:33
  110.2 12.0 %collective-permute-start.26 = (bf16[96,3072]{1,0:T(8,128)(2,1)}, bf16[96,3072]{1,0:T(8,128)(2,1)S(1)}, u32[]{:S(2)}, u32[]{:S(2)}) collective-permute-start(bf16[96,3072]{1,0:T(8,128)(2,1)} %get-tuple-element.169), channel_id=1, source_target_pairs={{0,1},{1,0},{2,3},{3,2},{4,5},{5,4},{6,7},{7,6},{8,9},{9,8},{10,11... | collective-permute-start | bytes 1769480 | tf_op jit(solution)/shard_map/ppermute | solution.py:33
  110.7 11.6 %collective-permute-start.27 = (bf16[96,3072]{1,0:T(8,128)(2,1)}, bf16[96,3072]{1,0:T(8,128)(2,1)S(1)}, u32[]{:S(2)}, u32[]{:S(2)}) collective-permute-start(bf16[96,3072]{1,0:T(8,128)(2,1)} %get-tuple-element.170), channel_id=1, source_target_pairs={{0,1},{1,0},{2,3},{3,2},{4,5},{5,4},{6,7},{7,6},{8,9},{9,8},{10,11... | collective-permute-start | bytes 1769480 | tf_op jit(solution)/shard_map/ppermute | solution.py:33
  110.8 11.6 %copy-start.10 = (bf16[4,96,3072]{2,1,0:T(8,128)(2,1)S(1)}, bf16[4,96,3072]{2,1,0:T(8,128)(2,1)}, u32[]{:S(2)}) copy-start(bf16[4,96,3072]{2,1,0:T(8,128)(2,1)} %get-tuple-element.180) | copy-start | bytes 7077892
  124.4 2.6 %collective-permute-start.28 = (bf16[2,128,1536]{2,1,0:T(8,128)(2,1)S(1)}, bf16[2,128,1536]{2,1,0:T(8,128)(2,1)S(1)}, u32[]{:S(2)}, u32[]{:S(2)}) collective-permute-start(bf16[2,128,1536]{2,1,0:T(8,128)(2,1)S(1)} %collective-permute-done.23.refs_2_), channel_id=1, source_target_pairs={{0,1},{1,0},{2,3},{3,2},{4,5},{5,4},{6,7},{7,6},{8,9},{9,8},{10,11... | collective-permute-start | bytes 2359304 | tf_op jit(solution)/shard_map/ppermute | solution.py:33
  124.8 8.3 %collective-permute-start.30 = (bf16[2,128,1536]{2,1,0:T(8,128)(2,1)S(1)}, bf16[2,128,1536]{2,1,0:T(8,128)(2,1)}, u32[]{:S(2)}, u32[]{:S(2)}) collective-permute-start(bf16[2,128,1536]{2,1,0:T(8,128)(2,1)S(1)} %copy-done.17), channel_id=1, source_target_pairs={{0,1},{1,0},{2,3},{3,2},{4,5},{5,4},{6,7},{7,6},{8,9},{9,8},{10,11... | collective-permute-start | bytes 2359304 | tf_op jit(solution)/shard_map/ppermute | solution.py:33
  127.0 23.3 %collective-permute-start.29 = (bf16[512,768]{1,0:T(8,128)(2,1)}, bf16[512,768]{1,0:T(8,128)(2,1)S(1)}, u32[]{:S(2)}, u32[]{:S(2)}) collective-permute-start(bf16[512,768]{1,0:T(8,128)(2,1)} %get-tuple-element.186), channel_id=1, source_target_pairs={{1,16},{3,18},{5,20},{7,22},{9,24},{11,26},{13,28},{15,30},{16,1},... | collective-permute-start | bytes 2359304 | tf_op jit(solution)/shard_map/ppermute | solution.py:50
  130.5 26.4 %collective-permute-start.33 = (bf16[96,3072]{1,0:T(8,128)(2,1)}, bf16[96,3072]{1,0:T(8,128)(2,1)S(1)}, u32[]{:S(2)}, u32[]{:S(2)}) collective-permute-start(bf16[96,3072]{1,0:T(8,128)(2,1)} %get-tuple-element.239), channel_id=1, source_target_pairs={{0,2},{1,3},{2,0},{3,1},{4,6},{5,7},{6,4},{7,5},{8,10},{9,11},{10,... | collective-permute-start | bytes 1769480 | tf_op jit(solution)/shard_map/ppermute | solution.py:33
  131.7 26.7 %collective-permute-start.34 = (bf16[96,3072]{1,0:T(8,128)(2,1)}, bf16[96,3072]{1,0:T(8,128)(2,1)S(1)}, u32[]{:S(2)}, u32[]{:S(2)}) collective-permute-start(bf16[96,3072]{1,0:T(8,128)(2,1)} %get-tuple-element.238), channel_id=1, source_target_pairs={{0,4},{1,5},{2,6},{3,7},{4,0},{5,1},{6,2},{7,3},{8,12},{9,13},{10,... | collective-permute-start | bytes 1769480 | tf_op jit(solution)/shard_map/ppermute | solution.py:33
  132.2 26.2 %collective-permute-start.35 = (bf16[96,3072]{1,0:T(8,128)(2,1)S(1)}, bf16[96,3072]{1,0:T(8,128)(2,1)S(1)}, u32[]{:S(2)}, u32[]{:S(2)}) collective-permute-start(bf16[96,3072]{1,0:T(8,128)(2,1)S(1)} %get-tuple-element.237), channel_id=1, source_target_pairs={{0,6},{1,7},{2,4},{3,5},{4,2},{5,3},{6,0},{7,1},{8,14},{9,15},{10,... | collective-permute-start | bytes 1769480 | tf_op jit(solution)/shard_map/ppermute | solution.py:33
  133.2 17.2 %copy-start.16 = (bf16[528,768]{1,0:T(8,128)(2,1)S(1)}, bf16[528,768]{1,0:T(8,128)(2,1)}, u32[]{:S(2)}) copy-start(bf16[528,768]{1,0:T(8,128)(2,1)} %get-tuple-element.155.refs_8_) | copy-start | bytes 2433028
  156.9 12.1 %collective-permute-start.31 = (bf16[4,96,1920]{2,1,0:T(8,128)(2,1)}, bf16[4,96,1920]{2,1,0:T(8,128)(2,1)}, u32[]{:S(2)}, u32[]{:S(2)}) collective-permute-start(bf16[4,96,1920]{2,1,0:T(8,128)(2,1)} %get-tuple-element.235), channel_id=1, source_target_pairs={{0,1},{1,0},{2,3},{3,2},{4,5},{5,4},{6,7},{7,6},{8,9},{9,8},{10,11... | collective-permute-start | bytes 4423688 | tf_op jit(solution)/shard_map/ppermute | solution.py:33
  158.8 10.2 %collective-permute-start.37 = (bf16[96,1536]{1,0:T(8,128)(2,1)S(1)}, bf16[96,1536]{1,0:T(8,128)(2,1)S(1)}, u32[]{:S(2)}, u32[]{:S(2)}) collective-permute-start(bf16[96,1536]{1,0:T(8,128)(2,1)S(1)} %constant_dynamic-slice_fusion.1), channel_id=1, source_target_pairs={{0,8},{8,0},{16,24},{24,16},{1,9},{9,1},{17,25},{25,17},{2,10},{10... | collective-permute-start | bytes 884744 | tf_op jit(solution)/shard_map/ppermute | solution.py:33
  161.6 7.4 %collective-permute-start.36 = (bf16[96,64]{1,0:T(8,128)(2,1)S(1)}, bf16[96,64]{1,0:T(8,128)(2,1)S(1)}, u32[]{:S(2)}, u32[]{:S(2)}) collective-permute-start(bf16[96,64]{1,0:T(8,128)(2,1)S(1)} %reshape.310), channel_id=1, source_target_pairs={{0,1},{1,0},{2,3},{3,2},{4,5},{5,4},{6,7},{7,6},{8,9},{9,8},{10,11... | collective-permute-start | bytes 36872 | tf_op jit(solution)/shard_map/ppermute | solution.py:33
  161.7 7.3 %collective-permute-start.32 = (f32[96,128]{1,0:T(8,128)S(1)}, f32[96,128]{1,0:T(8,128)S(1)}, u32[]{:S(2)}, u32[]{:S(2)}) collective-permute-start(f32[96,128]{1,0:T(8,128)S(1)} %copy-done.36), channel_id=1, source_target_pairs={{0,1},{1,0},{2,3},{3,2},{4,5},{5,4},{6,7},{7,6},{8,9},{9,8},{10,11... | collective-permute-start | bytes 147464 | tf_op jit(solution)/shard_map/ppermute | solution.py:33
  169.0 38.1 %copy-start.34 = (bf16[96,64]{1,0:T(8,128)(2,1)}, bf16[96,64]{1,0:T(8,128)(2,1)S(1)}, u32[]{:S(2)}) copy-start(bf16[96,64]{1,0:T(8,128)(2,1)S(1)} %collective-permute-done.36) | copy-start | bytes 36868
  172.7 32.2 %collective-permute-start.41 = (bf16[512,768]{1,0:T(8,128)(2,1)S(1)}, bf16[512,768]{1,0:T(8,128)(2,1)S(1)}, u32[]{:S(2)}, u32[]{:S(2)}) collective-permute-start(bf16[512,768]{1,0:T(8,128)(2,1)S(1)} %fusion.8), channel_id=1, source_target_pairs={{1,16},{3,18},{5,20},{7,22},{9,24},{11,26},{13,28},{15,30},{16,1},... | collective-permute-start | bytes 2359304 | tf_op jit(solution)/shard_map/ppermute | solution.py:50
  176.9 12.0 %collective-permute-start.38 = (bf16[96,2176]{1,0:T(8,128)(2,1)}, bf16[96,2176]{1,0:T(8,128)(2,1)S(1)}, u32[]{:S(2)}, u32[]{:S(2)}) collective-permute-start(bf16[96,2176]{1,0:T(8,128)(2,1)} %get-tuple-element.213), channel_id=1, source_target_pairs={{0,2},{1,3},{2,0},{3,1},{4,6},{5,7},{6,4},{7,5},{8,10},{9,11},{10,... | collective-permute-start | bytes 1253384 | tf_op jit(solution)/shard_map/ppermute | solution.py:33
  178.3 18.0 %collective-permute-start.39 = (bf16[96,2176]{1,0:T(8,128)(2,1)}, bf16[96,2176]{1,0:T(8,128)(2,1)S(1)}, u32[]{:S(2)}, u32[]{:S(2)}) collective-permute-start(bf16[96,2176]{1,0:T(8,128)(2,1)} %get-tuple-element.214), channel_id=1, source_target_pairs={{0,4},{1,5},{2,6},{3,7},{4,0},{5,1},{6,2},{7,3},{8,12},{9,13},{10,... | collective-permute-start | bytes 1253384 | tf_op jit(solution)/shard_map/ppermute | solution.py:33
  178.7 17.6 %collective-permute-start.40 = (bf16[96,2176]{1,0:T(8,128)(2,1)}, bf16[96,2176]{1,0:T(8,128)(2,1)S(1)}, u32[]{:S(2)}, u32[]{:S(2)}) collective-permute-start(bf16[96,2176]{1,0:T(8,128)(2,1)} %get-tuple-element.215), channel_id=1, source_target_pairs={{0,6},{1,7},{2,4},{3,5},{4,2},{5,3},{6,0},{7,1},{8,14},{9,15},{10,... | collective-permute-start | bytes 1253384 | tf_op jit(solution)/shard_map/ppermute | solution.py:33
  179.7 27.9 %collective-permute-start.43 = (bf16[96,1536]{1,0:T(8,128)(2,1)S(1)}, bf16[96,1536]{1,0:T(8,128)(2,1)S(1)}, u32[]{:S(2)}, u32[]{:S(2)}) collective-permute-start(bf16[96,1536]{1,0:T(8,128)(2,1)S(1)} %add_convert_fusion.4), channel_id=1, source_target_pairs={{0,16},{8,24},{16,0},{24,8},{1,17},{9,25},{17,1},{25,9},{2,18},{10... | collective-permute-start | bytes 884744 | tf_op jit(solution)/shard_map/ppermute | solution.py:33
  207.2 6.5 %collective-permute-start.42 = (bf16[96,1344]{1,0:T(8,128)(2,1)S(1)}, bf16[96,1344]{1,0:T(8,128)(2,1)S(1)}, u32[]{:S(2)}, u32[]{:S(2)}) collective-permute-start(bf16[96,1344]{1,0:T(8,128)(2,1)S(1)} %concatenate.44), channel_id=1, source_target_pairs={{0,8},{8,0},{16,24},{24,16},{1,9},{9,1},{17,25},{25,17},{2,10},{10... | collective-permute-start | bytes 774152 | tf_op jit(solution)/shard_map/ppermute | solution.py:33
  213.9 14.0 %collective-permute-start.45 = (bf16[96,1536]{1,0:T(8,128)(2,1)S(1)}, bf16[96,1536]{1,0:T(8,128)(2,1)S(1)}, u32[]{:S(2)}, u32[]{:S(2)}) collective-permute-start(bf16[96,1536]{1,0:T(8,128)(2,1)S(1)} %add_convert_fusion.3), channel_id=1, source_target_pairs={{0,8},{8,0},{16,24},{24,16},{1,9},{9,1},{17,25},{25,17},{2,10},{10... | collective-permute-start | bytes 884744 | tf_op jit(solution)/shard_map/ppermute | solution.py:33
  214.3 13.6 %collective-permute-start.44 = (bf16[96,1216]{1,0:T(8,128)(2,1)S(1)}, bf16[96,1216]{1,0:T(8,128)(2,1)S(1)}, u32[]{:S(2)}, u32[]{:S(2)}) collective-permute-start(bf16[96,1216]{1,0:T(8,128)(2,1)S(1)} %concatenate.46), channel_id=1, source_target_pairs={{0,16},{8,24},{16,0},{24,8},{1,17},{9,25},{17,1},{25,9},{2,18},{10... | collective-permute-start | bytes 700424 | tf_op jit(solution)/shard_map/ppermute | solution.py:33
  230.0 7.3 %collective-permute-start.47 = (bf16[96,960]{1,0:T(8,128)(2,1)S(1)}, bf16[96,960]{1,0:T(8,128)(2,1)S(1)}, u32[]{:S(2)}, u32[]{:S(2)}) collective-permute-start(bf16[96,960]{1,0:T(8,128)(2,1)S(1)} %add_convert_fusion.5), channel_id=1, source_target_pairs={{0,8},{8,0},{16,24},{24,16},{1,9},{9,1},{17,25},{25,17},{2,10},{10... | collective-permute-start | bytes 552968 | tf_op jit(solution)/shard_map/ppermute | solution.py:33
  230.0 6.8 %collective-permute-start.46 = (bf16[96,256]{1,0:T(8,128)(2,1)S(1)}, bf16[96,256]{1,0:T(8,128)(2,1)S(1)}, u32[]{:S(2)}, u32[]{:S(2)}) collective-permute-start(bf16[96,256]{1,0:T(8,128)(2,1)S(1)} %pad_maximum_fusion.4), channel_id=1, source_target_pairs={{1,16},{3,18},{5,20},{7,22},{9,24},{11,26},{13,28},{15,30},{16,1},... | collective-permute-start | bytes 147464 | tf_op jit(solution)/shard_map/ppermute | solution.py:50
  (36 other events, 138.4 us)

commit v3 on v2

--- a/solution.py
+++ b/solution.py
@@ -25,6 +25,7 @@
 NCW = DI // CW
 VMEM_ASK = 56 * 2**20
 VMEM_ROOM = 56 * 2**20
+VMEM_LESS = 44 * 2**20
 COST_SCALE = 0.4
 
 
@@ -314,8 +315,9 @@
     halos = refs[1 + len(layout) : 1 + len(layout) + n_halo]
     (
         tok_own, tok_got, conv_w, conv_b, dt_bias, a_log, table,
-        wa_out, tok, tok_halo, normal, normal_t, xbc, slope, xs, xt, bs, cs, raw, cum, cum_t, states,
-        wa, ext, small, sems, out_sem,
+        wa_out, tok_out, tok_halo, normal_out, normal_t_out, xbc, slope, xs, xt, bs_out, cs_out,
+        raw_out, cum_out, cum_t_out, states,
+        wa, ext, small, sems, out_sems, tok, normal, normal_t, bs, cs, raw, cum, cum_t,
     ) = refs[1 + len(layout) + n_halo :]
     step = pl.program_id(0)
     rows = tok_own.shape[0]
@@ -343,8 +345,10 @@
         xbc[rows:, :width] = jnp.concatenate(heads, axis=0).astype(BF)
         return acts
 
-    def out_copy():
-        return pltpu.make_async_copy(wa, wa_out, out_sem)
+    def leaving():
+        moves = [(wa, wa_out), (tok, tok_out), (normal, normal_out), (normal_t, normal_t_out)]
+        moves += [(bs, bs_out), (cs, cs_out), (raw, raw_out), (cum, cum_out), (cum_t, cum_t_out)]
+        return [pltpu.make_async_copy(v, there, out_sems.at[n]) for n, (v, there) in enumerate(moves)]
 
     @pl.when(step == 0)
     def _():
@@ -371,7 +375,8 @@
         tok_halo[...] = jnp.concatenate(found, axis=0).astype(BF)
         for n in range(len(layout)):
             copy_of(n).wait()
-        out_copy().start()
+        for copy in leaving()[:2]:
+            copy.start()
         gain = wa[:, XBC : XBC + LANES].astype(F32).T[NH : NH + 1, :]
         normal[:rows, :] = normal_rows(tok[...], gain)
         normal_t[...] = normal[:rows, :].T
@@ -398,6 +403,8 @@
             states[i, :16, DI:] = ends
             small[i, 0] = jnp.concatenate(pieces2(dt), axis=1)
             small[i, 1] = jnp.concatenate(pieces2(jnp.exp(last - run) * dt), axis=1)
+        for copy in leaving()[2:]:
+            copy.start()
 
     @pl.when(step > 0)
     def _():
@@ -411,7 +418,8 @@
 
     @pl.when(step == NCW)
     def _():
-        out_copy().wait()
+        for copy in leaving():
+            copy.wait()
 
 
 def run_project(info, parts, halos, tok_own, tok_got, conv_w, conv_b, dt_bias, a_log, table):
@@ -432,27 +440,29 @@
     ins += [(table, columns(table, before))]
     outs = {
         "wa": (shape((DM, WA), BF), in_hbm()),
-        "tok": (shape((rows, DM), BF), whole),
+        "tok": (shape((rows, DM), BF), in_hbm()),
         "tok_halo": (shape((nb * HALO, DM), BF), whole),
-        "normal": (shape((ext_rows, DM), BF), whole),
-        "normal_t": (shape((DM, rows), BF), whole),
+        "normal": (shape((ext_rows, DM), BF), in_hbm()),
+        "normal_t": (shape((DM, rows), BF), in_hbm()),
         "xbc": (shape((ext_rows, WA), BF), lambda v: columns(v, tail_first)),
         "slope": (shape((rows, WA), BF), lambda v: columns(v, tail_first)),
         "xs": (shape((rows, DI), BF), lambda v: columns(v, before)),
         "xt": (shape((rows, DI), BF), lambda v: columns(v, before)),
-        "bs": (shape((rows, NS), BF), whole),
-        "cs": (shape((rows, NS), BF), whole),
-        "raw": (shape((rows, LANES), F32), whole),
-        "cum": (shape((rows, LANES), F32), whole),
-        "cum_t": (shape((LANES, rows), F32), whole),
+        "bs": (shape((rows, NS), BF), in_hbm()),
+        "cs": (shape((rows, NS), BF), in_hbm()),
+        "raw": (shape((rows, LANES), F32), in_hbm()),
+        "cum": (shape((rows, LANES), F32), in_hbm()),
+        "cum_t": (shape((LANES, rows), F32), in_hbm()),
         "states": (shape((nb, NS, DI + LANES), BF), whole),
     }
     out_list = [(o, s(o) if callable(s) else s) for o, s in outs.values()]
     scratch = [
         pltpu.VMEM((DM, WA), BF), pltpu.VMEM((nb, HALO + CH, CW), F32),
         pltpu.VMEM((nb, 2, CH, 2 * LANES), BF), pltpu.SemaphoreType.DMA((len(parts),)),
-        pltpu.SemaphoreType.DMA,
+        pltpu.SemaphoreType.DMA((9,)),
     ]
+    kept = ("tok", "normal", "normal_t", "bs", "cs", "raw", "cum", "cum_t")
+    scratch += [pltpu.VMEM(outs[k][0].shape, outs[k][0].dtype) for k in kept]
     got = call(
         functools.partial(project_kernel, layout, len(halos)), 14, (NCW + 1,), ins, out_list, scratch, VMEM_ASK,
     )
@@ -520,9 +530,15 @@
     )[0]
 
 
+OW = 768
+ONW = DI // OW
+
+
 def open_kernel(layout, at, *refs):
     pieces = refs[: len(layout)]
-    normal, cot_own, cot_got, stay, z, q, cot, wz, wo, sems = refs[len(layout) :]
+    normal, cot_own, cot_got, stay, z, q, cot, wz_out, wo_out, wz, wo, sems, out_sems = refs[
+        len(layout) :
+    ]
     c = pl.program_id(0)
     k_rows = pieces[0].shape[0]
 
@@ -541,6 +557,12 @@
             for k, (ref, begin, lanes) in enumerate(parts)
         ]
 
+    def leaving():
+        return [
+            pltpu.make_async_copy(wz, wz_out, out_sems.at[0]),
+            pltpu.make_async_copy(wo, wo_out, out_sems.at[1]),
+        ]
+
     @pl.when(c == 0)
     def _():
         for n in range(len(layout)):
@@ -550,10 +572,17 @@
         for n in range(len(layout)):
             for copy in copies(n):
                 copy.wait()
-
-    here = pl.ds(pl.multiple_of(c * CW, CW), CW)
+        for copy in leaving():
+            copy.start()
+
+    here = pl.ds(pl.multiple_of(c * OW, OW), OW)
     z[...] = dot(normal[...], wz[:, here]).astype(BF)
     q[...] = dot_nt(cot[...], wo[here, :]).astype(BF)
+
+    @pl.when(c == ONW - 1)
+    def _():
+        for copy in leaving():
+            copy.wait()
 
 
 def run_open(at, parts, normal, cot_own, cot_got, stay):
@@ -563,11 +592,16 @@
     ins += [(normal, pl.BlockSpec((rows, DM), lambda c: (0, 0)))]
     ins += [(cot_own, whole(cot_own)), (cot_got, whole(cot_got)), (stay, in_smem())]
     wide = shape((rows, DI), BF)
-    outs = [(wide, columns(wide, lambda c: c))] * 2
-    outs += [(v, whole(v)) for v in (shape((rows, DM), BF), shape((DM, DI), BF), shape((DI, DM), BF))]
+    outs = [(wide, columns(wide, lambda c: c, OW))] * 2
+    outs += [(v, whole(v)) for v in (shape((rows, DM), BF),)]
+    outs += [(v, in_hbm()) for v in (shape((DM, DI), BF), shape((DI, DM), BF))]
     return call(
-        functools.partial(open_kernel, layout), 1, (NCW,), ins, outs,
-        [pltpu.SemaphoreType.DMA((3 * len(parts),))],
+        functools.partial(open_kernel, layout), 1, (ONW,), ins, outs,
+        [
+            pltpu.VMEM((DM, DI), BF), pltpu.VMEM((DI, DM), BF),
+            pltpu.SemaphoreType.DMA((3 * len(parts),)), pltpu.SemaphoreType.DMA((2,)),
+        ],
+        VMEM_LESS,
     )
 
 
@@ -676,7 +710,7 @@
         for i in range(nb):
             r = slice(i * CH, (i + 1) * CH)
             low = totals[i].astype(BF)
-            enter[i, :, here] = low
+            enter[i] = low
             scan = y_intra[r, :] + dot(small[r, :], table[...]) * dot(cs[r, :], low)
             y_scan[r, here] = scan
             y = scan + d_skip[...] * xs[r, :].astype(F32)
@@ -743,7 +777,7 @@
     wide_f = shape((rows, DI), F32)
     row = shape((1, DI), F32)
     state = shape((nb, NS, DI), BF)
-    outs = [(state, whole(state))]
+    outs = [(state, columns_g(state, early))]
     outs += [(v, columns_g(v, late)) for v in (wide, row, wide, wide, wide, wide_f, row, state)]
     scratch = [
         pltpu.VMEM((rows, DI), F32), pltpu.VMEM((rows, 2 * LANES), BF),
@@ -1164,10 +1198,11 @@
         [d_a_all, dz, tok, a["tok_halo"], wa], a_give, zo_give
     )
     gain = wa[:, XBC + NH].astype(F32)
-    halo_part = norm_back(dot_nt(d_a_all[rows:], wa), tok_halo, gain)
+    from_a = dot_nt(d_a_all, wa)
+    halo_part = norm_back(from_a[rows:], tok_halo, gain)
     halo_part = halo_part.reshape(nb, HALO, DM)[:, HALO - KC :].astype(BF).reshape(k_rows, -1)
     halos = [halo_part, trade(halo_part, "shard", 1)]
-    normal_grad = dot_nt(dz, wz) + dot_nt(d_a_all[:rows], wa)
+    normal_grad = dot_nt(dz, wz) + from_a[:rows]
     token_grad = (cot.astype(F32) + norm_back(normal_grad, tok, gain)).astype(BF)
 
     a_got, small_got, halos[1], zo_got = after_all([a_got, small_got, halos[1], zo_got], token_grad)
@@ -1180,7 +1215,7 @@
     token_got = move_home(after(token_grad, a_pairs[0]))
     zo_half = head_add(zo_keep, after(zo_got, a_pairs[0]))
     zo_got = trade(zo_half, "head", 2)
-    *a_far, token_got = after_all(a_far + [token_got])
+    *a_far, zo_got = after_all(a_far + [zo_got])
     a_own = chip_sum(a_pairs[0][:, :WA], [v[:, :WA] for v in a_far])
     sums = [join2(v[:, WA:]) for v in [a_pairs[0]] + a_far]
     while len(sums) > 1:
@@ -1198,7 +1233,7 @@
         sent = jnp.concatenate([a_give, parts] + (halos if bit < half else []), axis=1)
         sent = trade(sent, "head", bit)
         if bit == 1:
-            sent, zo_got = after_all([sent, zo_got])
+            sent, token_got, zo_got = after_all([sent, token_got, zo_got])
             zo_half = head_add(zo_half, zo_got)
             for more in bits[2:]:
                 zo_half = head_add(zo_half, trade(zo_half, "head", more))

time: 241 us -> 239 us (level)
  Pallas kernels: 84.9 us -> 78.8 us
  local copies, waits for them, and re-layouts: 16.9 us -> 22.1 us
  waiting for transfers between devices: 63.8 us -> 59.6 us
  starting transfers between devices: 43.9 us -> 47.7 us
    ppermute x5, waiting for transfers between devices: 11.6 us -> 2.24 us  [move_home(): return lax.ppermute(value, ('head', 'shard'), pairs)]
    pallas_call x8, Pallas kernels: 84.9 us -> 78.8 us  [call(): pl.pallas_call(kernel, grid=grid, out_shape=[o for o, _ in outs], in_spec...]
    ppermute x40, waiting for transfers between devices: 51.5 us -> 56.6 us  [trade(): return lax.ppermute(value, axis, [(i, i ^ bit) for i in range(size)])]
    ppermute x40, starting transfers between devices: 19 us -> 22.4 us  [trade(): return lax.ppermute(value, axis, [(i, i ^ bit) for i in range(size)])]
    unnamed x100 -> x72, local copies, waits for them, and re-layouts: 2.99 us -> 5.78 us
    dot_general x3 -> x2, matrix products: 7.9 us -> 6.11 us  [dot_nt(): lax.dot_general(a, b, (((1,), (1,)), ((), ())), preferred_element_type=F32)]
  transfers between devices with their start and end apart: 48 -> 48, of which waited for: 19 -> 18; matrix products, arithmetic and copies ran while one was open for 14% -> 14% of each run, Pallas kernels for 28% -> 26%
where the time goes in v3:
time: 239 us; the launch traced here: 238 us
  Pallas kernels  78.8 us (33%)
  waiting for transfers between devices  59.6 us (25%)
  starting transfers between devices  47.7 us (20%)
  local copies, waits for them, and re-layouts  22.1 us (9%)
  other arithmetic  17.4 us (7%)
  matrix products  10.5 us (4%)
    pallas_call x8, Pallas kernels, call(): pl.pallas_call(kernel, grid=grid, out_shape=[o for o, _ in outs], in_spec...  78.8 us
    ppermute x40, waiting for transfers between devices, trade(): return lax.ppermute(value, axis, [(i, i ^ bit) for i in range(size)])  56.6 us
    ppermute x5, starting transfers between devices, move_home(): return lax.ppermute(value, ('head', 'shard'), pairs)  23.4 us
    ppermute x40, starting transfers between devices, trade(): return lax.ppermute(value, axis, [(i, i ^ bit) for i in range(size)])  22.4 us
    dot_general x2, matrix products, dot_nt(): lax.dot_general(a, b, (((1,), (1,)), ((), ())), preferred_element_type=F32)  6.11 us
    unnamed x72, local copies, waits for them, and re-layouts  5.78 us
  transfers between devices with their start and end apart: 48, of which 18 were waited for; matrix products, arithmetic and copies ran while one was open for 14% of the time, Pallas kernels for 26%

profile of v3, /device:TPU:1, one launch (start us, length us, event | category | flops | bytes accessed | tf_op | source)
XLA Modules:
  0.0 238.4 jit_solution(17088829869463814520)
XLA Ops:
  0.7 1.1 slice.144
  1.8 0.8 copy.33
  2.7 3.1 %collective-permute-start.1 = (bf16[96,1920]{1,0:T(8,128)(2,1)S(1)}, bf16[96,1920]{1,0:T(8,128)(2,1)S(1)}, u32[]{:S(2)}, u32[]{:S(2)}) collective-permute-start(bf16[96,1920]{1,0:T(8,128)(2,1)S(1)} %concatenate.42.refs_1_), channel_id=1, source_target_pairs={{0,6},{1,7},{2,4},{3,5},{4,2},{5,3},{6,0},{7,1},{8,14},{9,15},{10,... | collective-permute-start | bytes 1105928 | tf_op jit(solution)/shard_map/ppermute | solution.py:34
  6.2 1.2 collective-permute-start.4
  8.3 0.9 collective-permute-done
  9.3 4.7 %collective-permute-start.8 = (bf16[512,768]{1,0:T(8,128)(2,1)S(1)}, bf16[512,768]{1,0:T(8,128)(2,1)S(1)}, u32[]{:S(2)}, u32[]{:S(2)}) collective-permute-start(bf16[512,768]{1,0:T(8,128)(2,1)S(1)} %copy-done.14), channel_id=1, source_target_pairs={{1,16},{3,18},{5,20},{7,22},{9,24},{11,26},{13,28},{15,30},{16,1},... | collective-permute-start | bytes 2359304 | tf_op jit(solution)/shard_map/ppermute | solution.py:51
  16.9 1.1 compare_convert_fusion.refs_19_.refs_17_.refs_25_
  18.0 4.8 %collective-permute-done.2.refs_3_ = bf16[96,1920]{1,0:T(8,128)(2,1)} collective-permute-done((bf16[96,1920]{1,0:T(8,128)(2,1)S(1)}, bf16[96,1920]{1,0:T(8,128)(2,1)}, u32[]{:S(2)}, u32[]{:S(2)}) %collective-permute-start.2) | collective-permute-done | bytes 368672 | tf_op jit(solution)/shard_map/ppermute | solution.py:34
  23.6 1.0 compare_convert_fusion.1.refs_26_
  26.1 1.4 pad.17.refs_15_.refs_22_
  28.6 1.2 pad_bitcast_fusion
  29.8 2.2 collective-permute-done.8.refs_14_
  32.2 0.8 collective-permute-start.11
  33.0 1.1 collective-permute-start.9
  34.1 1.0 fusion.27
  35.8 6.3 %collective-permute-start.20 = (bf16[512,768]{1,0:T(8,128)(2,1)S(1)}, bf16[512,768]{1,0:T(8,128)(2,1)S(1)}, u32[]{:S(2)}, u32[]{:S(2)}) collective-permute-start(bf16[512,768]{1,0:T(8,128)(2,1)S(1)} %copy-done.4), channel_id=1, source_target_pairs={{1,16},{3,18},{5,20},{7,22},{9,24},{11,26},{13,28},{15,30},{16,1},... | collective-permute-start | bytes 2359304 | tf_op jit(solution)/shard_map/ppermute | solution.py:51
  42.2 2.2 collective-permute-start.13
  45.0 13.4 %shard_map.212 = (bf16[768,1920]{1,0:T(8,128)(2,1)}, bf16[512,768]{1,0:T(8,128)(2,1)}, bf16[16,768]{1,0:T(8,128)(2,1)}, bf16[528,768]{1,0:T(8,128)(2,1)}, bf16[7...) custom-call(s32[26]{0:T(128)} %pad_add_fusion.2.refs_0_, ...), custom_call_target="tpu_custom_call" | custom-call | flops 1 | bytes 20720000 | tf_op jit(solution)/shard_map/pallas_call | solution.py:234
  58.5 6.6 %shard_map.213.refs_9_ = f32[512,1536]{1,0:T(8,128)} custom-call(bf16[512,128]{1,0:T(8,128)(2,1)} %get-tuple-element.144.bs.refs_16_, bf16[512,128]{1,0:T(8,128)(2,1)} %get-tuple-element.145.cs.refs_10_, bf16[512,1536]{1,0:T(8,128)(2,1)} %get-tuple-element.146.xt.refs_15_, f32[512,128]{1,0:T(8,128)} %get-tuple-element.147.cum.refs_11_.refs_18_, ...), custom_call_target="tpu_custom_call" | custom-call | flops 1 | bytes 8880000 | tf_op jit(solution)/shard_map/pallas_call | solution.py:234
  65.0 2.1 collective-permute-done.14.refs_2_
  68.3 1.0 collective-permute-done.17.refs_5_
  70.1 0.8 collective-permute-done.19.refs_7_
  71.0 0.8 collective-permute-done.16.refs_4_
  71.8 5.0 %shard_map.214 = (bf16[512,1536]{1,0:T(8,128)(2,1)S(1)}, bf16[512,1536]{1,0:T(8,128)(2,1)}, bf16[512,768]{1,0:T(8,128)(2,1)S(1)}, bf16[768,1536]{1,0:T(8,128)(2,1)}, bf16[1536,768]{1,0:T(8,128)(2,1)}) custom-call(s32[1]{0:T(128)} %bitcast.at, bf16[96,3072]{1,0:T(8,128)(2,1)S(1)} %pad_maximum_fusion.1.refs_0_, ...), custom_call_target="tpu_custom_call" | custom-call | flops 1 | bytes 1480000 | tf_op jit(solution)/shard_map/pallas_call | solution.py:234
  76.8 0.9 copy-done
  77.7 1.1 copy-done.2
  79.0 2.2 collective-permute-done.22.refs_4_.refs_8_
  81.3 0.9 copy-done.8
  82.2 14.4 %shard_map.215 = (bf16[2,128,1536]{2,1,0:T(8,128)(2,1)}, bf16[512,1536]{1,0:T(8,128)(2,1)}, f32[1,1536]{1,0:T(1,128)}, bf16[512,1536]{1,0:T(8,128)(2,1)}, bf16[5...) custom-call(s32[26]{0:T(128)} %pad_add_fusion.2.refs_0_, ...), custom_call_target="tpu_custom_call" | custom-call | flops 1 | bytes 23680000 | tf_op jit(solution)/shard_map/pallas_call | solution.py:234
  96.6 1.3 collective-permute-start.23
  97.8 7.7 %shard_map.216 = (bf16[4,96,3072]{2,1,0:T(8,128)(2,1)}, bf16[96,3072]{1,0:T(8,128)(2,1)}, bf16[96,3072]{1,0:T(8,128)(2,1)}, bf16[96,3072]{1,0:T(8,128)(2,1)}, bf16[96,3072]{1,0:T(8,128)(2,1)}) custom-call(s32[1]{0:T(128)} %bitcast.at, bf16[768,512]{1,0:T(8,128)(2,1)} %get-tuple-element.164.normal_t, bf16[512,1536]{1,0:T(8,128)(2,1)} %get-tuple-element.209.dz, ...), custom_call_target="tpu_custom_call" | custom-call | flops 1 | bytes 1480000 | tf_op jit(solution)/shard_map/pallas_call | solution.py:234
  106.6 11.5 %shard_map.217 = (f32[512,1536]{1,0:T(8,128)}, f32[512,128]{1,0:T(8,128)}, f32[512,128]{1,0:T(8,128)}, bf16[512,768]{1,0:T(8,128)(2,1)}) custom-call(bf16[512,128]{1,0:T(8,128)(2,1)} %get-tuple-element.144.bs.refs_16_, bf16[512,128]{1,0:T(8,128)(2,1)} %get-tuple-element.145.cs.refs_10_, bf16[512,1536]{1,0:T(8,128)(2,1)} %get-tuple-element.146.xt.refs_15_, ...), custom_call_target="tpu_custom_call" | custom-call | flops 1 | bytes 1480000 | tf_op jit(solution)/shard_map/pallas_call | solution.py:234
  118.2 2.2 add_convert_fusion
  120.4 1.3 dynamic-slice_bitcast_fusion.2
  122.3 1.7 collective-permute-done.28.refs_4_
  124.0 0.9 copy-done.19
  124.9 3.2 %collective-permute-start.29 = (bf16[512,768]{1,0:T(8,128)(2,1)}, bf16[512,768]{1,0:T(8,128)(2,1)S(1)}, u32[]{:S(2)}, u32[]{:S(2)}) collective-permute-start(bf16[512,768]{1,0:T(8,128)(2,1)} %get-tuple-element.187), channel_id=1, source_target_pairs={{1,16},{3,18},{5,20},{7,22},{9,24},{11,26},{13,28},{15,30},{16,1},... | collective-permute-start | bytes 2359304 | tf_op jit(solution)/shard_map/ppermute | solution.py:51
  128.5 1.3 collective-permute-start.33
  129.7 1.2 collective-permute-start.34
  131.2 17.1 %shard_map.218 = (bf16[528,1920]{1,0:T(8,128)(2,1)}, f32[96,128]{1,0:T(8,128)}) custom-call(s32[26]{0:T(128)} %pad_add_fusion.2.refs_0_, bf16[2,128,1536]{2,1,0:T(8,128)(2,1)} %get-tuple-element.178.refs_1_, bf16[2,128,1536]{2,1,0:T(8,128)(2,1)} %copy-done.18, bf16[2,128,1536]{2,1,0:T(8,128)(2,1)} %collective-permute-done.30.refs_3_, ...), custom_call_target="tpu_custom_call" | custom-call | flops 1 | bytes 2960000 | tf_op jit(solution)/shard_map/pallas_call | solution.py:234
  148.3 4.4 %convolution_convert_fusion = bf16[768,1920]{1,0:T(8,128)(2,1)S(1)} fusion(bf16[528,768]{1,0:T(8,128)(2,1)S(1)} %copy-done.3, bf16[528,1920]{1,0:T(8,128)(2,1)} %get-tuple-element.206), kind=kOutput, calls=%fused_computation.1 | convolution fusion | flops 1558609920 | bytes 5787648 | tf_op jit(solution)/shard_map/dot_general | solution.py:181
  152.8 1.8 dynamic-slice_bitcast_fusion
  154.6 1.8 collective-permute-done.34
  158.0 1.9 fusion.29
  160.3 0.8 copy-done.31
  162.0 4.2 %fusion.2 = (f32[512]{0:T(512)S(1)}, f32[512,768]{1,0:T(8,128)S(1)}) fusion(bf16[512,768]{1,0:T(8,128)(2,1)S(1)} %copy-done.9, f32[512]{0:T(512)S(1)} %add_rsqrt_fusion, f32[768]{0:T(1024)S(1)} %convert_reduce_fusion, f32[528,768]{1,0:T(8,128)} %copy-done.31, bf16[512,1536]{1,0:T(8,128)(2,1)} %get-tuple-element.209.dz, bf16[768,1536]{1,0:T(8,128)(2,1)} %get-tuple-element.210), kind=kOutput, calls=%fused_computation.6 | convolution fusion | flops 1210318336 | bytes 7871488 | tf_op jit(solution)/shard_map/dot_general | solution.py:177
  167.3 3.1 %shard_map.219 = (bf16[96,2176]{1,0:T(8,128)(2,1)}, bf16[96,2176]{1,0:T(8,128)(2,1)}, bf16[96,2176]{1,0:T(8,128)(2,1)}, bf16[96,2176]{1,0:T(8,128)(2,1)}) custom-call(s32[1]{0:T(128)} %bitcast.at, bf16[4,96,1920]{2,1,0:T(8,128)(2,1)} %get-tuple-element.238.keep, bf16[4,96,1920]{2,1,0:T(8,128)(2,1)} %collective-permute-done.31.got, ...), custom_call_target="tpu_custom_call" | custom-call | flops 1 | bytes 1480000 | tf_op jit(solution)/shard_map/pallas_call | solution.py:234
  170.8 1.1 collective-permute-start.39
  171.9 1.2 collective-permute-start.40
  173.2 1.0 collective-permute-start.41
  174.5 4.7 %collective-permute-start.43 = (bf16[512,768]{1,0:T(8,128)(2,1)S(1)}, bf16[512,768]{1,0:T(8,128)(2,1)}, u32[]{:S(2)}, u32[]{:S(2)}) collective-permute-start(bf16[512,768]{1,0:T(8,128)(2,1)S(1)} %fusion.6), channel_id=1, source_target_pairs={{1,16},{3,18},{5,20},{7,22},{9,24},{11,26},{13,28},{15,30},{16,1},... | collective-permute-start | bytes 2359304 | tf_op jit(solution)/shard_map/ppermute | solution.py:51
  179.1 17.7 %collective-permute-done.41 = bf16[96,1536]{1,0:T(8,128)(2,1)S(1)} collective-permute-done((bf16[96,1536]{1,0:T(8,128)(2,1)S(1)}, bf16[96,1536]{1,0:T(8,128)(2,1)S(1)}, u32[]{:S(2)}, u32[]{:S(2)}) %collective-permute-start.41) | collective-permute-done | bytes 294944 | tf_op jit(solution)/shard_map/ppermute | solution.py:34
  196.9 1.2 add_convert_fusion.2
  198.2 0.8 fusion.17
  199.2 1.0 broadcast_select_fusion.1
  200.2 11.9 %collective-permute-done.42 = bf16[96,1344]{1,0:T(8,128)(2,1)S(1)} collective-permute-done((bf16[96,1344]{1,0:T(8,128)(2,1)S(1)}, bf16[96,1344]{1,0:T(8,128)(2,1)S(1)}, u32[]{:S(2)}, u32[]{:S(2)}) %collective-permute-start.42) | collective-permute-done | bytes 258080 | tf_op jit(solution)/shard_map/ppermute | solution.py:34
  212.6 1.8 collective-permute-start.44
  214.5 1.2 broadcast_select_fusion
  215.7 8.1 %collective-permute-done.44 = bf16[96,1216]{1,0:T(8,128)(2,1)S(1)} collective-permute-done((bf16[96,1216]{1,0:T(8,128)(2,1)S(1)}, bf16[96,1216]{1,0:T(8,128)(2,1)S(1)}, u32[]{:S(2)}, u32[]{:S(2)}) %collective-permute-start.44) | collective-permute-done | bytes 233504 | tf_op jit(solution)/shard_map/ppermute | solution.py:34
  223.8 1.8 collective-permute-done.45
  227.7 0.8 collective-permute-start.47
  228.5 4.5 %collective-permute-start.46 = (bf16[96,256]{1,0:T(8,128)(2,1)S(1)}, bf16[96,256]{1,0:T(8,128)(2,1)S(1)}, u32[]{:S(2)}, u32[]{:S(2)}) collective-permute-start(bf16[96,256]{1,0:T(8,128)(2,1)S(1)} %pad_maximum_fusion.4), channel_id=1, source_target_pairs={{1,16},{3,18},{5,20},{7,22},{9,24},{11,26},{13,28},{15,30},{16,1},... | collective-permute-start | bytes 147464 | tf_op jit(solution)/shard_map/ppermute | solution.py:51
  233.0 0.9 pad_maximum_fusion.2
  236.5 1.3 multiply_reduce_fusion
  (212 shorter events, 23.6 us)
Async XLA Ops:
  0.7 8.6 %copy-start.14 = (bf16[512,768]{1,0:T(8,128)(2,1)S(1)}, bf16[512,768]{1,0:T(8,128)(2,1)}, u32[]{:S(2)}) copy-start(bf16[512,768]{1,0:T(8,128)(2,1)} %refs_13_.1) | copy-start | bytes 2359300
  1.8 25.7 %copy-start.30 = (f32[1792]{0:T(1024)S(1)}, f32[1792]{0:T(1024)}, u32[]{:S(2)}) copy-start(f32[1792]{0:T(1024)} %param.19) | copy-start | bytes 21508
  1.8 26.3 %copy-start.29 = (f32[1536]{0:T(1024)S(1)}, f32[1536]{0:T(1024)}, u32[]{:S(2)}) copy-start(f32[1536]{0:T(1024)} %param.23) | copy-start | bytes 18436
  2.7 39.5 %copy-start.13 = (bf16[96,1920]{1,0:T(8,128)(2,1)}, bf16[96,1920]{1,0:T(8,128)(2,1)S(1)}, u32[]{:S(2)}) copy-start(bf16[96,1920]{1,0:T(8,128)(2,1)S(1)} %concatenate.42.refs_1_) | copy-start | bytes 1105924
  2.7 33.1 %copy-start.4 = (bf16[512,768]{1,0:T(8,128)(2,1)S(1)}, bf16[512,768]{1,0:T(8,128)(2,1)}, u32[]{:S(2)}) copy-start(bf16[512,768]{1,0:T(8,128)(2,1)} %refs_9_.1) | copy-start | bytes 2359300
  2.7 39.4 %slice-start.1 = ((bf16[96,3352]{1,0:T(8,128)(2,1)}), bf16[96,1536]{1,0:T(8,128)(2,1)S(1)}, s32[]{:S(2)}) async-start(bf16[96,3352]{1,0:T(8,128)(2,1)} %param.17), calls=%async_computation.1 | async-start | bytes 589824 | tf_op jit(solution)/shard_map/slice | solution.py:1135
  2.7 14.2 %collective-permute-start.1 = (bf16[96,1920]{1,0:T(8,128)(2,1)S(1)}, bf16[96,1920]{1,0:T(8,128)(2,1)S(1)}, u32[]{:S(2)}, u32[]{:S(2)}) collective-permute-start(bf16[96,1920]{1,0:T(8,128)(2,1)S(1)} %concatenate.42.refs_1_), channel_id=1, source_target_pairs={{0,6},{1,7},{2,4},{3,5},{4,2},{5,3},{6,0},{7,1},{8,14},{9,15},{10,... | collective-permute-start | bytes 1105928 | tf_op jit(solution)/shard_map/ppermute | solution.py:34
  5.8 17.1 %collective-permute-start.2 = (bf16[96,1920]{1,0:T(8,128)(2,1)S(1)}, bf16[96,1920]{1,0:T(8,128)(2,1)}, u32[]{:S(2)}, u32[]{:S(2)}) collective-permute-start(bf16[96,1920]{1,0:T(8,128)(2,1)S(1)} %concatenate.42.refs_1_), channel_id=1, source_target_pairs={{0,4},{1,5},{2,6},{3,7},{4,0},{5,1},{6,2},{7,3},{8,12},{9,13},{10,... | collective-permute-start | bytes 1105928 | tf_op jit(solution)/shard_map/ppermute | solution.py:34
  6.0 17.3 %collective-permute-start.3 = (bf16[96,1920]{1,0:T(8,128)(2,1)S(1)}, bf16[96,1920]{1,0:T(8,128)(2,1)}, u32[]{:S(2)}, u32[]{:S(2)}) collective-permute-start(bf16[96,1920]{1,0:T(8,128)(2,1)S(1)} %concatenate.42.refs_1_), channel_id=1, source_target_pairs={{0,2},{1,3},{2,0},{3,1},{4,6},{5,7},{6,4},{7,5},{8,10},{9,11},{10,... | collective-permute-start | bytes 1105928 | tf_op jit(solution)/shard_map/ppermute | solution.py:34
  6.2 25.9 %collective-permute-start.4 = (bf16[96,1920]{1,0:T(8,128)(2,1)S(1)}, bf16[96,1920]{1,0:T(8,128)(2,1)}, u32[]{:S(2)}, u32[]{:S(2)}) collective-permute-start(bf16[96,1920]{1,0:T(8,128)(2,1)S(1)} %concatenate.42.refs_1_), channel_id=1, source_target_pairs={{0,1},{1,0},{2,3},{3,2},{4,5},{5,4},{6,7},{7,6},{8,9},{9,8},{10,11... | collective-permute-start | bytes 1105928 | tf_op jit(solution)/shard_map/ppermute | solution.py:34
  8.1 1.1 collective-permute-start
  9.3 22.8 %collective-permute-start.8 = (bf16[512,768]{1,0:T(8,128)(2,1)S(1)}, bf16[512,768]{1,0:T(8,128)(2,1)S(1)}, u32[]{:S(2)}, u32[]{:S(2)}) collective-permute-start(bf16[512,768]{1,0:T(8,128)(2,1)S(1)} %copy-done.14), channel_id=1, source_target_pairs={{1,16},{3,18},{5,20},{7,22},{9,24},{11,26},{13,28},{15,30},{16,1},... | collective-permute-start | bytes 2359304 | tf_op jit(solution)/shard_map/ppermute | solution.py:51
  16.9 25.3 %copy-start.20 = (bf16[96,1920]{1,0:T(8,128)(2,1)}, bf16[96,1920]{1,0:T(8,128)(2,1)S(1)}, u32[]{:S(2)}) copy-start(bf16[96,1920]{1,0:T(8,128)(2,1)S(1)} %collective-permute-done.1.refs_2_) | copy-start | bytes 1105924
  18.0 14.1 %collective-permute-start.5 = (bf16[96,1920]{1,0:T(8,128)(2,1)S(1)}, bf16[96,1920]{1,0:T(8,128)(2,1)}, u32[]{:S(2)}, u32[]{:S(2)}) collective-permute-start(bf16[96,1920]{1,0:T(8,128)(2,1)S(1)} %collective-permute-done.1.refs_2_), channel_id=1, source_target_pairs={{0,1},{1,0},{2,3},{3,2},{4,5},{5,4},{6,7},{7,6},{8,9},{9,8},{10,11... | collective-permute-start | bytes 1105928 | tf_op jit(solution)/shard_map/ppermute | solution.py:34
  22.8 9.3 %collective-permute-start.6 = (bf16[96,1920]{1,0:T(8,128)(2,1)}, bf16[96,1920]{1,0:T(8,128)(2,1)}, u32[]{:S(2)}, u32[]{:S(2)}) collective-permute-start(bf16[96,1920]{1,0:T(8,128)(2,1)} %collective-permute-done.2.refs_3_), channel_id=1, source_target_pairs={{0,1},{1,0},{2,3},{3,2},{4,5},{5,4},{6,7},{7,6},{8,9},{9,8},{10,11... | collective-permute-start | bytes 1105928 | tf_op jit(solution)/shard_map/ppermute | solution.py:34
  23.3 8.8 %collective-permute-start.7 = (bf16[96,1920]{1,0:T(8,128)(2,1)}, bf16[96,1920]{1,0:T(8,128)(2,1)}, u32[]{:S(2)}, u32[]{:S(2)}) collective-permute-start(bf16[96,1920]{1,0:T(8,128)(2,1)} %collective-permute-done.3.refs_4_), channel_id=1, source_target_pairs={{0,1},{1,0},{2,3},{3,2},{4,5},{5,4},{6,7},{7,6},{8,9},{9,8},{10,11... | collective-permute-start | bytes 1105928 | tf_op jit(solution)/shard_map/ppermute | solution.py:34
  32.0 12.9 %copy-start.15 = (bf16[512,768]{1,0:T(8,128)(2,1)}, bf16[512,768]{1,0:T(8,128)(2,1)S(1)}, u32[]{:S(2)}) copy-start(bf16[512,768]{1,0:T(8,128)(2,1)S(1)} %collective-permute-done.8.refs_14_) | copy-start | bytes 2359300
  32.1 12.9 %copy-start.22 = (bf16[16,768]{1,0:T(8,128)(2,1)}, bf16[16,768]{1,0:T(8,128)(2,1)S(1)}, u32[]{:S(2)}) copy-start(bf16[16,768]{1,0:T(8,128)(2,1)S(1)} %fusion.20.refs_9_) | copy-start | bytes 73732
  32.1 2.9 %collective-permute-start.10 = (bf16[16,768]{1,0:T(8,128)(2,1)S(1)}, bf16[16,768]{1,0:T(8,128)(2,1)S(1)}, u32[]{:S(2)}, u32[]{:S(2)}) collective-permute-start(bf16[16,768]{1,0:T(8,128)(2,1)S(1)} %fusion.20.refs_9_), channel_id=1, source_target_pairs={{0,1},{1,0},{2,3},{3,2},{4,5},{5,4},{6,7},{7,6},{8,9},{9,8},{10,11... | collective-permute-start | bytes 73736 | tf_op jit(solution)/shard_map/ppermute | solution.py:69
  32.2 3.4 %collective-permute-start.11 = (bf16[16,768]{1,0:T(8,128)(2,1)S(1)}, bf16[16,768]{1,0:T(8,128)(2,1)S(1)}, u32[]{:S(2)}, u32[]{:S(2)}) collective-permute-start(bf16[16,768]{1,0:T(8,128)(2,1)S(1)} %fusion.20.refs_9_), channel_id=1, source_target_pairs={{0,9},{1,8},{2,11},{3,10},{4,13},{5,12},{6,15},{7,14},{8,1},{9,0},... | collective-permute-start | bytes 73736 | tf_op jit(solution)/shard_map/ppermute | solution.py:69
  33.0 2.8 %collective-permute-start.9 = (bf16[16,768]{1,0:T(8,128)(2,1)S(1)}, bf16[16,768]{1,0:T(8,128)(2,1)S(1)}, u32[]{:S(2)}, u32[]{:S(2)}) collective-permute-start(bf16[16,768]{1,0:T(8,128)(2,1)S(1)} %fusion.20.refs_9_), channel_id=1, source_target_pairs={{0,8},{1,9},{2,10},{3,11},{4,12},{5,13},{6,14},{7,15},{8,0},{9,1},... | collective-permute-start | bytes 73736 | tf_op jit(solution)/shard_map/ppermute | solution.py:69
  35.1 9.9 %copy-start.25 = (bf16[16,768]{1,0:T(8,128)(2,1)}, bf16[16,768]{1,0:T(8,128)(2,1)S(1)}, u32[]{:S(2)}) copy-start(bf16[16,768]{1,0:T(8,128)(2,1)S(1)} %collective-permute-done.10.refs_11_) | copy-start | bytes 73732
  35.6 9.4 %copy-start.26 = (bf16[16,768]{1,0:T(8,128)(2,1)}, bf16[16,768]{1,0:T(8,128)(2,1)S(1)}, u32[]{:S(2)}) copy-start(bf16[16,768]{1,0:T(8,128)(2,1)S(1)} %collective-permute-done.11.refs_12_) | copy-start | bytes 73732
  35.8 9.2 %copy-start.27 = (bf16[16,768]{1,0:T(8,128)(2,1)}, bf16[16,768]{1,0:T(8,128)(2,1)S(1)}, u32[]{:S(2)}) copy-start(bf16[16,768]{1,0:T(8,128)(2,1)S(1)} %collective-permute-done.9.refs_10_) | copy-start | bytes 73732
  35.8 32.1 %collective-permute-start.20 = (bf16[512,768]{1,0:T(8,128)(2,1)S(1)}, bf16[512,768]{1,0:T(8,128)(2,1)S(1)}, u32[]{:S(2)}, u32[]{:S(2)}) collective-permute-start(bf16[512,768]{1,0:T(8,128)(2,1)S(1)} %copy-done.4), channel_id=1, source_target_pairs={{1,16},{3,18},{5,20},{7,22},{9,24},{11,26},{13,28},{15,30},{16,1},... | collective-permute-start | bytes 2359304 | tf_op jit(solution)/shard_map/ppermute | solution.py:51
  42.2 22.8 %collective-permute-start.13 = (bf16[96,3072]{1,0:T(8,128)(2,1)S(1)}, bf16[96,3072]{1,0:T(8,128)(2,1)S(1)}, u32[]{:S(2)}, u32[]{:S(2)}) collective-permute-start(bf16[96,3072]{1,0:T(8,128)(2,1)S(1)} %pad_maximum_fusion.1.refs_0_), channel_id=1, source_target_pairs={{0,6},{1,7},{2,4},{3,5},{4,2},{5,3},{6,0},{7,1},{8,14},{9,15},{10,... | collective-permute-start | bytes 1769480 | tf_op jit(solution)/shard_map/ppermute | solution.py:34
  44.5 22.7 %collective-permute-start.14 = (bf16[96,3072]{1,0:T(8,128)(2,1)S(1)}, bf16[96,3072]{1,0:T(8,128)(2,1)S(1)}, u32[]{:S(2)}, u32[]{:S(2)}) collective-permute-start(bf16[96,3072]{1,0:T(8,128)(2,1)S(1)} %pad_maximum_fusion.1.refs_0_), channel_id=1, source_target_pairs={{0,4},{1,5},{2,6},{3,7},{4,0},{5,1},{6,2},{7,3},{8,12},{9,13},{10,... | collective-permute-start | bytes 1769480 | tf_op jit(solution)/shard_map/ppermute | solution.py:34
  44.7 22.6 %collective-permute-start.15 = (bf16[96,3072]{1,0:T(8,128)(2,1)S(1)}, bf16[96,3072]{1,0:T(8,128)(2,1)S(1)}, u32[]{:S(2)}, u32[]{:S(2)}) collective-permute-start(bf16[96,3072]{1,0:T(8,128)(2,1)S(1)} %pad_maximum_fusion.1.refs_0_), channel_id=1, source_target_pairs={{0,2},{1,3},{2,0},{3,1},{4,6},{5,7},{6,4},{7,5},{8,10},{9,11},{10,... | collective-permute-start | bytes 1769480 | tf_op jit(solution)/shard_map/ppermute | solution.py:34
  58.4 20.5 %collective-permute-start.12 = (bf16[2,128,1664]{2,1,0:T(8,128)(2,1)}, bf16[2,128,1664]{2,1,0:T(8,128)(2,1)S(1)}, u32[]{:S(2)}, u32[]{:S(2)}) collective-permute-start(bf16[2,128,1664]{2,1,0:T(8,128)(2,1)} %get-tuple-element.149.refs_1_.refs_5_), channel_id=1, source_target_pairs={{0,8},{8,0},{16,24},{24,16},{1,9},{9,1},{17,25},{25,17},{2,10},{10... | collective-permute-start | bytes 2555912 | tf_op jit(solution)/shard_map/ppermute | solution.py:34
  58.5 10.8 %copy-start.5 = (bf16[2,128,1664]{2,1,0:T(8,128)(2,1)S(1)}, bf16[2,128,1664]{2,1,0:T(8,128)(2,1)}, u32[]{:S(2)}) copy-start(bf16[2,128,1664]{2,1,0:T(8,128)(2,1)} %get-tuple-element.149.refs_1_.refs_5_) | copy-start | bytes 2555908
  58.5 13.3 %copy-start.3 = (bf16[528,768]{1,0:T(8,128)(2,1)S(1)}, bf16[528,768]{1,0:T(8,128)(2,1)}, u32[]{:S(2)}) copy-start(bf16[528,768]{1,0:T(8,128)(2,1)} %get-tuple-element.156.refs_8_) | copy-start | bytes 2433028
  67.3 2.0 collective-permute-start.17
  67.4 2.7 %collective-permute-start.18 = (bf16[96,3072]{1,0:T(8,128)(2,1)S(1)}, bf16[96,3072]{1,0:T(8,128)(2,1)S(1)}, u32[]{:S(2)}, u32[]{:S(2)}) collective-permute-start(bf16[96,3072]{1,0:T(8,128)(2,1)S(1)} %collective-permute-done.14.refs_2_), channel_id=1, source_target_pairs={{0,1},{1,0},{2,3},{3,2},{4,5},{5,4},{6,7},{7,6},{8,9},{9,8},{10,11... | collective-permute-start | bytes 1769480 | tf_op jit(solution)/shard_map/ppermute | solution.py:34
  67.8 3.2 %collective-permute-start.19 = (bf16[96,3072]{1,0:T(8,128)(2,1)S(1)}, bf16[96,3072]{1,0:T(8,128)(2,1)S(1)}, u32[]{:S(2)}, u32[]{:S(2)}) collective-permute-start(bf16[96,3072]{1,0:T(8,128)(2,1)S(1)} %collective-permute-done.15.refs_3_), channel_id=1, source_target_pairs={{0,1},{1,0},{2,3},{3,2},{4,5},{5,4},{6,7},{7,6},{8,9},{9,8},{10,11... | collective-permute-start | bytes 1769480 | tf_op jit(solution)/shard_map/ppermute | solution.py:34
  67.9 3.9 %collective-permute-start.16 = (bf16[96,3072]{1,0:T(8,128)(2,1)S(1)}, bf16[96,3072]{1,0:T(8,128)(2,1)S(1)}, u32[]{:S(2)}, u32[]{:S(2)}) collective-permute-start(bf16[96,3072]{1,0:T(8,128)(2,1)S(1)} %pad_maximum_fusion.1.refs_0_), channel_id=1, source_target_pairs={{0,1},{1,0},{2,3},{3,2},{4,5},{5,4},{6,7},{7,6},{8,9},{9,8},{10,11... | collective-permute-start | bytes 1769480 | tf_op jit(solution)/shard_map/ppermute | solution.py:34
  69.3 9.8 %collective-permute-start.21 = (bf16[2,128,1664]{2,1,0:T(8,128)(2,1)S(1)}, bf16[2,128,1664]{2,1,0:T(8,128)(2,1)S(1)}, u32[]{:S(2)}, u32[]{:S(2)}) collective-permute-start(bf16[2,128,1664]{2,1,0:T(8,128)(2,1)S(1)} %copy-done.5), channel_id=1, source_target_pairs={{0,1},{1,0},{2,3},{3,2},{4,5},{5,4},{6,7},{7,6},{8,9},{9,8},{10,11... | collective-permute-start | bytes 2555912 | tf_op jit(solution)/shard_map/ppermute | solution.py:34
  78.9 2.4 collective-permute-start.22
  96.6 21.6 %collective-permute-start.23 = (bf16[2,128,1536]{2,1,0:T(8,128)(2,1)}, bf16[2,128,1536]{2,1,0:T(8,128)(2,1)S(1)}, u32[]{:S(2)}, u32[]{:S(2)}) collective-permute-start(bf16[2,128,1536]{2,1,0:T(8,128)(2,1)} %get-tuple-element.178.refs_1_), channel_id=1, source_target_pairs={{0,8},{8,0},{16,24},{24,16},{1,9},{9,1},{17,25},{25,17},{2,10},{10... | collective-permute-start | bytes 2359304 | tf_op jit(solution)/shard_map/ppermute | solution.py:34
  105.5 12.6 %collective-permute-start.24 = (bf16[96,3072]{1,0:T(8,128)(2,1)}, bf16[96,3072]{1,0:T(8,128)(2,1)S(1)}, u32[]{:S(2)}, u32[]{:S(2)}) collective-permute-start(bf16[96,3072]{1,0:T(8,128)(2,1)} %get-tuple-element.168), channel_id=1, source_target_pairs={{0,1},{1,0},{2,3},{3,2},{4,5},{5,4},{6,7},{7,6},{8,9},{9,8},{10,11... | collective-permute-start | bytes 1769480 | tf_op jit(solution)/shard_map/ppermute | solution.py:34
  106.0 12.1 %collective-permute-start.25 = (bf16[96,3072]{1,0:T(8,128)(2,1)}, bf16[96,3072]{1,0:T(8,128)(2,1)S(1)}, u32[]{:S(2)}, u32[]{:S(2)}) collective-permute-start(bf16[96,3072]{1,0:T(8,128)(2,1)} %get-tuple-element.169), channel_id=1, source_target_pairs={{0,1},{1,0},{2,3},{3,2},{4,5},{5,4},{6,7},{7,6},{8,9},{9,8},{10,11... | collective-permute-start | bytes 1769480 | tf_op jit(solution)/shard_map/ppermute | solution.py:34
  106.0 12.1 %collective-permute-start.26 = (bf16[96,3072]{1,0:T(8,128)(2,1)}, bf16[96,3072]{1,0:T(8,128)(2,1)}, u32[]{:S(2)}, u32[]{:S(2)}) collective-permute-start(bf16[96,3072]{1,0:T(8,128)(2,1)} %get-tuple-element.170), channel_id=1, source_target_pairs={{0,1},{1,0},{2,3},{3,2},{4,5},{5,4},{6,7},{7,6},{8,9},{9,8},{10,11... | collective-permute-start | bytes 1769480 | tf_op jit(solution)/shard_map/ppermute | solution.py:34
  106.5 11.6 %collective-permute-start.27 = (bf16[96,3072]{1,0:T(8,128)(2,1)}, bf16[96,3072]{1,0:T(8,128)(2,1)}, u32[]{:S(2)}, u32[]{:S(2)}) collective-permute-start(bf16[96,3072]{1,0:T(8,128)(2,1)} %get-tuple-element.171), channel_id=1, source_target_pairs={{0,1},{1,0},{2,3},{3,2},{4,5},{5,4},{6,7},{7,6},{8,9},{9,8},{10,11... | collective-permute-start | bytes 1769480 | tf_op jit(solution)/shard_map/ppermute | solution.py:34
  106.6 11.6 %copy-start.12 = (bf16[4,96,3072]{2,1,0:T(8,128)(2,1)S(1)}, bf16[4,96,3072]{2,1,0:T(8,128)(2,1)}, u32[]{:S(2)}) copy-start(bf16[4,96,3072]{2,1,0:T(8,128)(2,1)} %get-tuple-element.181) | copy-start | bytes 7077892
  120.4 7.9 %copy-start.33 = (s32[1,8]{1,0:T(1,128)S(1)}, s32[1,8]{1,0:T(1,128)}, u32[]{:S(2)}) copy-start(s32[1,8]{1,0:T(1,128)} %param.25) | copy-start | bytes 100
  121.7 2.3 collective-permute-start.28
  122.1 9.1 %collective-permute-start.30 = (bf16[2,128,1536]{2,1,0:T(8,128)(2,1)S(1)}, bf16[2,128,1536]{2,1,0:T(8,128)(2,1)}, u32[]{:S(2)}, u32[]{:S(2)}) collective-permute-start(bf16[2,128,1536]{2,1,0:T(8,128)(2,1)S(1)} %copy-done.17), channel_id=1, source_target_pairs={{0,1},{1,0},{2,3},{3,2},{4,5},{5,4},{6,7},{7,6},{8,9},{9,8},{10,11... | collective-permute-start | bytes 2359304 | tf_op jit(solution)/shard_map/ppermute | solution.py:34
  124.9 23.4 %collective-permute-start.29 = (bf16[512,768]{1,0:T(8,128)(2,1)}, bf16[512,768]{1,0:T(8,128)(2,1)S(1)}, u32[]{:S(2)}, u32[]{:S(2)}) collective-permute-start(bf16[512,768]{1,0:T(8,128)(2,1)} %get-tuple-element.187), channel_id=1, source_target_pairs={{1,16},{3,18},{5,20},{7,22},{9,24},{11,26},{13,28},{15,30},{16,1},... | collective-permute-start | bytes 2359304 | tf_op jit(solution)/shard_map/ppermute | solution.py:51
  128.5 26.1 %collective-permute-start.33 = (bf16[96,3072]{1,0:T(8,128)(2,1)}, bf16[96,3072]{1,0:T(8,128)(2,1)S(1)}, u32[]{:S(2)}, u32[]{:S(2)}) collective-permute-start(bf16[96,3072]{1,0:T(8,128)(2,1)} %get-tuple-element.241), channel_id=1, source_target_pairs={{0,2},{1,3},{2,0},{3,1},{4,6},{5,7},{6,4},{7,5},{8,10},{9,11},{10,... | collective-permute-start | bytes 1769480 | tf_op jit(solution)/shard_map/ppermute | solution.py:34
  129.7 26.6 %collective-permute-start.34 = (bf16[96,3072]{1,0:T(8,128)(2,1)}, bf16[96,3072]{1,0:T(8,128)(2,1)S(1)}, u32[]{:S(2)}, u32[]{:S(2)}) collective-permute-start(bf16[96,3072]{1,0:T(8,128)(2,1)} %get-tuple-element.240), channel_id=1, source_target_pairs={{0,4},{1,5},{2,6},{3,7},{4,0},{5,1},{6,2},{7,3},{8,12},{9,13},{10,... | collective-permute-start | bytes 1769480 | tf_op jit(solution)/shard_map/ppermute | solution.py:34
  130.9 25.4 %collective-permute-start.35 = (bf16[96,3072]{1,0:T(8,128)(2,1)}, bf16[96,3072]{1,0:T(8,128)(2,1)S(1)}, u32[]{:S(2)}, u32[]{:S(2)}) collective-permute-start(bf16[96,3072]{1,0:T(8,128)(2,1)} %get-tuple-element.239), channel_id=1, source_target_pairs={{0,6},{1,7},{2,4},{3,5},{4,2},{5,3},{6,0},{7,1},{8,14},{9,15},{10,... | collective-permute-start | bytes 1769480 | tf_op jit(solution)/shard_map/ppermute | solution.py:34
  154.6 12.2 %collective-permute-start.31 = (bf16[4,96,1920]{2,1,0:T(8,128)(2,1)}, bf16[4,96,1920]{2,1,0:T(8,128)(2,1)}, u32[]{:S(2)}, u32[]{:S(2)}) collective-permute-start(bf16[4,96,1920]{2,1,0:T(8,128)(2,1)} %get-tuple-element.237), channel_id=1, source_target_pairs={{0,1},{1,0},{2,3},{3,2},{4,5},{5,4},{6,7},{7,6},{8,9},{9,8},{10,11... | collective-permute-start | bytes 4423688 | tf_op jit(solution)/shard_map/ppermute | solution.py:34
  157.4 9.3 %collective-permute-start.37 = (bf16[96,1536]{1,0:T(8,128)(2,1)}, bf16[96,1536]{1,0:T(8,128)(2,1)S(1)}, u32[]{:S(2)}, u32[]{:S(2)}) collective-permute-start(bf16[96,1536]{1,0:T(8,128)(2,1)} %constant_dynamic-slice_fusion.1), channel_id=1, source_target_pairs={{0,8},{8,0},{16,24},{24,16},{1,9},{9,1},{17,25},{25,17},{2,10},{10... | collective-permute-start | bytes 884744 | tf_op jit(solution)/shard_map/ppermute | solution.py:34
  161.2 5.6 %collective-permute-start.36 = (bf16[96,64]{1,0:T(8,128)(2,1)S(1)}, bf16[96,64]{1,0:T(8,128)(2,1)S(1)}, u32[]{:S(2)}, u32[]{:S(2)}) collective-permute-start(bf16[96,64]{1,0:T(8,128)(2,1)S(1)} %reshape.310), channel_id=1, source_target_pairs={{0,1},{1,0},{2,3},{3,2},{4,5},{5,4},{6,7},{7,6},{8,9},{9,8},{10,11... | collective-permute-start | bytes 36872 | tf_op jit(solution)/shard_map/ppermute | solution.py:34
  161.3 5.5 %collective-permute-start.32 = (f32[96,128]{1,0:T(8,128)S(1)}, f32[96,128]{1,0:T(8,128)S(1)}, u32[]{:S(2)}, u32[]{:S(2)}) collective-permute-start(f32[96,128]{1,0:T(8,128)S(1)} %copy-done.23), channel_id=1, source_target_pairs={{0,1},{1,0},{2,3},{3,2},{4,5},{5,4},{6,7},{7,6},{8,9},{9,8},{10,11... | collective-permute-start | bytes 147464 | tf_op jit(solution)/shard_map/ppermute | solution.py:34
  170.4 26.4 %collective-permute-start.38 = (bf16[96,2176]{1,0:T(8,128)(2,1)}, bf16[96,2176]{1,0:T(8,128)(2,1)S(1)}, u32[]{:S(2)}, u32[]{:S(2)}) collective-permute-start(bf16[96,2176]{1,0:T(8,128)(2,1)} %get-tuple-element.214), channel_id=1, source_target_pairs={{0,2},{1,3},{2,0},{3,1},{4,6},{5,7},{6,4},{7,5},{8,10},{9,11},{10,... | collective-permute-start | bytes 1253384 | tf_op jit(solution)/shard_map/ppermute | solution.py:34
  170.8 26.0 %collective-permute-start.39 = (bf16[96,2176]{1,0:T(8,128)(2,1)}, bf16[96,2176]{1,0:T(8,128)(2,1)S(1)}, u32[]{:S(2)}, u32[]{:S(2)}) collective-permute-start(bf16[96,2176]{1,0:T(8,128)(2,1)} %get-tuple-element.215), channel_id=1, source_target_pairs={{0,4},{1,5},{2,6},{3,7},{4,0},{5,1},{6,2},{7,3},{8,12},{9,13},{10,... | collective-permute-start | bytes 1253384 | tf_op jit(solution)/shard_map/ppermute | solution.py:34
  171.9 24.9 %collective-permute-start.40 = (bf16[96,2176]{1,0:T(8,128)(2,1)}, bf16[96,2176]{1,0:T(8,128)(2,1)S(1)}, u32[]{:S(2)}, u32[]{:S(2)}) collective-permute-start(bf16[96,2176]{1,0:T(8,128)(2,1)} %get-tuple-element.216), channel_id=1, source_target_pairs={{0,6},{1,7},{2,4},{3,5},{4,2},{5,3},{6,0},{7,1},{8,14},{9,15},{10,... | collective-permute-start | bytes 1253384 | tf_op jit(solution)/shard_map/ppermute | solution.py:34
  173.2 23.7 %collective-permute-start.41 = (bf16[96,1536]{1,0:T(8,128)(2,1)S(1)}, bf16[96,1536]{1,0:T(8,128)(2,1)S(1)}, u32[]{:S(2)}, u32[]{:S(2)}) collective-permute-start(bf16[96,1536]{1,0:T(8,128)(2,1)S(1)} %add_convert_fusion.4), channel_id=1, source_target_pairs={{0,16},{8,24},{16,0},{24,8},{1,17},{9,25},{17,1},{25,9},{2,18},{10... | collective-permute-start | bytes 884744 | tf_op jit(solution)/shard_map/ppermute | solution.py:34
  174.5 37.6 %collective-permute-start.43 = (bf16[512,768]{1,0:T(8,128)(2,1)S(1)}, bf16[512,768]{1,0:T(8,128)(2,1)}, u32[]{:S(2)}, u32[]{:S(2)}) collective-permute-start(bf16[512,768]{1,0:T(8,128)(2,1)S(1)} %fusion.6), channel_id=1, source_target_pairs={{1,16},{3,18},{5,20},{7,22},{9,24},{11,26},{13,28},{15,30},{16,1},... | collective-permute-start | bytes 2359304 | tf_op jit(solution)/shard_map/ppermute | solution.py:51
  199.1 12.9 %collective-permute-start.42 = (bf16[96,1344]{1,0:T(8,128)(2,1)S(1)}, bf16[96,1344]{1,0:T(8,128)(2,1)S(1)}, u32[]{:S(2)}, u32[]{:S(2)}) collective-permute-start(bf16[96,1344]{1,0:T(8,128)(2,1)S(1)} %concatenate.44), channel_id=1, source_target_pairs={{0,8},{8,0},{16,24},{24,16},{1,9},{9,1},{17,25},{25,17},{2,10},{10... | collective-permute-start | bytes 774152 | tf_op jit(solution)/shard_map/ppermute | solution.py:34
  212.3 13.3 %collective-permute-start.45 = (bf16[96,1536]{1,0:T(8,128)(2,1)S(1)}, bf16[96,1536]{1,0:T(8,128)(2,1)S(1)}, u32[]{:S(2)}, u32[]{:S(2)}) collective-permute-start(bf16[96,1536]{1,0:T(8,128)(2,1)S(1)} %add_convert_fusion.3), channel_id=1, source_target_pairs={{0,8},{8,0},{16,24},{24,16},{1,9},{9,1},{17,25},{25,17},{2,10},{10... | collective-permute-start | bytes 884744 | tf_op jit(solution)/shard_map/ppermute | solution.py:34
  212.6 11.2 %collective-permute-start.44 = (bf16[96,1216]{1,0:T(8,128)(2,1)S(1)}, bf16[96,1216]{1,0:T(8,128)(2,1)S(1)}, u32[]{:S(2)}, u32[]{:S(2)}) collective-permute-start(bf16[96,1216]{1,0:T(8,128)(2,1)S(1)} %concatenate.46), channel_id=1, source_target_pairs={{0,16},{8,24},{16,0},{24,8},{1,17},{9,25},{17,1},{25,9},{2,18},{10... | collective-permute-start | bytes 700424 | tf_op jit(solution)/shard_map/ppermute | solution.py:34
  227.7 8.0 %collective-permute-start.47 = (bf16[96,960]{1,0:T(8,128)(2,1)S(1)}, bf16[96,960]{1,0:T(8,128)(2,1)S(1)}, u32[]{:S(2)}, u32[]{:S(2)}) collective-permute-start(bf16[96,960]{1,0:T(8,128)(2,1)S(1)} %add_convert_fusion.5), channel_id=1, source_target_pairs={{0,8},{8,0},{16,24},{24,16},{1,9},{9,1},{17,25},{25,17},{2,10},{10... | collective-permute-start | bytes 552968 | tf_op jit(solution)/shard_map/ppermute | solution.py:34
  228.5 6.7 %collective-permute-start.46 = (bf16[96,256]{1,0:T(8,128)(2,1)S(1)}, bf16[96,256]{1,0:T(8,128)(2,1)S(1)}, u32[]{:S(2)}, u32[]{:S(2)}) collective-permute-start(bf16[96,256]{1,0:T(8,128)(2,1)S(1)} %pad_maximum_fusion.4), channel_id=1, source_target_pairs={{1,16},{3,18},{5,20},{7,22},{9,24},{11,26},{13,28},{15,30},{16,1},... | collective-permute-start | bytes 147464 | tf_op jit(solution)/shard_map/ppermute | solution.py:51
  (22 other events, 58.0 us)

commit v4 on v3

--- a/solution.py
+++ b/solution.py
@@ -647,20 +647,21 @@
     return got[0], list(got[1:])
 
 
-def pair_small_kernel(at, keep, got, small, small_got, *outs):
-    n, _, cols = keep.shape
-    chip = at[0] // 2
+def pair_small_kernel(at, term, got, small, small_got, *outs):
+    cols = got.shape[-1]
+    chip, core = at[0] // 2, at[0] % 2
     total = small[...] + small_got[...]
     parts = jnp.concatenate(pieces2(total), axis=1)
     for k, out in enumerate(outs):
-        out[:, :cols] = (keep[chip ^ k].astype(F32) + got[chip ^ k].astype(F32)).astype(BF)
+        kept = term[2 * (chip ^ k) + core]
+        out[:, :cols] = (kept.astype(F32) + got[chip ^ k].astype(F32)).astype(BF)
         out[:, cols:] = parts
 
 
-def run_pair_small(at, keep, got, small, small_got):
-    n, rows, cols = keep.shape
+def run_pair_small(at, term, got, small, small_got):
+    n, rows, cols = got.shape
     out = shape((rows, cols + 2 * small.shape[1]), BF)
-    args = [keep, got, small, small_got]
+    args = [term, got, small, small_got]
     return call(
         pair_small_kernel, 1, (1,), [(at, in_smem())] + [(v, whole(v)) for v in args],
         [(out, whole(out))] * n, [],
@@ -1199,23 +1200,23 @@
     )
     gain = wa[:, XBC + NH].astype(F32)
     from_a = dot_nt(d_a_all, wa)
-    halo_part = norm_back(from_a[rows:], tok_halo, gain)
-    halo_part = halo_part.reshape(nb, HALO, DM)[:, HALO - KC :].astype(BF).reshape(k_rows, -1)
-    halos = [halo_part, trade(halo_part, "shard", 1)]
     normal_grad = dot_nt(dz, wz) + from_a[:rows]
     token_grad = (cot.astype(F32) + norm_back(normal_grad, tok, gain)).astype(BF)
 
-    a_got, small_got, halos[1], zo_got = after_all([a_got, small_got, halos[1], zo_got], token_grad)
+    a_got, small_got = after_all([a_got, small_got], token_grad)
     if k_rows % 32:
         parts = split2((small + small_got).reshape(k_rows, -1))
         a_pairs = [jnp.concatenate([v, parts], axis=1) for v in chip_pairs(a_keep, a_got)]
     else:
-        a_pairs = run_pair_small(at, a_keep, a_got, small, small_got)
+        a_pairs = run_pair_small(at, a_term, a_got, small, small_got)
     a_far = chip_send(a_pairs)
     token_got = move_home(after(token_grad, a_pairs[0]))
     zo_half = head_add(zo_keep, after(zo_got, a_pairs[0]))
     zo_got = trade(zo_half, "head", 2)
-    *a_far, zo_got = after_all(a_far + [zo_got])
+    halo_part = norm_back(after(from_a, a_pairs[0])[rows:], tok_halo, gain)
+    halo_part = halo_part.reshape(nb, HALO, DM)[:, HALO - KC :].astype(BF).reshape(k_rows, -1)
+    halos = [halo_part, trade(halo_part, "shard", 1)]
+    *a_far, zo_got, halos[1] = after_all(a_far + [zo_got, halos[1]])
     a_own = chip_sum(a_pairs[0][:, :WA], [v[:, :WA] for v in a_far])
     sums = [join2(v[:, WA:]) for v in [a_pairs[0]] + a_far]
     while len(sums) > 1:
@@ -1238,16 +1239,14 @@
             for more in bits[2:]:
                 zo_half = head_add(zo_half, trade(zo_half, "head", more))
             zo_other = trade(zo_half, "head", 1)
-        elif bit == bits[-1]:
-            sent, zo_other = after_all([sent, zo_other])
-            zo_grad = head_join(zo_half, zo_other).astype(F32)
         if bit < half:
             halos = halos + jnp.split(sent[:, edge:], len(halos), axis=1)
         total = total + sent[:, :cut].astype(F32)
         small = join2(parts) + join2(sent[:, cut:edge])
     low = total.astype(BF)
     other = trade(low, "head", 1)
-    halos = after(jnp.concatenate(halos, axis=1), low)
+    halos, small, zo_other = after_all([jnp.concatenate(halos, axis=1), small, zo_other], low)
+    zo_grad = head_join(zo_half, zo_other).astype(F32)
     halos = jnp.where(stay, halos, move_home(halos))
     halos = jnp.split(halos, group_blocks // nb, axis=1)
     other = after(other, *halos)

time: 239 us -> 232 us (0.971)
  waiting for transfers between devices: 59.6 us -> 51.4 us
  matrix products: 10.5 us -> 7.8 us
  other arithmetic: 17.4 us -> 19.9 us
    ppermute x40, waiting for transfers between devices: 56.6 us -> 48.5 us  [trade(): return lax.ppermute(value, axis, [(i, i ^ bit) for i in range(size)])]
    dot_general x2, matrix products: 6.11 us -> 3.43 us  [dot_nt(): lax.dot_general(a, b, (((1,), (1,)), ((), ())), preferred_element_type=F32)]
    unnamed x72 -> x98, local copies, waits for them, and re-layouts: 5.78 us -> 8.07 us
  transfers between devices with their start and end apart: 48 -> 48, of which waited for: 18 -> 19; matrix products, arithmetic and copies ran while one was open for 14% -> 15% of each run, Pallas kernels for 26% -> 28%
where the time goes in v4:
time: 232 us; the launch traced here: 231 us
  Pallas kernels  79.2 us (34%)
  waiting for transfers between devices  51.4 us (22%)
  starting transfers between devices  47.5 us (20%)
  local copies, waits for them, and re-layouts  22.8 us (10%)
  other arithmetic  19.9 us (9%)
  matrix products  7.8 us (3%)
  between operations  2.36 us (1%)
    pallas_call x8, Pallas kernels, call(): pl.pallas_call(kernel, grid=grid, out_shape=[o for o, _ in outs], in_spec...  79.2 us
    ppermute x40, waiting for transfers between devices, trade(): return lax.ppermute(value, axis, [(i, i ^ bit) for i in range(size)])  48.5 us
    ppermute x40, starting transfers between devices, trade(): return lax.ppermute(value, axis, [(i, i ^ bit) for i in range(size)])  24.2 us
    ppermute x5, starting transfers between devices, move_home(): return lax.ppermute(value, ('head', 'shard'), pairs)  21.4 us
    unnamed x98, local copies, waits for them, and re-layouts  8.07 us
  transfers between devices with their start and end apart: 48, of which 19 were waited for; matrix products, arithmetic and copies ran while one was open for 15% of the time, Pallas kernels for 28%

profile of v4, /device:TPU:1, one launch (start us, length us, event | category | flops | bytes accessed | tf_op | source)
XLA Modules:
  0.0 231.1 jit_solution(8574499961149011286)
XLA Ops:
  0.7 1.1 slice.144
  1.8 0.8 copy.31
  2.7 3.1 %collective-permute-start.1 = (bf16[96,1920]{1,0:T(8,128)(2,1)S(1)}, bf16[96,1920]{1,0:T(8,128)(2,1)S(1)}, u32[]{:S(2)}, u32[]{:S(2)}) collective-permute-start(bf16[96,1920]{1,0:T(8,128)(2,1)S(1)} %concatenate.42.refs_1_), channel_id=1, source_target_pairs={{0,6},{1,7},{2,4},{3,5},{4,2},{5,3},{6,0},{7,1},{8,14},{9,15},{10,... | collective-permute-start | bytes 1105928 | tf_op jit(solution)/shard_map/ppermute | solution.py:34
  6.2 1.2 collective-permute-start.4
  8.3 0.9 collective-permute-done
  9.3 4.7 %collective-permute-start.8 = (bf16[512,768]{1,0:T(8,128)(2,1)S(1)}, bf16[512,768]{1,0:T(8,128)(2,1)S(1)}, u32[]{:S(2)}, u32[]{:S(2)}) collective-permute-start(bf16[512,768]{1,0:T(8,128)(2,1)S(1)} %copy-done.17), channel_id=1, source_target_pairs={{1,16},{3,18},{5,20},{7,22},{9,24},{11,26},{13,28},{15,30},{16,1},... | collective-permute-start | bytes 2359304 | tf_op jit(solution)/shard_map/ppermute | solution.py:51
  16.9 1.1 compare_convert_fusion.refs_19_.refs_17_.refs_25_
  18.0 4.8 %collective-permute-done.2.refs_3_ = bf16[96,1920]{1,0:T(8,128)(2,1)} collective-permute-done((bf16[96,1920]{1,0:T(8,128)(2,1)S(1)}, bf16[96,1920]{1,0:T(8,128)(2,1)}, u32[]{:S(2)}, u32[]{:S(2)}) %collective-permute-start.2) | collective-permute-done | bytes 368672 | tf_op jit(solution)/shard_map/ppermute | solution.py:34
  23.6 1.0 compare_convert_fusion.1.refs_26_
  26.1 1.4 pad.17.refs_15_.refs_22_
  28.6 1.2 pad_bitcast_fusion
  29.8 2.2 collective-permute-done.8.refs_14_
  32.2 0.8 collective-permute-start.11
  33.0 1.1 collective-permute-start.9
  34.1 1.0 fusion.27
  35.8 6.3 %collective-permute-start.20 = (bf16[512,768]{1,0:T(8,128)(2,1)S(1)}, bf16[512,768]{1,0:T(8,128)(2,1)S(1)}, u32[]{:S(2)}, u32[]{:S(2)}) collective-permute-start(bf16[512,768]{1,0:T(8,128)(2,1)S(1)} %copy-done.4), channel_id=1, source_target_pairs={{1,16},{3,18},{5,20},{7,22},{9,24},{11,26},{13,28},{15,30},{16,1},... | collective-permute-start | bytes 2359304 | tf_op jit(solution)/shard_map/ppermute | solution.py:51
  42.2 2.2 collective-permute-start.13
  45.0 13.4 %shard_map.212 = (bf16[768,1920]{1,0:T(8,128)(2,1)}, bf16[512,768]{1,0:T(8,128)(2,1)}, bf16[16,768]{1,0:T(8,128)(2,1)}, bf16[528,768]{1,0:T(8,128)(2,1)}, bf16[7...) custom-call(s32[26]{0:T(128)} %pad_add_fusion.2.refs_0_, ...), custom_call_target="tpu_custom_call" | custom-call | flops 1 | bytes 20720000 | tf_op jit(solution)/shard_map/pallas_call | solution.py:234
  58.5 6.5 %shard_map.213.refs_9_ = f32[512,1536]{1,0:T(8,128)} custom-call(bf16[512,128]{1,0:T(8,128)(2,1)} %get-tuple-element.144.bs.refs_16_, bf16[512,128]{1,0:T(8,128)(2,1)} %get-tuple-element.145.cs.refs_10_, bf16[512,1536]{1,0:T(8,128)(2,1)} %get-tuple-element.146.xt.refs_15_, f32[512,128]{1,0:T(8,128)} %get-tuple-element.147.cum.refs_11_.refs_18_, ...), custom_call_target="tpu_custom_call" | custom-call | flops 1 | bytes 8880000 | tf_op jit(solution)/shard_map/pallas_call | solution.py:234
  65.0 2.1 collective-permute-done.14.refs_2_
  68.3 1.0 collective-permute-done.17.refs_5_
  70.1 0.8 collective-permute-done.19.refs_7_
  71.0 0.8 collective-permute-done.16.refs_4_
  71.8 5.0 %shard_map.214 = (bf16[512,1536]{1,0:T(8,128)(2,1)S(1)}, bf16[512,1536]{1,0:T(8,128)(2,1)}, bf16[512,768]{1,0:T(8,128)(2,1)S(1)}, bf16[768,1536]{1,0:T(8,128)(2,1)}, bf16[1536,768]{1,0:T(8,128)(2,1)}) custom-call(s32[1]{0:T(128)} %bitcast.at, bf16[96,3072]{1,0:T(8,128)(2,1)S(1)} %pad_maximum_fusion.1.refs_0_, ...), custom_call_target="tpu_custom_call" | custom-call | flops 1 | bytes 1480000 | tf_op jit(solution)/shard_map/pallas_call | solution.py:234
  76.8 1.0 copy-done
  77.8 1.2 copy-done.2
  79.1 2.2 collective-permute-done.22.refs_4_.refs_8_
  81.3 0.9 copy-done.8
  82.2 14.4 %shard_map.215 = (bf16[2,128,1536]{2,1,0:T(8,128)(2,1)}, bf16[512,1536]{1,0:T(8,128)(2,1)}, f32[1,1536]{1,0:T(1,128)}, bf16[512,1536]{1,0:T(8,128)(2,1)}, bf16[5...) custom-call(s32[26]{0:T(128)} %pad_add_fusion.2.refs_0_, ...), custom_call_target="tpu_custom_call" | custom-call | flops 1 | bytes 23680000 | tf_op jit(solution)/shard_map/pallas_call | solution.py:234
  96.6 1.3 collective-permute-start.23
  97.9 7.7 %shard_map.216 = (bf16[4,96,3072]{2,1,0:T(8,128)(2,1)}, bf16[96,3072]{1,0:T(8,128)(2,1)}, bf16[96,3072]{1,0:T(8,128)(2,1)}, bf16[96,3072]{1,0:T(8,128)(2,1)}, bf16[96,3072]{1,0:T(8,128)(2,1)}) custom-call(s32[1]{0:T(128)} %bitcast.at, bf16[768,512]{1,0:T(8,128)(2,1)} %get-tuple-element.164.normal_t, bf16[512,1536]{1,0:T(8,128)(2,1)} %get-tuple-element.206.dz, ...), custom_call_target="tpu_custom_call" | custom-call | flops 1 | bytes 1480000 | tf_op jit(solution)/shard_map/pallas_call | solution.py:234
  106.6 11.5 %shard_map.217 = (f32[512,1536]{1,0:T(8,128)}, f32[512,128]{1,0:T(8,128)}, f32[512,128]{1,0:T(8,128)}, bf16[512,768]{1,0:T(8,128)(2,1)}) custom-call(bf16[512,128]{1,0:T(8,128)(2,1)} %get-tuple-element.144.bs.refs_16_, bf16[512,128]{1,0:T(8,128)(2,1)} %get-tuple-element.145.cs.refs_10_, bf16[512,1536]{1,0:T(8,128)(2,1)} %get-tuple-element.146.xt.refs_15_, ...), custom_call_target="tpu_custom_call" | custom-call | flops 1 | bytes 1480000 | tf_op jit(solution)/shard_map/pallas_call | solution.py:234
  118.2 2.2 add_convert_fusion
  120.4 1.3 dynamic-slice_bitcast_fusion.1
  122.3 1.8 collective-permute-done.28.refs_4_
  124.2 3.2 %collective-permute-start.29 = (bf16[512,768]{1,0:T(8,128)(2,1)}, bf16[512,768]{1,0:T(8,128)(2,1)S(1)}, u32[]{:S(2)}, u32[]{:S(2)}) collective-permute-start(bf16[512,768]{1,0:T(8,128)(2,1)} %get-tuple-element.187), channel_id=1, source_target_pairs={{1,16},{3,18},{5,20},{7,22},{9,24},{11,26},{13,28},{15,30},{16,1},... | collective-permute-start | bytes 2359304 | tf_op jit(solution)/shard_map/ppermute | solution.py:51
  127.7 1.3 collective-permute-start.33
  129.0 1.2 collective-permute-start.34
  130.5 0.9 copy-done.22
  131.3 17.1 %shard_map.218 = (bf16[528,1920]{1,0:T(8,128)(2,1)}, f32[96,128]{1,0:T(8,128)}) custom-call(s32[26]{0:T(128)} %pad_add_fusion.2.refs_0_, bf16[2,128,1536]{2,1,0:T(8,128)(2,1)} %get-tuple-element.178.refs_1_, bf16[2,128,1536]{2,1,0:T(8,128)(2,1)} %copy-done.21, bf16[2,128,1536]{2,1,0:T(8,128)(2,1)} %copy-done.22, ...), custom_call_target="tpu_custom_call" | custom-call | flops 1 | bytes 2960000 | tf_op jit(solution)/shard_map/pallas_call | solution.py:234
  148.5 0.9 copy-done.24
  149.4 4.4 %convolution_convert_fusion = bf16[768,1920]{1,0:T(8,128)(2,1)S(1)} fusion(bf16[528,768]{1,0:T(8,128)(2,1)S(1)} %copy-done.3, bf16[528,1920]{1,0:T(8,128)(2,1)} %get-tuple-element.208), kind=kOutput, calls=%fused_computation.1 | convolution fusion | flops 1558609920 | bytes 5787648 | tf_op jit(solution)/shard_map/dot_general | solution.py:181
  154.0 1.6 collective-permute-done.34
  157.3 1.9 fusion.29
  159.7 1.6 fusion.2
  162.9 3.6 %shard_map.219 = (bf16[96,2176]{1,0:T(8,128)(2,1)}, bf16[96,2176]{1,0:T(8,128)(2,1)}, bf16[96,2176]{1,0:T(8,128)(2,1)}, bf16[96,2176]{1,0:T(8,128)(2,1)}) custom-call(s32[1]{0:T(128)} %bitcast.at, bf16[8,96,1920]{2,1,0:T(8,128)(2,1)} %bitcast.71, bf16[4,96,1920]{2,1,0:T(8,128)(2,1)} %copy-done.15, f32[96,128]{1,0:T(8,128)} %get-tuple-element.199.small, ...), custom_call_target="tpu_custom_call" | custom-call | flops 1 | bytes 1480000 | tf_op jit(solution)/shard_map/pallas_call | solution.py:234
  166.8 2.3 %collective-permute-start.40 = (bf16[96,1536]{1,0:T(8,128)(2,1)S(1)}, bf16[96,1536]{1,0:T(8,128)(2,1)S(1)}, u32[]{:S(2)}, u32[]{:S(2)}) collective-permute-start(bf16[96,1536]{1,0:T(8,128)(2,1)S(1)} %add_convert_fusion.4), channel_id=1, source_target_pairs={{0,16},{8,24},{16,0},{24,8},{1,17},{9,25},{17,1},{25,9},{2,18},{10... | collective-permute-start | bytes 884744 | tf_op jit(solution)/shard_map/ppermute | solution.py:34
  169.1 1.3 collective-permute-start.36
  170.8 0.9 collective-permute-start.38
  172.0 1.2 collective-permute-start.41
  174.1 2.9 %collective-permute-start.43 = (bf16[512,768]{1,0:T(8,128)(2,1)S(1)}, bf16[512,768]{1,0:T(8,128)(2,1)}, u32[]{:S(2)}, u32[]{:S(2)}) collective-permute-start(bf16[512,768]{1,0:T(8,128)(2,1)S(1)} %fusion.6), channel_id=1, source_target_pairs={{1,16},{3,18},{5,20},{7,22},{9,24},{11,26},{13,28},{15,30},{16,1},... | collective-permute-start | bytes 2359304 | tf_op jit(solution)/shard_map/ppermute | solution.py:51
  177.0 14.0 %collective-permute-done.40 = bf16[96,1536]{1,0:T(8,128)(2,1)S(1)} collective-permute-done((bf16[96,1536]{1,0:T(8,128)(2,1)S(1)}, bf16[96,1536]{1,0:T(8,128)(2,1)S(1)}, u32[]{:S(2)}, u32[]{:S(2)}) %collective-permute-start.40) | collective-permute-done | bytes 294944 | tf_op jit(solution)/shard_map/ppermute | solution.py:34
  191.8 1.5 add_convert_fusion.2
  193.4 1.5 fusion.17
  195.6 0.9 concatenate.44
  196.6 1.0 broadcast_select_fusion.1
  197.5 7.5 %collective-permute-done.42 = bf16[96,1344]{1,0:T(8,128)(2,1)S(1)} collective-permute-done((bf16[96,1344]{1,0:T(8,128)(2,1)S(1)}, bf16[96,1344]{1,0:T(8,128)(2,1)S(1)}, u32[]{:S(2)}, u32[]{:S(2)}) %collective-permute-start.42) | collective-permute-done | bytes 258080 | tf_op jit(solution)/shard_map/ppermute | solution.py:34
  205.5 1.0 add_convert_fusion.3
  206.6 2.1 collective-permute-start.45
  208.8 1.2 broadcast_select_fusion
  210.0 9.0 %collective-permute-done.44 = bf16[96,1216]{1,0:T(8,128)(2,1)S(1)} collective-permute-done((bf16[96,1216]{1,0:T(8,128)(2,1)S(1)}, bf16[96,1216]{1,0:T(8,128)(2,1)S(1)}, u32[]{:S(2)}, u32[]{:S(2)}) %collective-permute-start.44) | collective-permute-done | bytes 233504 | tf_op jit(solution)/shard_map/ppermute | solution.py:34
  221.3 4.3 %collective-permute-start.46 = (bf16[96,256]{1,0:T(8,128)(2,1)S(1)}, bf16[96,256]{1,0:T(8,128)(2,1)S(1)}, u32[]{:S(2)}, u32[]{:S(2)}) collective-permute-start(bf16[96,256]{1,0:T(8,128)(2,1)S(1)} %pad_maximum_fusion.4), channel_id=1, source_target_pairs={{1,16},{3,18},{5,20},{7,22},{9,24},{11,26},{13,28},{15,30},{16,1},... | collective-permute-start | bytes 147464 | tf_op jit(solution)/shard_map/ppermute | solution.py:51
  225.6 0.9 pad_maximum_fusion.2
  229.2 1.3 multiply_reduce_fusion
  (238 shorter events, 26.2 us)
Async XLA Ops:
  1.8 25.7 %copy-start.43 = (f32[1792]{0:T(1024)S(1)}, f32[1792]{0:T(1024)}, u32[]{:S(2)}) copy-start(f32[1792]{0:T(1024)} %param.19) | copy-start | bytes 21508
  1.8 26.3 %copy-start.42 = (f32[1536]{0:T(1024)S(1)}, f32[1536]{0:T(1024)}, u32[]{:S(2)}) copy-start(f32[1536]{0:T(1024)} %param.23) | copy-start | bytes 18436
  2.7 39.5 %copy-start.16 = (bf16[96,1920]{1,0:T(8,128)(2,1)}, bf16[96,1920]{1,0:T(8,128)(2,1)S(1)}, u32[]{:S(2)}) copy-start(bf16[96,1920]{1,0:T(8,128)(2,1)S(1)} %concatenate.42.refs_1_) | copy-start | bytes 1105924
  2.7 33.1 %copy-start.4 = (bf16[512,768]{1,0:T(8,128)(2,1)S(1)}, bf16[512,768]{1,0:T(8,128)(2,1)}, u32[]{:S(2)}) copy-start(bf16[512,768]{1,0:T(8,128)(2,1)} %refs_9_.1) | copy-start | bytes 2359300
  2.7 39.4 %slice-start.1 = ((bf16[96,3352]{1,0:T(8,128)(2,1)}), bf16[96,1536]{1,0:T(8,128)(2,1)S(1)}, s32[]{:S(2)}) async-start(bf16[96,3352]{1,0:T(8,128)(2,1)} %param.17), calls=%async_computation.1 | async-start | bytes 589824 | tf_op jit(solution)/shard_map/slice | solution.py:1136
  2.7 14.2 %collective-permute-start.1 = (bf16[96,1920]{1,0:T(8,128)(2,1)S(1)}, bf16[96,1920]{1,0:T(8,128)(2,1)S(1)}, u32[]{:S(2)}, u32[]{:S(2)}) collective-permute-start(bf16[96,1920]{1,0:T(8,128)(2,1)S(1)} %concatenate.42.refs_1_), channel_id=1, source_target_pairs={{0,6},{1,7},{2,4},{3,5},{4,2},{5,3},{6,0},{7,1},{8,14},{9,15},{10,... | collective-permute-start | bytes 1105928 | tf_op jit(solution)/shard_map/ppermute | solution.py:34
  5.8 17.1 %collective-permute-start.2 = (bf16[96,1920]{1,0:T(8,128)(2,1)S(1)}, bf16[96,1920]{1,0:T(8,128)(2,1)}, u32[]{:S(2)}, u32[]{:S(2)}) collective-permute-start(bf16[96,1920]{1,0:T(8,128)(2,1)S(1)} %concatenate.42.refs_1_), channel_id=1, source_target_pairs={{0,4},{1,5},{2,6},{3,7},{4,0},{5,1},{6,2},{7,3},{8,12},{9,13},{10,... | collective-permute-start | bytes 1105928 | tf_op jit(solution)/shard_map/ppermute | solution.py:34
  6.0 17.3 %collective-permute-start.3 = (bf16[96,1920]{1,0:T(8,128)(2,1)S(1)}, bf16[96,1920]{1,0:T(8,128)(2,1)}, u32[]{:S(2)}, u32[]{:S(2)}) collective-permute-start(bf16[96,1920]{1,0:T(8,128)(2,1)S(1)} %concatenate.42.refs_1_), channel_id=1, source_target_pairs={{0,2},{1,3},{2,0},{3,1},{4,6},{5,7},{6,4},{7,5},{8,10},{9,11},{10,... | collective-permute-start | bytes 1105928 | tf_op jit(solution)/shard_map/ppermute | solution.py:34
  6.2 25.9 %collective-permute-start.4 = (bf16[96,1920]{1,0:T(8,128)(2,1)S(1)}, bf16[96,1920]{1,0:T(8,128)(2,1)}, u32[]{:S(2)}, u32[]{:S(2)}) collective-permute-start(bf16[96,1920]{1,0:T(8,128)(2,1)S(1)} %concatenate.42.refs_1_), channel_id=1, source_target_pairs={{0,1},{1,0},{2,3},{3,2},{4,5},{5,4},{6,7},{7,6},{8,9},{9,8},{10,11... | collective-permute-start | bytes 1105928 | tf_op jit(solution)/shard_map/ppermute | solution.py:34
  8.1 1.1 collective-permute-start
  9.3 22.8 %collective-permute-start.8 = (bf16[512,768]{1,0:T(8,128)(2,1)S(1)}, bf16[512,768]{1,0:T(8,128)(2,1)S(1)}, u32[]{:S(2)}, u32[]{:S(2)}) collective-permute-start(bf16[512,768]{1,0:T(8,128)(2,1)S(1)} %copy-done.17), channel_id=1, source_target_pairs={{1,16},{3,18},{5,20},{7,22},{9,24},{11,26},{13,28},{15,30},{16,1},... | collective-permute-start | bytes 2359304 | tf_op jit(solution)/shard_map/ppermute | solution.py:51
  16.9 25.3 %copy-start.27 = (bf16[96,1920]{1,0:T(8,128)(2,1)}, bf16[96,1920]{1,0:T(8,128)(2,1)S(1)}, u32[]{:S(2)}) copy-start(bf16[96,1920]{1,0:T(8,128)(2,1)S(1)} %collective-permute-done.1.refs_2_) | copy-start | bytes 1105924
  18.0 14.1 %collective-permute-start.5 = (bf16[96,1920]{1,0:T(8,128)(2,1)S(1)}, bf16[96,1920]{1,0:T(8,128)(2,1)}, u32[]{:S(2)}, u32[]{:S(2)}) collective-permute-start(bf16[96,1920]{1,0:T(8,128)(2,1)S(1)} %collective-permute-done.1.refs_2_), channel_id=1, source_target_pairs={{0,1},{1,0},{2,3},{3,2},{4,5},{5,4},{6,7},{7,6},{8,9},{9,8},{10,11... | collective-permute-start | bytes 1105928 | tf_op jit(solution)/shard_map/ppermute | solution.py:34
  22.8 9.3 %collective-permute-start.6 = (bf16[96,1920]{1,0:T(8,128)(2,1)}, bf16[96,1920]{1,0:T(8,128)(2,1)}, u32[]{:S(2)}, u32[]{:S(2)}) collective-permute-start(bf16[96,1920]{1,0:T(8,128)(2,1)} %collective-permute-done.2.refs_3_), channel_id=1, source_target_pairs={{0,1},{1,0},{2,3},{3,2},{4,5},{5,4},{6,7},{7,6},{8,9},{9,8},{10,11... | collective-permute-start | bytes 1105928 | tf_op jit(solution)/shard_map/ppermute | solution.py:34
  23.3 8.8 %collective-permute-start.7 = (bf16[96,1920]{1,0:T(8,128)(2,1)}, bf16[96,1920]{1,0:T(8,128)(2,1)}, u32[]{:S(2)}, u32[]{:S(2)}) collective-permute-start(bf16[96,1920]{1,0:T(8,128)(2,1)} %collective-permute-done.3.refs_4_), channel_id=1, source_target_pairs={{0,1},{1,0},{2,3},{3,2},{4,5},{5,4},{6,7},{7,6},{8,9},{9,8},{10,11... | collective-permute-start | bytes 1105928 | tf_op jit(solution)/shard_map/ppermute | solution.py:34
  32.0 12.9 %copy-start.18 = (bf16[512,768]{1,0:T(8,128)(2,1)}, bf16[512,768]{1,0:T(8,128)(2,1)S(1)}, u32[]{:S(2)}) copy-start(bf16[512,768]{1,0:T(8,128)(2,1)S(1)} %collective-permute-done.8.refs_14_) | copy-start | bytes 2359300
  32.1 12.9 %copy-start.33 = (bf16[16,768]{1,0:T(8,128)(2,1)}, bf16[16,768]{1,0:T(8,128)(2,1)S(1)}, u32[]{:S(2)}) copy-start(bf16[16,768]{1,0:T(8,128)(2,1)S(1)} %fusion.20.refs_9_) | copy-start | bytes 73732
  32.1 2.9 %collective-permute-start.10 = (bf16[16,768]{1,0:T(8,128)(2,1)S(1)}, bf16[16,768]{1,0:T(8,128)(2,1)S(1)}, u32[]{:S(2)}, u32[]{:S(2)}) collective-permute-start(bf16[16,768]{1,0:T(8,128)(2,1)S(1)} %fusion.20.refs_9_), channel_id=1, source_target_pairs={{0,1},{1,0},{2,3},{3,2},{4,5},{5,4},{6,7},{7,6},{8,9},{9,8},{10,11... | collective-permute-start | bytes 73736 | tf_op jit(solution)/shard_map/ppermute | solution.py:69
  32.2 3.4 %collective-permute-start.11 = (bf16[16,768]{1,0:T(8,128)(2,1)S(1)}, bf16[16,768]{1,0:T(8,128)(2,1)S(1)}, u32[]{:S(2)}, u32[]{:S(2)}) collective-permute-start(bf16[16,768]{1,0:T(8,128)(2,1)S(1)} %fusion.20.refs_9_), channel_id=1, source_target_pairs={{0,9},{1,8},{2,11},{3,10},{4,13},{5,12},{6,15},{7,14},{8,1},{9,0},... | collective-permute-start | bytes 73736 | tf_op jit(solution)/shard_map/ppermute | solution.py:69
  33.0 2.8 %collective-permute-start.9 = (bf16[16,768]{1,0:T(8,128)(2,1)S(1)}, bf16[16,768]{1,0:T(8,128)(2,1)S(1)}, u32[]{:S(2)}, u32[]{:S(2)}) collective-permute-start(bf16[16,768]{1,0:T(8,128)(2,1)S(1)} %fusion.20.refs_9_), channel_id=1, source_target_pairs={{0,8},{1,9},{2,10},{3,11},{4,12},{5,13},{6,14},{7,15},{8,0},{9,1},... | collective-permute-start | bytes 73736 | tf_op jit(solution)/shard_map/ppermute | solution.py:69
  35.8 32.1 %collective-permute-start.20 = (bf16[512,768]{1,0:T(8,128)(2,1)S(1)}, bf16[512,768]{1,0:T(8,128)(2,1)S(1)}, u32[]{:S(2)}, u32[]{:S(2)}) collective-permute-start(bf16[512,768]{1,0:T(8,128)(2,1)S(1)} %copy-done.4), channel_id=1, source_target_pairs={{1,16},{3,18},{5,20},{7,22},{9,24},{11,26},{13,28},{15,30},{16,1},... | collective-permute-start | bytes 2359304 | tf_op jit(solution)/shard_map/ppermute | solution.py:51
  42.2 22.8 %collective-permute-start.13 = (bf16[96,3072]{1,0:T(8,128)(2,1)S(1)}, bf16[96,3072]{1,0:T(8,128)(2,1)S(1)}, u32[]{:S(2)}, u32[]{:S(2)}) collective-permute-start(bf16[96,3072]{1,0:T(8,128)(2,1)S(1)} %pad_maximum_fusion.1.refs_0_), channel_id=1, source_target_pairs={{0,6},{1,7},{2,4},{3,5},{4,2},{5,3},{6,0},{7,1},{8,14},{9,15},{10,... | collective-permute-start | bytes 1769480 | tf_op jit(solution)/shard_map/ppermute | solution.py:34
  44.5 22.7 %collective-permute-start.14 = (bf16[96,3072]{1,0:T(8,128)(2,1)S(1)}, bf16[96,3072]{1,0:T(8,128)(2,1)S(1)}, u32[]{:S(2)}, u32[]{:S(2)}) collective-permute-start(bf16[96,3072]{1,0:T(8,128)(2,1)S(1)} %pad_maximum_fusion.1.refs_0_), channel_id=1, source_target_pairs={{0,4},{1,5},{2,6},{3,7},{4,0},{5,1},{6,2},{7,3},{8,12},{9,13},{10,... | collective-permute-start | bytes 1769480 | tf_op jit(solution)/shard_map/ppermute | solution.py:34
  44.7 22.6 %collective-permute-start.15 = (bf16[96,3072]{1,0:T(8,128)(2,1)S(1)}, bf16[96,3072]{1,0:T(8,128)(2,1)S(1)}, u32[]{:S(2)}, u32[]{:S(2)}) collective-permute-start(bf16[96,3072]{1,0:T(8,128)(2,1)S(1)} %pad_maximum_fusion.1.refs_0_), channel_id=1, source_target_pairs={{0,2},{1,3},{2,0},{3,1},{4,6},{5,7},{6,4},{7,5},{8,10},{9,11},{10,... | collective-permute-start | bytes 1769480 | tf_op jit(solution)/shard_map/ppermute | solution.py:34
  58.4 20.5 %collective-permute-start.12 = (bf16[2,128,1664]{2,1,0:T(8,128)(2,1)}, bf16[2,128,1664]{2,1,0:T(8,128)(2,1)S(1)}, u32[]{:S(2)}, u32[]{:S(2)}) collective-permute-start(bf16[2,128,1664]{2,1,0:T(8,128)(2,1)} %get-tuple-element.149.refs_1_.refs_5_), channel_id=1, source_target_pairs={{0,8},{8,0},{16,24},{24,16},{1,9},{9,1},{17,25},{25,17},{2,10},{10... | collective-permute-start | bytes 2555912 | tf_op jit(solution)/shard_map/ppermute | solution.py:34
  58.5 13.3 %copy-start.3 = (bf16[528,768]{1,0:T(8,128)(2,1)S(1)}, bf16[528,768]{1,0:T(8,128)(2,1)}, u32[]{:S(2)}) copy-start(bf16[528,768]{1,0:T(8,128)(2,1)} %get-tuple-element.156.refs_8_) | copy-start | bytes 2433028
  67.3 2.0 collective-permute-start.17
  67.4 2.7 %collective-permute-start.18 = (bf16[96,3072]{1,0:T(8,128)(2,1)S(1)}, bf16[96,3072]{1,0:T(8,128)(2,1)S(1)}, u32[]{:S(2)}, u32[]{:S(2)}) collective-permute-start(bf16[96,3072]{1,0:T(8,128)(2,1)S(1)} %collective-permute-done.14.refs_2_), channel_id=1, source_target_pairs={{0,1},{1,0},{2,3},{3,2},{4,5},{5,4},{6,7},{7,6},{8,9},{9,8},{10,11... | collective-permute-start | bytes 1769480 | tf_op jit(solution)/shard_map/ppermute | solution.py:34
  67.8 3.2 %collective-permute-start.19 = (bf16[96,3072]{1,0:T(8,128)(2,1)S(1)}, bf16[96,3072]{1,0:T(8,128)(2,1)S(1)}, u32[]{:S(2)}, u32[]{:S(2)}) collective-permute-start(bf16[96,3072]{1,0:T(8,128)(2,1)S(1)} %collective-permute-done.15.refs_3_), channel_id=1, source_target_pairs={{0,1},{1,0},{2,3},{3,2},{4,5},{5,4},{6,7},{7,6},{8,9},{9,8},{10,11... | collective-permute-start | bytes 1769480 | tf_op jit(solution)/shard_map/ppermute | solution.py:34
  67.9 3.9 %collective-permute-start.16 = (bf16[96,3072]{1,0:T(8,128)(2,1)S(1)}, bf16[96,3072]{1,0:T(8,128)(2,1)S(1)}, u32[]{:S(2)}, u32[]{:S(2)}) collective-permute-start(bf16[96,3072]{1,0:T(8,128)(2,1)S(1)} %pad_maximum_fusion.1.refs_0_), channel_id=1, source_target_pairs={{0,1},{1,0},{2,3},{3,2},{4,5},{5,4},{6,7},{7,6},{8,9},{9,8},{10,11... | collective-permute-start | bytes 1769480 | tf_op jit(solution)/shard_map/ppermute | solution.py:34
  69.3 9.8 %collective-permute-start.21 = (bf16[2,128,1664]{2,1,0:T(8,128)(2,1)S(1)}, bf16[2,128,1664]{2,1,0:T(8,128)(2,1)S(1)}, u32[]{:S(2)}, u32[]{:S(2)}) collective-permute-start(bf16[2,128,1664]{2,1,0:T(8,128)(2,1)S(1)} %copy-done.5), channel_id=1, source_target_pairs={{0,1},{1,0},{2,3},{3,2},{4,5},{5,4},{6,7},{7,6},{8,9},{9,8},{10,11... | collective-permute-start | bytes 2555912 | tf_op jit(solution)/shard_map/ppermute | solution.py:34
  78.9 2.4 %collective-permute-start.22 = (bf16[2,128,1664]{2,1,0:T(8,128)(2,1)S(1)}, bf16[2,128,1664]{2,1,0:T(8,128)(2,1)S(1)}, u32[]{:S(2)}, u32[]{:S(2)}) collective-permute-start(bf16[2,128,1664]{2,1,0:T(8,128)(2,1)S(1)} %collective-permute-done.12.refs_2_.refs_6_), channel_id=1, source_target_pairs={{0,1},{1,0},{2,3},{3,2},{4,5},{5,4},{6,7},{7,6},{8,9},{9,8},{10,11... | collective-permute-start | bytes 2555912 | tf_op jit(solution)/shard_map/ppermute | solution.py:34
  96.6 21.5 %collective-permute-start.23 = (bf16[2,128,1536]{2,1,0:T(8,128)(2,1)}, bf16[2,128,1536]{2,1,0:T(8,128)(2,1)S(1)}, u32[]{:S(2)}, u32[]{:S(2)}) collective-permute-start(bf16[2,128,1536]{2,1,0:T(8,128)(2,1)} %get-tuple-element.178.refs_1_), channel_id=1, source_target_pairs={{0,8},{8,0},{16,24},{24,16},{1,9},{9,1},{17,25},{25,17},{2,10},{10... | collective-permute-start | bytes 2359304 | tf_op jit(solution)/shard_map/ppermute | solution.py:34
  105.6 12.5 %collective-permute-start.24 = (bf16[96,3072]{1,0:T(8,128)(2,1)}, bf16[96,3072]{1,0:T(8,128)(2,1)S(1)}, u32[]{:S(2)}, u32[]{:S(2)}) collective-permute-start(bf16[96,3072]{1,0:T(8,128)(2,1)} %get-tuple-element.168), channel_id=1, source_target_pairs={{0,1},{1,0},{2,3},{3,2},{4,5},{5,4},{6,7},{7,6},{8,9},{9,8},{10,11... | collective-permute-start | bytes 1769480 | tf_op jit(solution)/shard_map/ppermute | solution.py:34
  106.0 12.1 %collective-permute-start.25 = (bf16[96,3072]{1,0:T(8,128)(2,1)}, bf16[96,3072]{1,0:T(8,128)(2,1)S(1)}, u32[]{:S(2)}, u32[]{:S(2)}) collective-permute-start(bf16[96,3072]{1,0:T(8,128)(2,1)} %get-tuple-element.169), channel_id=1, source_target_pairs={{0,1},{1,0},{2,3},{3,2},{4,5},{5,4},{6,7},{7,6},{8,9},{9,8},{10,11... | collective-permute-start | bytes 1769480 | tf_op jit(solution)/shard_map/ppermute | solution.py:34
  106.1 12.0 %collective-permute-start.26 = (bf16[96,3072]{1,0:T(8,128)(2,1)}, bf16[96,3072]{1,0:T(8,128)(2,1)}, u32[]{:S(2)}, u32[]{:S(2)}) collective-permute-start(bf16[96,3072]{1,0:T(8,128)(2,1)} %get-tuple-element.170), channel_id=1, source_target_pairs={{0,1},{1,0},{2,3},{3,2},{4,5},{5,4},{6,7},{7,6},{8,9},{9,8},{10,11... | collective-permute-start | bytes 1769480 | tf_op jit(solution)/shard_map/ppermute | solution.py:34
  106.6 11.6 %collective-permute-start.27 = (bf16[96,3072]{1,0:T(8,128)(2,1)}, bf16[96,3072]{1,0:T(8,128)(2,1)}, u32[]{:S(2)}, u32[]{:S(2)}) collective-permute-start(bf16[96,3072]{1,0:T(8,128)(2,1)} %get-tuple-element.171), channel_id=1, source_target_pairs={{0,1},{1,0},{2,3},{3,2},{4,5},{5,4},{6,7},{7,6},{8,9},{9,8},{10,11... | collective-permute-start | bytes 1769480 | tf_op jit(solution)/shard_map/ppermute | solution.py:34
  106.6 11.6 %copy-start.13 = (bf16[4,96,3072]{2,1,0:T(8,128)(2,1)S(1)}, bf16[4,96,3072]{2,1,0:T(8,128)(2,1)}, u32[]{:S(2)}) copy-start(bf16[4,96,3072]{2,1,0:T(8,128)(2,1)} %get-tuple-element.181) | copy-start | bytes 7077892
  121.7 2.5 %collective-permute-start.28 = (bf16[2,128,1536]{2,1,0:T(8,128)(2,1)S(1)}, bf16[2,128,1536]{2,1,0:T(8,128)(2,1)}, u32[]{:S(2)}, u32[]{:S(2)}) collective-permute-start(bf16[2,128,1536]{2,1,0:T(8,128)(2,1)S(1)} %collective-permute-done.23.refs_2_), channel_id=1, source_target_pairs={{0,1},{1,0},{2,3},{3,2},{4,5},{5,4},{6,7},{7,6},{8,9},{9,8},{10,11... | collective-permute-start | bytes 2359304 | tf_op jit(solution)/shard_map/ppermute | solution.py:34
  122.2 8.3 %collective-permute-start.30 = (bf16[2,128,1536]{2,1,0:T(8,128)(2,1)S(1)}, bf16[2,128,1536]{2,1,0:T(8,128)(2,1)S(1)}, u32[]{:S(2)}, u32[]{:S(2)}) collective-permute-start(bf16[2,128,1536]{2,1,0:T(8,128)(2,1)S(1)} %copy-done.20), channel_id=1, source_target_pairs={{0,1},{1,0},{2,3},{3,2},{4,5},{5,4},{6,7},{7,6},{8,9},{9,8},{10,11... | collective-permute-start | bytes 2359304 | tf_op jit(solution)/shard_map/ppermute | solution.py:34
  124.2 24.3 %collective-permute-start.29 = (bf16[512,768]{1,0:T(8,128)(2,1)}, bf16[512,768]{1,0:T(8,128)(2,1)S(1)}, u32[]{:S(2)}, u32[]{:S(2)}) collective-permute-start(bf16[512,768]{1,0:T(8,128)(2,1)} %get-tuple-element.187), channel_id=1, source_target_pairs={{1,16},{3,18},{5,20},{7,22},{9,24},{11,26},{13,28},{15,30},{16,1},... | collective-permute-start | bytes 2359304 | tf_op jit(solution)/shard_map/ppermute | solution.py:51
  127.7 26.2 %collective-permute-start.33 = (bf16[96,3072]{1,0:T(8,128)(2,1)}, bf16[96,3072]{1,0:T(8,128)(2,1)S(1)}, u32[]{:S(2)}, u32[]{:S(2)}) collective-permute-start(bf16[96,3072]{1,0:T(8,128)(2,1)} %get-tuple-element.239), channel_id=1, source_target_pairs={{0,2},{1,3},{2,0},{3,1},{4,6},{5,7},{6,4},{7,5},{8,10},{9,11},{10,... | collective-permute-start | bytes 1769480 | tf_op jit(solution)/shard_map/ppermute | solution.py:34
  129.0 26.6 %collective-permute-start.34 = (bf16[96,3072]{1,0:T(8,128)(2,1)}, bf16[96,3072]{1,0:T(8,128)(2,1)S(1)}, u32[]{:S(2)}, u32[]{:S(2)}) collective-permute-start(bf16[96,3072]{1,0:T(8,128)(2,1)} %get-tuple-element.238), channel_id=1, source_target_pairs={{0,4},{1,5},{2,6},{3,7},{4,0},{5,1},{6,2},{7,3},{8,12},{9,13},{10,... | collective-permute-start | bytes 1769480 | tf_op jit(solution)/shard_map/ppermute | solution.py:34
  130.2 25.5 %collective-permute-start.35 = (bf16[96,3072]{1,0:T(8,128)(2,1)}, bf16[96,3072]{1,0:T(8,128)(2,1)S(1)}, u32[]{:S(2)}, u32[]{:S(2)}) collective-permute-start(bf16[96,3072]{1,0:T(8,128)(2,1)} %get-tuple-element.237), channel_id=1, source_target_pairs={{0,6},{1,7},{2,4},{3,5},{4,2},{5,3},{6,0},{7,1},{8,14},{9,15},{10,... | collective-permute-start | bytes 1769480 | tf_op jit(solution)/shard_map/ppermute | solution.py:34
  153.9 7.9 %collective-permute-start.31 = (bf16[4,96,1920]{2,1,0:T(8,128)(2,1)S(1)}, bf16[4,96,1920]{2,1,0:T(8,128)(2,1)S(1)}, u32[]{:S(2)}, u32[]{:S(2)}) collective-permute-start(bf16[4,96,1920]{2,1,0:T(8,128)(2,1)S(1)} %dynamic-slice_bitcast_fusion), channel_id=1, source_target_pairs={{0,1},{1,0},{2,3},{3,2},{4,5},{5,4},{6,7},{7,6},{8,9},{9,8},{10,11... | collective-permute-start | bytes 4423688 | tf_op jit(solution)/shard_map/ppermute | solution.py:34
  156.0 10.7 %collective-permute-start.39 = (bf16[96,1536]{1,0:T(8,128)(2,1)S(1)}, bf16[96,1536]{1,0:T(8,128)(2,1)S(1)}, u32[]{:S(2)}, u32[]{:S(2)}) collective-permute-start(bf16[96,1536]{1,0:T(8,128)(2,1)S(1)} %constant_dynamic-slice_fusion.1), channel_id=1, source_target_pairs={{0,8},{8,0},{16,24},{24,16},{1,9},{9,1},{17,25},{25,17},{2,10},{10... | collective-permute-start | bytes 884744 | tf_op jit(solution)/shard_map/ppermute | solution.py:34
  159.4 2.3 %collective-permute-start.32 = (f32[96,128]{1,0:T(8,128)S(1)}, f32[96,128]{1,0:T(8,128)S(1)}, u32[]{:S(2)}, u32[]{:S(2)}) collective-permute-start(f32[96,128]{1,0:T(8,128)S(1)} %copy-done.36), channel_id=1, source_target_pairs={{0,1},{1,0},{2,3},{3,2},{4,5},{5,4},{6,7},{7,6},{8,9},{9,8},{10,11... | collective-permute-start | bytes 147464 | tf_op jit(solution)/shard_map/ppermute | solution.py:34
  166.8 24.2 %collective-permute-start.40 = (bf16[96,1536]{1,0:T(8,128)(2,1)S(1)}, bf16[96,1536]{1,0:T(8,128)(2,1)S(1)}, u32[]{:S(2)}, u32[]{:S(2)}) collective-permute-start(bf16[96,1536]{1,0:T(8,128)(2,1)S(1)} %add_convert_fusion.4), channel_id=1, source_target_pairs={{0,16},{8,24},{16,0},{24,8},{1,17},{9,25},{17,1},{25,9},{2,18},{10... | collective-permute-start | bytes 884744 | tf_op jit(solution)/shard_map/ppermute | solution.py:34
  169.1 21.9 %collective-permute-start.36 = (bf16[96,2176]{1,0:T(8,128)(2,1)}, bf16[96,2176]{1,0:T(8,128)(2,1)S(1)}, u32[]{:S(2)}, u32[]{:S(2)}) collective-permute-start(bf16[96,2176]{1,0:T(8,128)(2,1)} %get-tuple-element.213), channel_id=1, source_target_pairs={{0,2},{1,3},{2,0},{3,1},{4,6},{5,7},{6,4},{7,5},{8,10},{9,11},{10,... | collective-permute-start | bytes 1253384 | tf_op jit(solution)/shard_map/ppermute | solution.py:34
  170.4 20.6 %collective-permute-start.37 = (bf16[96,2176]{1,0:T(8,128)(2,1)}, bf16[96,2176]{1,0:T(8,128)(2,1)}, u32[]{:S(2)}, u32[]{:S(2)}) collective-permute-start(bf16[96,2176]{1,0:T(8,128)(2,1)} %get-tuple-element.214), channel_id=1, source_target_pairs={{0,4},{1,5},{2,6},{3,7},{4,0},{5,1},{6,2},{7,3},{8,12},{9,13},{10,... | collective-permute-start | bytes 1253384 | tf_op jit(solution)/shard_map/ppermute | solution.py:34
  170.8 21.0 %collective-permute-start.38 = (bf16[96,2176]{1,0:T(8,128)(2,1)}, bf16[96,2176]{1,0:T(8,128)(2,1)}, u32[]{:S(2)}, u32[]{:S(2)}) collective-permute-start(bf16[96,2176]{1,0:T(8,128)(2,1)} %get-tuple-element.215), channel_id=1, source_target_pairs={{0,6},{1,7},{2,4},{3,5},{4,2},{5,3},{6,0},{7,1},{8,14},{9,15},{10,... | collective-permute-start | bytes 1253384 | tf_op jit(solution)/shard_map/ppermute | solution.py:34
  172.0 19.0 %copy-start.30 = (bf16[96,64]{1,0:T(8,128)(2,1)}, bf16[96,64]{1,0:T(8,128)(2,1)S(1)}, u32[]{:S(2)}) copy-start(bf16[96,64]{1,0:T(8,128)(2,1)S(1)} %reshape.314) | copy-start | bytes 36868
  172.0 2.1 collective-permute-start.41
  173.3 23.3 %copy-start.23 = (bf16[512,768]{1,0:T(8,128)(2,1)S(1)}, bf16[512,768]{1,0:T(8,128)(2,1)}, u32[]{:S(2)}) copy-start(bf16[512,768]{1,0:T(8,128)(2,1)} %get-tuple-element.187) | copy-start | bytes 2359300
  173.3 23.3 %copy-start.25 = (bf16[512,768]{1,0:T(8,128)(2,1)S(1)}, bf16[512,768]{1,0:T(8,128)(2,1)}, u32[]{:S(2)}) copy-start(bf16[512,768]{1,0:T(8,128)(2,1)} %copy-done.24) | copy-start | bytes 2359300
  174.1 17.0 %copy-start.34 = (bf16[96,64]{1,0:T(8,128)(2,1)}, bf16[96,64]{1,0:T(8,128)(2,1)S(1)}, u32[]{:S(2)}) copy-start(bf16[96,64]{1,0:T(8,128)(2,1)S(1)} %collective-permute-done.41) | copy-start | bytes 36868
  174.1 30.9 %collective-permute-start.43 = (bf16[512,768]{1,0:T(8,128)(2,1)S(1)}, bf16[512,768]{1,0:T(8,128)(2,1)}, u32[]{:S(2)}, u32[]{:S(2)}) collective-permute-start(bf16[512,768]{1,0:T(8,128)(2,1)S(1)} %fusion.6), channel_id=1, source_target_pairs={{1,16},{3,18},{5,20},{7,22},{9,24},{11,26},{13,28},{15,30},{16,1},... | collective-permute-start | bytes 2359304 | tf_op jit(solution)/shard_map/ppermute | solution.py:51
  196.5 8.5 %collective-permute-start.42 = (bf16[96,1344]{1,0:T(8,128)(2,1)S(1)}, bf16[96,1344]{1,0:T(8,128)(2,1)S(1)}, u32[]{:S(2)}, u32[]{:S(2)}) collective-permute-start(bf16[96,1344]{1,0:T(8,128)(2,1)S(1)} %concatenate.44), channel_id=1, source_target_pairs={{0,8},{8,0},{16,24},{24,16},{1,9},{9,1},{17,25},{25,17},{2,10},{10... | collective-permute-start | bytes 774152 | tf_op jit(solution)/shard_map/ppermute | solution.py:34
  197.5 11.1 %copy-start.31 = (bf16[96,64]{1,0:T(8,128)(2,1)S(1)}, bf16[96,64]{1,0:T(8,128)(2,1)}, u32[]{:S(2)}) copy-start(bf16[96,64]{1,0:T(8,128)(2,1)} %copy-done.30) | copy-start | bytes 36868
  197.5 11.1 %copy-start.35 = (bf16[96,64]{1,0:T(8,128)(2,1)S(1)}, bf16[96,64]{1,0:T(8,128)(2,1)}, u32[]{:S(2)}) copy-start(bf16[96,64]{1,0:T(8,128)(2,1)} %copy-done.34) | copy-start | bytes 36868
  205.4 13.6 %collective-permute-start.44 = (bf16[96,1216]{1,0:T(8,128)(2,1)S(1)}, bf16[96,1216]{1,0:T(8,128)(2,1)S(1)}, u32[]{:S(2)}, u32[]{:S(2)}) collective-permute-start(bf16[96,1216]{1,0:T(8,128)(2,1)S(1)} %concatenate.46), channel_id=1, source_target_pairs={{0,16},{8,24},{16,0},{24,8},{1,17},{9,25},{17,1},{25,9},{2,18},{10... | collective-permute-start | bytes 700424 | tf_op jit(solution)/shard_map/ppermute | solution.py:34
  206.6 12.8 %collective-permute-start.45 = (bf16[96,1536]{1,0:T(8,128)(2,1)S(1)}, bf16[96,1536]{1,0:T(8,128)(2,1)S(1)}, u32[]{:S(2)}, u32[]{:S(2)}) collective-permute-start(bf16[96,1536]{1,0:T(8,128)(2,1)S(1)} %add_convert_fusion.3), channel_id=1, source_target_pairs={{0,8},{8,0},{16,24},{24,16},{1,9},{9,1},{17,25},{25,17},{2,10},{10... | collective-permute-start | bytes 884744 | tf_op jit(solution)/shard_map/ppermute | solution.py:34
  219.1 9.2 %collective-permute-start.47 = (bf16[96,960]{1,0:T(8,128)(2,1)S(1)}, bf16[96,960]{1,0:T(8,128)(2,1)S(1)}, u32[]{:S(2)}, u32[]{:S(2)}) collective-permute-start(bf16[96,960]{1,0:T(8,128)(2,1)S(1)} %add_convert_fusion.5), channel_id=1, source_target_pairs={{0,8},{8,0},{16,24},{24,16},{1,9},{9,1},{17,25},{25,17},{2,10},{10... | collective-permute-start | bytes 552968 | tf_op jit(solution)/shard_map/ppermute | solution.py:34
  221.3 6.5 %collective-permute-start.46 = (bf16[96,256]{1,0:T(8,128)(2,1)S(1)}, bf16[96,256]{1,0:T(8,128)(2,1)S(1)}, u32[]{:S(2)}, u32[]{:S(2)}) collective-permute-start(bf16[96,256]{1,0:T(8,128)(2,1)S(1)} %pad_maximum_fusion.4), channel_id=1, source_target_pairs={{1,16},{3,18},{5,20},{7,22},{9,24},{11,26},{13,28},{15,30},{16,1},... | collective-permute-start | bytes 147464 | tf_op jit(solution)/shard_map/ppermute | solution.py:51
  (35 other events, 125.8 us)

commit v5 on v4

--- a/solution.py
+++ b/solution.py
@@ -26,6 +26,7 @@
 VMEM_ASK = 56 * 2**20
 VMEM_ROOM = 56 * 2**20
 VMEM_LESS = 44 * 2**20
+VMEM_LITTLE = 24 * 2**20
 COST_SCALE = 0.4
 
 
@@ -664,7 +665,37 @@
     args = [term, got, small, small_got]
     return call(
         pair_small_kernel, 1, (1,), [(at, in_smem())] + [(v, whole(v)) for v in args],
-        [(out, whole(out))] * n, [],
+        [(out, whole(out))] * n, [], VMEM_LITTLE,
+    )
+
+
+def chip_sum_kernel(odd, *refs):
+    n = len(refs) - 5
+    terms, halos, (sent, keep, small_sum) = refs[:n], refs[n : n + 2], refs[n + 2 :]
+    total = terms[0][:, :WA].astype(F32)
+    for term in terms[1:]:
+        total = total + term[:, :WA].astype(F32)
+    low = total.astype(BF)
+    cut = WA // 2
+    right_kept = odd[0] > 0
+    sent[:, :cut] = jnp.where(right_kept, low[:, :cut], low[:, cut:])
+    keep[...] = jnp.where(right_kept, low[:, cut:], low[:, :cut])
+    sums = [t[:, WA : WA + LANES].astype(F32) + t[:, WA + LANES :].astype(F32) for t in terms]
+    while len(sums) > 1:
+        sums = [sums[k] + sums[k + 1] for k in range(0, len(sums), 2)]
+    high, rest = pieces2(sums[0])
+    small_sum[...] = high.astype(F32) + rest.astype(F32)
+    sent[:, cut:] = jnp.concatenate([high, rest] + [v[...] for v in halos], axis=1)
+
+
+def run_chip_sum(odd, terms, halos):
+    rows = terms[0].shape[0]
+    width = WA // 2 + 2 * LANES + 2 * halos[0].shape[1]
+    outs = [shape((rows, width), BF), shape((rows, WA // 2), BF), shape((rows, LANES), F32)]
+    return call(
+        chip_sum_kernel, 1, (1,),
+        [(odd, in_smem())] + [(v, whole(v)) for v in list(terms) + halos],
+        [(v, whole(v)) for v in outs], [], VMEM_LITTLE,
     )
 
 
@@ -1216,25 +1247,33 @@
     halo_part = norm_back(after(from_a, a_pairs[0])[rows:], tok_halo, gain)
     halo_part = halo_part.reshape(nb, HALO, DM)[:, HALO - KC :].astype(BF).reshape(k_rows, -1)
     halos = [halo_part, trade(halo_part, "shard", 1)]
-    *a_far, zo_got, halos[1] = after_all(a_far + [zo_got, halos[1]])
-    a_own = chip_sum(a_pairs[0][:, :WA], [v[:, :WA] for v in a_far])
-    sums = [join2(v[:, WA:]) for v in [a_pairs[0]] + a_far]
-    while len(sums) > 1:
-        sums = [sums[k] + sums[k + 1] for k in range(0, len(sums), 2)]
-    small = sums[0]
-    a_keep, a_give = head_split(a_own)
-    cut, edge = a_keep.shape[1], a_keep.shape[1] + 2 * small.shape[1]
-    total = a_keep.astype(F32)
+    *a_far, token_got, halos[1] = after_all(a_far + [token_got, halos[1]])
+    cut, edge = WA // 2, WA // 2 + 2 * SUM_ROWS * LANES // k_rows
+    if k_rows % 32:
+        a_own = chip_sum(a_pairs[0][:, :WA], [v[:, :WA] for v in a_far])
+        sums = [join2(v[:, WA:]) for v in [a_pairs[0]] + a_far]
+        while len(sums) > 1:
+            sums = [sums[k] + sums[k + 1] for k in range(0, len(sums), 2)]
+        small = sums[0]
+        total, a_give = head_split(a_own)
+        parts = split2(small)
+        sent = jnp.concatenate([a_give, parts] + (halos if half > 1 else []), axis=1)
+        small = join2(parts)
+    else:
+        odd = (head_at % 2).astype(jnp.int32).reshape(1)
+        sent, total, small = run_chip_sum(odd, [a_pairs[0]] + a_far, halos)
+    own_total = total = total.astype(F32)
     bits = [b for b in (1, 2, 4, 8, 16) if b < n_head]
     for bit in bits:
         if bit > 1:
             a_give = total.astype(BF)
             total = a_give.astype(F32)
-        parts = split2(small)
-        sent = jnp.concatenate([a_give, parts] + (halos if bit < half else []), axis=1)
+            parts = split2(small)
+            small = join2(parts)
+            sent = jnp.concatenate([a_give, parts] + (halos if bit < half else []), axis=1)
         sent = trade(sent, "head", bit)
         if bit == 1:
-            sent, token_got, zo_got = after_all([sent, token_got, zo_got])
+            sent, zo_got = after_all([sent, zo_got])
             zo_half = head_add(zo_half, zo_got)
             for more in bits[2:]:
                 zo_half = head_add(zo_half, trade(zo_half, "head", more))
@@ -1242,7 +1281,7 @@
         if bit < half:
             halos = halos + jnp.split(sent[:, edge:], len(halos), axis=1)
         total = total + sent[:, :cut].astype(F32)
-        small = join2(parts) + join2(sent[:, cut:edge])
+        small = small + join2(sent[:, cut:edge])
     low = total.astype(BF)
     other = trade(low, "head", 1)
     halos, small, zo_other = after_all([jnp.concatenate(halos, axis=1), small, zo_other], low)
@@ -1279,7 +1318,7 @@
     token_grad = token_grad.at[:, CH - KC :].set(
         (token_grad[:, CH - KC :].astype(F32) + halo_back).astype(BF)
     ).reshape(rows, DM)
-    mixed = jnp.where(stay, mixed, after(mixed_got, a_own))
+    mixed = jnp.where(stay, mixed, after(mixed_got, own_total))
 
     in_grad = jnp.concatenate([zo_grad[:, :DI], a_grad[:, : XBC + NH]], axis=1)
     out_grad = jnp.concatenate([zo_grad[:, DI : DI + DM], zo_grad[:, DI + DM :]], axis=0)

time: 232 us -> 230 us (level)
  waiting for transfers between devices: 51.4 us -> 61.3 us
  local copies, waits for them, and re-layouts: 22.8 us -> 18 us
  starting transfers between devices: 47.5 us -> 43.2 us
  Pallas kernels: 79.2 us -> 76.4 us
    ppermute x5, waiting for transfers between devices: 2.22 us -> 10.5 us  [move_home(): return lax.ppermute(value, ('head', 'shard'), pairs)]
    ppermute x40, starting transfers between devices: 24.2 us -> 20.3 us  [trade(): return lax.ppermute(value, axis, [(i, i ^ bit) for i in range(size)])]
    unnamed x98 -> x72, local copies, waits for them, and re-layouts: 8.07 us -> 4.51 us
    pallas_call x8 -> x9, Pallas kernels: 79.2 us -> 76.4 us  [call(): pl.pallas_call(kernel, grid=grid, out_shape=[o for o, _ in outs], in_spec...]
  transfers between devices with their start and end apart: 48 -> 48, of which waited for: 19 -> 22; matrix products, arithmetic and copies ran while one was open for 15% -> 15% of each run, Pallas kernels for 28% -> 27%
where the time goes in v5:
time: 230 us; the launch traced here: 229 us
  Pallas kernels  76.4 us (33%)
  waiting for transfers between devices  61.3 us (27%)
  starting transfers between devices  43.2 us (19%)
  other arithmetic  19.6 us (9%)
  local copies, waits for them, and re-layouts  18 us (8%)
  matrix products  8.12 us (4%)
    pallas_call x9, Pallas kernels, call(): pl.pallas_call(kernel, grid=grid, out_shape=[o for o, _ in outs], in_spec...  76.4 us
    ppermute x40, waiting for transfers between devices, trade(): return lax.ppermute(value, axis, [(i, i ^ bit) for i in range(size)])  50.1 us
    ppermute x5, starting transfers between devices, move_home(): return lax.ppermute(value, ('head', 'shard'), pairs)  21 us
    ppermute x40, starting transfers between devices, trade(): return lax.ppermute(value, axis, [(i, i ^ bit) for i in range(size)])  20.3 us
    ppermute x5, waiting for transfers between devices, move_home(): return lax.ppermute(value, ('head', 'shard'), pairs)  10.5 us
    dot_general x1, matrix products, dot_tn(): lax.dot_general(a, b, (((0,), (0,)), ((), ())), preferred_element_type=F32)  4.67 us
  transfers between devices with their start and end apart: 48, of which 22 were waited for; matrix products, arithmetic and copies ran while one was open for 15% of the time, Pallas kernels for 27%

profile of v5, /device:TPU:1, one launch (start us, length us, event | category | flops | bytes accessed | tf_op | source)
XLA Modules:
  0.0 228.8 jit_solution(2405827965399453740)
XLA Ops:
  0.7 1.1 slice.120
  1.8 0.8 copy.31
  2.7 3.1 %collective-permute-start.1 = (bf16[96,1920]{1,0:T(8,128)(2,1)S(1)}, bf16[96,1920]{1,0:T(8,128)(2,1)S(1)}, u32[]{:S(2)}, u32[]{:S(2)}) collective-permute-start(bf16[96,1920]{1,0:T(8,128)(2,1)S(1)} %concatenate.39.refs_1_), channel_id=1, source_target_pairs={{0,6},{1,7},{2,4},{3,5},{4,2},{5,3},{6,0},{7,1},{8,14},{9,15},{10,... | collective-permute-start | bytes 1105928 | tf_op jit(solution)/shard_map/ppermute | solution.py:35
  6.2 1.2 collective-permute-start.4
  8.3 0.9 collective-permute-done
  9.3 4.7 %collective-permute-start.8 = (bf16[512,768]{1,0:T(8,128)(2,1)S(1)}, bf16[512,768]{1,0:T(8,128)(2,1)S(1)}, u32[]{:S(2)}, u32[]{:S(2)}) collective-permute-start(bf16[512,768]{1,0:T(8,128)(2,1)S(1)} %copy-done.16), channel_id=1, source_target_pairs={{1,16},{3,18},{5,20},{7,22},{9,24},{11,26},{13,28},{15,30},{16,1},... | collective-permute-start | bytes 2359304 | tf_op jit(solution)/shard_map/ppermute | solution.py:52
  14.0 0.7 broadcast_select_fusion.7
  16.9 1.1 compare_convert_fusion.refs_19_.refs_17_.refs_25_
  18.0 4.8 %collective-permute-done.2.refs_3_ = bf16[96,1920]{1,0:T(8,128)(2,1)} collective-permute-done((bf16[96,1920]{1,0:T(8,128)(2,1)S(1)}, bf16[96,1920]{1,0:T(8,128)(2,1)}, u32[]{:S(2)}, u32[]{:S(2)}) %collective-permute-start.2) | collective-permute-done | bytes 368672 | tf_op jit(solution)/shard_map/ppermute | solution.py:35
  23.6 1.0 compare_convert_fusion.1.refs_26_
  24.6 0.7 broadcast_in_dim.112
  25.4 0.7 broadcast_in_dim_reshape.3.refs_16_.refs_24_
  26.0 1.4 pad.17.refs_15_.refs_22_
  28.6 1.2 pad_bitcast_fusion
  29.8 2.2 collective-permute-done.8.refs_14_
  32.2 0.8 collective-permute-start.11
  33.0 1.1 collective-permute-start.9
  34.1 1.0 fusion.26
  35.8 6.3 %collective-permute-start.20 = (bf16[512,768]{1,0:T(8,128)(2,1)S(1)}, bf16[512,768]{1,0:T(8,128)(2,1)S(1)}, u32[]{:S(2)}, u32[]{:S(2)}) collective-permute-start(bf16[512,768]{1,0:T(8,128)(2,1)S(1)} %copy-done.4), channel_id=1, source_target_pairs={{1,16},{3,18},{5,20},{7,22},{9,24},{11,26},{13,28},{15,30},{16,1},... | collective-permute-start | bytes 2359304 | tf_op jit(solution)/shard_map/ppermute | solution.py:52
  42.2 2.2 collective-permute-start.13
  45.0 13.4 %shard_map.212 = (bf16[768,1920]{1,0:T(8,128)(2,1)}, bf16[512,768]{1,0:T(8,128)(2,1)}, bf16[16,768]{1,0:T(8,128)(2,1)}, bf16[528,768]{1,0:T(8,128)(2,1)}, bf16[7...) custom-call(s32[26]{0:T(128)} %pad_add_fusion.2.refs_0_, ...), custom_call_target="tpu_custom_call" | custom-call | flops 1 | bytes 20720000 | tf_op jit(solution)/shard_map/pallas_call | solution.py:235
  58.5 6.5 %shard_map.213.refs_9_ = f32[512,1536]{1,0:T(8,128)} custom-call(bf16[512,128]{1,0:T(8,128)(2,1)} %get-tuple-element.146.bs.refs_16_, bf16[512,128]{1,0:T(8,128)(2,1)} %get-tuple-element.147.cs.refs_10_, bf16[512,1536]{1,0:T(8,128)(2,1)} %get-tuple-element.148.xt.refs_15_, f32[512,128]{1,0:T(8,128)} %get-tuple-element.149.cum.refs_11_.refs_18_, ...), custom_call_target="tpu_custom_call" | custom-call | flops 1 | bytes 8880000 | tf_op jit(solution)/shard_map/pallas_call | solution.py:235
  65.0 2.1 collective-permute-done.14.refs_2_
  68.3 1.0 collective-permute-done.17.refs_5_
  69.4 0.7 collective-permute-done.18.refs_6_
  70.1 0.8 collective-permute-done.19.refs_7_
  71.0 0.8 collective-permute-done.16.refs_4_
  71.8 5.0 %shard_map.214 = (bf16[512,1536]{1,0:T(8,128)(2,1)S(1)}, bf16[512,1536]{1,0:T(8,128)(2,1)}, bf16[512,768]{1,0:T(8,128)(2,1)S(1)}, bf16[768,1536]{1,0:T(8,128)(2,1)}, bf16[1536,768]{1,0:T(8,128)(2,1)}) custom-call(s32[1]{0:T(128)} %bitcast.at, bf16[96,3072]{1,0:T(8,128)(2,1)S(1)} %pad_maximum_fusion.1.refs_0_, ...), custom_call_target="tpu_custom_call" | custom-call | flops 1 | bytes 1480000 | tf_op jit(solution)/shard_map/pallas_call | solution.py:235
  76.8 0.9 copy-done
  77.7 1.1 copy-done.2
  79.0 2.2 collective-permute-done.22.refs_4_.refs_8_
  81.3 0.9 copy-done.9
  82.2 14.4 %shard_map.215 = (bf16[2,128,1536]{2,1,0:T(8,128)(2,1)}, bf16[512,1536]{1,0:T(8,128)(2,1)}, f32[1,1536]{1,0:T(1,128)}, bf16[512,1536]{1,0:T(8,128)(2,1)}, bf16[5...) custom-call(s32[26]{0:T(128)} %pad_add_fusion.2.refs_0_, ...), custom_call_target="tpu_custom_call" | custom-call | flops 1 | bytes 23680000 | tf_op jit(solution)/shard_map/pallas_call | solution.py:235
  96.6 1.3 collective-permute-start.23
  97.8 7.7 %shard_map.216 = (bf16[4,96,3072]{2,1,0:T(8,128)(2,1)}, bf16[96,3072]{1,0:T(8,128)(2,1)}, bf16[96,3072]{1,0:T(8,128)(2,1)}, bf16[96,3072]{1,0:T(8,128)(2,1)}, bf16[96,3072]{1,0:T(8,128)(2,1)}) custom-call(s32[1]{0:T(128)} %bitcast.at, bf16[768,512]{1,0:T(8,128)(2,1)} %get-tuple-element.166.normal_t, bf16[512,1536]{1,0:T(8,128)(2,1)} %get-tuple-element.208.dz, ...), custom_call_target="tpu_custom_call" | custom-call | flops 1 | bytes 1480000 | tf_op jit(solution)/shard_map/pallas_call | solution.py:235
  106.6 11.5 %shard_map.217 = (f32[512,1536]{1,0:T(8,128)}, f32[512,128]{1,0:T(8,128)}, f32[512,128]{1,0:T(8,128)}, bf16[512,768]{1,0:T(8,128)(2,1)}) custom-call(bf16[512,128]{1,0:T(8,128)(2,1)} %get-tuple-element.146.bs.refs_16_, bf16[512,128]{1,0:T(8,128)(2,1)} %get-tuple-element.147.cs.refs_10_, bf16[512,1536]{1,0:T(8,128)(2,1)} %get-tuple-element.148.xt.refs_15_, ...), custom_call_target="tpu_custom_call" | custom-call | flops 1 | bytes 1480000 | tf_op jit(solution)/shard_map/pallas_call | solution.py:235
  118.1 2.2 add_convert_fusion
  120.3 1.3 dynamic-slice_bitcast_fusion.1
  122.5 1.6 collective-permute-done.28.refs_4_
  124.1 3.2 %collective-permute-start.29 = (bf16[512,768]{1,0:T(8,128)(2,1)}, bf16[512,768]{1,0:T(8,128)(2,1)S(1)}, u32[]{:S(2)}, u32[]{:S(2)}) collective-permute-start(bf16[512,768]{1,0:T(8,128)(2,1)} %get-tuple-element.189), channel_id=1, source_target_pairs={{1,16},{3,18},{5,20},{7,22},{9,24},{11,26},{13,28},{15,30},{16,1},... | collective-permute-start | bytes 2359304 | tf_op jit(solution)/shard_map/ppermute | solution.py:52
  127.5 1.2 collective-permute-start.33
  128.8 1.2 collective-permute-start.34
  130.2 17.1 %shard_map.218 = (bf16[528,1920]{1,0:T(8,128)(2,1)}, f32[96,128]{1,0:T(8,128)}) custom-call(s32[26]{0:T(128)} %pad_add_fusion.2.refs_0_, bf16[2,128,1536]{2,1,0:T(8,128)(2,1)} %get-tuple-element.180.refs_1_, bf16[2,128,1536]{2,1,0:T(8,128)(2,1)} %copy-done.19, bf16[2,128,1536]{2,1,0:T(8,128)(2,1)} %collective-permute-done.30.refs_3_, ...), custom_call_target="tpu_custom_call" | custom-call | flops 1 | bytes 2960000 | tf_op jit(solution)/shard_map/pallas_call | solution.py:235
  147.4 4.7 %convolution_convert_fusion = bf16[768,1920]{1,0:T(8,128)(2,1)S(1)} fusion(bf16[528,768]{1,0:T(8,128)(2,1)S(1)} %copy-done.3, bf16[528,1920]{1,0:T(8,128)(2,1)} %get-tuple-element.210), kind=kOutput, calls=%fused_computation.1 | convolution fusion | flops 1558609920 | bytes 5787648 | tf_op jit(solution)/shard_map/dot_general | solution.py:182
  152.9 2.5 %collective-permute-done.34 = bf16[96,3072]{1,0:T(8,128)(2,1)S(1)} collective-permute-done((bf16[96,3072]{1,0:T(8,128)(2,1)}, bf16[96,3072]{1,0:T(8,128)(2,1)S(1)}, u32[]{:S(2)}, u32[]{:S(2)}) %collective-permute-start.34) | collective-permute-done | bytes 589856 | tf_op jit(solution)/shard_map/ppermute | solution.py:35
  156.4 1.9 fusion.28
  158.7 1.6 fusion.2
  161.4 3.2 %collective-permute-start.39 = (bf16[512,768]{1,0:T(8,128)(2,1)S(1)}, bf16[512,768]{1,0:T(8,128)(2,1)}, u32[]{:S(2)}, u32[]{:S(2)}) collective-permute-start(bf16[512,768]{1,0:T(8,128)(2,1)S(1)} %fusion.6), channel_id=1, source_target_pairs={{1,16},{3,18},{5,20},{7,22},{9,24},{11,26},{13,28},{15,30},{16,1},... | collective-permute-start | bytes 2359304 | tf_op jit(solution)/shard_map/ppermute | solution.py:52
  164.7 0.7 copy-done.22
  165.6 0.9 collective-permute-start.36
  167.0 1.3 collective-permute-start.38
  168.3 1.0 add_convert_fusion.3
  169.3 1.5 collective-permute-start.43
  170.8 2.1 broadcast_select_fusion.1
  172.9 3.5 %collective-permute-done.36.refs_1_ = bf16[96,2176]{1,0:T(8,128)(2,1)S(1)} collective-permute-done((bf16[96,2176]{1,0:T(8,128)(2,1)S(1)}, bf16[96,2176]{1,0:T(8,128)(2,1)S(1)}, u32[]{:S(2)}, u32[]{:S(2)}) %collective-permute-start.36) | collective-permute-done | bytes 417824 | tf_op jit(solution)/shard_map/ppermute | solution.py:35
  176.9 9.1 %collective-permute-done.38.refs_3_ = bf16[96,2176]{1,0:T(8,128)(2,1)S(1)} collective-permute-done((bf16[96,2176]{1,0:T(8,128)(2,1)S(1)}, bf16[96,2176]{1,0:T(8,128)(2,1)S(1)}, u32[]{:S(2)}, u32[]{:S(2)}) %collective-permute-start.38) | collective-permute-done | bytes 417824 | tf_op jit(solution)/shard_map/ppermute | solution.py:35
  185.9 7.8 %collective-permute-done.39 = bf16[512,768]{1,0:T(8,128)(2,1)} collective-permute-done((bf16[512,768]{1,0:T(8,128)(2,1)S(1)}, bf16[512,768]{1,0:T(8,128)(2,1)}, u32[]{:S(2)}, u32[]{:S(2)}) %collective-permute-start.39) | collective-permute-done | bytes 786464 | tf_op jit(solution)/shard_map/ppermute | solution.py:52
  194.2 2.1 broadcast_select_fusion
  196.3 6.4 %collective-permute-done.41 = bf16[96,1344]{1,0:T(8,128)(2,1)S(1)} collective-permute-done((bf16[96,1344]{1,0:T(8,128)(2,1)S(1)}, bf16[96,1344]{1,0:T(8,128)(2,1)S(1)}, u32[]{:S(2)}, u32[]{:S(2)}) %collective-permute-start.41) | collective-permute-done | bytes 258080 | tf_op jit(solution)/shard_map/ppermute | solution.py:35
  203.6 12.7 %collective-permute-done.44 = bf16[96,1216]{1,0:T(8,128)(2,1)S(1)} collective-permute-done((bf16[96,1216]{1,0:T(8,128)(2,1)S(1)}, bf16[96,1216]{1,0:T(8,128)(2,1)S(1)}, u32[]{:S(2)}, u32[]{:S(2)}) %collective-permute-start.44) | collective-permute-done | bytes 233504 | tf_op jit(solution)/shard_map/ppermute | solution.py:35
  218.6 3.6 %collective-permute-start.46 = (bf16[96,256]{1,0:T(8,128)(2,1)S(1)}, bf16[96,256]{1,0:T(8,128)(2,1)S(1)}, u32[]{:S(2)}, u32[]{:S(2)}) collective-permute-start(bf16[96,256]{1,0:T(8,128)(2,1)S(1)} %pad_maximum_fusion.4), channel_id=1, source_target_pairs={{1,16},{3,18},{5,20},{7,22},{9,24},{11,26},{13,28},{15,30},{16,1},... | collective-permute-start | bytes 147464 | tf_op jit(solution)/shard_map/ppermute | solution.py:52
  222.2 0.9 pad_maximum_fusion.2
  225.4 1.4 fusion.20
  226.9 1.3 multiply_reduce_fusion
  (208 shorter events, 21.4 us)
Async XLA Ops:
  0.7 8.6 %copy-start.16 = (bf16[512,768]{1,0:T(8,128)(2,1)S(1)}, bf16[512,768]{1,0:T(8,128)(2,1)}, u32[]{:S(2)}) copy-start(bf16[512,768]{1,0:T(8,128)(2,1)} %refs_13_.1) | copy-start | bytes 2359300
  1.8 25.6 %copy-start.30 = (f32[1792]{0:T(1024)S(1)}, f32[1792]{0:T(1024)}, u32[]{:S(2)}) copy-start(f32[1792]{0:T(1024)} %param.19) | copy-start | bytes 21508
  1.8 26.2 %copy-start.29 = (f32[1536]{0:T(1024)S(1)}, f32[1536]{0:T(1024)}, u32[]{:S(2)}) copy-start(f32[1536]{0:T(1024)} %param.23) | copy-start | bytes 18436
  2.7 39.5 %copy-start.15 = (bf16[96,1920]{1,0:T(8,128)(2,1)}, bf16[96,1920]{1,0:T(8,128)(2,1)S(1)}, u32[]{:S(2)}) copy-start(bf16[96,1920]{1,0:T(8,128)(2,1)S(1)} %concatenate.39.refs_1_) | copy-start | bytes 1105924
  2.7 33.1 %copy-start.4 = (bf16[512,768]{1,0:T(8,128)(2,1)S(1)}, bf16[512,768]{1,0:T(8,128)(2,1)}, u32[]{:S(2)}) copy-start(bf16[512,768]{1,0:T(8,128)(2,1)} %refs_9_.1) | copy-start | bytes 2359300
  2.7 39.4 %slice-start.1 = ((bf16[96,3352]{1,0:T(8,128)(2,1)}), bf16[96,1536]{1,0:T(8,128)(2,1)S(1)}, s32[]{:S(2)}) async-start(bf16[96,3352]{1,0:T(8,128)(2,1)} %param.17), calls=%async_computation.1 | async-start | bytes 589824 | tf_op jit(solution)/shard_map/slice | solution.py:1167
  2.7 14.2 %collective-permute-start.1 = (bf16[96,1920]{1,0:T(8,128)(2,1)S(1)}, bf16[96,1920]{1,0:T(8,128)(2,1)S(1)}, u32[]{:S(2)}, u32[]{:S(2)}) collective-permute-start(bf16[96,1920]{1,0:T(8,128)(2,1)S(1)} %concatenate.39.refs_1_), channel_id=1, source_target_pairs={{0,6},{1,7},{2,4},{3,5},{4,2},{5,3},{6,0},{7,1},{8,14},{9,15},{10,... | collective-permute-start | bytes 1105928 | tf_op jit(solution)/shard_map/ppermute | solution.py:35
  5.8 17.1 %collective-permute-start.2 = (bf16[96,1920]{1,0:T(8,128)(2,1)S(1)}, bf16[96,1920]{1,0:T(8,128)(2,1)}, u32[]{:S(2)}, u32[]{:S(2)}) collective-permute-start(bf16[96,1920]{1,0:T(8,128)(2,1)S(1)} %concatenate.39.refs_1_), channel_id=1, source_target_pairs={{0,4},{1,5},{2,6},{3,7},{4,0},{5,1},{6,2},{7,3},{8,12},{9,13},{10,... | collective-permute-start | bytes 1105928 | tf_op jit(solution)/shard_map/ppermute | solution.py:35
  6.0 17.3 %collective-permute-start.3 = (bf16[96,1920]{1,0:T(8,128)(2,1)S(1)}, bf16[96,1920]{1,0:T(8,128)(2,1)}, u32[]{:S(2)}, u32[]{:S(2)}) collective-permute-start(bf16[96,1920]{1,0:T(8,128)(2,1)S(1)} %concatenate.39.refs_1_), channel_id=1, source_target_pairs={{0,2},{1,3},{2,0},{3,1},{4,6},{5,7},{6,4},{7,5},{8,10},{9,11},{10,... | collective-permute-start | bytes 1105928 | tf_op jit(solution)/shard_map/ppermute | solution.py:35
  6.2 25.9 %collective-permute-start.4 = (bf16[96,1920]{1,0:T(8,128)(2,1)S(1)}, bf16[96,1920]{1,0:T(8,128)(2,1)}, u32[]{:S(2)}, u32[]{:S(2)}) collective-permute-start(bf16[96,1920]{1,0:T(8,128)(2,1)S(1)} %concatenate.39.refs_1_), channel_id=1, source_target_pairs={{0,1},{1,0},{2,3},{3,2},{4,5},{5,4},{6,7},{7,6},{8,9},{9,8},{10,11... | collective-permute-start | bytes 1105928 | tf_op jit(solution)/shard_map/ppermute | solution.py:35
  8.1 1.1 collective-permute-start
  9.3 22.8 %collective-permute-start.8 = (bf16[512,768]{1,0:T(8,128)(2,1)S(1)}, bf16[512,768]{1,0:T(8,128)(2,1)S(1)}, u32[]{:S(2)}, u32[]{:S(2)}) collective-permute-start(bf16[512,768]{1,0:T(8,128)(2,1)S(1)} %copy-done.16), channel_id=1, source_target_pairs={{1,16},{3,18},{5,20},{7,22},{9,24},{11,26},{13,28},{15,30},{16,1},... | collective-permute-start | bytes 2359304 | tf_op jit(solution)/shard_map/ppermute | solution.py:52
  16.9 25.3 %copy-start.21 = (bf16[96,1920]{1,0:T(8,128)(2,1)}, bf16[96,1920]{1,0:T(8,128)(2,1)S(1)}, u32[]{:S(2)}) copy-start(bf16[96,1920]{1,0:T(8,128)(2,1)S(1)} %collective-permute-done.1.refs_2_) | copy-start | bytes 1105924
  18.0 14.1 %collective-permute-start.5 = (bf16[96,1920]{1,0:T(8,128)(2,1)S(1)}, bf16[96,1920]{1,0:T(8,128)(2,1)}, u32[]{:S(2)}, u32[]{:S(2)}) collective-permute-start(bf16[96,1920]{1,0:T(8,128)(2,1)S(1)} %collective-permute-done.1.refs_2_), channel_id=1, source_target_pairs={{0,1},{1,0},{2,3},{3,2},{4,5},{5,4},{6,7},{7,6},{8,9},{9,8},{10,11... | collective-permute-start | bytes 1105928 | tf_op jit(solution)/shard_map/ppermute | solution.py:35
  22.8 9.3 %collective-permute-start.6 = (bf16[96,1920]{1,0:T(8,128)(2,1)}, bf16[96,1920]{1,0:T(8,128)(2,1)}, u32[]{:S(2)}, u32[]{:S(2)}) collective-permute-start(bf16[96,1920]{1,0:T(8,128)(2,1)} %collective-permute-done.2.refs_3_), channel_id=1, source_target_pairs={{0,1},{1,0},{2,3},{3,2},{4,5},{5,4},{6,7},{7,6},{8,9},{9,8},{10,11... | collective-permute-start | bytes 1105928 | tf_op jit(solution)/shard_map/ppermute | solution.py:35
  23.3 8.8 %collective-permute-start.7 = (bf16[96,1920]{1,0:T(8,128)(2,1)}, bf16[96,1920]{1,0:T(8,128)(2,1)}, u32[]{:S(2)}, u32[]{:S(2)}) collective-permute-start(bf16[96,1920]{1,0:T(8,128)(2,1)} %collective-permute-done.3.refs_4_), channel_id=1, source_target_pairs={{0,1},{1,0},{2,3},{3,2},{4,5},{5,4},{6,7},{7,6},{8,9},{9,8},{10,11... | collective-permute-start | bytes 1105928 | tf_op jit(solution)/shard_map/ppermute | solution.py:35
  32.0 12.9 %copy-start.17 = (bf16[512,768]{1,0:T(8,128)(2,1)}, bf16[512,768]{1,0:T(8,128)(2,1)S(1)}, u32[]{:S(2)}) copy-start(bf16[512,768]{1,0:T(8,128)(2,1)S(1)} %collective-permute-done.8.refs_14_) | copy-start | bytes 2359300
  32.1 12.9 %copy-start.24 = (bf16[16,768]{1,0:T(8,128)(2,1)}, bf16[16,768]{1,0:T(8,128)(2,1)S(1)}, u32[]{:S(2)}) copy-start(bf16[16,768]{1,0:T(8,128)(2,1)S(1)} %fusion.19.refs_9_) | copy-start | bytes 73732
  32.1 2.9 %collective-permute-start.10 = (bf16[16,768]{1,0:T(8,128)(2,1)S(1)}, bf16[16,768]{1,0:T(8,128)(2,1)S(1)}, u32[]{:S(2)}, u32[]{:S(2)}) collective-permute-start(bf16[16,768]{1,0:T(8,128)(2,1)S(1)} %fusion.19.refs_9_), channel_id=1, source_target_pairs={{0,1},{1,0},{2,3},{3,2},{4,5},{5,4},{6,7},{7,6},{8,9},{9,8},{10,11... | collective-permute-start | bytes 73736 | tf_op jit(solution)/shard_map/ppermute | solution.py:70
  32.2 3.4 %collective-permute-start.11 = (bf16[16,768]{1,0:T(8,128)(2,1)S(1)}, bf16[16,768]{1,0:T(8,128)(2,1)S(1)}, u32[]{:S(2)}, u32[]{:S(2)}) collective-permute-start(bf16[16,768]{1,0:T(8,128)(2,1)S(1)} %fusion.19.refs_9_), channel_id=1, source_target_pairs={{0,9},{1,8},{2,11},{3,10},{4,13},{5,12},{6,15},{7,14},{8,1},{9,0},... | collective-permute-start | bytes 73736 | tf_op jit(solution)/shard_map/ppermute | solution.py:70
  33.0 2.8 %collective-permute-start.9 = (bf16[16,768]{1,0:T(8,128)(2,1)S(1)}, bf16[16,768]{1,0:T(8,128)(2,1)S(1)}, u32[]{:S(2)}, u32[]{:S(2)}) collective-permute-start(bf16[16,768]{1,0:T(8,128)(2,1)S(1)} %fusion.19.refs_9_), channel_id=1, source_target_pairs={{0,8},{1,9},{2,10},{3,11},{4,12},{5,13},{6,14},{7,15},{8,0},{9,1},... | collective-permute-start | bytes 73736 | tf_op jit(solution)/shard_map/ppermute | solution.py:70
  35.1 9.9 %copy-start.25 = (bf16[16,768]{1,0:T(8,128)(2,1)}, bf16[16,768]{1,0:T(8,128)(2,1)S(1)}, u32[]{:S(2)}) copy-start(bf16[16,768]{1,0:T(8,128)(2,1)S(1)} %collective-permute-done.10.refs_11_) | copy-start | bytes 73732
  35.6 9.4 %copy-start.26 = (bf16[16,768]{1,0:T(8,128)(2,1)}, bf16[16,768]{1,0:T(8,128)(2,1)S(1)}, u32[]{:S(2)}) copy-start(bf16[16,768]{1,0:T(8,128)(2,1)S(1)} %collective-permute-done.11.refs_12_) | copy-start | bytes 73732
  35.8 9.2 %copy-start.27 = (bf16[16,768]{1,0:T(8,128)(2,1)}, bf16[16,768]{1,0:T(8,128)(2,1)S(1)}, u32[]{:S(2)}) copy-start(bf16[16,768]{1,0:T(8,128)(2,1)S(1)} %collective-permute-done.9.refs_10_) | copy-start | bytes 73732
  35.8 32.1 %collective-permute-start.20 = (bf16[512,768]{1,0:T(8,128)(2,1)S(1)}, bf16[512,768]{1,0:T(8,128)(2,1)S(1)}, u32[]{:S(2)}, u32[]{:S(2)}) collective-permute-start(bf16[512,768]{1,0:T(8,128)(2,1)S(1)} %copy-done.4), channel_id=1, source_target_pairs={{1,16},{3,18},{5,20},{7,22},{9,24},{11,26},{13,28},{15,30},{16,1},... | collective-permute-start | bytes 2359304 | tf_op jit(solution)/shard_map/ppermute | solution.py:52
  42.2 22.8 %collective-permute-start.13 = (bf16[96,3072]{1,0:T(8,128)(2,1)S(1)}, bf16[96,3072]{1,0:T(8,128)(2,1)S(1)}, u32[]{:S(2)}, u32[]{:S(2)}) collective-permute-start(bf16[96,3072]{1,0:T(8,128)(2,1)S(1)} %pad_maximum_fusion.1.refs_0_), channel_id=1, source_target_pairs={{0,6},{1,7},{2,4},{3,5},{4,2},{5,3},{6,0},{7,1},{8,14},{9,15},{10,... | collective-permute-start | bytes 1769480 | tf_op jit(solution)/shard_map/ppermute | solution.py:35
  44.5 22.7 %collective-permute-start.14 = (bf16[96,3072]{1,0:T(8,128)(2,1)S(1)}, bf16[96,3072]{1,0:T(8,128)(2,1)S(1)}, u32[]{:S(2)}, u32[]{:S(2)}) collective-permute-start(bf16[96,3072]{1,0:T(8,128)(2,1)S(1)} %pad_maximum_fusion.1.refs_0_), channel_id=1, source_target_pairs={{0,4},{1,5},{2,6},{3,7},{4,0},{5,1},{6,2},{7,3},{8,12},{9,13},{10,... | collective-permute-start | bytes 1769480 | tf_op jit(solution)/shard_map/ppermute | solution.py:35
  44.7 22.6 %collective-permute-start.15 = (bf16[96,3072]{1,0:T(8,128)(2,1)S(1)}, bf16[96,3072]{1,0:T(8,128)(2,1)S(1)}, u32[]{:S(2)}, u32[]{:S(2)}) collective-permute-start(bf16[96,3072]{1,0:T(8,128)(2,1)S(1)} %pad_maximum_fusion.1.refs_0_), channel_id=1, source_target_pairs={{0,2},{1,3},{2,0},{3,1},{4,6},{5,7},{6,4},{7,5},{8,10},{9,11},{10,... | collective-permute-start | bytes 1769480 | tf_op jit(solution)/shard_map/ppermute | solution.py:35
  58.4 20.5 %collective-permute-start.12 = (bf16[2,128,1664]{2,1,0:T(8,128)(2,1)}, bf16[2,128,1664]{2,1,0:T(8,128)(2,1)S(1)}, u32[]{:S(2)}, u32[]{:S(2)}) collective-permute-start(bf16[2,128,1664]{2,1,0:T(8,128)(2,1)} %get-tuple-element.151.refs_1_.refs_5_), channel_id=1, source_target_pairs={{0,8},{8,0},{16,24},{24,16},{1,9},{9,1},{17,25},{25,17},{2,10},{10... | collective-permute-start | bytes 2555912 | tf_op jit(solution)/shard_map/ppermute | solution.py:35
  58.5 10.8 %copy-start.6 = (bf16[2,128,1664]{2,1,0:T(8,128)(2,1)S(1)}, bf16[2,128,1664]{2,1,0:T(8,128)(2,1)}, u32[]{:S(2)}) copy-start(bf16[2,128,1664]{2,1,0:T(8,128)(2,1)} %get-tuple-element.151.refs_1_.refs_5_) | copy-start | bytes 2555908
  58.5 13.3 %copy-start.3 = (bf16[528,768]{1,0:T(8,128)(2,1)S(1)}, bf16[528,768]{1,0:T(8,128)(2,1)}, u32[]{:S(2)}) copy-start(bf16[528,768]{1,0:T(8,128)(2,1)} %get-tuple-element.158.refs_8_) | copy-start | bytes 2433028
  67.3 2.0 collective-permute-start.17
  67.4 2.7 %collective-permute-start.18 = (bf16[96,3072]{1,0:T(8,128)(2,1)S(1)}, bf16[96,3072]{1,0:T(8,128)(2,1)S(1)}, u32[]{:S(2)}, u32[]{:S(2)}) collective-permute-start(bf16[96,3072]{1,0:T(8,128)(2,1)S(1)} %collective-permute-done.14.refs_2_), channel_id=1, source_target_pairs={{0,1},{1,0},{2,3},{3,2},{4,5},{5,4},{6,7},{7,6},{8,9},{9,8},{10,11... | collective-permute-start | bytes 1769480 | tf_op jit(solution)/shard_map/ppermute | solution.py:35
  67.8 3.2 %collective-permute-start.19 = (bf16[96,3072]{1,0:T(8,128)(2,1)S(1)}, bf16[96,3072]{1,0:T(8,128)(2,1)S(1)}, u32[]{:S(2)}, u32[]{:S(2)}) collective-permute-start(bf16[96,3072]{1,0:T(8,128)(2,1)S(1)} %collective-permute-done.15.refs_3_), channel_id=1, source_target_pairs={{0,1},{1,0},{2,3},{3,2},{4,5},{5,4},{6,7},{7,6},{8,9},{9,8},{10,11... | collective-permute-start | bytes 1769480 | tf_op jit(solution)/shard_map/ppermute | solution.py:35
  67.9 3.9 %collective-permute-start.16 = (bf16[96,3072]{1,0:T(8,128)(2,1)S(1)}, bf16[96,3072]{1,0:T(8,128)(2,1)S(1)}, u32[]{:S(2)}, u32[]{:S(2)}) collective-permute-start(bf16[96,3072]{1,0:T(8,128)(2,1)S(1)} %pad_maximum_fusion.1.refs_0_), channel_id=1, source_target_pairs={{0,1},{1,0},{2,3},{3,2},{4,5},{5,4},{6,7},{7,6},{8,9},{9,8},{10,11... | collective-permute-start | bytes 1769480 | tf_op jit(solution)/shard_map/ppermute | solution.py:35
  69.3 9.8 %collective-permute-start.21 = (bf16[2,128,1664]{2,1,0:T(8,128)(2,1)S(1)}, bf16[2,128,1664]{2,1,0:T(8,128)(2,1)S(1)}, u32[]{:S(2)}, u32[]{:S(2)}) collective-permute-start(bf16[2,128,1664]{2,1,0:T(8,128)(2,1)S(1)} %copy-done.6), channel_id=1, source_target_pairs={{0,1},{1,0},{2,3},{3,2},{4,5},{5,4},{6,7},{7,6},{8,9},{9,8},{10,11... | collective-permute-start | bytes 2555912 | tf_op jit(solution)/shard_map/ppermute | solution.py:35
  78.9 2.4 %collective-permute-start.22 = (bf16[2,128,1664]{2,1,0:T(8,128)(2,1)S(1)}, bf16[2,128,1664]{2,1,0:T(8,128)(2,1)S(1)}, u32[]{:S(2)}, u32[]{:S(2)}) collective-permute-start(bf16[2,128,1664]{2,1,0:T(8,128)(2,1)S(1)} %collective-permute-done.12.refs_2_.refs_6_), channel_id=1, source_target_pairs={{0,1},{1,0},{2,3},{3,2},{4,5},{5,4},{6,7},{7,6},{8,9},{9,8},{10,11... | collective-permute-start | bytes 2555912 | tf_op jit(solution)/shard_map/ppermute | solution.py:35
  96.6 21.5 %collective-permute-start.23 = (bf16[2,128,1536]{2,1,0:T(8,128)(2,1)}, bf16[2,128,1536]{2,1,0:T(8,128)(2,1)S(1)}, u32[]{:S(2)}, u32[]{:S(2)}) collective-permute-start(bf16[2,128,1536]{2,1,0:T(8,128)(2,1)} %get-tuple-element.180.refs_1_), channel_id=1, source_target_pairs={{0,8},{8,0},{16,24},{24,16},{1,9},{9,1},{17,25},{25,17},{2,10},{10... | collective-permute-start | bytes 2359304 | tf_op jit(solution)/shard_map/ppermute | solution.py:35
  105.5 12.5 %collective-permute-start.24 = (bf16[96,3072]{1,0:T(8,128)(2,1)}, bf16[96,3072]{1,0:T(8,128)(2,1)S(1)}, u32[]{:S(2)}, u32[]{:S(2)}) collective-permute-start(bf16[96,3072]{1,0:T(8,128)(2,1)} %get-tuple-element.170), channel_id=1, source_target_pairs={{0,1},{1,0},{2,3},{3,2},{4,5},{5,4},{6,7},{7,6},{8,9},{9,8},{10,11... | collective-permute-start | bytes 1769480 | tf_op jit(solution)/shard_map/ppermute | solution.py:35
  106.0 12.1 %collective-permute-start.25 = (bf16[96,3072]{1,0:T(8,128)(2,1)}, bf16[96,3072]{1,0:T(8,128)(2,1)S(1)}, u32[]{:S(2)}, u32[]{:S(2)}) collective-permute-start(bf16[96,3072]{1,0:T(8,128)(2,1)} %get-tuple-element.171), channel_id=1, source_target_pairs={{0,1},{1,0},{2,3},{3,2},{4,5},{5,4},{6,7},{7,6},{8,9},{9,8},{10,11... | collective-permute-start | bytes 1769480 | tf_op jit(solution)/shard_map/ppermute | solution.py:35
  106.0 12.0 %collective-permute-start.26 = (bf16[96,3072]{1,0:T(8,128)(2,1)}, bf16[96,3072]{1,0:T(8,128)(2,1)}, u32[]{:S(2)}, u32[]{:S(2)}) collective-permute-start(bf16[96,3072]{1,0:T(8,128)(2,1)} %get-tuple-element.172), channel_id=1, source_target_pairs={{0,1},{1,0},{2,3},{3,2},{4,5},{5,4},{6,7},{7,6},{8,9},{9,8},{10,11... | collective-permute-start | bytes 1769480 | tf_op jit(solution)/shard_map/ppermute | solution.py:35
  106.5 11.6 %collective-permute-start.27 = (bf16[96,3072]{1,0:T(8,128)(2,1)}, bf16[96,3072]{1,0:T(8,128)(2,1)}, u32[]{:S(2)}, u32[]{:S(2)}) collective-permute-start(bf16[96,3072]{1,0:T(8,128)(2,1)} %get-tuple-element.173), channel_id=1, source_target_pairs={{0,1},{1,0},{2,3},{3,2},{4,5},{5,4},{6,7},{7,6},{8,9},{9,8},{10,11... | collective-permute-start | bytes 1769480 | tf_op jit(solution)/shard_map/ppermute | solution.py:35
  106.6 11.5 %copy-start.13 = (bf16[4,96,3072]{2,1,0:T(8,128)(2,1)S(1)}, bf16[4,96,3072]{2,1,0:T(8,128)(2,1)}, u32[]{:S(2)}) copy-start(bf16[4,96,3072]{2,1,0:T(8,128)(2,1)} %get-tuple-element.183) | copy-start | bytes 7077892
  121.6 2.5 %collective-permute-start.28 = (bf16[2,128,1536]{2,1,0:T(8,128)(2,1)S(1)}, bf16[2,128,1536]{2,1,0:T(8,128)(2,1)}, u32[]{:S(2)}, u32[]{:S(2)}) collective-permute-start(bf16[2,128,1536]{2,1,0:T(8,128)(2,1)S(1)} %collective-permute-done.23.refs_2_), channel_id=1, source_target_pairs={{0,1},{1,0},{2,3},{3,2},{4,5},{5,4},{6,7},{7,6},{8,9},{9,8},{10,11... | collective-permute-start | bytes 2359304 | tf_op jit(solution)/shard_map/ppermute | solution.py:35
  122.3 7.9 %collective-permute-start.30 = (bf16[2,128,1536]{2,1,0:T(8,128)(2,1)S(1)}, bf16[2,128,1536]{2,1,0:T(8,128)(2,1)}, u32[]{:S(2)}, u32[]{:S(2)}) collective-permute-start(bf16[2,128,1536]{2,1,0:T(8,128)(2,1)S(1)} %copy-done.18), channel_id=1, source_target_pairs={{0,1},{1,0},{2,3},{3,2},{4,5},{5,4},{6,7},{7,6},{8,9},{9,8},{10,11... | collective-permute-start | bytes 2359304 | tf_op jit(solution)/shard_map/ppermute | solution.py:35
  124.1 23.2 %collective-permute-start.29 = (bf16[512,768]{1,0:T(8,128)(2,1)}, bf16[512,768]{1,0:T(8,128)(2,1)S(1)}, u32[]{:S(2)}, u32[]{:S(2)}) collective-permute-start(bf16[512,768]{1,0:T(8,128)(2,1)} %get-tuple-element.189), channel_id=1, source_target_pairs={{1,16},{3,18},{5,20},{7,22},{9,24},{11,26},{13,28},{15,30},{16,1},... | collective-permute-start | bytes 2359304 | tf_op jit(solution)/shard_map/ppermute | solution.py:52
  127.5 25.3 %collective-permute-start.33 = (bf16[96,3072]{1,0:T(8,128)(2,1)}, bf16[96,3072]{1,0:T(8,128)(2,1)S(1)}, u32[]{:S(2)}, u32[]{:S(2)}) collective-permute-start(bf16[96,3072]{1,0:T(8,128)(2,1)} %get-tuple-element.241), channel_id=1, source_target_pairs={{0,2},{1,3},{2,0},{3,1},{4,6},{5,7},{6,4},{7,5},{8,10},{9,11},{10,... | collective-permute-start | bytes 1769480 | tf_op jit(solution)/shard_map/ppermute | solution.py:35
  128.8 26.6 %collective-permute-start.34 = (bf16[96,3072]{1,0:T(8,128)(2,1)}, bf16[96,3072]{1,0:T(8,128)(2,1)S(1)}, u32[]{:S(2)}, u32[]{:S(2)}) collective-permute-start(bf16[96,3072]{1,0:T(8,128)(2,1)} %get-tuple-element.240), channel_id=1, source_target_pairs={{0,4},{1,5},{2,6},{3,7},{4,0},{5,1},{6,2},{7,3},{8,12},{9,13},{10,... | collective-permute-start | bytes 1769480 | tf_op jit(solution)/shard_map/ppermute | solution.py:35
  130.0 25.4 %collective-permute-start.35 = (bf16[96,3072]{1,0:T(8,128)(2,1)}, bf16[96,3072]{1,0:T(8,128)(2,1)S(1)}, u32[]{:S(2)}, u32[]{:S(2)}) collective-permute-start(bf16[96,3072]{1,0:T(8,128)(2,1)} %get-tuple-element.239), channel_id=1, source_target_pairs={{0,6},{1,7},{2,4},{3,5},{4,2},{5,3},{6,0},{7,1},{8,14},{9,15},{10,... | collective-permute-start | bytes 1769480 | tf_op jit(solution)/shard_map/ppermute | solution.py:35
  152.2 8.6 %collective-permute-start.31 = (bf16[4,96,1920]{2,1,0:T(8,128)(2,1)S(1)}, bf16[4,96,1920]{2,1,0:T(8,128)(2,1)S(1)}, u32[]{:S(2)}, u32[]{:S(2)}) collective-permute-start(bf16[4,96,1920]{2,1,0:T(8,128)(2,1)S(1)} %dynamic-slice_bitcast_fusion), channel_id=1, source_target_pairs={{0,1},{1,0},{2,3},{3,2},{4,5},{5,4},{6,7},{7,6},{8,9},{9,8},{10,11... | collective-permute-start | bytes 4423688 | tf_op jit(solution)/shard_map/ppermute | solution.py:35
  152.8 8.0 %collective-permute-start.32 = (f32[96,128]{1,0:T(8,128)S(1)}, f32[96,128]{1,0:T(8,128)S(1)}, u32[]{:S(2)}, u32[]{:S(2)}) collective-permute-start(f32[96,128]{1,0:T(8,128)S(1)} %copy-done.5), channel_id=1, source_target_pairs={{0,1},{1,0},{2,3},{3,2},{4,5},{5,4},{6,7},{7,6},{8,9},{9,8},{10,11... | collective-permute-start | bytes 147464 | tf_op jit(solution)/shard_map/ppermute | solution.py:35
  155.8 8.9 %collective-permute-start.42 = (bf16[96,1536]{1,0:T(8,128)(2,1)S(1)}, bf16[96,1536]{1,0:T(8,128)(2,1)S(1)}, u32[]{:S(2)}, u32[]{:S(2)}) collective-permute-start(bf16[96,1536]{1,0:T(8,128)(2,1)S(1)} %constant_dynamic-slice_fusion), channel_id=1, source_target_pairs={{0,8},{8,0},{16,24},{24,16},{1,9},{9,1},{17,25},{25,17},{2,10},{10... | collective-permute-start | bytes 884744 | tf_op jit(solution)/shard_map/ppermute | solution.py:35
  161.4 32.3 %collective-permute-start.39 = (bf16[512,768]{1,0:T(8,128)(2,1)S(1)}, bf16[512,768]{1,0:T(8,128)(2,1)}, u32[]{:S(2)}, u32[]{:S(2)}) collective-permute-start(bf16[512,768]{1,0:T(8,128)(2,1)S(1)} %fusion.6), channel_id=1, source_target_pairs={{1,16},{3,18},{5,20},{7,22},{9,24},{11,26},{13,28},{15,30},{16,1},... | collective-permute-start | bytes 2359304 | tf_op jit(solution)/shard_map/ppermute | solution.py:52
  165.5 3.8 %collective-permute-start.40 = (bf16[96,64]{1,0:T(8,128)(2,1)S(1)}, bf16[96,64]{1,0:T(8,128)(2,1)S(1)}, u32[]{:S(2)}, u32[]{:S(2)}) collective-permute-start(bf16[96,64]{1,0:T(8,128)(2,1)S(1)} %reshape.318.refs_4_), channel_id=1, source_target_pairs={{0,1},{1,0},{2,3},{3,2},{4,5},{5,4},{6,7},{7,6},{8,9},{9,8},{10,11... | collective-permute-start | bytes 36872 | tf_op jit(solution)/shard_map/ppermute | solution.py:35
  165.6 10.8 %collective-permute-start.36 = (bf16[96,2176]{1,0:T(8,128)(2,1)S(1)}, bf16[96,2176]{1,0:T(8,128)(2,1)S(1)}, u32[]{:S(2)}, u32[]{:S(2)}) collective-permute-start(bf16[96,2176]{1,0:T(8,128)(2,1)S(1)} %get-tuple-element.215), channel_id=1, source_target_pairs={{0,2},{1,3},{2,0},{3,1},{4,6},{5,7},{6,4},{7,5},{8,10},{9,11},{10,... | collective-permute-start | bytes 1253384 | tf_op jit(solution)/shard_map/ppermute | solution.py:35
  166.4 10.5 %collective-permute-start.37 = (bf16[96,2176]{1,0:T(8,128)(2,1)S(1)}, bf16[96,2176]{1,0:T(8,128)(2,1)S(1)}, u32[]{:S(2)}, u32[]{:S(2)}) collective-permute-start(bf16[96,2176]{1,0:T(8,128)(2,1)S(1)} %get-tuple-element.216), channel_id=1, source_target_pairs={{0,4},{1,5},{2,6},{3,7},{4,0},{5,1},{6,2},{7,3},{8,12},{9,13},{10,... | collective-permute-start | bytes 1253384 | tf_op jit(solution)/shard_map/ppermute | solution.py:35
  167.0 18.9 %collective-permute-start.38 = (bf16[96,2176]{1,0:T(8,128)(2,1)S(1)}, bf16[96,2176]{1,0:T(8,128)(2,1)S(1)}, u32[]{:S(2)}, u32[]{:S(2)}) collective-permute-start(bf16[96,2176]{1,0:T(8,128)(2,1)S(1)} %get-tuple-element.217), channel_id=1, source_target_pairs={{0,6},{1,7},{2,4},{3,5},{4,2},{5,3},{6,0},{7,1},{8,14},{9,15},{10,... | collective-permute-start | bytes 1253384 | tf_op jit(solution)/shard_map/ppermute | solution.py:35
  169.3 26.9 %collective-permute-start.43 = (bf16[96,1536]{1,0:T(8,128)(2,1)S(1)}, bf16[96,1536]{1,0:T(8,128)(2,1)S(1)}, u32[]{:S(2)}, u32[]{:S(2)}) collective-permute-start(bf16[96,1536]{1,0:T(8,128)(2,1)S(1)} %add_convert_fusion.3), channel_id=1, source_target_pairs={{0,16},{8,24},{16,0},{24,8},{1,17},{9,25},{17,1},{25,9},{2,18},{10... | collective-permute-start | bytes 884744 | tf_op jit(solution)/shard_map/ppermute | solution.py:35
  194.1 8.6 %collective-permute-start.41 = (bf16[96,1344]{1,0:T(8,128)(2,1)S(1)}, bf16[96,1344]{1,0:T(8,128)(2,1)S(1)}, u32[]{:S(2)}, u32[]{:S(2)}) collective-permute-start(bf16[96,1344]{1,0:T(8,128)(2,1)S(1)} %get-tuple-element.228), channel_id=1, source_target_pairs={{0,8},{8,0},{16,24},{24,16},{1,9},{9,1},{17,25},{25,17},{2,10},{10... | collective-permute-start | bytes 774152 | tf_op jit(solution)/shard_map/ppermute | solution.py:35
  202.9 13.3 %collective-permute-start.44 = (bf16[96,1216]{1,0:T(8,128)(2,1)S(1)}, bf16[96,1216]{1,0:T(8,128)(2,1)S(1)}, u32[]{:S(2)}, u32[]{:S(2)}) collective-permute-start(bf16[96,1216]{1,0:T(8,128)(2,1)S(1)} %concatenate.42), channel_id=1, source_target_pairs={{0,16},{8,24},{16,0},{24,8},{1,17},{9,25},{17,1},{25,9},{2,18},{10... | collective-permute-start | bytes 700424 | tf_op jit(solution)/shard_map/ppermute | solution.py:35
  203.2 13.5 %collective-permute-start.45 = (bf16[96,1536]{1,0:T(8,128)(2,1)S(1)}, bf16[96,1536]{1,0:T(8,128)(2,1)S(1)}, u32[]{:S(2)}, u32[]{:S(2)}) collective-permute-start(bf16[96,1536]{1,0:T(8,128)(2,1)S(1)} %add_convert_fusion.2), channel_id=1, source_target_pairs={{0,8},{8,0},{16,24},{24,16},{1,9},{9,1},{17,25},{25,17},{2,10},{10... | collective-permute-start | bytes 884744 | tf_op jit(solution)/shard_map/ppermute | solution.py:35
  216.3 10.4 %collective-permute-start.47 = (bf16[96,960]{1,0:T(8,128)(2,1)S(1)}, bf16[96,960]{1,0:T(8,128)(2,1)S(1)}, u32[]{:S(2)}, u32[]{:S(2)}) collective-permute-start(bf16[96,960]{1,0:T(8,128)(2,1)S(1)} %add_convert_fusion.4), channel_id=1, source_target_pairs={{0,8},{8,0},{16,24},{24,16},{1,9},{9,1},{17,25},{25,17},{2,10},{10... | collective-permute-start | bytes 552968 | tf_op jit(solution)/shard_map/ppermute | solution.py:35
  216.8 8.2 %copy-start.11 = (f32[96,3072]{1,0:T(8,128)}, f32[96,3072]{1,0:T(8,128)S(1)}, u32[]{:S(2)}) copy-start(f32[96,3072]{1,0:T(8,128)S(1)} %maximum_convert_fusion) | copy-start | bytes 3538948
  218.6 6.3 %collective-permute-start.46 = (bf16[96,256]{1,0:T(8,128)(2,1)S(1)}, bf16[96,256]{1,0:T(8,128)(2,1)S(1)}, u32[]{:S(2)}, u32[]{:S(2)}) collective-permute-start(bf16[96,256]{1,0:T(8,128)(2,1)S(1)} %pad_maximum_fusion.4), channel_id=1, source_target_pairs={{1,16},{3,18},{5,20},{7,22},{9,24},{11,26},{13,28},{15,30},{16,1},... | collective-permute-start | bytes 147464 | tf_op jit(solution)/shard_map/ppermute | solution.py:52
  (22 other events, 51.4 us)

commit v6 on v5

--- a/solution.py
+++ b/solution.py
@@ -1243,7 +1243,8 @@
     a_far = chip_send(a_pairs)
     token_got = move_home(after(token_grad, a_pairs[0]))
     zo_half = head_add(zo_keep, after(zo_got, a_pairs[0]))
-    zo_got = trade(zo_half, "head", 2)
+    zo_parts = jnp.split(zo_half, 2, axis=1)
+    zo_first = trade(zo_parts[0], "head", 2)
     halo_part = norm_back(after(from_a, a_pairs[0])[rows:], tok_halo, gain)
     halo_part = halo_part.reshape(nb, HALO, DM)[:, HALO - KC :].astype(BF).reshape(k_rows, -1)
     halos = [halo_part, trade(halo_part, "shard", 1)]
@@ -1262,6 +1263,7 @@
     else:
         odd = (head_at % 2).astype(jnp.int32).reshape(1)
         sent, total, small = run_chip_sum(odd, [a_pairs[0]] + a_far, halos)
+    zo_second = after(zo_parts[1], sent)
     own_total = total = total.astype(F32)
     bits = [b for b in (1, 2, 4, 8, 16) if b < n_head]
     for bit in bits:
@@ -1273,7 +1275,8 @@
             sent = jnp.concatenate([a_give, parts] + (halos if bit < half else []), axis=1)
         sent = trade(sent, "head", bit)
         if bit == 1:
-            sent, zo_got = after_all([sent, zo_got])
+            sent, zo_first = after_all([sent, zo_first])
+            zo_got = jnp.concatenate([zo_first, trade(zo_second, "head", 2)], axis=1)
             zo_half = head_add(zo_half, zo_got)
             for more in bits[2:]:
                 zo_half = head_add(zo_half, trade(zo_half, "head", more))
@@ -1284,11 +1287,11 @@
         small = small + join2(sent[:, cut:edge])
     low = total.astype(BF)
     other = trade(low, "head", 1)
-    halos, small, zo_other = after_all([jnp.concatenate(halos, axis=1), small, zo_other], low)
-    zo_grad = head_join(zo_half, zo_other).astype(F32)
+    halos, small = after_all([jnp.concatenate(halos, axis=1), small], low)
     halos = jnp.where(stay, halos, move_home(halos))
     halos = jnp.split(halos, group_blocks // nb, axis=1)
-    other = after(other, *halos)
+    other, zo_other = after_all([other, zo_other], *halos)
+    zo_grad = head_join(zo_half, zo_other).astype(F32)
     a_grad = head_join(low, other).astype(F32)
     small = small.reshape(SUM_ROWS, LANES)
 

time: 230 us -> 228 us (level)
  other arithmetic: 19.6 us -> 16.3 us
    ppermute x40 -> x41, waiting for transfers between devices: 50.1 us -> 54.1 us  [trade(): return lax.ppermute(value, axis, [(i, i ^ bit) for i in range(size)])]
    ppermute x5, waiting for transfers between devices: 10.5 us -> 7.61 us  [move_home(): return lax.ppermute(value, ('head', 'shard'), pairs)]
    ppermute x40 -> x41, starting transfers between devices: 20.3 us -> 20.1 us  [trade(): return lax.ppermute(value, axis, [(i, i ^ bit) for i in range(size)])]
  transfers between devices with their start and end apart: 48 -> 49, of which waited for: 22 -> 21; matrix products, arithmetic and copies ran while one was open for 15% -> 13% of each run, Pallas kernels for 27% -> 27%
where the time goes in v6:
time: 228 us; the launch traced here: 227 us
  Pallas kernels  76.4 us (34%)
  waiting for transfers between devices  62.4 us (27%)
  starting transfers between devices  42.4 us (19%)
  local copies, waits for them, and re-layouts  19.2 us (8%)
  other arithmetic  16.3 us (7%)
  matrix products  7.87 us (3%)
    pallas_call x9, Pallas kernels, call(): pl.pallas_call(kernel, grid=grid, out_shape=[o for o, _ in outs], in_spec...  76.4 us
    ppermute x41, waiting for transfers between devices, trade(): return lax.ppermute(value, axis, [(i, i ^ bit) for i in range(size)])  54.1 us
    ppermute x5, starting transfers between devices, move_home(): return lax.ppermute(value, ('head', 'shard'), pairs)  20.3 us
    ppermute x41, starting transfers between devices, trade(): return lax.ppermute(value, axis, [(i, i ^ bit) for i in range(size)])  20.1 us
    ppermute x5, waiting for transfers between devices, move_home(): return lax.ppermute(value, ('head', 'shard'), pairs)  7.61 us
    unnamed x72, local copies, waits for them, and re-layouts  5.73 us
  transfers between devices with their start and end apart: 49, of which 21 were waited for; matrix products, arithmetic and copies ran while one was open for 13% of the time, Pallas kernels for 27%

profile of v6, /device:TPU:1, one launch (start us, length us, event | category | flops | bytes accessed | tf_op | source)
XLA Modules:
  0.0 226.8 jit_solution(988759302907402703)
XLA Ops:
  0.7 1.1 slice.120
  1.8 0.8 copy.31
  2.7 3.1 %collective-permute-start.1 = (bf16[96,1920]{1,0:T(8,128)(2,1)S(1)}, bf16[96,1920]{1,0:T(8,128)(2,1)S(1)}, u32[]{:S(2)}, u32[]{:S(2)}) collective-permute-start(bf16[96,1920]{1,0:T(8,128)(2,1)S(1)} %concatenate.42.refs_1_), channel_id=1, source_target_pairs={{0,6},{1,7},{2,4},{3,5},{4,2},{5,3},{6,0},{7,1},{8,14},{9,15},{10,... | collective-permute-start | bytes 1105928 | tf_op jit(solution)/shard_map/ppermute | solution.py:35
  6.2 1.2 collective-permute-start.4
  8.3 0.9 collective-permute-done
  9.3 4.7 %collective-permute-start.8 = (bf16[512,768]{1,0:T(8,128)(2,1)S(1)}, bf16[512,768]{1,0:T(8,128)(2,1)S(1)}, u32[]{:S(2)}, u32[]{:S(2)}) collective-permute-start(bf16[512,768]{1,0:T(8,128)(2,1)S(1)} %copy-done.15), channel_id=1, source_target_pairs={{1,16},{3,18},{5,20},{7,22},{9,24},{11,26},{13,28},{15,30},{16,1},... | collective-permute-start | bytes 2359304 | tf_op jit(solution)/shard_map/ppermute | solution.py:52
  14.0 0.7 broadcast_select_fusion.7
  16.9 1.1 compare_convert_fusion.refs_19_.refs_17_.refs_25_
  18.0 4.8 %collective-permute-done.2.refs_3_ = bf16[96,1920]{1,0:T(8,128)(2,1)} collective-permute-done((bf16[96,1920]{1,0:T(8,128)(2,1)S(1)}, bf16[96,1920]{1,0:T(8,128)(2,1)}, u32[]{:S(2)}, u32[]{:S(2)}) %collective-permute-start.2) | collective-permute-done | bytes 368672 | tf_op jit(solution)/shard_map/ppermute | solution.py:35
  23.6 1.0 compare_convert_fusion.1.refs_26_
  24.6 0.7 broadcast_in_dim.112
  25.4 0.7 broadcast_in_dim_reshape.3.refs_16_.refs_24_
  26.0 1.4 pad.17.refs_15_.refs_22_
  28.6 1.2 pad_bitcast_fusion
  29.8 2.2 collective-permute-done.8.refs_14_
  32.2 0.8 collective-permute-start.11
  33.0 1.1 collective-permute-start.9
  34.1 1.0 fusion.27
  35.8 6.3 %collective-permute-start.20 = (bf16[512,768]{1,0:T(8,128)(2,1)S(1)}, bf16[512,768]{1,0:T(8,128)(2,1)S(1)}, u32[]{:S(2)}, u32[]{:S(2)}) collective-permute-start(bf16[512,768]{1,0:T(8,128)(2,1)S(1)} %copy-done.4), channel_id=1, source_target_pairs={{1,16},{3,18},{5,20},{7,22},{9,24},{11,26},{13,28},{15,30},{16,1},... | collective-permute-start | bytes 2359304 | tf_op jit(solution)/shard_map/ppermute | solution.py:52
  42.2 2.2 collective-permute-start.13
  45.0 13.4 %shard_map.212 = (bf16[768,1920]{1,0:T(8,128)(2,1)}, bf16[512,768]{1,0:T(8,128)(2,1)}, bf16[16,768]{1,0:T(8,128)(2,1)}, bf16[528,768]{1,0:T(8,128)(2,1)}, bf16[7...) custom-call(s32[26]{0:T(128)} %pad_add_fusion.2.refs_0_, ...), custom_call_target="tpu_custom_call" | custom-call | flops 1 | bytes 20720000 | tf_op jit(solution)/shard_map/pallas_call | solution.py:235
  58.5 6.5 %shard_map.213.refs_9_ = f32[512,1536]{1,0:T(8,128)} custom-call(bf16[512,128]{1,0:T(8,128)(2,1)} %get-tuple-element.147.bs.refs_16_, bf16[512,128]{1,0:T(8,128)(2,1)} %get-tuple-element.148.cs.refs_10_, bf16[512,1536]{1,0:T(8,128)(2,1)} %get-tuple-element.149.xt.refs_15_, f32[512,128]{1,0:T(8,128)} %get-tuple-element.150.cum.refs_11_.refs_18_, ...), custom_call_target="tpu_custom_call" | custom-call | flops 1 | bytes 8880000 | tf_op jit(solution)/shard_map/pallas_call | solution.py:235
  65.0 2.1 collective-permute-done.14.refs_2_
  68.3 1.0 collective-permute-done.17.refs_5_
  69.4 0.7 collective-permute-done.18.refs_6_
  70.1 0.8 collective-permute-done.19.refs_7_
  71.0 0.8 collective-permute-done.16.refs_4_
  71.8 5.0 %shard_map.214 = (bf16[512,1536]{1,0:T(8,128)(2,1)S(1)}, bf16[512,1536]{1,0:T(8,128)(2,1)}, bf16[512,768]{1,0:T(8,128)(2,1)S(1)}, bf16[768,1536]{1,0:T(8,128)(2,1)}, bf16[1536,768]{1,0:T(8,128)(2,1)}) custom-call(s32[1]{0:T(128)} %bitcast.at, bf16[96,3072]{1,0:T(8,128)(2,1)S(1)} %pad_maximum_fusion.1.refs_0_, ...), custom_call_target="tpu_custom_call" | custom-call | flops 1 | bytes 1480000 | tf_op jit(solution)/shard_map/pallas_call | solution.py:235
  76.8 0.9 copy-done
  77.7 1.1 copy-done.2
  79.0 2.2 collective-permute-done.22.refs_4_.refs_8_
  81.3 0.9 copy-done.9
  82.2 14.4 %shard_map.215 = (bf16[2,128,1536]{2,1,0:T(8,128)(2,1)}, bf16[512,1536]{1,0:T(8,128)(2,1)}, f32[1,1536]{1,0:T(1,128)}, bf16[512,1536]{1,0:T(8,128)(2,1)}, bf16[5...) custom-call(s32[26]{0:T(128)} %pad_add_fusion.2.refs_0_, ...), custom_call_target="tpu_custom_call" | custom-call | flops 1 | bytes 23680000 | tf_op jit(solution)/shard_map/pallas_call | solution.py:235
  96.6 1.3 collective-permute-start.23
  97.9 7.7 %shard_map.216 = (bf16[4,96,3072]{2,1,0:T(8,128)(2,1)}, bf16[96,3072]{1,0:T(8,128)(2,1)}, bf16[96,3072]{1,0:T(8,128)(2,1)}, bf16[96,3072]{1,0:T(8,128)(2,1)}, bf16[96,3072]{1,0:T(8,128)(2,1)}) custom-call(s32[1]{0:T(128)} %bitcast.at, bf16[768,512]{1,0:T(8,128)(2,1)} %get-tuple-element.167.normal_t, bf16[512,1536]{1,0:T(8,128)(2,1)} %get-tuple-element.209.dz, ...), custom_call_target="tpu_custom_call" | custom-call | flops 1 | bytes 1480000 | tf_op jit(solution)/shard_map/pallas_call | solution.py:235
  106.6 11.5 %shard_map.217 = (f32[512,1536]{1,0:T(8,128)}, f32[512,128]{1,0:T(8,128)}, f32[512,128]{1,0:T(8,128)}, bf16[512,768]{1,0:T(8,128)(2,1)}) custom-call(bf16[512,128]{1,0:T(8,128)(2,1)} %get-tuple-element.147.bs.refs_16_, bf16[512,128]{1,0:T(8,128)(2,1)} %get-tuple-element.148.cs.refs_10_, bf16[512,1536]{1,0:T(8,128)(2,1)} %get-tuple-element.149.xt.refs_15_, ...), custom_call_target="tpu_custom_call" | custom-call | flops 1 | bytes 1480000 | tf_op jit(solution)/shard_map/pallas_call | solution.py:235
  118.2 2.2 add_convert_fusion
  120.4 1.3 dynamic-slice_bitcast_fusion.1
  122.5 1.6 collective-permute-done.28.refs_4_
  124.1 3.2 %collective-permute-start.29 = (bf16[512,768]{1,0:T(8,128)(2,1)}, bf16[512,768]{1,0:T(8,128)(2,1)S(1)}, u32[]{:S(2)}, u32[]{:S(2)}) collective-permute-start(bf16[512,768]{1,0:T(8,128)(2,1)} %get-tuple-element.190), channel_id=1, source_target_pairs={{1,16},{3,18},{5,20},{7,22},{9,24},{11,26},{13,28},{15,30},{16,1},... | collective-permute-start | bytes 2359304 | tf_op jit(solution)/shard_map/ppermute | solution.py:52
  127.6 1.2 collective-permute-start.33
  128.8 1.2 collective-permute-start.34
  130.2 17.1 %shard_map.218 = (bf16[528,1920]{1,0:T(8,128)(2,1)}, f32[96,128]{1,0:T(8,128)}) custom-call(s32[26]{0:T(128)} %pad_add_fusion.2.refs_0_, bf16[2,128,1536]{2,1,0:T(8,128)(2,1)} %get-tuple-element.181.refs_1_, bf16[2,128,1536]{2,1,0:T(8,128)(2,1)} %copy-done.19, bf16[2,128,1536]{2,1,0:T(8,128)(2,1)} %collective-permute-done.30.refs_3_, ...), custom_call_target="tpu_custom_call" | custom-call | flops 1 | bytes 2960000 | tf_op jit(solution)/shard_map/pallas_call | solution.py:235
  147.4 4.4 %convolution_convert_fusion = bf16[768,1920]{1,0:T(8,128)(2,1)S(1)} fusion(bf16[528,768]{1,0:T(8,128)(2,1)S(1)} %copy-done.3, bf16[528,1920]{1,0:T(8,128)(2,1)} %get-tuple-element.211), kind=kOutput, calls=%fused_computation.1 | convolution fusion | flops 1558609920 | bytes 5787648 | tf_op jit(solution)/shard_map/dot_general | solution.py:182
  152.6 2.8 %collective-permute-done.34 = bf16[96,3072]{1,0:T(8,128)(2,1)S(1)} collective-permute-done((bf16[96,3072]{1,0:T(8,128)(2,1)}, bf16[96,3072]{1,0:T(8,128)(2,1)S(1)}, u32[]{:S(2)}, u32[]{:S(2)}) %collective-permute-start.34) | collective-permute-done | bytes 589856 | tf_op jit(solution)/shard_map/ppermute | solution.py:35
  156.4 1.9 fusion.29
  158.8 1.6 fusion.2
  160.4 1.0 broadcast_select_fusion.1
  162.9 3.2 %collective-permute-start.39 = (bf16[512,768]{1,0:T(8,128)(2,1)S(1)}, bf16[512,768]{1,0:T(8,128)(2,1)}, u32[]{:S(2)}, u32[]{:S(2)}) collective-permute-start(bf16[512,768]{1,0:T(8,128)(2,1)S(1)} %fusion.6), channel_id=1, source_target_pairs={{1,16},{3,18},{5,20},{7,22},{9,24},{11,26},{13,28},{15,30},{16,1},... | collective-permute-start | bytes 2359304 | tf_op jit(solution)/shard_map/ppermute | solution.py:52
  166.9 0.9 collective-permute-start.37
  167.8 1.2 collective-permute-start.38
  169.0 1.0 add_convert_fusion.3
  170.1 1.5 collective-permute-start.43
  171.6 5.5 %collective-permute-done.36.refs_1_ = bf16[96,2176]{1,0:T(8,128)(2,1)S(1)} collective-permute-done((bf16[96,2176]{1,0:T(8,128)(2,1)S(1)}, bf16[96,2176]{1,0:T(8,128)(2,1)S(1)}, u32[]{:S(2)}, u32[]{:S(2)}) %collective-permute-start.36) | collective-permute-done | bytes 417824 | tf_op jit(solution)/shard_map/ppermute | solution.py:35
  177.4 9.1 %collective-permute-done.38.refs_3_ = bf16[96,2176]{1,0:T(8,128)(2,1)S(1)} collective-permute-done((bf16[96,2176]{1,0:T(8,128)(2,1)S(1)}, bf16[96,2176]{1,0:T(8,128)(2,1)S(1)}, u32[]{:S(2)}, u32[]{:S(2)}) %collective-permute-start.38) | collective-permute-done | bytes 417824 | tf_op jit(solution)/shard_map/ppermute | solution.py:35
  186.4 3.9 %collective-permute-done.39 = bf16[512,768]{1,0:T(8,128)(2,1)} collective-permute-done((bf16[512,768]{1,0:T(8,128)(2,1)S(1)}, bf16[512,768]{1,0:T(8,128)(2,1)}, u32[]{:S(2)}, u32[]{:S(2)}) %collective-permute-start.39) | collective-permute-done | bytes 786464 | tf_op jit(solution)/shard_map/ppermute | solution.py:52
  190.9 1.2 broadcast_select_fusion
  192.1 8.7 %collective-permute-done.41 = bf16[96,1344]{1,0:T(8,128)(2,1)S(1)} collective-permute-done((bf16[96,1344]{1,0:T(8,128)(2,1)S(1)}, bf16[96,1344]{1,0:T(8,128)(2,1)S(1)}, u32[]{:S(2)}, u32[]{:S(2)}) %collective-permute-start.41) | collective-permute-done | bytes 258080 | tf_op jit(solution)/shard_map/ppermute | solution.py:35
  201.5 12.4 %collective-permute-done.44 = bf16[96,1216]{1,0:T(8,128)(2,1)S(1)} collective-permute-done((bf16[96,1216]{1,0:T(8,128)(2,1)S(1)}, bf16[96,1216]{1,0:T(8,128)(2,1)S(1)}, u32[]{:S(2)}, u32[]{:S(2)}) %collective-permute-start.44) | collective-permute-done | bytes 233504 | tf_op jit(solution)/shard_map/ppermute | solution.py:35
  215.3 3.0 %collective-permute-start.45 = (bf16[96,256]{1,0:T(8,128)(2,1)S(1)}, bf16[96,256]{1,0:T(8,128)(2,1)S(1)}, u32[]{:S(2)}, u32[]{:S(2)}) collective-permute-start(bf16[96,256]{1,0:T(8,128)(2,1)S(1)} %pad_maximum_fusion.4), channel_id=1, source_target_pairs={{1,16},{3,18},{5,20},{7,22},{9,24},{11,26},{13,28},{15,30},{16,1},... | collective-permute-start | bytes 147464 | tf_op jit(solution)/shard_map/ppermute | solution.py:52
  220.1 1.5 collective-permute-done.45
  223.1 0.9 copy-done.11
  224.0 1.3 multiply_reduce_fusion
  225.9 0.9 pad_maximum_fusion.2
  (210 shorter events, 21.3 us)
Async XLA Ops:
  0.7 8.6 %copy-start.15 = (bf16[512,768]{1,0:T(8,128)(2,1)S(1)}, bf16[512,768]{1,0:T(8,128)(2,1)}, u32[]{:S(2)}) copy-start(bf16[512,768]{1,0:T(8,128)(2,1)} %refs_13_.1) | copy-start | bytes 2359300
  1.8 25.6 %copy-start.30 = (f32[1792]{0:T(1024)S(1)}, f32[1792]{0:T(1024)}, u32[]{:S(2)}) copy-start(f32[1792]{0:T(1024)} %param.19) | copy-start | bytes 21508
  1.8 26.2 %copy-start.29 = (f32[1536]{0:T(1024)S(1)}, f32[1536]{0:T(1024)}, u32[]{:S(2)}) copy-start(f32[1536]{0:T(1024)} %param.23) | copy-start | bytes 18436
  2.7 39.5 %copy-start.14 = (bf16[96,1920]{1,0:T(8,128)(2,1)}, bf16[96,1920]{1,0:T(8,128)(2,1)S(1)}, u32[]{:S(2)}) copy-start(bf16[96,1920]{1,0:T(8,128)(2,1)S(1)} %concatenate.42.refs_1_) | copy-start | bytes 1105924
  2.7 33.1 %copy-start.4 = (bf16[512,768]{1,0:T(8,128)(2,1)S(1)}, bf16[512,768]{1,0:T(8,128)(2,1)}, u32[]{:S(2)}) copy-start(bf16[512,768]{1,0:T(8,128)(2,1)} %refs_9_.1) | copy-start | bytes 2359300
  2.7 39.4 %slice-start = ((bf16[96,3352]{1,0:T(8,128)(2,1)}), bf16[96,1536]{1,0:T(8,128)(2,1)S(1)}, s32[]{:S(2)}) async-start(bf16[96,3352]{1,0:T(8,128)(2,1)} %param.17), calls=%async_computation | async-start | bytes 589824 | tf_op jit(solution)/shard_map/slice | solution.py:1167
  2.7 14.2 %collective-permute-start.1 = (bf16[96,1920]{1,0:T(8,128)(2,1)S(1)}, bf16[96,1920]{1,0:T(8,128)(2,1)S(1)}, u32[]{:S(2)}, u32[]{:S(2)}) collective-permute-start(bf16[96,1920]{1,0:T(8,128)(2,1)S(1)} %concatenate.42.refs_1_), channel_id=1, source_target_pairs={{0,6},{1,7},{2,4},{3,5},{4,2},{5,3},{6,0},{7,1},{8,14},{9,15},{10,... | collective-permute-start | bytes 1105928 | tf_op jit(solution)/shard_map/ppermute | solution.py:35
  5.8 17.1 %collective-permute-start.2 = (bf16[96,1920]{1,0:T(8,128)(2,1)S(1)}, bf16[96,1920]{1,0:T(8,128)(2,1)}, u32[]{:S(2)}, u32[]{:S(2)}) collective-permute-start(bf16[96,1920]{1,0:T(8,128)(2,1)S(1)} %concatenate.42.refs_1_), channel_id=1, source_target_pairs={{0,4},{1,5},{2,6},{3,7},{4,0},{5,1},{6,2},{7,3},{8,12},{9,13},{10,... | collective-permute-start | bytes 1105928 | tf_op jit(solution)/shard_map/ppermute | solution.py:35
  6.0 17.3 %collective-permute-start.3 = (bf16[96,1920]{1,0:T(8,128)(2,1)S(1)}, bf16[96,1920]{1,0:T(8,128)(2,1)}, u32[]{:S(2)}, u32[]{:S(2)}) collective-permute-start(bf16[96,1920]{1,0:T(8,128)(2,1)S(1)} %concatenate.42.refs_1_), channel_id=1, source_target_pairs={{0,2},{1,3},{2,0},{3,1},{4,6},{5,7},{6,4},{7,5},{8,10},{9,11},{10,... | collective-permute-start | bytes 1105928 | tf_op jit(solution)/shard_map/ppermute | solution.py:35
  6.2 25.9 %collective-permute-start.4 = (bf16[96,1920]{1,0:T(8,128)(2,1)S(1)}, bf16[96,1920]{1,0:T(8,128)(2,1)}, u32[]{:S(2)}, u32[]{:S(2)}) collective-permute-start(bf16[96,1920]{1,0:T(8,128)(2,1)S(1)} %concatenate.42.refs_1_), channel_id=1, source_target_pairs={{0,1},{1,0},{2,3},{3,2},{4,5},{5,4},{6,7},{7,6},{8,9},{9,8},{10,11... | collective-permute-start | bytes 1105928 | tf_op jit(solution)/shard_map/ppermute | solution.py:35
  8.1 1.1 collective-permute-start
  9.3 22.8 %collective-permute-start.8 = (bf16[512,768]{1,0:T(8,128)(2,1)S(1)}, bf16[512,768]{1,0:T(8,128)(2,1)S(1)}, u32[]{:S(2)}, u32[]{:S(2)}) collective-permute-start(bf16[512,768]{1,0:T(8,128)(2,1)S(1)} %copy-done.15), channel_id=1, source_target_pairs={{1,16},{3,18},{5,20},{7,22},{9,24},{11,26},{13,28},{15,30},{16,1},... | collective-permute-start | bytes 2359304 | tf_op jit(solution)/shard_map/ppermute | solution.py:52
  16.9 25.3 %copy-start.21 = (bf16[96,1920]{1,0:T(8,128)(2,1)}, bf16[96,1920]{1,0:T(8,128)(2,1)S(1)}, u32[]{:S(2)}) copy-start(bf16[96,1920]{1,0:T(8,128)(2,1)S(1)} %collective-permute-done.1.refs_2_) | copy-start | bytes 1105924
  18.0 14.1 %collective-permute-start.5 = (bf16[96,1920]{1,0:T(8,128)(2,1)S(1)}, bf16[96,1920]{1,0:T(8,128)(2,1)}, u32[]{:S(2)}, u32[]{:S(2)}) collective-permute-start(bf16[96,1920]{1,0:T(8,128)(2,1)S(1)} %collective-permute-done.1.refs_2_), channel_id=1, source_target_pairs={{0,1},{1,0},{2,3},{3,2},{4,5},{5,4},{6,7},{7,6},{8,9},{9,8},{10,11... | collective-permute-start | bytes 1105928 | tf_op jit(solution)/shard_map/ppermute | solution.py:35
  22.8 9.3 %collective-permute-start.6 = (bf16[96,1920]{1,0:T(8,128)(2,1)}, bf16[96,1920]{1,0:T(8,128)(2,1)}, u32[]{:S(2)}, u32[]{:S(2)}) collective-permute-start(bf16[96,1920]{1,0:T(8,128)(2,1)} %collective-permute-done.2.refs_3_), channel_id=1, source_target_pairs={{0,1},{1,0},{2,3},{3,2},{4,5},{5,4},{6,7},{7,6},{8,9},{9,8},{10,11... | collective-permute-start | bytes 1105928 | tf_op jit(solution)/shard_map/ppermute | solution.py:35
  23.3 8.8 %collective-permute-start.7 = (bf16[96,1920]{1,0:T(8,128)(2,1)}, bf16[96,1920]{1,0:T(8,128)(2,1)}, u32[]{:S(2)}, u32[]{:S(2)}) collective-permute-start(bf16[96,1920]{1,0:T(8,128)(2,1)} %collective-permute-done.3.refs_4_), channel_id=1, source_target_pairs={{0,1},{1,0},{2,3},{3,2},{4,5},{5,4},{6,7},{7,6},{8,9},{9,8},{10,11... | collective-permute-start | bytes 1105928 | tf_op jit(solution)/shard_map/ppermute | solution.py:35
  32.0 12.9 %copy-start.16 = (bf16[512,768]{1,0:T(8,128)(2,1)}, bf16[512,768]{1,0:T(8,128)(2,1)S(1)}, u32[]{:S(2)}) copy-start(bf16[512,768]{1,0:T(8,128)(2,1)S(1)} %collective-permute-done.8.refs_14_) | copy-start | bytes 2359300
  32.1 12.9 %copy-start.24 = (bf16[16,768]{1,0:T(8,128)(2,1)}, bf16[16,768]{1,0:T(8,128)(2,1)S(1)}, u32[]{:S(2)}) copy-start(bf16[16,768]{1,0:T(8,128)(2,1)S(1)} %fusion.19.refs_9_) | copy-start | bytes 73732
  32.1 2.9 %collective-permute-start.10 = (bf16[16,768]{1,0:T(8,128)(2,1)S(1)}, bf16[16,768]{1,0:T(8,128)(2,1)S(1)}, u32[]{:S(2)}, u32[]{:S(2)}) collective-permute-start(bf16[16,768]{1,0:T(8,128)(2,1)S(1)} %fusion.19.refs_9_), channel_id=1, source_target_pairs={{0,1},{1,0},{2,3},{3,2},{4,5},{5,4},{6,7},{7,6},{8,9},{9,8},{10,11... | collective-permute-start | bytes 73736 | tf_op jit(solution)/shard_map/ppermute | solution.py:70
  32.2 3.4 %collective-permute-start.11 = (bf16[16,768]{1,0:T(8,128)(2,1)S(1)}, bf16[16,768]{1,0:T(8,128)(2,1)S(1)}, u32[]{:S(2)}, u32[]{:S(2)}) collective-permute-start(bf16[16,768]{1,0:T(8,128)(2,1)S(1)} %fusion.19.refs_9_), channel_id=1, source_target_pairs={{0,9},{1,8},{2,11},{3,10},{4,13},{5,12},{6,15},{7,14},{8,1},{9,0},... | collective-permute-start | bytes 73736 | tf_op jit(solution)/shard_map/ppermute | solution.py:70
  33.0 2.8 %collective-permute-start.9 = (bf16[16,768]{1,0:T(8,128)(2,1)S(1)}, bf16[16,768]{1,0:T(8,128)(2,1)S(1)}, u32[]{:S(2)}, u32[]{:S(2)}) collective-permute-start(bf16[16,768]{1,0:T(8,128)(2,1)S(1)} %fusion.19.refs_9_), channel_id=1, source_target_pairs={{0,8},{1,9},{2,10},{3,11},{4,12},{5,13},{6,14},{7,15},{8,0},{9,1},... | collective-permute-start | bytes 73736 | tf_op jit(solution)/shard_map/ppermute | solution.py:70
  35.1 9.9 %copy-start.25 = (bf16[16,768]{1,0:T(8,128)(2,1)}, bf16[16,768]{1,0:T(8,128)(2,1)S(1)}, u32[]{:S(2)}) copy-start(bf16[16,768]{1,0:T(8,128)(2,1)S(1)} %collective-permute-done.10.refs_11_) | copy-start | bytes 73732
  35.6 9.4 %copy-start.26 = (bf16[16,768]{1,0:T(8,128)(2,1)}, bf16[16,768]{1,0:T(8,128)(2,1)S(1)}, u32[]{:S(2)}) copy-start(bf16[16,768]{1,0:T(8,128)(2,1)S(1)} %collective-permute-done.11.refs_12_) | copy-start | bytes 73732
  35.8 9.2 %copy-start.27 = (bf16[16,768]{1,0:T(8,128)(2,1)}, bf16[16,768]{1,0:T(8,128)(2,1)S(1)}, u32[]{:S(2)}) copy-start(bf16[16,768]{1,0:T(8,128)(2,1)S(1)} %collective-permute-done.9.refs_10_) | copy-start | bytes 73732
  35.8 32.1 %collective-permute-start.20 = (bf16[512,768]{1,0:T(8,128)(2,1)S(1)}, bf16[512,768]{1,0:T(8,128)(2,1)S(1)}, u32[]{:S(2)}, u32[]{:S(2)}) collective-permute-start(bf16[512,768]{1,0:T(8,128)(2,1)S(1)} %copy-done.4), channel_id=1, source_target_pairs={{1,16},{3,18},{5,20},{7,22},{9,24},{11,26},{13,28},{15,30},{16,1},... | collective-permute-start | bytes 2359304 | tf_op jit(solution)/shard_map/ppermute | solution.py:52
  42.2 22.8 %collective-permute-start.13 = (bf16[96,3072]{1,0:T(8,128)(2,1)S(1)}, bf16[96,3072]{1,0:T(8,128)(2,1)S(1)}, u32[]{:S(2)}, u32[]{:S(2)}) collective-permute-start(bf16[96,3072]{1,0:T(8,128)(2,1)S(1)} %pad_maximum_fusion.1.refs_0_), channel_id=1, source_target_pairs={{0,6},{1,7},{2,4},{3,5},{4,2},{5,3},{6,0},{7,1},{8,14},{9,15},{10,... | collective-permute-start | bytes 1769480 | tf_op jit(solution)/shard_map/ppermute | solution.py:35
  44.5 22.7 %collective-permute-start.14 = (bf16[96,3072]{1,0:T(8,128)(2,1)S(1)}, bf16[96,3072]{1,0:T(8,128)(2,1)S(1)}, u32[]{:S(2)}, u32[]{:S(2)}) collective-permute-start(bf16[96,3072]{1,0:T(8,128)(2,1)S(1)} %pad_maximum_fusion.1.refs_0_), channel_id=1, source_target_pairs={{0,4},{1,5},{2,6},{3,7},{4,0},{5,1},{6,2},{7,3},{8,12},{9,13},{10,... | collective-permute-start | bytes 1769480 | tf_op jit(solution)/shard_map/ppermute | solution.py:35
  44.7 22.6 %collective-permute-start.15 = (bf16[96,3072]{1,0:T(8,128)(2,1)S(1)}, bf16[96,3072]{1,0:T(8,128)(2,1)S(1)}, u32[]{:S(2)}, u32[]{:S(2)}) collective-permute-start(bf16[96,3072]{1,0:T(8,128)(2,1)S(1)} %pad_maximum_fusion.1.refs_0_), channel_id=1, source_target_pairs={{0,2},{1,3},{2,0},{3,1},{4,6},{5,7},{6,4},{7,5},{8,10},{9,11},{10,... | collective-permute-start | bytes 1769480 | tf_op jit(solution)/shard_map/ppermute | solution.py:35
  58.4 20.5 %collective-permute-start.12 = (bf16[2,128,1664]{2,1,0:T(8,128)(2,1)}, bf16[2,128,1664]{2,1,0:T(8,128)(2,1)S(1)}, u32[]{:S(2)}, u32[]{:S(2)}) collective-permute-start(bf16[2,128,1664]{2,1,0:T(8,128)(2,1)} %get-tuple-element.152.refs_1_.refs_5_), channel_id=1, source_target_pairs={{0,8},{8,0},{16,24},{24,16},{1,9},{9,1},{17,25},{25,17},{2,10},{10... | collective-permute-start | bytes 2555912 | tf_op jit(solution)/shard_map/ppermute | solution.py:35
  58.5 10.8 %copy-start.6 = (bf16[2,128,1664]{2,1,0:T(8,128)(2,1)S(1)}, bf16[2,128,1664]{2,1,0:T(8,128)(2,1)}, u32[]{:S(2)}) copy-start(bf16[2,128,1664]{2,1,0:T(8,128)(2,1)} %get-tuple-element.152.refs_1_.refs_5_) | copy-start | bytes 2555908
  58.5 13.3 %copy-start.3 = (bf16[528,768]{1,0:T(8,128)(2,1)S(1)}, bf16[528,768]{1,0:T(8,128)(2,1)}, u32[]{:S(2)}) copy-start(bf16[528,768]{1,0:T(8,128)(2,1)} %get-tuple-element.159.refs_8_) | copy-start | bytes 2433028
  67.3 2.0 collective-permute-start.17
  67.4 2.7 %collective-permute-start.18 = (bf16[96,3072]{1,0:T(8,128)(2,1)S(1)}, bf16[96,3072]{1,0:T(8,128)(2,1)S(1)}, u32[]{:S(2)}, u32[]{:S(2)}) collective-permute-start(bf16[96,3072]{1,0:T(8,128)(2,1)S(1)} %collective-permute-done.14.refs_2_), channel_id=1, source_target_pairs={{0,1},{1,0},{2,3},{3,2},{4,5},{5,4},{6,7},{7,6},{8,9},{9,8},{10,11... | collective-permute-start | bytes 1769480 | tf_op jit(solution)/shard_map/ppermute | solution.py:35
  67.8 3.2 %collective-permute-start.19 = (bf16[96,3072]{1,0:T(8,128)(2,1)S(1)}, bf16[96,3072]{1,0:T(8,128)(2,1)S(1)}, u32[]{:S(2)}, u32[]{:S(2)}) collective-permute-start(bf16[96,3072]{1,0:T(8,128)(2,1)S(1)} %collective-permute-done.15.refs_3_), channel_id=1, source_target_pairs={{0,1},{1,0},{2,3},{3,2},{4,5},{5,4},{6,7},{7,6},{8,9},{9,8},{10,11... | collective-permute-start | bytes 1769480 | tf_op jit(solution)/shard_map/ppermute | solution.py:35
  67.9 3.9 %collective-permute-start.16 = (bf16[96,3072]{1,0:T(8,128)(2,1)S(1)}, bf16[96,3072]{1,0:T(8,128)(2,1)S(1)}, u32[]{:S(2)}, u32[]{:S(2)}) collective-permute-start(bf16[96,3072]{1,0:T(8,128)(2,1)S(1)} %pad_maximum_fusion.1.refs_0_), channel_id=1, source_target_pairs={{0,1},{1,0},{2,3},{3,2},{4,5},{5,4},{6,7},{7,6},{8,9},{9,8},{10,11... | collective-permute-start | bytes 1769480 | tf_op jit(solution)/shard_map/ppermute | solution.py:35
  69.3 9.8 %collective-permute-start.21 = (bf16[2,128,1664]{2,1,0:T(8,128)(2,1)S(1)}, bf16[2,128,1664]{2,1,0:T(8,128)(2,1)S(1)}, u32[]{:S(2)}, u32[]{:S(2)}) collective-permute-start(bf16[2,128,1664]{2,1,0:T(8,128)(2,1)S(1)} %copy-done.6), channel_id=1, source_target_pairs={{0,1},{1,0},{2,3},{3,2},{4,5},{5,4},{6,7},{7,6},{8,9},{9,8},{10,11... | collective-permute-start | bytes 2555912 | tf_op jit(solution)/shard_map/ppermute | solution.py:35
  78.9 2.4 %collective-permute-start.22 = (bf16[2,128,1664]{2,1,0:T(8,128)(2,1)S(1)}, bf16[2,128,1664]{2,1,0:T(8,128)(2,1)S(1)}, u32[]{:S(2)}, u32[]{:S(2)}) collective-permute-start(bf16[2,128,1664]{2,1,0:T(8,128)(2,1)S(1)} %collective-permute-done.12.refs_2_.refs_6_), channel_id=1, source_target_pairs={{0,1},{1,0},{2,3},{3,2},{4,5},{5,4},{6,7},{7,6},{8,9},{9,8},{10,11... | collective-permute-start | bytes 2555912 | tf_op jit(solution)/shard_map/ppermute | solution.py:35
  96.6 21.5 %collective-permute-start.23 = (bf16[2,128,1536]{2,1,0:T(8,128)(2,1)}, bf16[2,128,1536]{2,1,0:T(8,128)(2,1)S(1)}, u32[]{:S(2)}, u32[]{:S(2)}) collective-permute-start(bf16[2,128,1536]{2,1,0:T(8,128)(2,1)} %get-tuple-element.181.refs_1_), channel_id=1, source_target_pairs={{0,8},{8,0},{16,24},{24,16},{1,9},{9,1},{17,25},{25,17},{2,10},{10... | collective-permute-start | bytes 2359304 | tf_op jit(solution)/shard_map/ppermute | solution.py:35
  105.6 12.5 %collective-permute-start.24 = (bf16[96,3072]{1,0:T(8,128)(2,1)}, bf16[96,3072]{1,0:T(8,128)(2,1)S(1)}, u32[]{:S(2)}, u32[]{:S(2)}) collective-permute-start(bf16[96,3072]{1,0:T(8,128)(2,1)} %get-tuple-element.171), channel_id=1, source_target_pairs={{0,1},{1,0},{2,3},{3,2},{4,5},{5,4},{6,7},{7,6},{8,9},{9,8},{10,11... | collective-permute-start | bytes 1769480 | tf_op jit(solution)/shard_map/ppermute | solution.py:35
  106.0 12.1 %collective-permute-start.25 = (bf16[96,3072]{1,0:T(8,128)(2,1)}, bf16[96,3072]{1,0:T(8,128)(2,1)S(1)}, u32[]{:S(2)}, u32[]{:S(2)}) collective-permute-start(bf16[96,3072]{1,0:T(8,128)(2,1)} %get-tuple-element.172), channel_id=1, source_target_pairs={{0,1},{1,0},{2,3},{3,2},{4,5},{5,4},{6,7},{7,6},{8,9},{9,8},{10,11... | collective-permute-start | bytes 1769480 | tf_op jit(solution)/shard_map/ppermute | solution.py:35
  106.1 12.0 %collective-permute-start.26 = (bf16[96,3072]{1,0:T(8,128)(2,1)}, bf16[96,3072]{1,0:T(8,128)(2,1)}, u32[]{:S(2)}, u32[]{:S(2)}) collective-permute-start(bf16[96,3072]{1,0:T(8,128)(2,1)} %get-tuple-element.173), channel_id=1, source_target_pairs={{0,1},{1,0},{2,3},{3,2},{4,5},{5,4},{6,7},{7,6},{8,9},{9,8},{10,11... | collective-permute-start | bytes 1769480 | tf_op jit(solution)/shard_map/ppermute | solution.py:35
  106.5 11.6 %collective-permute-start.27 = (bf16[96,3072]{1,0:T(8,128)(2,1)}, bf16[96,3072]{1,0:T(8,128)(2,1)}, u32[]{:S(2)}, u32[]{:S(2)}) collective-permute-start(bf16[96,3072]{1,0:T(8,128)(2,1)} %get-tuple-element.174), channel_id=1, source_target_pairs={{0,1},{1,0},{2,3},{3,2},{4,5},{5,4},{6,7},{7,6},{8,9},{9,8},{10,11... | collective-permute-start | bytes 1769480 | tf_op jit(solution)/shard_map/ppermute | solution.py:35
  106.6 11.5 %copy-start.12 = (bf16[4,96,3072]{2,1,0:T(8,128)(2,1)S(1)}, bf16[4,96,3072]{2,1,0:T(8,128)(2,1)}, u32[]{:S(2)}) copy-start(bf16[4,96,3072]{2,1,0:T(8,128)(2,1)} %get-tuple-element.184) | copy-start | bytes 7077892
  121.7 2.5 %collective-permute-start.28 = (bf16[2,128,1536]{2,1,0:T(8,128)(2,1)S(1)}, bf16[2,128,1536]{2,1,0:T(8,128)(2,1)}, u32[]{:S(2)}, u32[]{:S(2)}) collective-permute-start(bf16[2,128,1536]{2,1,0:T(8,128)(2,1)S(1)} %collective-permute-done.23.refs_2_), channel_id=1, source_target_pairs={{0,1},{1,0},{2,3},{3,2},{4,5},{5,4},{6,7},{7,6},{8,9},{9,8},{10,11... | collective-permute-start | bytes 2359304 | tf_op jit(solution)/shard_map/ppermute | solution.py:35
  122.4 7.9 %collective-permute-start.30 = (bf16[2,128,1536]{2,1,0:T(8,128)(2,1)S(1)}, bf16[2,128,1536]{2,1,0:T(8,128)(2,1)}, u32[]{:S(2)}, u32[]{:S(2)}) collective-permute-start(bf16[2,128,1536]{2,1,0:T(8,128)(2,1)S(1)} %copy-done.18), channel_id=1, source_target_pairs={{0,1},{1,0},{2,3},{3,2},{4,5},{5,4},{6,7},{7,6},{8,9},{9,8},{10,11... | collective-permute-start | bytes 2359304 | tf_op jit(solution)/shard_map/ppermute | solution.py:35
  124.1 23.2 %collective-permute-start.29 = (bf16[512,768]{1,0:T(8,128)(2,1)}, bf16[512,768]{1,0:T(8,128)(2,1)S(1)}, u32[]{:S(2)}, u32[]{:S(2)}) collective-permute-start(bf16[512,768]{1,0:T(8,128)(2,1)} %get-tuple-element.190), channel_id=1, source_target_pairs={{1,16},{3,18},{5,20},{7,22},{9,24},{11,26},{13,28},{15,30},{16,1},... | collective-permute-start | bytes 2359304 | tf_op jit(solution)/shard_map/ppermute | solution.py:52
  127.6 25.0 %collective-permute-start.33 = (bf16[96,3072]{1,0:T(8,128)(2,1)}, bf16[96,3072]{1,0:T(8,128)(2,1)S(1)}, u32[]{:S(2)}, u32[]{:S(2)}) collective-permute-start(bf16[96,3072]{1,0:T(8,128)(2,1)} %get-tuple-element.243), channel_id=1, source_target_pairs={{0,2},{1,3},{2,0},{3,1},{4,6},{5,7},{6,4},{7,5},{8,10},{9,11},{10,... | collective-permute-start | bytes 1769480 | tf_op jit(solution)/shard_map/ppermute | solution.py:35
  128.8 26.6 %collective-permute-start.34 = (bf16[96,3072]{1,0:T(8,128)(2,1)}, bf16[96,3072]{1,0:T(8,128)(2,1)S(1)}, u32[]{:S(2)}, u32[]{:S(2)}) collective-permute-start(bf16[96,3072]{1,0:T(8,128)(2,1)} %get-tuple-element.242), channel_id=1, source_target_pairs={{0,4},{1,5},{2,6},{3,7},{4,0},{5,1},{6,2},{7,3},{8,12},{9,13},{10,... | collective-permute-start | bytes 1769480 | tf_op jit(solution)/shard_map/ppermute | solution.py:35
  130.0 25.4 %collective-permute-start.35 = (bf16[96,3072]{1,0:T(8,128)(2,1)}, bf16[96,3072]{1,0:T(8,128)(2,1)S(1)}, u32[]{:S(2)}, u32[]{:S(2)}) collective-permute-start(bf16[96,3072]{1,0:T(8,128)(2,1)} %get-tuple-element.241), channel_id=1, source_target_pairs={{0,6},{1,7},{2,4},{3,5},{4,2},{5,3},{6,0},{7,1},{8,14},{9,15},{10,... | collective-permute-start | bytes 1769480 | tf_op jit(solution)/shard_map/ppermute | solution.py:35
  151.9 10.4 %collective-permute-start.31 = (bf16[4,96,1920]{2,1,0:T(8,128)(2,1)S(1)}, bf16[4,96,1920]{2,1,0:T(8,128)(2,1)S(1)}, u32[]{:S(2)}, u32[]{:S(2)}) collective-permute-start(bf16[4,96,1920]{2,1,0:T(8,128)(2,1)S(1)} %dynamic-slice_bitcast_fusion), channel_id=1, source_target_pairs={{0,1},{1,0},{2,3},{3,2},{4,5},{5,4},{6,7},{7,6},{8,9},{9,8},{10,11... | collective-permute-start | bytes 4423688 | tf_op jit(solution)/shard_map/ppermute | solution.py:35
  152.6 9.7 %collective-permute-start.32 = (f32[96,128]{1,0:T(8,128)S(1)}, f32[96,128]{1,0:T(8,128)S(1)}, u32[]{:S(2)}, u32[]{:S(2)}) collective-permute-start(f32[96,128]{1,0:T(8,128)S(1)} %copy-done.5), channel_id=1, source_target_pairs={{0,1},{1,0},{2,3},{3,2},{4,5},{5,4},{6,7},{7,6},{8,9},{9,8},{10,11... | collective-permute-start | bytes 147464 | tf_op jit(solution)/shard_map/ppermute | solution.py:35
  155.8 10.3 %collective-permute-start.42 = (bf16[96,1536]{1,0:T(8,128)(2,1)S(1)}, bf16[96,1536]{1,0:T(8,128)(2,1)S(1)}, u32[]{:S(2)}, u32[]{:S(2)}) collective-permute-start(bf16[96,1536]{1,0:T(8,128)(2,1)S(1)} %constant_dynamic-slice_fusion), channel_id=1, source_target_pairs={{0,8},{8,0},{16,24},{24,16},{1,9},{9,1},{17,25},{25,17},{2,10},{10... | collective-permute-start | bytes 884744 | tf_op jit(solution)/shard_map/ppermute | solution.py:35
  162.9 27.5 %collective-permute-start.39 = (bf16[512,768]{1,0:T(8,128)(2,1)S(1)}, bf16[512,768]{1,0:T(8,128)(2,1)}, u32[]{:S(2)}, u32[]{:S(2)}) collective-permute-start(bf16[512,768]{1,0:T(8,128)(2,1)S(1)} %fusion.6), channel_id=1, source_target_pairs={{1,16},{3,18},{5,20},{7,22},{9,24},{11,26},{13,28},{15,30},{16,1},... | collective-permute-start | bytes 2359304 | tf_op jit(solution)/shard_map/ppermute | solution.py:52
  166.2 3.9 %collective-permute-start.40 = (bf16[96,64]{1,0:T(8,128)(2,1)S(1)}, bf16[96,64]{1,0:T(8,128)(2,1)S(1)}, u32[]{:S(2)}, u32[]{:S(2)}) collective-permute-start(bf16[96,64]{1,0:T(8,128)(2,1)S(1)} %reshape.318.refs_4_), channel_id=1, source_target_pairs={{0,1},{1,0},{2,3},{3,2},{4,5},{5,4},{6,7},{7,6},{8,9},{9,8},{10,11... | collective-permute-start | bytes 36872 | tf_op jit(solution)/shard_map/ppermute | solution.py:35
  166.3 10.8 %collective-permute-start.36 = (bf16[96,2176]{1,0:T(8,128)(2,1)S(1)}, bf16[96,2176]{1,0:T(8,128)(2,1)S(1)}, u32[]{:S(2)}, u32[]{:S(2)}) collective-permute-start(bf16[96,2176]{1,0:T(8,128)(2,1)S(1)} %get-tuple-element.216), channel_id=1, source_target_pairs={{0,2},{1,3},{2,0},{3,1},{4,6},{5,7},{6,4},{7,5},{8,10},{9,11},{10,... | collective-permute-start | bytes 1253384 | tf_op jit(solution)/shard_map/ppermute | solution.py:35
  166.9 10.5 %collective-permute-start.37 = (bf16[96,2176]{1,0:T(8,128)(2,1)S(1)}, bf16[96,2176]{1,0:T(8,128)(2,1)S(1)}, u32[]{:S(2)}, u32[]{:S(2)}) collective-permute-start(bf16[96,2176]{1,0:T(8,128)(2,1)S(1)} %get-tuple-element.217), channel_id=1, source_target_pairs={{0,4},{1,5},{2,6},{3,7},{4,0},{5,1},{6,2},{7,3},{8,12},{9,13},{10,... | collective-permute-start | bytes 1253384 | tf_op jit(solution)/shard_map/ppermute | solution.py:35
  167.8 18.6 %collective-permute-start.38 = (bf16[96,2176]{1,0:T(8,128)(2,1)S(1)}, bf16[96,2176]{1,0:T(8,128)(2,1)S(1)}, u32[]{:S(2)}, u32[]{:S(2)}) collective-permute-start(bf16[96,2176]{1,0:T(8,128)(2,1)S(1)} %get-tuple-element.218), channel_id=1, source_target_pairs={{0,6},{1,7},{2,4},{3,5},{4,2},{5,3},{6,0},{7,1},{8,14},{9,15},{10,... | collective-permute-start | bytes 1253384 | tf_op jit(solution)/shard_map/ppermute | solution.py:35
  170.1 22.0 %collective-permute-start.43 = (bf16[96,768]{1,0:T(8,128)(2,1)S(1)}, bf16[96,768]{1,0:T(8,128)(2,1)S(1)}, u32[]{:S(2)}, u32[]{:S(2)}) collective-permute-start(bf16[96,768]{1,0:T(8,128)(2,1)S(1)} %get-tuple-element.254), channel_id=1, source_target_pairs={{0,16},{8,24},{16,0},{24,8},{1,17},{9,25},{17,1},{25,9},{2,18},{10... | collective-permute-start | bytes 442376 | tf_op jit(solution)/shard_map/ppermute | solution.py:35
  190.7 10.1 %collective-permute-start.41 = (bf16[96,1344]{1,0:T(8,128)(2,1)S(1)}, bf16[96,1344]{1,0:T(8,128)(2,1)S(1)}, u32[]{:S(2)}, u32[]{:S(2)}) collective-permute-start(bf16[96,1344]{1,0:T(8,128)(2,1)S(1)} %get-tuple-element.229), channel_id=1, source_target_pairs={{0,8},{8,0},{16,24},{24,16},{1,9},{9,1},{17,25},{25,17},{2,10},{10... | collective-permute-start | bytes 774152 | tf_op jit(solution)/shard_map/ppermute | solution.py:35
  190.8 10.4 %collective-permute-start.47 = (bf16[96,768]{1,0:T(8,128)(2,1)S(1)}, bf16[96,768]{1,0:T(8,128)(2,1)S(1)}, u32[]{:S(2)}, u32[]{:S(2)}) collective-permute-start(bf16[96,768]{1,0:T(8,128)(2,1)S(1)} %get-tuple-element.235), channel_id=1, source_target_pairs={{0,16},{8,24},{16,0},{24,8},{1,17},{9,25},{17,1},{25,9},{2,18},{10... | collective-permute-start | bytes 442376 | tf_op jit(solution)/shard_map/ppermute | solution.py:35
  201.1 12.8 %collective-permute-start.44 = (bf16[96,1216]{1,0:T(8,128)(2,1)S(1)}, bf16[96,1216]{1,0:T(8,128)(2,1)S(1)}, u32[]{:S(2)}, u32[]{:S(2)}) collective-permute-start(bf16[96,1216]{1,0:T(8,128)(2,1)S(1)} %concatenate.45), channel_id=1, source_target_pairs={{0,16},{8,24},{16,0},{24,8},{1,17},{9,25},{17,1},{25,9},{2,18},{10... | collective-permute-start | bytes 700424 | tf_op jit(solution)/shard_map/ppermute | solution.py:35
  201.4 20.7 %collective-permute-start.48 = (bf16[96,1536]{1,0:T(8,128)(2,1)S(1)}, bf16[96,1536]{1,0:T(8,128)(2,1)S(1)}, u32[]{:S(2)}, u32[]{:S(2)}) collective-permute-start(bf16[96,1536]{1,0:T(8,128)(2,1)S(1)} %add_convert_fusion.2), channel_id=1, source_target_pairs={{0,8},{8,0},{16,24},{24,16},{1,9},{9,1},{17,25},{25,17},{2,10},{10... | collective-permute-start | bytes 884744 | tf_op jit(solution)/shard_map/ppermute | solution.py:35
  213.9 8.1 %collective-permute-start.46 = (bf16[96,960]{1,0:T(8,128)(2,1)S(1)}, bf16[96,960]{1,0:T(8,128)(2,1)S(1)}, u32[]{:S(2)}, u32[]{:S(2)}) collective-permute-start(bf16[96,960]{1,0:T(8,128)(2,1)S(1)} %add_convert_fusion.4), channel_id=1, source_target_pairs={{0,8},{8,0},{16,24},{24,16},{1,9},{9,1},{17,25},{25,17},{2,10},{10... | collective-permute-start | bytes 552968 | tf_op jit(solution)/shard_map/ppermute | solution.py:35
  215.3 6.3 %collective-permute-start.45 = (bf16[96,256]{1,0:T(8,128)(2,1)S(1)}, bf16[96,256]{1,0:T(8,128)(2,1)S(1)}, u32[]{:S(2)}, u32[]{:S(2)}) collective-permute-start(bf16[96,256]{1,0:T(8,128)(2,1)S(1)} %pad_maximum_fusion.4), channel_id=1, source_target_pairs={{1,16},{3,18},{5,20},{7,22},{9,24},{11,26},{13,28},{15,30},{16,1},... | collective-permute-start | bytes 147464 | tf_op jit(solution)/shard_map/ppermute | solution.py:52
  (22 other events, 48.1 us)

commit v7 on v6

--- a/solution.py
+++ b/solution.py
@@ -1290,8 +1290,9 @@
     halos, small = after_all([jnp.concatenate(halos, axis=1), small], low)
     halos = jnp.where(stay, halos, move_home(halos))
     halos = jnp.split(halos, group_blocks // nb, axis=1)
-    other, zo_other = after_all([other, zo_other], *halos)
+    zo_other = after(zo_other, *halos)
     zo_grad = head_join(zo_half, zo_other).astype(F32)
+    other = after(other, zo_other)
     a_grad = head_join(low, other).astype(F32)
     small = small.reshape(SUM_ROWS, LANES)
 

time: 228 us -> 228 us (level)
    unnamed x72 -> x74, local copies, waits for them, and re-layouts: 5.73 us -> 5.16 us
where the time goes in v7:
time: 228 us; the launch traced here: 227 us
  Pallas kernels  76.3 us (33%)
  waiting for transfers between devices  62.4 us (27%)
  starting transfers between devices  42.4 us (19%)
  local copies, waits for them, and re-layouts  19.3 us (8%)
  other arithmetic  16.3 us (7%)
  matrix products  7.86 us (3%)
    pallas_call x9, Pallas kernels, call(): pl.pallas_call(kernel, grid=grid, out_shape=[o for o, _ in outs], in_spec...  76.3 us
    ppermute x41, waiting for transfers between devices, trade(): return lax.ppermute(value, axis, [(i, i ^ bit) for i in range(size)])  54.1 us
    ppermute x5, starting transfers between devices, move_home(): return lax.ppermute(value, ('head', 'shard'), pairs)  20.3 us
    ppermute x41, starting transfers between devices, trade(): return lax.ppermute(value, axis, [(i, i ^ bit) for i in range(size)])  20.1 us
    ppermute x5, waiting for transfers between devices, move_home(): return lax.ppermute(value, ('head', 'shard'), pairs)  7.65 us
    unnamed x74, local copies, waits for them, and re-layouts  5.16 us
  transfers between devices with their start and end apart: 49, of which 21 were waited for; matrix products, arithmetic and copies ran while one was open for 13% of the time, Pallas kernels for 27%

profile of v7, /device:TPU:1, one launch (start us, length us, event | category | flops | bytes accessed | tf_op | source)
XLA Modules:
  0.0 226.8 jit_solution(14602749645067185592)
XLA Ops:
  0.7 1.1 slice.120
  1.8 0.8 copy.31
  2.7 3.1 %collective-permute-start.1 = (bf16[96,1920]{1,0:T(8,128)(2,1)S(1)}, bf16[96,1920]{1,0:T(8,128)(2,1)S(1)}, u32[]{:S(2)}, u32[]{:S(2)}) collective-permute-start(bf16[96,1920]{1,0:T(8,128)(2,1)S(1)} %concatenate.42.refs_1_), channel_id=1, source_target_pairs={{0,6},{1,7},{2,4},{3,5},{4,2},{5,3},{6,0},{7,1},{8,14},{9,15},{10,... | collective-permute-start | bytes 1105928 | tf_op jit(solution)/shard_map/ppermute | solution.py:35
  6.2 1.2 collective-permute-start.4
  8.3 0.9 collective-permute-done
  9.3 4.7 %collective-permute-start.8 = (bf16[512,768]{1,0:T(8,128)(2,1)S(1)}, bf16[512,768]{1,0:T(8,128)(2,1)S(1)}, u32[]{:S(2)}, u32[]{:S(2)}) collective-permute-start(bf16[512,768]{1,0:T(8,128)(2,1)S(1)} %copy-done.16), channel_id=1, source_target_pairs={{1,16},{3,18},{5,20},{7,22},{9,24},{11,26},{13,28},{15,30},{16,1},... | collective-permute-start | bytes 2359304 | tf_op jit(solution)/shard_map/ppermute | solution.py:52
  14.0 0.7 broadcast_select_fusion.7
  16.9 1.1 compare_convert_fusion.refs_19_.refs_17_.refs_25_
  18.0 4.8 %collective-permute-done.2.refs_3_ = bf16[96,1920]{1,0:T(8,128)(2,1)} collective-permute-done((bf16[96,1920]{1,0:T(8,128)(2,1)S(1)}, bf16[96,1920]{1,0:T(8,128)(2,1)}, u32[]{:S(2)}, u32[]{:S(2)}) %collective-permute-start.2) | collective-permute-done | bytes 368672 | tf_op jit(solution)/shard_map/ppermute | solution.py:35
  23.6 1.0 compare_convert_fusion.1.refs_26_
  24.7 0.7 broadcast_in_dim.112
  25.4 0.7 broadcast_in_dim_reshape.3.refs_16_.refs_24_
  26.0 1.4 pad.17.refs_15_.refs_22_
  28.6 1.2 pad_bitcast_fusion
  29.8 2.2 collective-permute-done.8.refs_14_
  32.2 0.8 collective-permute-start.11
  33.0 1.1 collective-permute-start.9
  34.1 1.0 fusion.27
  35.8 6.3 %collective-permute-start.20 = (bf16[512,768]{1,0:T(8,128)(2,1)S(1)}, bf16[512,768]{1,0:T(8,128)(2,1)S(1)}, u32[]{:S(2)}, u32[]{:S(2)}) collective-permute-start(bf16[512,768]{1,0:T(8,128)(2,1)S(1)} %copy-done.4), channel_id=1, source_target_pairs={{1,16},{3,18},{5,20},{7,22},{9,24},{11,26},{13,28},{15,30},{16,1},... | collective-permute-start | bytes 2359304 | tf_op jit(solution)/shard_map/ppermute | solution.py:52
  42.2 2.2 collective-permute-start.13
  45.0 13.4 %shard_map.212 = (bf16[768,1920]{1,0:T(8,128)(2,1)}, bf16[512,768]{1,0:T(8,128)(2,1)}, bf16[16,768]{1,0:T(8,128)(2,1)}, bf16[528,768]{1,0:T(8,128)(2,1)}, bf16[7...) custom-call(s32[26]{0:T(128)} %pad_add_fusion.2.refs_0_, ...), custom_call_target="tpu_custom_call" | custom-call | flops 1 | bytes 20720000 | tf_op jit(solution)/shard_map/pallas_call | solution.py:235
  58.5 6.5 %shard_map.213.refs_9_ = f32[512,1536]{1,0:T(8,128)} custom-call(bf16[512,128]{1,0:T(8,128)(2,1)} %get-tuple-element.147.bs.refs_16_, bf16[512,128]{1,0:T(8,128)(2,1)} %get-tuple-element.148.cs.refs_10_, bf16[512,1536]{1,0:T(8,128)(2,1)} %get-tuple-element.149.xt.refs_15_, f32[512,128]{1,0:T(8,128)} %get-tuple-element.150.cum.refs_11_.refs_18_, ...), custom_call_target="tpu_custom_call" | custom-call | flops 1 | bytes 8880000 | tf_op jit(solution)/shard_map/pallas_call | solution.py:235
  65.0 2.1 collective-permute-done.14.refs_2_
  68.3 1.0 collective-permute-done.17.refs_5_
  69.4 0.7 collective-permute-done.18.refs_6_
  70.1 0.8 collective-permute-done.19.refs_7_
  71.0 0.8 collective-permute-done.16.refs_4_
  71.8 5.0 %shard_map.214 = (bf16[512,1536]{1,0:T(8,128)(2,1)S(1)}, bf16[512,1536]{1,0:T(8,128)(2,1)}, bf16[512,768]{1,0:T(8,128)(2,1)S(1)}, bf16[768,1536]{1,0:T(8,128)(2,1)}, bf16[1536,768]{1,0:T(8,128)(2,1)}) custom-call(s32[1]{0:T(128)} %bitcast.at, bf16[96,3072]{1,0:T(8,128)(2,1)S(1)} %pad_maximum_fusion.1.refs_0_, ...), custom_call_target="tpu_custom_call" | custom-call | flops 1 | bytes 1480000 | tf_op jit(solution)/shard_map/pallas_call | solution.py:235
  76.8 0.9 copy-done
  77.8 1.1 copy-done.2
  79.0 2.2 collective-permute-done.22.refs_4_.refs_8_
  81.3 0.9 copy-done.9
  82.2 14.4 %shard_map.215 = (bf16[2,128,1536]{2,1,0:T(8,128)(2,1)}, bf16[512,1536]{1,0:T(8,128)(2,1)}, f32[1,1536]{1,0:T(1,128)}, bf16[512,1536]{1,0:T(8,128)(2,1)}, bf16[5...) custom-call(s32[26]{0:T(128)} %pad_add_fusion.2.refs_0_, ...), custom_call_target="tpu_custom_call" | custom-call | flops 1 | bytes 23680000 | tf_op jit(solution)/shard_map/pallas_call | solution.py:235
  96.6 1.3 collective-permute-start.23
  97.9 7.7 %shard_map.216 = (bf16[4,96,3072]{2,1,0:T(8,128)(2,1)}, bf16[96,3072]{1,0:T(8,128)(2,1)}, bf16[96,3072]{1,0:T(8,128)(2,1)}, bf16[96,3072]{1,0:T(8,128)(2,1)}, bf16[96,3072]{1,0:T(8,128)(2,1)}) custom-call(s32[1]{0:T(128)} %bitcast.at, bf16[768,512]{1,0:T(8,128)(2,1)} %get-tuple-element.167.normal_t, bf16[512,1536]{1,0:T(8,128)(2,1)} %get-tuple-element.209.dz, ...), custom_call_target="tpu_custom_call" | custom-call | flops 1 | bytes 1480000 | tf_op jit(solution)/shard_map/pallas_call | solution.py:235
  106.6 11.5 %shard_map.217 = (f32[512,1536]{1,0:T(8,128)}, f32[512,128]{1,0:T(8,128)}, f32[512,128]{1,0:T(8,128)}, bf16[512,768]{1,0:T(8,128)(2,1)}) custom-call(bf16[512,128]{1,0:T(8,128)(2,1)} %get-tuple-element.147.bs.refs_16_, bf16[512,128]{1,0:T(8,128)(2,1)} %get-tuple-element.148.cs.refs_10_, bf16[512,1536]{1,0:T(8,128)(2,1)} %get-tuple-element.149.xt.refs_15_, ...), custom_call_target="tpu_custom_call" | custom-call | flops 1 | bytes 1480000 | tf_op jit(solution)/shard_map/pallas_call | solution.py:235
  118.2 2.2 add_convert_fusion
  120.4 1.3 dynamic-slice_bitcast_fusion.1
  122.5 1.6 collective-permute-done.28.refs_4_
  124.1 3.2 %collective-permute-start.29 = (bf16[512,768]{1,0:T(8,128)(2,1)}, bf16[512,768]{1,0:T(8,128)(2,1)S(1)}, u32[]{:S(2)}, u32[]{:S(2)}) collective-permute-start(bf16[512,768]{1,0:T(8,128)(2,1)} %get-tuple-element.190), channel_id=1, source_target_pairs={{1,16},{3,18},{5,20},{7,22},{9,24},{11,26},{13,28},{15,30},{16,1},... | collective-permute-start | bytes 2359304 | tf_op jit(solution)/shard_map/ppermute | solution.py:52
  127.6 1.2 collective-permute-start.33
  128.8 1.2 collective-permute-start.34
  130.2 17.1 %shard_map.218 = (bf16[528,1920]{1,0:T(8,128)(2,1)}, f32[96,128]{1,0:T(8,128)}) custom-call(s32[26]{0:T(128)} %pad_add_fusion.2.refs_0_, bf16[2,128,1536]{2,1,0:T(8,128)(2,1)} %get-tuple-element.181.refs_1_, bf16[2,128,1536]{2,1,0:T(8,128)(2,1)} %copy-done.20, bf16[2,128,1536]{2,1,0:T(8,128)(2,1)} %collective-permute-done.30.refs_3_, ...), custom_call_target="tpu_custom_call" | custom-call | flops 1 | bytes 2960000 | tf_op jit(solution)/shard_map/pallas_call | solution.py:235
  147.4 4.4 %convolution_convert_fusion = bf16[768,1920]{1,0:T(8,128)(2,1)S(1)} fusion(bf16[528,768]{1,0:T(8,128)(2,1)S(1)} %copy-done.3, bf16[528,1920]{1,0:T(8,128)(2,1)} %get-tuple-element.211), kind=kOutput, calls=%fused_computation.1 | convolution fusion | flops 1558609920 | bytes 5787648 | tf_op jit(solution)/shard_map/dot_general | solution.py:182
  152.6 2.8 %collective-permute-done.34 = bf16[96,3072]{1,0:T(8,128)(2,1)S(1)} collective-permute-done((bf16[96,3072]{1,0:T(8,128)(2,1)}, bf16[96,3072]{1,0:T(8,128)(2,1)S(1)}, u32[]{:S(2)}, u32[]{:S(2)}) %collective-permute-start.34) | collective-permute-done | bytes 589856 | tf_op jit(solution)/shard_map/ppermute | solution.py:35
  156.4 1.9 fusion.29
  158.8 1.6 fusion.2
  160.4 1.0 broadcast_select_fusion.1
  162.9 3.2 %collective-permute-start.39 = (bf16[512,768]{1,0:T(8,128)(2,1)S(1)}, bf16[512,768]{1,0:T(8,128)(2,1)}, u32[]{:S(2)}, u32[]{:S(2)}) collective-permute-start(bf16[512,768]{1,0:T(8,128)(2,1)S(1)} %fusion.6), channel_id=1, source_target_pairs={{1,16},{3,18},{5,20},{7,22},{9,24},{11,26},{13,28},{15,30},{16,1},... | collective-permute-start | bytes 2359304 | tf_op jit(solution)/shard_map/ppermute | solution.py:52
  166.9 0.9 collective-permute-start.37
  167.8 1.2 collective-permute-start.38
  169.1 1.0 add_convert_fusion.3
  170.1 1.5 collective-permute-start.43
  171.6 5.6 %collective-permute-done.36.refs_1_ = bf16[96,2176]{1,0:T(8,128)(2,1)S(1)} collective-permute-done((bf16[96,2176]{1,0:T(8,128)(2,1)S(1)}, bf16[96,2176]{1,0:T(8,128)(2,1)S(1)}, u32[]{:S(2)}, u32[]{:S(2)}) %collective-permute-start.36) | collective-permute-done | bytes 417824 | tf_op jit(solution)/shard_map/ppermute | solution.py:35
  177.4 9.1 %collective-permute-done.38.refs_3_ = bf16[96,2176]{1,0:T(8,128)(2,1)S(1)} collective-permute-done((bf16[96,2176]{1,0:T(8,128)(2,1)S(1)}, bf16[96,2176]{1,0:T(8,128)(2,1)S(1)}, u32[]{:S(2)}, u32[]{:S(2)}) %collective-permute-start.38) | collective-permute-done | bytes 417824 | tf_op jit(solution)/shard_map/ppermute | solution.py:35
  186.4 3.9 %collective-permute-done.39 = bf16[512,768]{1,0:T(8,128)(2,1)} collective-permute-done((bf16[512,768]{1,0:T(8,128)(2,1)S(1)}, bf16[512,768]{1,0:T(8,128)(2,1)}, u32[]{:S(2)}, u32[]{:S(2)}) %collective-permute-start.39) | collective-permute-done | bytes 786464 | tf_op jit(solution)/shard_map/ppermute | solution.py:52
  190.9 1.2 broadcast_select_fusion
  192.1 8.7 %collective-permute-done.41 = bf16[96,1344]{1,0:T(8,128)(2,1)S(1)} collective-permute-done((bf16[96,1344]{1,0:T(8,128)(2,1)S(1)}, bf16[96,1344]{1,0:T(8,128)(2,1)S(1)}, u32[]{:S(2)}, u32[]{:S(2)}) %collective-permute-start.41) | collective-permute-done | bytes 258080 | tf_op jit(solution)/shard_map/ppermute | solution.py:35
  201.5 12.4 %collective-permute-done.44 = bf16[96,1216]{1,0:T(8,128)(2,1)S(1)} collective-permute-done((bf16[96,1216]{1,0:T(8,128)(2,1)S(1)}, bf16[96,1216]{1,0:T(8,128)(2,1)S(1)}, u32[]{:S(2)}, u32[]{:S(2)}) %collective-permute-start.44) | collective-permute-done | bytes 233504 | tf_op jit(solution)/shard_map/ppermute | solution.py:35
  215.3 3.0 %collective-permute-start.45 = (bf16[96,256]{1,0:T(8,128)(2,1)S(1)}, bf16[96,256]{1,0:T(8,128)(2,1)S(1)}, u32[]{:S(2)}, u32[]{:S(2)}) collective-permute-start(bf16[96,256]{1,0:T(8,128)(2,1)S(1)} %pad_maximum_fusion.4), channel_id=1, source_target_pairs={{1,16},{3,18},{5,20},{7,22},{9,24},{11,26},{13,28},{15,30},{16,1},... | collective-permute-start | bytes 147464 | tf_op jit(solution)/shard_map/ppermute | solution.py:52
  220.2 1.5 collective-permute-done.45
  223.0 0.9 pad_maximum_fusion.2
  224.3 0.7 slice-done
  224.9 1.3 multiply_reduce_fusion
  (213 shorter events, 21.4 us)
Async XLA Ops:
  0.7 8.6 %copy-start.16 = (bf16[512,768]{1,0:T(8,128)(2,1)S(1)}, bf16[512,768]{1,0:T(8,128)(2,1)}, u32[]{:S(2)}) copy-start(bf16[512,768]{1,0:T(8,128)(2,1)} %refs_13_.1) | copy-start | bytes 2359300
  1.8 25.7 %copy-start.31 = (f32[1792]{0:T(1024)S(1)}, f32[1792]{0:T(1024)}, u32[]{:S(2)}) copy-start(f32[1792]{0:T(1024)} %param.19) | copy-start | bytes 21508
  1.8 26.2 %copy-start.30 = (f32[1536]{0:T(1024)S(1)}, f32[1536]{0:T(1024)}, u32[]{:S(2)}) copy-start(f32[1536]{0:T(1024)} %param.23) | copy-start | bytes 18436
  2.7 39.5 %copy-start.15 = (bf16[96,1920]{1,0:T(8,128)(2,1)}, bf16[96,1920]{1,0:T(8,128)(2,1)S(1)}, u32[]{:S(2)}) copy-start(bf16[96,1920]{1,0:T(8,128)(2,1)S(1)} %concatenate.42.refs_1_) | copy-start | bytes 1105924
  2.7 33.1 %copy-start.4 = (bf16[512,768]{1,0:T(8,128)(2,1)S(1)}, bf16[512,768]{1,0:T(8,128)(2,1)}, u32[]{:S(2)}) copy-start(bf16[512,768]{1,0:T(8,128)(2,1)} %refs_9_.1) | copy-start | bytes 2359300
  2.7 39.4 %slice-start.1 = ((bf16[96,3352]{1,0:T(8,128)(2,1)}), bf16[96,1536]{1,0:T(8,128)(2,1)S(1)}, s32[]{:S(2)}) async-start(bf16[96,3352]{1,0:T(8,128)(2,1)} %param.17), calls=%async_computation.1 | async-start | bytes 589824 | tf_op jit(solution)/shard_map/slice | solution.py:1167
  2.7 14.2 %collective-permute-start.1 = (bf16[96,1920]{1,0:T(8,128)(2,1)S(1)}, bf16[96,1920]{1,0:T(8,128)(2,1)S(1)}, u32[]{:S(2)}, u32[]{:S(2)}) collective-permute-start(bf16[96,1920]{1,0:T(8,128)(2,1)S(1)} %concatenate.42.refs_1_), channel_id=1, source_target_pairs={{0,6},{1,7},{2,4},{3,5},{4,2},{5,3},{6,0},{7,1},{8,14},{9,15},{10,... | collective-permute-start | bytes 1105928 | tf_op jit(solution)/shard_map/ppermute | solution.py:35
  5.8 17.1 %collective-permute-start.2 = (bf16[96,1920]{1,0:T(8,128)(2,1)S(1)}, bf16[96,1920]{1,0:T(8,128)(2,1)}, u32[]{:S(2)}, u32[]{:S(2)}) collective-permute-start(bf16[96,1920]{1,0:T(8,128)(2,1)S(1)} %concatenate.42.refs_1_), channel_id=1, source_target_pairs={{0,4},{1,5},{2,6},{3,7},{4,0},{5,1},{6,2},{7,3},{8,12},{9,13},{10,... | collective-permute-start | bytes 1105928 | tf_op jit(solution)/shard_map/ppermute | solution.py:35
  6.0 17.3 %collective-permute-start.3 = (bf16[96,1920]{1,0:T(8,128)(2,1)S(1)}, bf16[96,1920]{1,0:T(8,128)(2,1)}, u32[]{:S(2)}, u32[]{:S(2)}) collective-permute-start(bf16[96,1920]{1,0:T(8,128)(2,1)S(1)} %concatenate.42.refs_1_), channel_id=1, source_target_pairs={{0,2},{1,3},{2,0},{3,1},{4,6},{5,7},{6,4},{7,5},{8,10},{9,11},{10,... | collective-permute-start | bytes 1105928 | tf_op jit(solution)/shard_map/ppermute | solution.py:35
  6.2 25.9 %collective-permute-start.4 = (bf16[96,1920]{1,0:T(8,128)(2,1)S(1)}, bf16[96,1920]{1,0:T(8,128)(2,1)}, u32[]{:S(2)}, u32[]{:S(2)}) collective-permute-start(bf16[96,1920]{1,0:T(8,128)(2,1)S(1)} %concatenate.42.refs_1_), channel_id=1, source_target_pairs={{0,1},{1,0},{2,3},{3,2},{4,5},{5,4},{6,7},{7,6},{8,9},{9,8},{10,11... | collective-permute-start | bytes 1105928 | tf_op jit(solution)/shard_map/ppermute | solution.py:35
  8.1 1.1 collective-permute-start
  9.3 22.8 %collective-permute-start.8 = (bf16[512,768]{1,0:T(8,128)(2,1)S(1)}, bf16[512,768]{1,0:T(8,128)(2,1)S(1)}, u32[]{:S(2)}, u32[]{:S(2)}) collective-permute-start(bf16[512,768]{1,0:T(8,128)(2,1)S(1)} %copy-done.16), channel_id=1, source_target_pairs={{1,16},{3,18},{5,20},{7,22},{9,24},{11,26},{13,28},{15,30},{16,1},... | collective-permute-start | bytes 2359304 | tf_op jit(solution)/shard_map/ppermute | solution.py:52
  16.9 25.3 %copy-start.22 = (bf16[96,1920]{1,0:T(8,128)(2,1)}, bf16[96,1920]{1,0:T(8,128)(2,1)S(1)}, u32[]{:S(2)}) copy-start(bf16[96,1920]{1,0:T(8,128)(2,1)S(1)} %collective-permute-done.1.refs_2_) | copy-start | bytes 1105924
  18.0 14.1 %collective-permute-start.5 = (bf16[96,1920]{1,0:T(8,128)(2,1)S(1)}, bf16[96,1920]{1,0:T(8,128)(2,1)}, u32[]{:S(2)}, u32[]{:S(2)}) collective-permute-start(bf16[96,1920]{1,0:T(8,128)(2,1)S(1)} %collective-permute-done.1.refs_2_), channel_id=1, source_target_pairs={{0,1},{1,0},{2,3},{3,2},{4,5},{5,4},{6,7},{7,6},{8,9},{9,8},{10,11... | collective-permute-start | bytes 1105928 | tf_op jit(solution)/shard_map/ppermute | solution.py:35
  22.8 9.3 %collective-permute-start.6 = (bf16[96,1920]{1,0:T(8,128)(2,1)}, bf16[96,1920]{1,0:T(8,128)(2,1)}, u32[]{:S(2)}, u32[]{:S(2)}) collective-permute-start(bf16[96,1920]{1,0:T(8,128)(2,1)} %collective-permute-done.2.refs_3_), channel_id=1, source_target_pairs={{0,1},{1,0},{2,3},{3,2},{4,5},{5,4},{6,7},{7,6},{8,9},{9,8},{10,11... | collective-permute-start | bytes 1105928 | tf_op jit(solution)/shard_map/ppermute | solution.py:35
  23.3 8.8 %collective-permute-start.7 = (bf16[96,1920]{1,0:T(8,128)(2,1)}, bf16[96,1920]{1,0:T(8,128)(2,1)}, u32[]{:S(2)}, u32[]{:S(2)}) collective-permute-start(bf16[96,1920]{1,0:T(8,128)(2,1)} %collective-permute-done.3.refs_4_), channel_id=1, source_target_pairs={{0,1},{1,0},{2,3},{3,2},{4,5},{5,4},{6,7},{7,6},{8,9},{9,8},{10,11... | collective-permute-start | bytes 1105928 | tf_op jit(solution)/shard_map/ppermute | solution.py:35
  32.0 12.9 %copy-start.17 = (bf16[512,768]{1,0:T(8,128)(2,1)}, bf16[512,768]{1,0:T(8,128)(2,1)S(1)}, u32[]{:S(2)}) copy-start(bf16[512,768]{1,0:T(8,128)(2,1)S(1)} %collective-permute-done.8.refs_14_) | copy-start | bytes 2359300
  32.1 12.9 %copy-start.25 = (bf16[16,768]{1,0:T(8,128)(2,1)}, bf16[16,768]{1,0:T(8,128)(2,1)S(1)}, u32[]{:S(2)}) copy-start(bf16[16,768]{1,0:T(8,128)(2,1)S(1)} %fusion.19.refs_9_) | copy-start | bytes 73732
  32.1 2.9 %collective-permute-start.10 = (bf16[16,768]{1,0:T(8,128)(2,1)S(1)}, bf16[16,768]{1,0:T(8,128)(2,1)S(1)}, u32[]{:S(2)}, u32[]{:S(2)}) collective-permute-start(bf16[16,768]{1,0:T(8,128)(2,1)S(1)} %fusion.19.refs_9_), channel_id=1, source_target_pairs={{0,1},{1,0},{2,3},{3,2},{4,5},{5,4},{6,7},{7,6},{8,9},{9,8},{10,11... | collective-permute-start | bytes 73736 | tf_op jit(solution)/shard_map/ppermute | solution.py:70
  32.2 3.4 %collective-permute-start.11 = (bf16[16,768]{1,0:T(8,128)(2,1)S(1)}, bf16[16,768]{1,0:T(8,128)(2,1)S(1)}, u32[]{:S(2)}, u32[]{:S(2)}) collective-permute-start(bf16[16,768]{1,0:T(8,128)(2,1)S(1)} %fusion.19.refs_9_), channel_id=1, source_target_pairs={{0,9},{1,8},{2,11},{3,10},{4,13},{5,12},{6,15},{7,14},{8,1},{9,0},... | collective-permute-start | bytes 73736 | tf_op jit(solution)/shard_map/ppermute | solution.py:70
  33.0 2.8 %collective-permute-start.9 = (bf16[16,768]{1,0:T(8,128)(2,1)S(1)}, bf16[16,768]{1,0:T(8,128)(2,1)S(1)}, u32[]{:S(2)}, u32[]{:S(2)}) collective-permute-start(bf16[16,768]{1,0:T(8,128)(2,1)S(1)} %fusion.19.refs_9_), channel_id=1, source_target_pairs={{0,8},{1,9},{2,10},{3,11},{4,12},{5,13},{6,14},{7,15},{8,0},{9,1},... | collective-permute-start | bytes 73736 | tf_op jit(solution)/shard_map/ppermute | solution.py:70
  35.1 9.9 %copy-start.26 = (bf16[16,768]{1,0:T(8,128)(2,1)}, bf16[16,768]{1,0:T(8,128)(2,1)S(1)}, u32[]{:S(2)}) copy-start(bf16[16,768]{1,0:T(8,128)(2,1)S(1)} %collective-permute-done.10.refs_11_) | copy-start | bytes 73732
  35.6 9.4 %copy-start.27 = (bf16[16,768]{1,0:T(8,128)(2,1)}, bf16[16,768]{1,0:T(8,128)(2,1)S(1)}, u32[]{:S(2)}) copy-start(bf16[16,768]{1,0:T(8,128)(2,1)S(1)} %collective-permute-done.11.refs_12_) | copy-start | bytes 73732
  35.8 9.2 %copy-start.28 = (bf16[16,768]{1,0:T(8,128)(2,1)}, bf16[16,768]{1,0:T(8,128)(2,1)S(1)}, u32[]{:S(2)}) copy-start(bf16[16,768]{1,0:T(8,128)(2,1)S(1)} %collective-permute-done.9.refs_10_) | copy-start | bytes 73732
  35.8 32.1 %collective-permute-start.20 = (bf16[512,768]{1,0:T(8,128)(2,1)S(1)}, bf16[512,768]{1,0:T(8,128)(2,1)S(1)}, u32[]{:S(2)}, u32[]{:S(2)}) collective-permute-start(bf16[512,768]{1,0:T(8,128)(2,1)S(1)} %copy-done.4), channel_id=1, source_target_pairs={{1,16},{3,18},{5,20},{7,22},{9,24},{11,26},{13,28},{15,30},{16,1},... | collective-permute-start | bytes 2359304 | tf_op jit(solution)/shard_map/ppermute | solution.py:52
  42.2 22.8 %collective-permute-start.13 = (bf16[96,3072]{1,0:T(8,128)(2,1)S(1)}, bf16[96,3072]{1,0:T(8,128)(2,1)S(1)}, u32[]{:S(2)}, u32[]{:S(2)}) collective-permute-start(bf16[96,3072]{1,0:T(8,128)(2,1)S(1)} %pad_maximum_fusion.1.refs_0_), channel_id=1, source_target_pairs={{0,6},{1,7},{2,4},{3,5},{4,2},{5,3},{6,0},{7,1},{8,14},{9,15},{10,... | collective-permute-start | bytes 1769480 | tf_op jit(solution)/shard_map/ppermute | solution.py:35
  44.5 22.7 %collective-permute-start.14 = (bf16[96,3072]{1,0:T(8,128)(2,1)S(1)}, bf16[96,3072]{1,0:T(8,128)(2,1)S(1)}, u32[]{:S(2)}, u32[]{:S(2)}) collective-permute-start(bf16[96,3072]{1,0:T(8,128)(2,1)S(1)} %pad_maximum_fusion.1.refs_0_), channel_id=1, source_target_pairs={{0,4},{1,5},{2,6},{3,7},{4,0},{5,1},{6,2},{7,3},{8,12},{9,13},{10,... | collective-permute-start | bytes 1769480 | tf_op jit(solution)/shard_map/ppermute | solution.py:35
  44.7 22.6 %collective-permute-start.15 = (bf16[96,3072]{1,0:T(8,128)(2,1)S(1)}, bf16[96,3072]{1,0:T(8,128)(2,1)S(1)}, u32[]{:S(2)}, u32[]{:S(2)}) collective-permute-start(bf16[96,3072]{1,0:T(8,128)(2,1)S(1)} %pad_maximum_fusion.1.refs_0_), channel_id=1, source_target_pairs={{0,2},{1,3},{2,0},{3,1},{4,6},{5,7},{6,4},{7,5},{8,10},{9,11},{10,... | collective-permute-start | bytes 1769480 | tf_op jit(solution)/shard_map/ppermute | solution.py:35
  58.4 20.5 %collective-permute-start.12 = (bf16[2,128,1664]{2,1,0:T(8,128)(2,1)}, bf16[2,128,1664]{2,1,0:T(8,128)(2,1)S(1)}, u32[]{:S(2)}, u32[]{:S(2)}) collective-permute-start(bf16[2,128,1664]{2,1,0:T(8,128)(2,1)} %get-tuple-element.152.refs_1_.refs_5_), channel_id=1, source_target_pairs={{0,8},{8,0},{16,24},{24,16},{1,9},{9,1},{17,25},{25,17},{2,10},{10... | collective-permute-start | bytes 2555912 | tf_op jit(solution)/shard_map/ppermute | solution.py:35
  58.5 10.8 %copy-start.6 = (bf16[2,128,1664]{2,1,0:T(8,128)(2,1)S(1)}, bf16[2,128,1664]{2,1,0:T(8,128)(2,1)}, u32[]{:S(2)}) copy-start(bf16[2,128,1664]{2,1,0:T(8,128)(2,1)} %get-tuple-element.152.refs_1_.refs_5_) | copy-start | bytes 2555908
  58.5 13.3 %copy-start.3 = (bf16[528,768]{1,0:T(8,128)(2,1)S(1)}, bf16[528,768]{1,0:T(8,128)(2,1)}, u32[]{:S(2)}) copy-start(bf16[528,768]{1,0:T(8,128)(2,1)} %get-tuple-element.159.refs_8_) | copy-start | bytes 2433028
  67.3 2.0 collective-permute-start.17
  67.4 2.7 %collective-permute-start.18 = (bf16[96,3072]{1,0:T(8,128)(2,1)S(1)}, bf16[96,3072]{1,0:T(8,128)(2,1)S(1)}, u32[]{:S(2)}, u32[]{:S(2)}) collective-permute-start(bf16[96,3072]{1,0:T(8,128)(2,1)S(1)} %collective-permute-done.14.refs_2_), channel_id=1, source_target_pairs={{0,1},{1,0},{2,3},{3,2},{4,5},{5,4},{6,7},{7,6},{8,9},{9,8},{10,11... | collective-permute-start | bytes 1769480 | tf_op jit(solution)/shard_map/ppermute | solution.py:35
  67.8 3.2 %collective-permute-start.19 = (bf16[96,3072]{1,0:T(8,128)(2,1)S(1)}, bf16[96,3072]{1,0:T(8,128)(2,1)S(1)}, u32[]{:S(2)}, u32[]{:S(2)}) collective-permute-start(bf16[96,3072]{1,0:T(8,128)(2,1)S(1)} %collective-permute-done.15.refs_3_), channel_id=1, source_target_pairs={{0,1},{1,0},{2,3},{3,2},{4,5},{5,4},{6,7},{7,6},{8,9},{9,8},{10,11... | collective-permute-start | bytes 1769480 | tf_op jit(solution)/shard_map/ppermute | solution.py:35
  67.9 3.9 %collective-permute-start.16 = (bf16[96,3072]{1,0:T(8,128)(2,1)S(1)}, bf16[96,3072]{1,0:T(8,128)(2,1)S(1)}, u32[]{:S(2)}, u32[]{:S(2)}) collective-permute-start(bf16[96,3072]{1,0:T(8,128)(2,1)S(1)} %pad_maximum_fusion.1.refs_0_), channel_id=1, source_target_pairs={{0,1},{1,0},{2,3},{3,2},{4,5},{5,4},{6,7},{7,6},{8,9},{9,8},{10,11... | collective-permute-start | bytes 1769480 | tf_op jit(solution)/shard_map/ppermute | solution.py:35
  69.3 9.8 %collective-permute-start.21 = (bf16[2,128,1664]{2,1,0:T(8,128)(2,1)S(1)}, bf16[2,128,1664]{2,1,0:T(8,128)(2,1)S(1)}, u32[]{:S(2)}, u32[]{:S(2)}) collective-permute-start(bf16[2,128,1664]{2,1,0:T(8,128)(2,1)S(1)} %copy-done.6), channel_id=1, source_target_pairs={{0,1},{1,0},{2,3},{3,2},{4,5},{5,4},{6,7},{7,6},{8,9},{9,8},{10,11... | collective-permute-start | bytes 2555912 | tf_op jit(solution)/shard_map/ppermute | solution.py:35
  78.9 2.4 %collective-permute-start.22 = (bf16[2,128,1664]{2,1,0:T(8,128)(2,1)S(1)}, bf16[2,128,1664]{2,1,0:T(8,128)(2,1)S(1)}, u32[]{:S(2)}, u32[]{:S(2)}) collective-permute-start(bf16[2,128,1664]{2,1,0:T(8,128)(2,1)S(1)} %collective-permute-done.12.refs_2_.refs_6_), channel_id=1, source_target_pairs={{0,1},{1,0},{2,3},{3,2},{4,5},{5,4},{6,7},{7,6},{8,9},{9,8},{10,11... | collective-permute-start | bytes 2555912 | tf_op jit(solution)/shard_map/ppermute | solution.py:35
  96.6 21.5 %collective-permute-start.23 = (bf16[2,128,1536]{2,1,0:T(8,128)(2,1)}, bf16[2,128,1536]{2,1,0:T(8,128)(2,1)S(1)}, u32[]{:S(2)}, u32[]{:S(2)}) collective-permute-start(bf16[2,128,1536]{2,1,0:T(8,128)(2,1)} %get-tuple-element.181.refs_1_), channel_id=1, source_target_pairs={{0,8},{8,0},{16,24},{24,16},{1,9},{9,1},{17,25},{25,17},{2,10},{10... | collective-permute-start | bytes 2359304 | tf_op jit(solution)/shard_map/ppermute | solution.py:35
  105.6 12.5 %collective-permute-start.24 = (bf16[96,3072]{1,0:T(8,128)(2,1)}, bf16[96,3072]{1,0:T(8,128)(2,1)S(1)}, u32[]{:S(2)}, u32[]{:S(2)}) collective-permute-start(bf16[96,3072]{1,0:T(8,128)(2,1)} %get-tuple-element.171), channel_id=1, source_target_pairs={{0,1},{1,0},{2,3},{3,2},{4,5},{5,4},{6,7},{7,6},{8,9},{9,8},{10,11... | collective-permute-start | bytes 1769480 | tf_op jit(solution)/shard_map/ppermute | solution.py:35
  106.0 12.1 %collective-permute-start.25 = (bf16[96,3072]{1,0:T(8,128)(2,1)}, bf16[96,3072]{1,0:T(8,128)(2,1)S(1)}, u32[]{:S(2)}, u32[]{:S(2)}) collective-permute-start(bf16[96,3072]{1,0:T(8,128)(2,1)} %get-tuple-element.172), channel_id=1, source_target_pairs={{0,1},{1,0},{2,3},{3,2},{4,5},{5,4},{6,7},{7,6},{8,9},{9,8},{10,11... | collective-permute-start | bytes 1769480 | tf_op jit(solution)/shard_map/ppermute | solution.py:35
  106.1 12.0 %collective-permute-start.26 = (bf16[96,3072]{1,0:T(8,128)(2,1)}, bf16[96,3072]{1,0:T(8,128)(2,1)}, u32[]{:S(2)}, u32[]{:S(2)}) collective-permute-start(bf16[96,3072]{1,0:T(8,128)(2,1)} %get-tuple-element.173), channel_id=1, source_target_pairs={{0,1},{1,0},{2,3},{3,2},{4,5},{5,4},{6,7},{7,6},{8,9},{9,8},{10,11... | collective-permute-start | bytes 1769480 | tf_op jit(solution)/shard_map/ppermute | solution.py:35
  106.5 11.6 %collective-permute-start.27 = (bf16[96,3072]{1,0:T(8,128)(2,1)}, bf16[96,3072]{1,0:T(8,128)(2,1)}, u32[]{:S(2)}, u32[]{:S(2)}) collective-permute-start(bf16[96,3072]{1,0:T(8,128)(2,1)} %get-tuple-element.174), channel_id=1, source_target_pairs={{0,1},{1,0},{2,3},{3,2},{4,5},{5,4},{6,7},{7,6},{8,9},{9,8},{10,11... | collective-permute-start | bytes 1769480 | tf_op jit(solution)/shard_map/ppermute | solution.py:35
  106.6 11.5 %copy-start.13 = (bf16[4,96,3072]{2,1,0:T(8,128)(2,1)S(1)}, bf16[4,96,3072]{2,1,0:T(8,128)(2,1)}, u32[]{:S(2)}) copy-start(bf16[4,96,3072]{2,1,0:T(8,128)(2,1)} %get-tuple-element.184) | copy-start | bytes 7077892
  121.7 2.5 %collective-permute-start.28 = (bf16[2,128,1536]{2,1,0:T(8,128)(2,1)S(1)}, bf16[2,128,1536]{2,1,0:T(8,128)(2,1)}, u32[]{:S(2)}, u32[]{:S(2)}) collective-permute-start(bf16[2,128,1536]{2,1,0:T(8,128)(2,1)S(1)} %collective-permute-done.23.refs_2_), channel_id=1, source_target_pairs={{0,1},{1,0},{2,3},{3,2},{4,5},{5,4},{6,7},{7,6},{8,9},{9,8},{10,11... | collective-permute-start | bytes 2359304 | tf_op jit(solution)/shard_map/ppermute | solution.py:35
  122.4 7.9 %collective-permute-start.30 = (bf16[2,128,1536]{2,1,0:T(8,128)(2,1)S(1)}, bf16[2,128,1536]{2,1,0:T(8,128)(2,1)}, u32[]{:S(2)}, u32[]{:S(2)}) collective-permute-start(bf16[2,128,1536]{2,1,0:T(8,128)(2,1)S(1)} %copy-done.19), channel_id=1, source_target_pairs={{0,1},{1,0},{2,3},{3,2},{4,5},{5,4},{6,7},{7,6},{8,9},{9,8},{10,11... | collective-permute-start | bytes 2359304 | tf_op jit(solution)/shard_map/ppermute | solution.py:35
  124.1 23.2 %collective-permute-start.29 = (bf16[512,768]{1,0:T(8,128)(2,1)}, bf16[512,768]{1,0:T(8,128)(2,1)S(1)}, u32[]{:S(2)}, u32[]{:S(2)}) collective-permute-start(bf16[512,768]{1,0:T(8,128)(2,1)} %get-tuple-element.190), channel_id=1, source_target_pairs={{1,16},{3,18},{5,20},{7,22},{9,24},{11,26},{13,28},{15,30},{16,1},... | collective-permute-start | bytes 2359304 | tf_op jit(solution)/shard_map/ppermute | solution.py:52
  127.6 25.0 %collective-permute-start.33 = (bf16[96,3072]{1,0:T(8,128)(2,1)}, bf16[96,3072]{1,0:T(8,128)(2,1)S(1)}, u32[]{:S(2)}, u32[]{:S(2)}) collective-permute-start(bf16[96,3072]{1,0:T(8,128)(2,1)} %get-tuple-element.243), channel_id=1, source_target_pairs={{0,2},{1,3},{2,0},{3,1},{4,6},{5,7},{6,4},{7,5},{8,10},{9,11},{10,... | collective-permute-start | bytes 1769480 | tf_op jit(solution)/shard_map/ppermute | solution.py:35
  128.8 26.6 %collective-permute-start.34 = (bf16[96,3072]{1,0:T(8,128)(2,1)}, bf16[96,3072]{1,0:T(8,128)(2,1)S(1)}, u32[]{:S(2)}, u32[]{:S(2)}) collective-permute-start(bf16[96,3072]{1,0:T(8,128)(2,1)} %get-tuple-element.242), channel_id=1, source_target_pairs={{0,4},{1,5},{2,6},{3,7},{4,0},{5,1},{6,2},{7,3},{8,12},{9,13},{10,... | collective-permute-start | bytes 1769480 | tf_op jit(solution)/shard_map/ppermute | solution.py:35
  130.0 25.4 %collective-permute-start.35 = (bf16[96,3072]{1,0:T(8,128)(2,1)}, bf16[96,3072]{1,0:T(8,128)(2,1)S(1)}, u32[]{:S(2)}, u32[]{:S(2)}) collective-permute-start(bf16[96,3072]{1,0:T(8,128)(2,1)} %get-tuple-element.241), channel_id=1, source_target_pairs={{0,6},{1,7},{2,4},{3,5},{4,2},{5,3},{6,0},{7,1},{8,14},{9,15},{10,... | collective-permute-start | bytes 1769480 | tf_op jit(solution)/shard_map/ppermute | solution.py:35
  151.9 10.4 %collective-permute-start.31 = (bf16[4,96,1920]{2,1,0:T(8,128)(2,1)S(1)}, bf16[4,96,1920]{2,1,0:T(8,128)(2,1)S(1)}, u32[]{:S(2)}, u32[]{:S(2)}) collective-permute-start(bf16[4,96,1920]{2,1,0:T(8,128)(2,1)S(1)} %dynamic-slice_bitcast_fusion), channel_id=1, source_target_pairs={{0,1},{1,0},{2,3},{3,2},{4,5},{5,4},{6,7},{7,6},{8,9},{9,8},{10,11... | collective-permute-start | bytes 4423688 | tf_op jit(solution)/shard_map/ppermute | solution.py:35
  152.6 9.7 %collective-permute-start.32 = (f32[96,128]{1,0:T(8,128)S(1)}, f32[96,128]{1,0:T(8,128)S(1)}, u32[]{:S(2)}, u32[]{:S(2)}) collective-permute-start(f32[96,128]{1,0:T(8,128)S(1)} %copy-done.5), channel_id=1, source_target_pairs={{0,1},{1,0},{2,3},{3,2},{4,5},{5,4},{6,7},{7,6},{8,9},{9,8},{10,11... | collective-permute-start | bytes 147464 | tf_op jit(solution)/shard_map/ppermute | solution.py:35
  155.8 10.3 %collective-permute-start.42 = (bf16[96,1536]{1,0:T(8,128)(2,1)S(1)}, bf16[96,1536]{1,0:T(8,128)(2,1)S(1)}, u32[]{:S(2)}, u32[]{:S(2)}) collective-permute-start(bf16[96,1536]{1,0:T(8,128)(2,1)S(1)} %constant_dynamic-slice_fusion), channel_id=1, source_target_pairs={{0,8},{8,0},{16,24},{24,16},{1,9},{9,1},{17,25},{25,17},{2,10},{10... | collective-permute-start | bytes 884744 | tf_op jit(solution)/shard_map/ppermute | solution.py:35
  162.9 27.5 %collective-permute-start.39 = (bf16[512,768]{1,0:T(8,128)(2,1)S(1)}, bf16[512,768]{1,0:T(8,128)(2,1)}, u32[]{:S(2)}, u32[]{:S(2)}) collective-permute-start(bf16[512,768]{1,0:T(8,128)(2,1)S(1)} %fusion.6), channel_id=1, source_target_pairs={{1,16},{3,18},{5,20},{7,22},{9,24},{11,26},{13,28},{15,30},{16,1},... | collective-permute-start | bytes 2359304 | tf_op jit(solution)/shard_map/ppermute | solution.py:52
  166.3 3.9 %collective-permute-start.40 = (bf16[96,64]{1,0:T(8,128)(2,1)S(1)}, bf16[96,64]{1,0:T(8,128)(2,1)S(1)}, u32[]{:S(2)}, u32[]{:S(2)}) collective-permute-start(bf16[96,64]{1,0:T(8,128)(2,1)S(1)} %reshape.318.refs_4_), channel_id=1, source_target_pairs={{0,1},{1,0},{2,3},{3,2},{4,5},{5,4},{6,7},{7,6},{8,9},{9,8},{10,11... | collective-permute-start | bytes 36872 | tf_op jit(solution)/shard_map/ppermute | solution.py:35
  166.3 10.8 %collective-permute-start.36 = (bf16[96,2176]{1,0:T(8,128)(2,1)S(1)}, bf16[96,2176]{1,0:T(8,128)(2,1)S(1)}, u32[]{:S(2)}, u32[]{:S(2)}) collective-permute-start(bf16[96,2176]{1,0:T(8,128)(2,1)S(1)} %get-tuple-element.216), channel_id=1, source_target_pairs={{0,2},{1,3},{2,0},{3,1},{4,6},{5,7},{6,4},{7,5},{8,10},{9,11},{10,... | collective-permute-start | bytes 1253384 | tf_op jit(solution)/shard_map/ppermute | solution.py:35
  166.9 10.5 %collective-permute-start.37 = (bf16[96,2176]{1,0:T(8,128)(2,1)S(1)}, bf16[96,2176]{1,0:T(8,128)(2,1)S(1)}, u32[]{:S(2)}, u32[]{:S(2)}) collective-permute-start(bf16[96,2176]{1,0:T(8,128)(2,1)S(1)} %get-tuple-element.217), channel_id=1, source_target_pairs={{0,4},{1,5},{2,6},{3,7},{4,0},{5,1},{6,2},{7,3},{8,12},{9,13},{10,... | collective-permute-start | bytes 1253384 | tf_op jit(solution)/shard_map/ppermute | solution.py:35
  167.8 18.6 %collective-permute-start.38 = (bf16[96,2176]{1,0:T(8,128)(2,1)S(1)}, bf16[96,2176]{1,0:T(8,128)(2,1)S(1)}, u32[]{:S(2)}, u32[]{:S(2)}) collective-permute-start(bf16[96,2176]{1,0:T(8,128)(2,1)S(1)} %get-tuple-element.218), channel_id=1, source_target_pairs={{0,6},{1,7},{2,4},{3,5},{4,2},{5,3},{6,0},{7,1},{8,14},{9,15},{10,... | collective-permute-start | bytes 1253384 | tf_op jit(solution)/shard_map/ppermute | solution.py:35
  170.1 22.0 %collective-permute-start.43 = (bf16[96,768]{1,0:T(8,128)(2,1)S(1)}, bf16[96,768]{1,0:T(8,128)(2,1)S(1)}, u32[]{:S(2)}, u32[]{:S(2)}) collective-permute-start(bf16[96,768]{1,0:T(8,128)(2,1)S(1)} %get-tuple-element.254), channel_id=1, source_target_pairs={{0,16},{8,24},{16,0},{24,8},{1,17},{9,25},{17,1},{25,9},{2,18},{10... | collective-permute-start | bytes 442376 | tf_op jit(solution)/shard_map/ppermute | solution.py:35
  190.7 10.1 %collective-permute-start.41 = (bf16[96,1344]{1,0:T(8,128)(2,1)S(1)}, bf16[96,1344]{1,0:T(8,128)(2,1)S(1)}, u32[]{:S(2)}, u32[]{:S(2)}) collective-permute-start(bf16[96,1344]{1,0:T(8,128)(2,1)S(1)} %get-tuple-element.229), channel_id=1, source_target_pairs={{0,8},{8,0},{16,24},{24,16},{1,9},{9,1},{17,25},{25,17},{2,10},{10... | collective-permute-start | bytes 774152 | tf_op jit(solution)/shard_map/ppermute | solution.py:35
  190.8 10.4 %collective-permute-start.46 = (bf16[96,768]{1,0:T(8,128)(2,1)S(1)}, bf16[96,768]{1,0:T(8,128)(2,1)S(1)}, u32[]{:S(2)}, u32[]{:S(2)}) collective-permute-start(bf16[96,768]{1,0:T(8,128)(2,1)S(1)} %get-tuple-element.235), channel_id=1, source_target_pairs={{0,16},{8,24},{16,0},{24,8},{1,17},{9,25},{17,1},{25,9},{2,18},{10... | collective-permute-start | bytes 442376 | tf_op jit(solution)/shard_map/ppermute | solution.py:35
  201.1 12.8 %collective-permute-start.44 = (bf16[96,1216]{1,0:T(8,128)(2,1)S(1)}, bf16[96,1216]{1,0:T(8,128)(2,1)S(1)}, u32[]{:S(2)}, u32[]{:S(2)}) collective-permute-start(bf16[96,1216]{1,0:T(8,128)(2,1)S(1)} %concatenate.45), channel_id=1, source_target_pairs={{0,16},{8,24},{16,0},{24,8},{1,17},{9,25},{17,1},{25,9},{2,18},{10... | collective-permute-start | bytes 700424 | tf_op jit(solution)/shard_map/ppermute | solution.py:35
  201.4 20.7 %collective-permute-start.47 = (bf16[96,1536]{1,0:T(8,128)(2,1)S(1)}, bf16[96,1536]{1,0:T(8,128)(2,1)S(1)}, u32[]{:S(2)}, u32[]{:S(2)}) collective-permute-start(bf16[96,1536]{1,0:T(8,128)(2,1)S(1)} %add_convert_fusion.2), channel_id=1, source_target_pairs={{0,8},{8,0},{16,24},{24,16},{1,9},{9,1},{17,25},{25,17},{2,10},{10... | collective-permute-start | bytes 884744 | tf_op jit(solution)/shard_map/ppermute | solution.py:35
  214.0 9.8 %collective-permute-start.48 = (bf16[96,960]{1,0:T(8,128)(2,1)S(1)}, bf16[96,960]{1,0:T(8,128)(2,1)S(1)}, u32[]{:S(2)}, u32[]{:S(2)}) collective-permute-start(bf16[96,960]{1,0:T(8,128)(2,1)S(1)} %add_convert_fusion.4), channel_id=1, source_target_pairs={{0,8},{8,0},{16,24},{24,16},{1,9},{9,1},{17,25},{25,17},{2,10},{10... | collective-permute-start | bytes 552968 | tf_op jit(solution)/shard_map/ppermute | solution.py:35
  215.3 6.3 %collective-permute-start.45 = (bf16[96,256]{1,0:T(8,128)(2,1)S(1)}, bf16[96,256]{1,0:T(8,128)(2,1)S(1)}, u32[]{:S(2)}, u32[]{:S(2)}) collective-permute-start(bf16[96,256]{1,0:T(8,128)(2,1)S(1)} %pad_maximum_fusion.4), channel_id=1, source_target_pairs={{1,16},{3,18},{5,20},{7,22},{9,24},{11,26},{13,28},{15,30},{16,1},... | collective-permute-start | bytes 147464 | tf_op jit(solution)/shard_map/ppermute | solution.py:52
  (24 other events, 51.0 us)
